TPU v7x, 128 devices: a whole 4x4x4 slice. The times are simulated.
128 devices in a mesh: mem: 4 (over y), lat: 8 (over z_lo, x), lon: 4 (over z_hi, core).
Axes of the slice: x: 4, y: 4, z: 4 (z_hi: 2, z_lo: 2; z = z_hi * 2 + z_lo), core: 2. Of those that a mesh axis runs over, the one named last changes fastest.
Arguments:
- control: float32 [20, 128, 512], P('mem', 'lat', 'lon'), may hold values from -7 to 7
- anomalies: bfloat16 [20, 2, 4, 70, 128, 512], P('mem', None, None, None, 'lat', 'lon'), may hold values from -6 to 6
- diffusivity: float32 [128, 512], P('lat', 'lon'), may hold values from 0.03 to 0.24
- loc_norm: float32 [128, 512], P('lat', 'lon'), may hold values from 0.5 to 1.5
- innovation: float32 [4, 70, 128, 512], P(None, None, 'lat', 'lon'), may hold values from -6 to 6
- obs_precision: float32 [4, 70, 128, 512], P(None, None, 'lat', 'lon'), may hold values from 0.03 to 0.9
- obs_time: int32 [128, 512], P('lat', 'lon'), may hold values from 0 to 1
Outputs:
- gradient: float32 [20, 128, 512], P('mem', 'lat', 'lon')
- cost: float32 [], replicated
All inputs are finite; a program needn't handle non-finite values.
Results may differ from a plain program's by a relative error of at most 0.0025.
Values may be sent and summed in bfloat16 or wider, within the bound.
No kernel may reach another device: no remote copies, remote signals or barrier semaphores. Data moves between devices by JAX's collectives and lax.ppermute only.
A program may use at most 64 MiB of HBM per device.

v0:
```python
import math

import jax
import jax.numpy as jnp
from jax import lax
from jax.sharding import PartitionSpec as P

TIMES = 2
PASSES = 10


def with_halo(cells, sides, width, closed):
    for axis, dim in sides:
        count = lax.axis_size(axis)
        ends = count if closed else count - 1
        head = lax.slice_in_dim(cells, 0, width, axis=dim)
        tail = lax.slice_in_dim(cells, cells.shape[dim] - width, cells.shape[dim], axis=dim)
        cells = jnp.concatenate(
            [
                lax.ppermute(tail, axis, [(i, (i + 1) % count) for i in range(ends)]),
                cells,
                lax.ppermute(head, axis, [((i + 1) % count, i) for i in range(ends)]),
            ],
            axis=dim,
        )
    return cells


def rim_stencil(field):
    lat_wide = with_halo(field, (("lat", 1),), 1, False)
    lon_wide = with_halo(field, (("lon", 2),), 1, True)
    return (
        lat_wide[:, 2:, :]
        + lat_wide[:, :-2, :]
        + lon_wide[:, :, 2:]
        + lon_wide[:, :, :-2]
        - 4.0 * field
    )


def on_device(control, anomalies, diffusivity, loc_norm, innovation, obs_precision, obs_time):
    rows = control.shape[1]
    members = control.shape[0] * lax.axis_size("mem")
    lat_total = rows * lax.axis_size("lat")
    lon_total = control.shape[2] * lax.axis_size("lon")
    factor = 1.0 / math.sqrt(members - 1)

    def forward_pass(index, state):
        return state + diffusivity * rim_stencil(state)

    spread = lax.fori_loop(0, PASSES, forward_pass, control)
    weights = (loc_norm * spread).astype(jnp.bfloat16)
    chosen = [obs_time == t for t in range(TIMES)]
    partial_total = None
    for t in range(TIMES):
        masked = weights * chosen[t].astype(jnp.bfloat16)
        term = jnp.einsum(
            "mflyx,myx->flyx", anomalies[:, t], masked, preferred_element_type=jnp.float32
        )
        partial_total = term if partial_total is None else partial_total + term
    share = innovation.shape[0] // lax.axis_size("mem")
    first = lax.axis_index("mem") * share
    increment = factor * lax.psum(partial_total.astype(jnp.bfloat16), "mem").astype(jnp.float32)
    misfit = increment - innovation
    scaled = obs_precision * misfit
    weighted = scaled.astype(jnp.bfloat16)
    misfit_share = lax.dynamic_slice_in_dim(misfit, first, share, 0)
    scaled_share = lax.dynamic_slice_in_dim(scaled, first, share, 0)
    residual_part = jnp.sum(misfit_share * scaled_share)
    pulled = None
    for t in range(TIMES):
        term = jnp.einsum(
            "mflyx,flyx->myx", anomalies[:, t], weighted, preferred_element_type=jnp.float32
        )
        term = chosen[t].astype(jnp.float32) * term
        pulled = term if pulled is None else pulled + term
    pulled = factor * pulled
    source = loc_norm * pulled

    def adjoint_pass(index, state):
        return state + rim_stencil(diffusivity * state)

    back = lax.fori_loop(0, PASSES, adjoint_pass, source)
    gradient = control + back
    local_terms = 0.5 * (jnp.sum(control * control) + residual_part)
    total = lax.psum(local_terms, ("mem", "lat", "lon"))
    cost = total / (members * lat_total * lon_total)
    return (gradient, cost)


def solution(mesh):
    return jax.shard_map(
        on_device,
        mesh=mesh,
        in_specs=(
            P("mem", "lat", "lon"),
            P("mem", None, None, None, "lat", "lon"),
            P("lat", "lon"),
            P("lat", "lon"),
            P(None, None, "lat", "lon"),
            P(None, None, "lat", "lon"),
            P("lat", "lon"),
        ),
        out_specs=(P("mem", "lat", "lon"), P()),
        check_vma=False,
    )
```

profile of v0, /device:TPU:1, one launch (start us, length us, event | category | flops | bytes accessed | tf_op | source)
XLA Modules:
  0.0 424.0 jit_solution(13356592166244427922)
XLA Ops:
  8.7 133.4 %while.20 = (s32[]{:T(128)}, f32[5,16,128]{2,1,0:T(8,128)S(1)}, f32[16,128]{1,0:T(8,128)}, s32[]{:T(128)}) while((s32[]{:T(128)}, f32[5,16,128]{2,1,0:T(8,128)S(1)}, f32[16,128]{1,0:T(8,128)}, s32[]{:T(128)}) %tuple.57), condition=%wide.region_1.0_spmd, body=%wide.region_0.0_spmd.sunk | while | flops 112642 | bytes 212565 | solution.py:51
  8.7 3.9 collective-permute-start.2
  14.1 4.5 %collective-permute-start = (f32[5,16,1]{2,1,0:T(8,128)S(1)}, f32[5,16,1]{2,1,0:T(8,128)S(1)}, u32[]{:S(2)}, u32[]{:S(2)}) collective-permute-start(f32[5,16,1]{2,1,0:T(8,128)S(1)} %get-tuple-element.118), channel_id=1, source_target_pairs={{0,1},{1,2},{2,3},{3,0},{4,5},{5,6},{6,7},{7,4},{8,9},{9,10},{10,1... | collective-permute-start | bytes 968 | tf_op jit(solution)/shard_map/while/body/eval_jaxpr/ppermute | solution.py:20
  24.3 4.3 %collective-permute-start.2 = (f32[5,1,128]{2,1,0:T(1,128)S(1)}, f32[5,1,128]{2,1,0:T(1,128)S(1)}, u32[]{:S(2)}, u32[]{:S(2)}) collective-permute-start(f32[5,1,128]{2,1,0:T(1,128)S(1)} %get-tuple-element.120), channel_id=1, source_target_pairs={{0,4},{4,8},{8,12},{12,16},{16,20},{20,24},{24,28},{1,5},{5,9},{9,... | collective-permute-start | bytes 7688 | tf_op jit(solution)/shard_map/while/body/eval_jaxpr/ppermute | solution.py:20
  36.4 4.3 %collective-permute-start.2 = (f32[5,1,128]{2,1,0:T(1,128)S(1)}, f32[5,1,128]{2,1,0:T(1,128)S(1)}, u32[]{:S(2)}, u32[]{:S(2)}) collective-permute-start(f32[5,1,128]{2,1,0:T(1,128)S(1)} %get-tuple-element.120), channel_id=1, source_target_pairs={{0,4},{4,8},{8,12},{12,16},{16,20},{20,24},{24,28},{1,5},{5,9},{9,... | collective-permute-start | bytes 7688 | tf_op jit(solution)/shard_map/while/body/eval_jaxpr/ppermute | solution.py:20
  48.4 4.3 %collective-permute-start.2 = (f32[5,1,128]{2,1,0:T(1,128)S(1)}, f32[5,1,128]{2,1,0:T(1,128)S(1)}, u32[]{:S(2)}, u32[]{:S(2)}) collective-permute-start(f32[5,1,128]{2,1,0:T(1,128)S(1)} %get-tuple-element.120), channel_id=1, source_target_pairs={{0,4},{4,8},{8,12},{12,16},{16,20},{20,24},{24,28},{1,5},{5,9},{9,... | collective-permute-start | bytes 7688 | tf_op jit(solution)/shard_map/while/body/eval_jaxpr/ppermute | solution.py:20
  60.5 4.5 %collective-permute-start.2 = (f32[5,1,128]{2,1,0:T(1,128)S(1)}, f32[5,1,128]{2,1,0:T(1,128)S(1)}, u32[]{:S(2)}, u32[]{:S(2)}) collective-permute-start(f32[5,1,128]{2,1,0:T(1,128)S(1)} %get-tuple-element.120), channel_id=1, source_target_pairs={{0,4},{4,8},{8,12},{12,16},{16,20},{20,24},{24,28},{1,5},{5,9},{9,... | collective-permute-start | bytes 7688 | tf_op jit(solution)/shard_map/while/body/eval_jaxpr/ppermute | solution.py:20
  72.9 6.0 %collective-permute-start.2 = (f32[5,1,128]{2,1,0:T(1,128)S(1)}, f32[5,1,128]{2,1,0:T(1,128)S(1)}, u32[]{:S(2)}, u32[]{:S(2)}) collective-permute-start(f32[5,1,128]{2,1,0:T(1,128)S(1)} %get-tuple-element.120), channel_id=1, source_target_pairs={{0,4},{4,8},{8,12},{12,16},{16,20},{20,24},{24,28},{1,5},{5,9},{9,... | collective-permute-start | bytes 7688 | tf_op jit(solution)/shard_map/while/body/eval_jaxpr/ppermute | solution.py:20
  86.7 6.0 %collective-permute-start.2 = (f32[5,1,128]{2,1,0:T(1,128)S(1)}, f32[5,1,128]{2,1,0:T(1,128)S(1)}, u32[]{:S(2)}, u32[]{:S(2)}) collective-permute-start(f32[5,1,128]{2,1,0:T(1,128)S(1)} %get-tuple-element.120), channel_id=1, source_target_pairs={{0,4},{4,8},{8,12},{12,16},{16,20},{20,24},{24,28},{1,5},{5,9},{9,... | collective-permute-start | bytes 7688 | tf_op jit(solution)/shard_map/while/body/eval_jaxpr/ppermute | solution.py:20
  100.6 6.0 %collective-permute-start.2 = (f32[5,1,128]{2,1,0:T(1,128)S(1)}, f32[5,1,128]{2,1,0:T(1,128)S(1)}, u32[]{:S(2)}, u32[]{:S(2)}) collective-permute-start(f32[5,1,128]{2,1,0:T(1,128)S(1)} %get-tuple-element.120), channel_id=1, source_target_pairs={{0,4},{4,8},{8,12},{12,16},{16,20},{20,24},{24,28},{1,5},{5,9},{9,... | collective-permute-start | bytes 7688 | tf_op jit(solution)/shard_map/while/body/eval_jaxpr/ppermute | solution.py:20
  114.4 6.0 %collective-permute-start.2 = (f32[5,1,128]{2,1,0:T(1,128)S(1)}, f32[5,1,128]{2,1,0:T(1,128)S(1)}, u32[]{:S(2)}, u32[]{:S(2)}) collective-permute-start(f32[5,1,128]{2,1,0:T(1,128)S(1)} %get-tuple-element.120), channel_id=1, source_target_pairs={{0,4},{4,8},{8,12},{12,16},{16,20},{20,24},{24,28},{1,5},{5,9},{9,... | collective-permute-start | bytes 7688 | tf_op jit(solution)/shard_map/while/body/eval_jaxpr/ppermute | solution.py:20
  128.3 6.0 %collective-permute-start.2 = (f32[5,1,128]{2,1,0:T(1,128)S(1)}, f32[5,1,128]{2,1,0:T(1,128)S(1)}, u32[]{:S(2)}, u32[]{:S(2)}) collective-permute-start(f32[5,1,128]{2,1,0:T(1,128)S(1)} %get-tuple-element.120), channel_id=1, source_target_pairs={{0,4},{4,8},{8,12},{12,16},{16,20},{20,24},{24,28},{1,5},{5,9},{9,... | collective-permute-start | bytes 7688 | tf_op jit(solution)/shard_map/while/body/eval_jaxpr/ppermute | solution.py:20
  142.1 6.6 %multiply_reduce_fusion.2 = (f32[16,128,4,70]{1,0,3,2:T(8,128)S(1)}, f32[16,128,4,70]{1,0,3,2:T(8,128)S(1)}) fusion(f32[16,128,5]{1,0,2:T(8,128)S(1)} %get-tuple-element.70, bf16[5,2,4,70,16,128]{5,4,3,2,1,0:T(8,128)(2,1)} %param.12, f32[16,128,5]{1,0,2:T(8,128)S(1)} %get-tuple-element.69), kind=kLoop, calls=%fused_computation.22 | loop fusion | flops 16056320 | bytes 16138240 | tf_op jit(solution)/shard_map/mflyx,myx->flyx/dot_general | solution.py:57
  150.0 51.9 %all-reduce.2.cloned.1.call-done = bf16[4,70,16,128]{3,2,1,0:T(8,128)(2,1)} async-done(((bf16[4,70,16,128]{3,2,1,0:T(8,128)(2,1)}), bf16[4,70,16,128]{3,2,1,0:T(8,128)(2,1)}) %all-reduce.2.cloned.1.call-update) | async-done | bytes 1146896 | tf_op jit(solution)/shard_map/psum | solution.py:63
  202.0 4.7 %bitcast_convert_fusion = (f32[16,128,4,70]{1,0,3,2:T(8,128)S(1)}, f32[4,70,16,128]{3,2,1,0:T(8,128)S(1)}, f32[4,70,16,128]{3,2,1,0:T(8,128)}) fusion(f32[4,70,16,128]{3,2,1,0:T(8,128)} %param.16, f32[4,70,16,128]{3,2,1,0:T(8,128)} %param.15, bf16[4,70,16,128]{3,2,1,0:T(8,128)(2,1)} %all-reduce.2.cloned.1.call-done), kind=kLoop, calls=%fused_computation.27 | loop fusion | flops 3440640 | bytes 12615680
  206.6 5.9 %multiply_reduce_fusion.1 = (f32[16,128,5]{1,0,2:T(8,128)S(1)}, f32[16,128,5]{1,0,2:T(8,128)S(1)}) fusion(f32[16,128,4,70]{1,0,3,2:T(8,128)S(1)} %get-tuple-element.58, bf16[5,2,4,70,16,128]{5,4,3,2,1,0:T(8,128)(2,1)} %param.12), kind=kLoop, calls=%fused_computation.21 | loop fusion | flops 17182720 | bytes 13844480 | tf_op jit(solution)/shard_map/mflyx,flyx->myx/dot_general | solution.py:72
  212.6 125.6 %while.21 = (s32[]{:T(128)}, f32[5,16,128]{2,1,0:T(8,128)S(1)}, f32[16,128]{1,0:T(8,128)S(1)}, s32[]{:T(128)}) while((s32[]{:T(128)}, f32[5,16,128]{2,1,0:T(8,128)S(1)}, f32[16,128]{1,0:T(8,128)S(1)}, s32[]{:T(128)}) %tuple.65), condition=%wide.region_4.0_spmd, body=%wide.region_3.0_spmd.sunk | while | flops 112642 | bytes 253525 | solution.py:83
  217.1 4.8 %collective-permute-start.4 = (f32[5,16,1]{2,1,0:T(8,128)S(1)}, f32[5,16,1]{2,1,0:T(8,128)S(1)}, u32[]{:S(2)}, u32[]{:S(2)}) collective-permute-start(f32[5,16,1]{2,1,0:T(8,128)S(1)} %get-tuple-element.125), channel_id=1, source_target_pairs={{0,1},{1,2},{2,3},{3,0},{4,5},{5,6},{6,7},{7,4},{8,9},{9,10},{10,1... | collective-permute-start | bytes 968 | tf_op jit(solution)/shard_map/while/body/eval_jaxpr/ppermute | solution.py:20
  223.1 3.8 collective-permute-done.5
  227.0 4.3 %collective-permute-start.6 = (f32[5,1,128]{2,1,0:T(1,128)S(1)}, f32[5,1,128]{2,1,0:T(1,128)S(1)}, u32[]{:S(2)}, u32[]{:S(2)}) collective-permute-start(f32[5,1,128]{2,1,0:T(1,128)S(1)} %get-tuple-element.127), channel_id=1, source_target_pairs={{0,4},{4,8},{8,12},{12,16},{16,20},{20,24},{24,28},{1,5},{5,9},{9,... | collective-permute-start | bytes 7688 | tf_op jit(solution)/shard_map/while/body/eval_jaxpr/ppermute | solution.py:20
  234.1 3.8 collective-permute-done.5
  238.1 4.3 %collective-permute-start.6 = (f32[5,1,128]{2,1,0:T(1,128)S(1)}, f32[5,1,128]{2,1,0:T(1,128)S(1)}, u32[]{:S(2)}, u32[]{:S(2)}) collective-permute-start(f32[5,1,128]{2,1,0:T(1,128)S(1)} %get-tuple-element.127), channel_id=1, source_target_pairs={{0,4},{4,8},{8,12},{12,16},{16,20},{20,24},{24,28},{1,5},{5,9},{9,... | collective-permute-start | bytes 7688 | tf_op jit(solution)/shard_map/while/body/eval_jaxpr/ppermute | solution.py:20
  245.1 3.8 collective-permute-done.5
  249.1 4.3 %collective-permute-start.6 = (f32[5,1,128]{2,1,0:T(1,128)S(1)}, f32[5,1,128]{2,1,0:T(1,128)S(1)}, u32[]{:S(2)}, u32[]{:S(2)}) collective-permute-start(f32[5,1,128]{2,1,0:T(1,128)S(1)} %get-tuple-element.127), channel_id=1, source_target_pairs={{0,4},{4,8},{8,12},{12,16},{16,20},{20,24},{24,28},{1,5},{5,9},{9,... | collective-permute-start | bytes 7688 | tf_op jit(solution)/shard_map/while/body/eval_jaxpr/ppermute | solution.py:20
  256.2 3.8 collective-permute-done.5
  260.2 4.9 %collective-permute-start.6 = (f32[5,1,128]{2,1,0:T(1,128)S(1)}, f32[5,1,128]{2,1,0:T(1,128)S(1)}, u32[]{:S(2)}, u32[]{:S(2)}) collective-permute-start(f32[5,1,128]{2,1,0:T(1,128)S(1)} %get-tuple-element.127), channel_id=1, source_target_pairs={{0,4},{4,8},{8,12},{12,16},{16,20},{20,24},{24,28},{1,5},{5,9},{9,... | collective-permute-start | bytes 7688 | tf_op jit(solution)/shard_map/while/body/eval_jaxpr/ppermute | solution.py:20
  272.5 5.8 %collective-permute-start.6 = (f32[5,1,128]{2,1,0:T(1,128)S(1)}, f32[5,1,128]{2,1,0:T(1,128)S(1)}, u32[]{:S(2)}, u32[]{:S(2)}) collective-permute-start(f32[5,1,128]{2,1,0:T(1,128)S(1)} %get-tuple-element.127), channel_id=1, source_target_pairs={{0,4},{4,8},{8,12},{12,16},{16,20},{20,24},{24,28},{1,5},{5,9},{9,... | collective-permute-start | bytes 7688 | tf_op jit(solution)/shard_map/while/body/eval_jaxpr/ppermute | solution.py:20
  285.6 5.8 %collective-permute-start.6 = (f32[5,1,128]{2,1,0:T(1,128)S(1)}, f32[5,1,128]{2,1,0:T(1,128)S(1)}, u32[]{:S(2)}, u32[]{:S(2)}) collective-permute-start(f32[5,1,128]{2,1,0:T(1,128)S(1)} %get-tuple-element.127), channel_id=1, source_target_pairs={{0,4},{4,8},{8,12},{12,16},{16,20},{20,24},{24,28},{1,5},{5,9},{9,... | collective-permute-start | bytes 7688 | tf_op jit(solution)/shard_map/while/body/eval_jaxpr/ppermute | solution.py:20
  298.8 5.8 %collective-permute-start.6 = (f32[5,1,128]{2,1,0:T(1,128)S(1)}, f32[5,1,128]{2,1,0:T(1,128)S(1)}, u32[]{:S(2)}, u32[]{:S(2)}) collective-permute-start(f32[5,1,128]{2,1,0:T(1,128)S(1)} %get-tuple-element.127), channel_id=1, source_target_pairs={{0,4},{4,8},{8,12},{12,16},{16,20},{20,24},{24,28},{1,5},{5,9},{9,... | collective-permute-start | bytes 7688 | tf_op jit(solution)/shard_map/while/body/eval_jaxpr/ppermute | solution.py:20
  311.9 5.8 %collective-permute-start.6 = (f32[5,1,128]{2,1,0:T(1,128)S(1)}, f32[5,1,128]{2,1,0:T(1,128)S(1)}, u32[]{:S(2)}, u32[]{:S(2)}) collective-permute-start(f32[5,1,128]{2,1,0:T(1,128)S(1)} %get-tuple-element.127), channel_id=1, source_target_pairs={{0,4},{4,8},{8,12},{12,16},{16,20},{20,24},{24,28},{1,5},{5,9},{9,... | collective-permute-start | bytes 7688 | tf_op jit(solution)/shard_map/while/body/eval_jaxpr/ppermute | solution.py:20
  325.1 5.8 %collective-permute-start.6 = (f32[5,1,128]{2,1,0:T(1,128)S(1)}, f32[5,1,128]{2,1,0:T(1,128)S(1)}, u32[]{:S(2)}, u32[]{:S(2)}) collective-permute-start(f32[5,1,128]{2,1,0:T(1,128)S(1)} %get-tuple-element.127), channel_id=1, source_target_pairs={{0,4},{4,8},{8,12},{12,16},{16,20},{20,24},{24,28},{1,5},{5,9},{9,... | collective-permute-start | bytes 7688 | tf_op jit(solution)/shard_map/while/body/eval_jaxpr/ppermute | solution.py:20
  342.5 72.9 %psum.15 = f32[]{:T(128)} all-reduce(f32[]{:T(128)S(6)} %mul_shard_map.3), channel_id=1, replica_groups=mesh['mem'=4,'lat'=8,'lon'=4] {'mem','lat','lon'}, use_global_device_ids=true, to_apply=%region_7.0 | all-reduce | flops 1 | bytes 8 | tf_op jit(solution)/shard_map/psum | solution.py:86
  (233 shorter events, 141.7 us)
Async XLA Ops:
  7.2 194.8 %all-reduce.2.cloned.1.call-start = ((), (), s32[]{:S(2)}) async-start(), calls=%async_computation | async-start | bytes 2293760 | tf_op jit(solution)/shard_map/psum | solution.py:63
  8.7 14.7 %collective-permute-start.2 = (f32[5,1,128]{2,1,0:T(1,128)S(1)}, f32[5,1,128]{2,1,0:T(1,128)S(1)}, u32[]{:S(2)}, u32[]{:S(2)}) collective-permute-start(f32[5,1,128]{2,1,0:T(1,128)S(1)} %get-tuple-element.120), channel_id=1, source_target_pairs={{0,4},{4,8},{8,12},{12,16},{16,20},{20,24},{24,28},{1,5},{5,9},{9,... | collective-permute-start | bytes 7688 | tf_op jit(solution)/shard_map/while/body/eval_jaxpr/ppermute | solution.py:20
  12.7 10.8 %collective-permute-start.3 = (f32[5,1,128]{2,1,0:T(1,128)S(1)}, f32[5,1,128]{2,1,0:T(1,128)S(1)}, u32[]{:S(2)}, u32[]{:S(2)}) collective-permute-start(f32[5,1,128]{2,1,0:T(1,128)S(1)} %get-tuple-element.121), channel_id=1, source_target_pairs={{4,0},{8,4},{12,8},{16,12},{20,16},{24,20},{28,24},{5,1},{9,5},{13... | collective-permute-start | bytes 7688 | tf_op jit(solution)/shard_map/while/body/eval_jaxpr/ppermute | solution.py:22
  24.3 11.3 %collective-permute-start.2 = (f32[5,1,128]{2,1,0:T(1,128)S(1)}, f32[5,1,128]{2,1,0:T(1,128)S(1)}, u32[]{:S(2)}, u32[]{:S(2)}) collective-permute-start(f32[5,1,128]{2,1,0:T(1,128)S(1)} %get-tuple-element.120), channel_id=1, source_target_pairs={{0,4},{4,8},{8,12},{12,16},{16,20},{20,24},{24,28},{1,5},{5,9},{9,... | collective-permute-start | bytes 7688 | tf_op jit(solution)/shard_map/while/body/eval_jaxpr/ppermute | solution.py:20
  36.4 11.1 %collective-permute-start.2 = (f32[5,1,128]{2,1,0:T(1,128)S(1)}, f32[5,1,128]{2,1,0:T(1,128)S(1)}, u32[]{:S(2)}, u32[]{:S(2)}) collective-permute-start(f32[5,1,128]{2,1,0:T(1,128)S(1)} %get-tuple-element.120), channel_id=1, source_target_pairs={{0,4},{4,8},{8,12},{12,16},{16,20},{20,24},{24,28},{1,5},{5,9},{9,... | collective-permute-start | bytes 7688 | tf_op jit(solution)/shard_map/while/body/eval_jaxpr/ppermute | solution.py:20
  48.4 11.2 %collective-permute-start.2 = (f32[5,1,128]{2,1,0:T(1,128)S(1)}, f32[5,1,128]{2,1,0:T(1,128)S(1)}, u32[]{:S(2)}, u32[]{:S(2)}) collective-permute-start(f32[5,1,128]{2,1,0:T(1,128)S(1)} %get-tuple-element.120), channel_id=1, source_target_pairs={{0,4},{4,8},{8,12},{12,16},{16,20},{20,24},{24,28},{1,5},{5,9},{9,... | collective-permute-start | bytes 7688 | tf_op jit(solution)/shard_map/while/body/eval_jaxpr/ppermute | solution.py:20
  60.5 11.5 %collective-permute-start.2 = (f32[5,1,128]{2,1,0:T(1,128)S(1)}, f32[5,1,128]{2,1,0:T(1,128)S(1)}, u32[]{:S(2)}, u32[]{:S(2)}) collective-permute-start(f32[5,1,128]{2,1,0:T(1,128)S(1)} %get-tuple-element.120), channel_id=1, source_target_pairs={{0,4},{4,8},{8,12},{12,16},{16,20},{20,24},{24,28},{1,5},{5,9},{9,... | collective-permute-start | bytes 7688 | tf_op jit(solution)/shard_map/while/body/eval_jaxpr/ppermute | solution.py:20
  65.0 7.0 %collective-permute-start.3 = (f32[5,1,128]{2,1,0:T(1,128)S(1)}, f32[5,1,128]{2,1,0:T(1,128)S(1)}, u32[]{:S(2)}, u32[]{:S(2)}) collective-permute-start(f32[5,1,128]{2,1,0:T(1,128)S(1)} %get-tuple-element.121), channel_id=1, source_target_pairs={{4,0},{8,4},{12,8},{16,12},{20,16},{24,20},{28,24},{5,1},{9,5},{13... | collective-permute-start | bytes 7688 | tf_op jit(solution)/shard_map/while/body/eval_jaxpr/ppermute | solution.py:22
  72.9 13.0 %collective-permute-start.2 = (f32[5,1,128]{2,1,0:T(1,128)S(1)}, f32[5,1,128]{2,1,0:T(1,128)S(1)}, u32[]{:S(2)}, u32[]{:S(2)}) collective-permute-start(f32[5,1,128]{2,1,0:T(1,128)S(1)} %get-tuple-element.120), channel_id=1, source_target_pairs={{0,4},{4,8},{8,12},{12,16},{16,20},{20,24},{24,28},{1,5},{5,9},{9,... | collective-permute-start | bytes 7688 | tf_op jit(solution)/shard_map/while/body/eval_jaxpr/ppermute | solution.py:20
  78.8 7.0 %collective-permute-start.3 = (f32[5,1,128]{2,1,0:T(1,128)S(1)}, f32[5,1,128]{2,1,0:T(1,128)S(1)}, u32[]{:S(2)}, u32[]{:S(2)}) collective-permute-start(f32[5,1,128]{2,1,0:T(1,128)S(1)} %get-tuple-element.121), channel_id=1, source_target_pairs={{4,0},{8,4},{12,8},{16,12},{20,16},{24,20},{28,24},{5,1},{9,5},{13... | collective-permute-start | bytes 7688 | tf_op jit(solution)/shard_map/while/body/eval_jaxpr/ppermute | solution.py:22
  86.7 13.0 %collective-permute-start.2 = (f32[5,1,128]{2,1,0:T(1,128)S(1)}, f32[5,1,128]{2,1,0:T(1,128)S(1)}, u32[]{:S(2)}, u32[]{:S(2)}) collective-permute-start(f32[5,1,128]{2,1,0:T(1,128)S(1)} %get-tuple-element.120), channel_id=1, source_target_pairs={{0,4},{4,8},{8,12},{12,16},{16,20},{20,24},{24,28},{1,5},{5,9},{9,... | collective-permute-start | bytes 7688 | tf_op jit(solution)/shard_map/while/body/eval_jaxpr/ppermute | solution.py:20
  92.7 7.0 %collective-permute-start.3 = (f32[5,1,128]{2,1,0:T(1,128)S(1)}, f32[5,1,128]{2,1,0:T(1,128)S(1)}, u32[]{:S(2)}, u32[]{:S(2)}) collective-permute-start(f32[5,1,128]{2,1,0:T(1,128)S(1)} %get-tuple-element.121), channel_id=1, source_target_pairs={{4,0},{8,4},{12,8},{16,12},{20,16},{24,20},{28,24},{5,1},{9,5},{13... | collective-permute-start | bytes 7688 | tf_op jit(solution)/shard_map/while/body/eval_jaxpr/ppermute | solution.py:22
  100.6 13.0 %collective-permute-start.2 = (f32[5,1,128]{2,1,0:T(1,128)S(1)}, f32[5,1,128]{2,1,0:T(1,128)S(1)}, u32[]{:S(2)}, u32[]{:S(2)}) collective-permute-start(f32[5,1,128]{2,1,0:T(1,128)S(1)} %get-tuple-element.120), channel_id=1, source_target_pairs={{0,4},{4,8},{8,12},{12,16},{16,20},{20,24},{24,28},{1,5},{5,9},{9,... | collective-permute-start | bytes 7688 | tf_op jit(solution)/shard_map/while/body/eval_jaxpr/ppermute | solution.py:20
  114.4 13.0 %collective-permute-start.2 = (f32[5,1,128]{2,1,0:T(1,128)S(1)}, f32[5,1,128]{2,1,0:T(1,128)S(1)}, u32[]{:S(2)}, u32[]{:S(2)}) collective-permute-start(f32[5,1,128]{2,1,0:T(1,128)S(1)} %get-tuple-element.120), channel_id=1, source_target_pairs={{0,4},{4,8},{8,12},{12,16},{16,20},{20,24},{24,28},{1,5},{5,9},{9,... | collective-permute-start | bytes 7688 | tf_op jit(solution)/shard_map/while/body/eval_jaxpr/ppermute | solution.py:20
  128.3 13.0 %collective-permute-start.2 = (f32[5,1,128]{2,1,0:T(1,128)S(1)}, f32[5,1,128]{2,1,0:T(1,128)S(1)}, u32[]{:S(2)}, u32[]{:S(2)}) collective-permute-start(f32[5,1,128]{2,1,0:T(1,128)S(1)} %get-tuple-element.120), channel_id=1, source_target_pairs={{0,4},{4,8},{8,12},{12,16},{16,20},{20,24},{24,28},{1,5},{5,9},{9,... | collective-permute-start | bytes 7688 | tf_op jit(solution)/shard_map/while/body/eval_jaxpr/ppermute | solution.py:20
  212.7 14.2 %collective-permute-start.6 = (f32[5,1,128]{2,1,0:T(1,128)S(1)}, f32[5,1,128]{2,1,0:T(1,128)S(1)}, u32[]{:S(2)}, u32[]{:S(2)}) collective-permute-start(f32[5,1,128]{2,1,0:T(1,128)S(1)} %get-tuple-element.127), channel_id=1, source_target_pairs={{0,4},{4,8},{8,12},{12,16},{16,20},{20,24},{24,28},{1,5},{5,9},{9,... | collective-permute-start | bytes 7688 | tf_op jit(solution)/shard_map/while/body/eval_jaxpr/ppermute | solution.py:20
  215.8 11.1 %collective-permute-start.7 = (f32[5,1,128]{2,1,0:T(1,128)S(1)}, f32[5,1,128]{2,1,0:T(1,128)S(1)}, u32[]{:S(2)}, u32[]{:S(2)}) collective-permute-start(f32[5,1,128]{2,1,0:T(1,128)S(1)} %get-tuple-element.128), channel_id=1, source_target_pairs={{4,0},{8,4},{12,8},{16,12},{20,16},{24,20},{28,24},{5,1},{9,5},{13... | collective-permute-start | bytes 7688 | tf_op jit(solution)/shard_map/while/body/eval_jaxpr/ppermute | solution.py:22
  227.0 10.9 %collective-permute-start.6 = (f32[5,1,128]{2,1,0:T(1,128)S(1)}, f32[5,1,128]{2,1,0:T(1,128)S(1)}, u32[]{:S(2)}, u32[]{:S(2)}) collective-permute-start(f32[5,1,128]{2,1,0:T(1,128)S(1)} %get-tuple-element.127), channel_id=1, source_target_pairs={{0,4},{4,8},{8,12},{12,16},{16,20},{20,24},{24,28},{1,5},{5,9},{9,... | collective-permute-start | bytes 7688 | tf_op jit(solution)/shard_map/while/body/eval_jaxpr/ppermute | solution.py:20
  238.1 10.9 %collective-permute-start.6 = (f32[5,1,128]{2,1,0:T(1,128)S(1)}, f32[5,1,128]{2,1,0:T(1,128)S(1)}, u32[]{:S(2)}, u32[]{:S(2)}) collective-permute-start(f32[5,1,128]{2,1,0:T(1,128)S(1)} %get-tuple-element.127), channel_id=1, source_target_pairs={{0,4},{4,8},{8,12},{12,16},{16,20},{20,24},{24,28},{1,5},{5,9},{9,... | collective-permute-start | bytes 7688 | tf_op jit(solution)/shard_map/while/body/eval_jaxpr/ppermute | solution.py:20
  249.1 10.9 %collective-permute-start.6 = (f32[5,1,128]{2,1,0:T(1,128)S(1)}, f32[5,1,128]{2,1,0:T(1,128)S(1)}, u32[]{:S(2)}, u32[]{:S(2)}) collective-permute-start(f32[5,1,128]{2,1,0:T(1,128)S(1)} %get-tuple-element.127), channel_id=1, source_target_pairs={{0,4},{4,8},{8,12},{12,16},{16,20},{20,24},{24,28},{1,5},{5,9},{9,... | collective-permute-start | bytes 7688 | tf_op jit(solution)/shard_map/while/body/eval_jaxpr/ppermute | solution.py:20
  260.2 12.1 %collective-permute-start.6 = (f32[5,1,128]{2,1,0:T(1,128)S(1)}, f32[5,1,128]{2,1,0:T(1,128)S(1)}, u32[]{:S(2)}, u32[]{:S(2)}) collective-permute-start(f32[5,1,128]{2,1,0:T(1,128)S(1)} %get-tuple-element.127), channel_id=1, source_target_pairs={{0,4},{4,8},{8,12},{12,16},{16,20},{20,24},{24,28},{1,5},{5,9},{9,... | collective-permute-start | bytes 7688 | tf_op jit(solution)/shard_map/while/body/eval_jaxpr/ppermute | solution.py:20
  265.1 7.2 %collective-permute-start.7 = (f32[5,1,128]{2,1,0:T(1,128)S(1)}, f32[5,1,128]{2,1,0:T(1,128)S(1)}, u32[]{:S(2)}, u32[]{:S(2)}) collective-permute-start(f32[5,1,128]{2,1,0:T(1,128)S(1)} %get-tuple-element.128), channel_id=1, source_target_pairs={{4,0},{8,4},{12,8},{16,12},{20,16},{24,20},{28,24},{5,1},{9,5},{13... | collective-permute-start | bytes 7688 | tf_op jit(solution)/shard_map/while/body/eval_jaxpr/ppermute | solution.py:22
  272.5 13.0 %collective-permute-start.6 = (f32[5,1,128]{2,1,0:T(1,128)S(1)}, f32[5,1,128]{2,1,0:T(1,128)S(1)}, u32[]{:S(2)}, u32[]{:S(2)}) collective-permute-start(f32[5,1,128]{2,1,0:T(1,128)S(1)} %get-tuple-element.127), channel_id=1, source_target_pairs={{0,4},{4,8},{8,12},{12,16},{16,20},{20,24},{24,28},{1,5},{5,9},{9,... | collective-permute-start | bytes 7688 | tf_op jit(solution)/shard_map/while/body/eval_jaxpr/ppermute | solution.py:20
  278.2 7.2 %collective-permute-start.7 = (f32[5,1,128]{2,1,0:T(1,128)S(1)}, f32[5,1,128]{2,1,0:T(1,128)S(1)}, u32[]{:S(2)}, u32[]{:S(2)}) collective-permute-start(f32[5,1,128]{2,1,0:T(1,128)S(1)} %get-tuple-element.128), channel_id=1, source_target_pairs={{4,0},{8,4},{12,8},{16,12},{20,16},{24,20},{28,24},{5,1},{9,5},{13... | collective-permute-start | bytes 7688 | tf_op jit(solution)/shard_map/while/body/eval_jaxpr/ppermute | solution.py:22
  285.6 13.0 %collective-permute-start.6 = (f32[5,1,128]{2,1,0:T(1,128)S(1)}, f32[5,1,128]{2,1,0:T(1,128)S(1)}, u32[]{:S(2)}, u32[]{:S(2)}) collective-permute-start(f32[5,1,128]{2,1,0:T(1,128)S(1)} %get-tuple-element.127), channel_id=1, source_target_pairs={{0,4},{4,8},{8,12},{12,16},{16,20},{20,24},{24,28},{1,5},{5,9},{9,... | collective-permute-start | bytes 7688 | tf_op jit(solution)/shard_map/while/body/eval_jaxpr/ppermute | solution.py:20
  291.4 7.2 %collective-permute-start.7 = (f32[5,1,128]{2,1,0:T(1,128)S(1)}, f32[5,1,128]{2,1,0:T(1,128)S(1)}, u32[]{:S(2)}, u32[]{:S(2)}) collective-permute-start(f32[5,1,128]{2,1,0:T(1,128)S(1)} %get-tuple-element.128), channel_id=1, source_target_pairs={{4,0},{8,4},{12,8},{16,12},{20,16},{24,20},{28,24},{5,1},{9,5},{13... | collective-permute-start | bytes 7688 | tf_op jit(solution)/shard_map/while/body/eval_jaxpr/ppermute | solution.py:22
  298.8 13.0 %collective-permute-start.6 = (f32[5,1,128]{2,1,0:T(1,128)S(1)}, f32[5,1,128]{2,1,0:T(1,128)S(1)}, u32[]{:S(2)}, u32[]{:S(2)}) collective-permute-start(f32[5,1,128]{2,1,0:T(1,128)S(1)} %get-tuple-element.127), channel_id=1, source_target_pairs={{0,4},{4,8},{8,12},{12,16},{16,20},{20,24},{24,28},{1,5},{5,9},{9,... | collective-permute-start | bytes 7688 | tf_op jit(solution)/shard_map/while/body/eval_jaxpr/ppermute | solution.py:20
  304.5 7.2 %collective-permute-start.7 = (f32[5,1,128]{2,1,0:T(1,128)S(1)}, f32[5,1,128]{2,1,0:T(1,128)S(1)}, u32[]{:S(2)}, u32[]{:S(2)}) collective-permute-start(f32[5,1,128]{2,1,0:T(1,128)S(1)} %get-tuple-element.128), channel_id=1, source_target_pairs={{4,0},{8,4},{12,8},{16,12},{20,16},{24,20},{28,24},{5,1},{9,5},{13... | collective-permute-start | bytes 7688 | tf_op jit(solution)/shard_map/while/body/eval_jaxpr/ppermute | solution.py:22
  311.9 13.0 %collective-permute-start.6 = (f32[5,1,128]{2,1,0:T(1,128)S(1)}, f32[5,1,128]{2,1,0:T(1,128)S(1)}, u32[]{:S(2)}, u32[]{:S(2)}) collective-permute-start(f32[5,1,128]{2,1,0:T(1,128)S(1)} %get-tuple-element.127), channel_id=1, source_target_pairs={{0,4},{4,8},{8,12},{12,16},{16,20},{20,24},{24,28},{1,5},{5,9},{9,... | collective-permute-start | bytes 7688 | tf_op jit(solution)/shard_map/while/body/eval_jaxpr/ppermute | solution.py:20
  317.7 7.2 %collective-permute-start.7 = (f32[5,1,128]{2,1,0:T(1,128)S(1)}, f32[5,1,128]{2,1,0:T(1,128)S(1)}, u32[]{:S(2)}, u32[]{:S(2)}) collective-permute-start(f32[5,1,128]{2,1,0:T(1,128)S(1)} %get-tuple-element.128), channel_id=1, source_target_pairs={{4,0},{8,4},{12,8},{16,12},{20,16},{24,20},{28,24},{5,1},{9,5},{13... | collective-permute-start | bytes 7688 | tf_op jit(solution)/shard_map/while/body/eval_jaxpr/ppermute | solution.py:22
  325.1 13.0 %collective-permute-start.6 = (f32[5,1,128]{2,1,0:T(1,128)S(1)}, f32[5,1,128]{2,1,0:T(1,128)S(1)}, u32[]{:S(2)}, u32[]{:S(2)}) collective-permute-start(f32[5,1,128]{2,1,0:T(1,128)S(1)} %get-tuple-element.127), channel_id=1, source_target_pairs={{0,4},{4,8},{8,12},{12,16},{16,20},{20,24},{24,28},{1,5},{5,9},{9,... | collective-permute-start | bytes 7688 | tf_op jit(solution)/shard_map/while/body/eval_jaxpr/ppermute | solution.py:20
  330.8 7.2 %collective-permute-start.7 = (f32[5,1,128]{2,1,0:T(1,128)S(1)}, f32[5,1,128]{2,1,0:T(1,128)S(1)}, u32[]{:S(2)}, u32[]{:S(2)}) collective-permute-start(f32[5,1,128]{2,1,0:T(1,128)S(1)} %get-tuple-element.128), channel_id=1, source_target_pairs={{4,0},{8,4},{12,8},{16,12},{20,16},{24,20},{28,24},{5,1},{9,5},{13... | collective-permute-start | bytes 7688 | tf_op jit(solution)/shard_map/while/body/eval_jaxpr/ppermute | solution.py:22
  (52 other events, 472.0 us)
Sparse Core Ops, SparseCore 0:
  150.1 51.7 all-reduce.1
where the time goes:
time: 426 us; the launch traced here: 424 us
  waiting for transfers between devices  150 us (35%)
  starting transfers between devices  149 us (35%)
  blocking collectives  72.9 us (17%)
  other arithmetic  31.4 us (7%)
  between operations  17.2 us (4%)
    ppermute x40, starting transfers between devices, with_halo(): lax.ppermute(tail, axis, [(i, (i + 1) % count) for i in range(ends)])  122 us
    ppermute x40, waiting for transfers between devices, with_halo(): lax.ppermute(head, axis, [((i + 1) % count, i) for i in range(ends)])  75.4 us
    psum x1, blocking collectives, on_device(): total = lax.psum(local_terms, ('mem', 'lat', 'lon'))  72.9 us
    psum x1, waiting for transfers between devices, on_device(): lax.psum(partial_total.astype(jnp.bfloat16), 'mem').astype(jnp.float32)  51.9 us
    ppermute x40, starting transfers between devices, with_halo(): lax.ppermute(head, axis, [((i + 1) % count, i) for i in range(ends)])  26.6 us
    ppermute x40, waiting for transfers between devices, with_halo(): lax.ppermute(tail, axis, [(i, (i + 1) % count) for i in range(ends)])  22.6 us
  transfers between devices with their start and end apart: 81, of which 41 were waited for; matrix products, arithmetic and copies ran while one was open for 0% of the time, Pallas kernels for 0%

commit v1 on v0

v1 whole, which is shorter than its diff:
```python
import functools
import math

import jax
import jax.numpy as jnp
from jax import lax
from jax.experimental import pallas as pl
from jax.experimental.pallas import tpu as pltpu
from jax.sharding import PartitionSpec as P

F32 = jnp.float32
BF16 = jnp.bfloat16
PASSES = 10
REACH = 10
ROWS, COLS = 16, 128
MEMBERS = 5
PLANES = 280
PIECE = PLANES // 8
CHUNKS = ((0, PIECE),)
MIB = 1 << 20

VMEM_SPEC = pl.BlockSpec(memory_space=pltpu.VMEM)
SMEM_SPEC = pl.BlockSpec(memory_space=pltpu.SMEM)
ANY_SPEC = pl.BlockSpec(memory_space=pl.ANY)


def call(body, outs, args, specs, scratch=(), limit=8 * MIB, us=1.0, aliases=None):
    return pl.pallas_call(
        body,
        out_shape=outs,
        in_specs=specs,
        out_specs=[VMEM_SPEC] * len(outs),
        scratch_shapes=list(scratch),
        input_output_aliases=aliases or {},
        compiler_params=pltpu.CompilerParams(vmem_limit_bytes=limit),
        cost_estimate=pl.CostEstimate(
            flops=int(us * 1e6), bytes_accessed=int(us * 3e6), transcendentals=0
        ),
    )(*args)


def swap(cells, axis, odd):
    count = lax.axis_size(axis)
    pairs = []
    for i in range(count):
        to = i ^ 1 if not odd else ((i + 1) ^ 1) - 1
        pairs.append((i, to % count))
    return lax.ppermute(cells, axis, pairs)


def trade(cells, axis, bit):
    count = lax.axis_size(axis)
    return lax.ppermute(cells, axis, [(i, i ^ bit) for i in range(count)])


def pack_body(fields, mask_edges, ids, own, even, odd, ext, packed):
    lat = ids[1]
    is_even = lax.rem(lat, 2) == 0
    lane = lax.broadcasted_iota(jnp.int32, (3 * ROWS, COLS), 1)
    out = jnp.zeros((3 * ROWS, COLS), F32)
    for f in range(fields):
        a, b = even[f], odd[f]
        up = jnp.where(is_even, b, a)
        down = jnp.where(is_even, a, b)
        if mask_edges:
            up = jnp.where(lat == 0, 0.0, up)
            down = jnp.where(lat == lax.axis_size("lat") - 1, 0.0, down)
        whole = jnp.concatenate([up, own[f], down], axis=0)
        ext[f] = whole
        at = 2 * REACH * f
        turned = pltpu.roll(whole, (at + REACH) % COLS, 1)
        out = jnp.where((lane >= at) & (lane < at + 2 * REACH), turned, out)
    packed[...] = out


def pack(fields, mask_edges, ids, own, even, odd):
    return call(
        functools.partial(pack_body, fields, mask_edges),
        [pltpu.VMEM((fields, 3 * ROWS, COLS), F32), pltpu.VMEM((3 * ROWS, COLS), F32)],
        (ids, own, even, odd),
        [SMEM_SPEC] + [VMEM_SPEC] * 3,
        us=0.3,
    )


def halo_of(fields, ids, even, odd):
    is_even = lax.rem(ids[2], 2) == 0
    lane = lax.broadcasted_iota(jnp.int32, (3 * ROWS, COLS), 1)
    west = lane < 0
    for f in range(fields):
        at = 2 * REACH * f
        west = west | ((lane >= at) & (lane < at + REACH))
    a, b = even[...], odd[...]
    return jnp.where(west, jnp.where(is_even, b, a), jnp.where(is_even, a, b))


def spread_halo(halo, f):
    return pltpu.roll(halo, (2 * COLS - REACH - 2 * REACH * f) % COLS, 1)


def lap(own, side):
    rows = own.shape[0]
    lane = lax.broadcasted_iota(jnp.int32, own.shape, 1)
    first, last = lane == 0, lane == COLS - 1
    own_w, side_w = pltpu.roll(own, 1, 1), pltpu.roll(side, 1, 1)
    own_e, side_e = pltpu.roll(own, COLS - 1, 1), pltpu.roll(side, COLS - 1, 1)

    def total(v, west, east):
        above = pltpu.roll(v, 1, 0)
        below = pltpu.roll(v, rows - 1, 0)
        return (above + below) + (west + east) - 4.0 * v

    return (
        total(own, jnp.where(first, side_w, own_w), jnp.where(last, side_e, own_e)),
        total(side, jnp.where(first, own_w, side_w), jnp.where(last, own_e, side_e)),
    )


def forward_pass(state, rate):
    a, b = lap(*state)
    return state[0] + rate[0] * a, state[1] + rate[1] * b


def adjoint_pass(state, rate):
    a, b = lap(state[0] * rate[0], state[1] * rate[1])
    return state[0] + a, state[1] + b


def sweep(step, state, rate):
    cut = ROWS // 2
    for _ in range(2):
        state = step(state, rate)
    state = tuple(v[cut:-cut] for v in state)
    rate = tuple(v[cut:-cut] for v in rate)
    state = lax.fori_loop(0, PASSES - 2, lambda _, s: step(s, rate), state)
    return state[0][ROWS - cut : -(ROWS - cut)]


def select_body(anomalies, obs_time, innovation, precision, ids, sel, inn_own, prec_own, buf, sems, own_sems):
    parts = buf.shape[2] // 56
    for m in range(MEMBERS):
        for p in range(parts):
            at = pl.ds(56 * p, 56)
            pltpu.make_async_copy(anomalies.at[m, :, at], buf.at[m, :, at], sems.at[m * parts + p]).start()
    mem = ids[0]
    own_copies = []
    for n, start in enumerate(own_starts(mem)):
        for k, (src, dst) in enumerate(((innovation, inn_own), (precision, prec_own))):
            copy = pltpu.make_async_copy(
                src.at[pl.ds(start, PIECE)], dst.at[pl.ds(n * PIECE, PIECE)], own_sems.at[2 * n + k]
            )
            copy.start()
            own_copies.append(copy)
    at_zero = obs_time[...].astype(F32).astype(BF16) == 0
    for m in range(MEMBERS):

        def part(p, carry):
            at = pl.ds(56 * p, 56)
            pltpu.make_async_copy(anomalies.at[m, :, at], buf.at[m, :, at], sems.at[m * parts + p]).wait()

            def plane(r, c):
                r = 56 * p + r
                sel[m, r] = jnp.where(at_zero, buf[m, 0, r], buf[m, 1, r])
                return c

            return lax.fori_loop(0, 56, plane, carry, unroll=8)

        lax.fori_loop(0, parts, part, 0)
    for copy in own_copies:
        copy.wait()


def keeps(mem):
    high = lax.div(mem, 2)
    low = lax.rem(mem, 2)
    return (lax.rem(high + low, 2), high), (high, low)


def start_of(group, half, quarter):
    return 4 * PIECE * group + 2 * PIECE * half + PIECE * quarter


def own_starts(mem):
    return [start_of(g, *k) for g, k in enumerate(keeps(mem))]


def add_members(sel, w, start, count, store):
    ws = [w[m] for m in range(MEMBERS)]

    def plane(r, c):
        total = sel[0, start + r].astype(F32) * ws[0]
        for m in range(1, MEMBERS):
            total = total + sel[m, start + r].astype(F32) * ws[m]
        store(r, total)
        return c

    lax.fori_loop(0, count, plane, 0, unroll=5 if count % 5 == 0 else 1)


def first_sends(chunk, ids, sel, w, send1, send2):
    first, count = chunk
    for g, (out, (half, _)) in enumerate(zip((send1, send2), keeps(ids[0]))):
        for q in range(2):

            def store(r, total, out=out, q=q):
                out[q * count + r] = total.astype(BF16)

            add_members(sel, w, start_of(g, 1 - half, q) + first, count, store)


def forward_body(chunk, ids, ext, even, odd, loc_norm, sel, w, rate, terms, send1, send2):
    halo = halo_of(MEMBERS + 1, ids, even, odd)
    lane = lax.broadcasted_iota(jnp.int32, (3 * ROWS, COLS), 1)
    near = (lane < REACH) | (lane >= COLS - REACH)
    rate_own = ext[MEMBERS]
    rate_side = jnp.where(near, spread_halo(halo, MEMBERS), 0.0)
    rate[0] = rate_own
    rate[1] = rate_side
    squares = jnp.zeros((ROWS, COLS), F32)
    for m in range(MEMBERS):
        own = ext[m]
        mine = own[ROWS : 2 * ROWS]
        squares = squares + mine * mine
        spread = sweep(forward_pass, (own, spread_halo(halo, m)), (rate_own, rate_side))
        w[m] = (loc_norm[...] * spread).astype(BF16).astype(F32)
    terms[...] = squares[:8] + squares[8:]
    first_sends(chunk, ids, sel, w, send1, send2)


def own_body(chunk, ids, sel, w, own1, own2):
    first, count = chunk
    for g, (out, (half, _)) in enumerate(zip((own1, own2), keeps(ids[0]))):
        for q in range(2):

            def store(r, total, out=out, q=q):
                out[q * count + r] = total

            add_members(sel, w, start_of(g, half, q) + first, count, store)


def second_body(count, ids, own1, own2, got1, got2, send1, send2):
    for own, got, out, (_, quarter) in zip((own1, own2), (got1, got2), (send1, send2), keeps(ids[0])):
        at = (1 - quarter) * count

        def plane(r, c, own=own, got=got, out=out, at=at):
            out[r] = (own[at + r] + got[at + r].astype(F32)).astype(BF16)
            return c

        lax.fori_loop(0, count, plane, 0, unroll=5 if count % 5 == 0 else 1)


def misfit_body(chunk, factor, ids, own1, own2, got1, got2, last1, last2, inn, prec, terms, weighted, new_terms):
    first, count = chunk
    total = jnp.zeros((ROWS, COLS), F32)
    for g, (own, got, last, (_, quarter)) in enumerate(
        zip((own1, own2), (got1, got2), (last1, last2), keeps(ids[0]))
    ):
        at = quarter * count

        def plane(r, c, own=own, got=got, last=last, at=at, g=g):
            sums = own[at + r] + got[at + r].astype(F32) + last[r].astype(F32)
            misfit = factor * sums - inn[g * PIECE + first + r]
            scaled = prec[g * PIECE + first + r] * misfit
            weighted[g * count + r] = scaled.astype(BF16)
            return c + misfit * scaled

        total = lax.fori_loop(0, count, plane, total, unroll=5 if count % 5 == 0 else 1)
    new_terms[...] = terms[...] + (total[:8] + total[8:])


def pull(sel, parts, acc):
    for ref, at, start, count in parts:

        def plane(r, acc, ref=ref, at=at, start=start):
            x = ref[at + r].astype(F32)
            return tuple(acc[m] + sel[m, start + r].astype(F32) * x for m in range(MEMBERS))

        acc = lax.fori_loop(0, count, plane, acc, unroll=5 if count % 5 == 0 else 1)
    return acc


def pieces_of(stage, chunk, mem, refs):
    first, count = chunk
    (h1, q1), (h2, q2) = keeps(mem)
    if stage == "own":
        where = [(0, h1, q1), (1, h2, q2)]
        blocks = [(refs[0], 0), (refs[0], count)]
    elif stage == "near":
        where = [(0, 1 - h1, q1), (1, h2, 1 - q2), (0, h1, 1 - q1), (1, 1 - h2, 1 - q2)]
        blocks = [(refs[0], 0), (refs[0], count), (refs[1], 0), (refs[1], count)]
    else:
        where = [(0, 1 - h1, 1 - q1), (1, 1 - h2, q2)]
        blocks = [(refs[0], 0), (refs[1], 0)]
    return [(ref, at, start_of(*place) + first, count) for (ref, at), place in zip(blocks, where)]


def pull_body(stage, chunk, ids, sel, old, *rest):
    refs, new = rest[:-1], rest[-1]
    acc = tuple(old[m] for m in range(MEMBERS))
    acc = pull(sel, pieces_of(stage, chunk, ids[0], refs), acc)
    for m in range(MEMBERS):
        new[m] = acc[m]


def first_pull_body(chunk, ids, sel, ref, new):
    acc = tuple(jnp.zeros((ROWS, COLS), F32) for _ in range(MEMBERS))
    acc = pull(sel, pieces_of("own", chunk, ids[0], [ref]), acc)
    for m in range(MEMBERS):
        new[m] = acc[m]


def last_pull_body(chunk, factor, ids, sel, old, loc_norm, ref1, ref2, new):
    acc = tuple(old[m] for m in range(MEMBERS))
    acc = pull(sel, pieces_of("far", chunk, ids[0], [ref1, ref2]), acc)
    for m in range(MEMBERS):
        new[m] = loc_norm[...] * (factor * acc[m])


def adjoint_body(ids, ext, even, odd, rate, control, out):
    halo = halo_of(MEMBERS, ids, even, odd)
    rates = (rate[0], rate[1])
    for m in range(MEMBERS):
        out[m] = control[m] + sweep(adjoint_pass, (ext[m], spread_halo(halo, m)), rates)


def on_device(control, anomalies, diffusivity, loc_norm, innovation, obs_precision, obs_time):
    members = MEMBERS * lax.axis_size("mem")
    cells = members * ROWS * COLS * lax.axis_size("lat") * lax.axis_size("lon")
    factor = 1.0 / math.sqrt(members - 1)
    ids = jnp.stack([lax.axis_index(a) for a in ("mem", "lat", "lon")]).astype(jnp.int32)
    anomalies = anomalies.reshape(MEMBERS, 2, PLANES, ROWS, COLS)
    innovation = innovation.reshape(PLANES, ROWS, COLS)
    obs_precision = obs_precision.reshape(PLANES, ROWS, COLS)
    block = (MEMBERS, ROWS, COLS)

    fields = jnp.concatenate([control, diffusivity[None]], axis=0)
    even, odd = swap(fields, "lat", False), swap(fields, "lat", True)
    sel, inn, prec = call(
        select_body,
        [
            pltpu.VMEM((MEMBERS, PLANES, ROWS, COLS), BF16),
            pltpu.VMEM((2 * PIECE, ROWS, COLS), F32),
            pltpu.VMEM((2 * PIECE, ROWS, COLS), F32),
        ],
        (anomalies, obs_time, innovation, obs_precision, ids),
        [ANY_SPEC, VMEM_SPEC, ANY_SPEC, ANY_SPEC, SMEM_SPEC],
        scratch=[
            pltpu.VMEM((MEMBERS, 2, PLANES, ROWS, COLS), BF16),
            pltpu.SemaphoreType.DMA((25,)),
            pltpu.SemaphoreType.DMA((4,)),
        ],
        limit=24 * MIB,
        us=4.0,
    )
    ext, packed = pack(MEMBERS + 1, True, ids, fields, even, odd)
    even, odd = swap(packed, "lon", False), swap(packed, "lon", True)

    def sends(count):
        return [pltpu.VMEM((2 * count, ROWS, COLS), BF16)] * 2

    w = None
    got, own = [], []
    for chunk in CHUNKS:
        if w is None:
            w, rate, terms, *send = call(
                functools.partial(forward_body, chunk),
                [
                    pltpu.VMEM(block, F32),
                    pltpu.VMEM((2, 3 * ROWS, COLS), F32),
                    pltpu.VMEM((8, COLS), F32),
                    *sends(chunk[1]),
                ],
                (ids, ext, even, odd, loc_norm, sel),
                [SMEM_SPEC] + [VMEM_SPEC] * 5,
                us=2.0,
            )
        else:
            send = call(
                functools.partial(first_sends, chunk),
                sends(chunk[1]),
                (ids, sel, w),
                [SMEM_SPEC] + [VMEM_SPEC] * 2,
                us=0.5,
            )
        got.append((swap(send[0], "mem", False), swap(send[1], "mem", True)))
        own.append(
            call(
                functools.partial(own_body, chunk),
                [pltpu.VMEM((2 * chunk[1], ROWS, COLS), F32)] * 2,
                (ids, sel, w),
                [SMEM_SPEC] + [VMEM_SPEC] * 2,
                us=0.5,
            )
        )
    last = []
    for i, (_, count) in enumerate(CHUNKS):
        send = call(
            functools.partial(second_body, count),
            [pltpu.VMEM((count, ROWS, COLS), BF16)] * 2,
            (ids, *own[i], *got[i]),
            [SMEM_SPEC] + [VMEM_SPEC] * 4,
            us=0.2,
        )
        last.append((swap(send[0], "mem", True), swap(send[1], "mem", False)))
    weighted, near = [], []
    for i, chunk in enumerate(CHUNKS):
        piece, terms = call(
            functools.partial(misfit_body, chunk, factor),
            [pltpu.VMEM((2 * chunk[1], ROWS, COLS), BF16), pltpu.VMEM((8, COLS), F32)],
            (ids, *own[i], *got[i], *last[i], inn, prec, terms),
            [SMEM_SPEC] + [VMEM_SPEC] * 9,
            us=0.3,
        )
        weighted.append(piece)
        near.append((swap(piece, "mem", False), swap(piece, "mem", True)))
    for axis, bit in (("lon", 1), ("lat", 1), ("mem", 1), ("lat", 4), ("lat", 2), ("lon", 2), ("mem", 2)):
        terms = terms + trade(terms, axis, bit)
    cost = jnp.sum(terms) * (0.5 / cells)

    acc = None
    for i, chunk in enumerate(CHUNKS):
        if acc is None:
            body, extra, specs = functools.partial(first_pull_body, chunk), (), 2
        else:
            body, extra, specs = functools.partial(pull_body, "own", chunk), (acc,), 3
        (acc,) = call(
            body,
            [pltpu.VMEM(block, F32)],
            (ids, sel, *extra, weighted[i]),
            [SMEM_SPEC] + [VMEM_SPEC] * specs,
            us=0.3,
        )
    far = []
    for i, chunk in enumerate(CHUNKS):
        a, b = near[i]
        far.append((swap(b[: chunk[1]], "mem", False), swap(a[chunk[1] :], "mem", True)))
        (acc,) = call(
            functools.partial(pull_body, "near", chunk),
            [pltpu.VMEM(block, F32)],
            (ids, sel, acc, a, b),
            [SMEM_SPEC] + [VMEM_SPEC] * 4,
            us=0.6,
        )
    for i, chunk in enumerate(CHUNKS):
        if i < len(CHUNKS) - 1:
            (acc,) = call(
                functools.partial(pull_body, "far", chunk),
                [pltpu.VMEM(block, F32)],
                (ids, sel, acc, *far[i]),
                [SMEM_SPEC] + [VMEM_SPEC] * 4,
                us=0.3,
            )
        else:
            (source,) = call(
                functools.partial(last_pull_body, chunk, factor),
                [pltpu.VMEM(block, F32)],
                (ids, sel, acc, loc_norm, *far[i]),
                [SMEM_SPEC] + [VMEM_SPEC] * 5,
                us=0.3,
            )
    even, odd = swap(source, "lat", False), swap(source, "lat", True)
    ext, packed = pack(MEMBERS, False, ids, source, even, odd)
    even, odd = swap(packed, "lon", False), swap(packed, "lon", True)
    (gradient,) = call(
        adjoint_body,
        [jax.ShapeDtypeStruct(block, F32)],
        (ids, ext, even, odd, rate, control),
        [SMEM_SPEC] + [VMEM_SPEC] * 5,
        us=1.5,
    )
    return gradient, cost


def solution(mesh):
    return jax.shard_map(
        on_device,
        mesh=mesh,
        in_specs=(
            P("mem", "lat", "lon"),
            P("mem", None, None, None, "lat", "lon"),
            P("lat", "lon"),
            P("lat", "lon"),
            P(None, None, "lat", "lon"),
            P(None, None, "lat", "lon"),
            P("lat", "lon"),
        ),
        out_specs=(P("mem", "lat", "lon"), P()),
        check_vma=False,
    )
```

time: 426 us -> 110 us (0.26)
  waiting for transfers between devices: 150 us -> 31.9 us
  starting transfers between devices: 149 us -> 38.9 us
  blocking collectives: 72.9 us -> 0 us
  other arithmetic: 31.4 us -> 1.49 us
  Pallas kernels: 0 us -> 25.5 us
  between operations: 17.2 us -> 2.58 us
  local copies, waits for them, and re-layouts: 2.49 us -> 8.28 us
    ppermute x80 -> x23, starting transfers between devices: 149 us -> 38.9 us  [the longest x16 25.8 us: swap(): return lax.ppermute(cells, axis, pairs)]
    psum x1 -> x0, blocking collectives: 72.9 us -> none  [on_device(): total = lax.psum(local_terms, ('mem', 'lat', 'lon'))]
    ppermute x80 -> x23, waiting for transfers between devices: 98 us -> 31.9 us  [the longest x16 20 us: swap(): return lax.ppermute(cells, axis, pairs)]
    psum x1 -> x0, waiting for transfers between devices: 51.9 us -> none  [on_device(): lax.psum(partial_total.astype(jnp.bfloat16), 'mem').astype(jnp.float32)]
    pallas_call x0 -> x11, Pallas kernels: none -> 25.5 us  [call(): pl.pallas_call(body, out_shape=outs, in_specs=specs, out_specs=[VMEM_SPEC...]
    dot_general x2 -> x0, other arithmetic: 12.5 us -> none  [the longest x1 6.57 us: on_device(): jnp.einsum('mflyx,myx->flyx', anomalies[:, t], masked, preferred_element_...]
    add x20 -> x6, other arithmetic: 9.03 us -> 0.02 us  [on_device(): terms = terms + trade(terms, axis, bit)]
    unnamed x7 -> x12, local copies, waits for them, and re-layouts: 0.8 us -> 8.26 us
  transfers between devices with their start and end apart: 81 -> 23, of which waited for: 41 -> 16; matrix products, arithmetic and copies ran while one was open for 0% -> 1% of each run, Pallas kernels for 0% -> 10%
where the time goes in v1:
time: 110 us; the launch traced here: 109 us
  starting transfers between devices  38.9 us (35%)
  waiting for transfers between devices  31.9 us (29%)
  Pallas kernels  25.5 us (23%)
  local copies, waits for them, and re-layouts  8.28 us (8%)
  between operations  2.58 us (2%)
  other arithmetic  1.49 us (1%)
    ppermute x16, starting transfers between devices, swap(): return lax.ppermute(cells, axis, pairs)  25.8 us
    pallas_call x11, Pallas kernels, call(): pl.pallas_call(body, out_shape=outs, in_specs=specs, out_specs=[VMEM_SPEC...  25.5 us
    ppermute x16, waiting for transfers between devices, swap(): return lax.ppermute(cells, axis, pairs)  20 us
    ppermute x7, starting transfers between devices, trade(): return lax.ppermute(cells, axis, [(i, i ^ bit) for i in range(count)])  13.1 us
    ppermute x7, waiting for transfers between devices, trade(): return lax.ppermute(cells, axis, [(i, i ^ bit) for i in range(count)])  11.8 us
    unnamed x12, local copies, waits for them, and re-layouts  8.26 us
  transfers between devices with their start and end apart: 23, of which 16 were waited for; matrix products, arithmetic and copies ran while one was open for 1% of the time, Pallas kernels for 10%

profile of v1, /device:TPU:1, one launch (start us, length us, event | category | flops | bytes accessed | tf_op | source)
XLA Modules:
  0.0 108.6 jit_solution(2493087975676415282)
XLA Ops:
  1.4 4.7 %collective-permute-start.1 = (f32[6,16,128]{2,1,0:T(8,128)S(1)}, f32[6,16,128]{2,1,0:T(8,128)S(1)}, u32[]{:S(2)}, u32[]{:S(2)}) collective-permute-start(f32[6,16,128]{2,1,0:T(8,128)S(1)} %pad_maximum_fusion.own), channel_id=1, source_target_pairs={{0,28},{4,8},{8,4},{12,16},{16,12},{20,24},{24,20},{28,0},{1,29},{... | collective-permute-start | bytes 147464 | tf_op jit(solution)/shard_map/ppermute | solution.py:48
  6.2 1.4 %collective-permute-done.1.odd = f32[6,16,128]{2,1,0:T(8,128)S(1)} collective-permute-done((f32[6,16,128]{2,1,0:T(8,128)S(1)}, f32[6,16,128]{2,1,0:T(8,128)S(1)}, u32[]{:S(2)}, u32[]{:S(2)}) %collective-permute-start.1) | collective-permute-done | bytes 49184 | tf_op jit(solution)/shard_map/ppermute | solution.py:48
  7.6 1.5 %collective-permute-done.even = f32[6,16,128]{2,1,0:T(8,128)S(1)} collective-permute-done((f32[6,16,128]{2,1,0:T(8,128)S(1)}, f32[6,16,128]{2,1,0:T(8,128)S(1)}, u32[]{:S(2)}, u32[]{:S(2)}) %collective-permute-start) | collective-permute-done | bytes 49184 | tf_op jit(solution)/shard_map/ppermute | solution.py:48
  9.7 5.4 %collective-permute-start.3 = (f32[48,128]{1,0:T(8,128)S(1)}, f32[48,128]{1,0:T(8,128)S(1)}, u32[]{:S(2)}, u32[]{:S(2)}) collective-permute-start(f32[48,128]{1,0:T(8,128)S(1)} %get-tuple-element.22), channel_id=1, source_target_pairs={{0,3},{1,2},{2,1},{3,0},{4,7},{5,6},{6,5},{7,4},{8,11},{9,10},{10,... | collective-permute-start | bytes 73736 | tf_op jit(solution)/shard_map/ppermute | solution.py:48
  15.1 4.3 %copy-done = bf16[5,2,4,70,16,128]{5,4,3,2,1,0:T(8,128)(2,1)S(1)} copy-done((bf16[5,2,4,70,16,128]{5,4,3,2,1,0:T(8,128)(2,1)S(1)}, bf16[5,2,4,70,16,128]{5,4,3,2,1,0:T(8,128)(2,1)}, u32[]{:S(2)}) %copy-start) | copy-done | bytes 11468824
  19.3 1.6 %copy-done.1 = f32[4,70,16,128]{3,2,1,0:T(8,128)S(1)} copy-done((f32[4,70,16,128]{3,2,1,0:T(8,128)S(1)}, f32[4,70,16,128]{3,2,1,0:T(8,128)}, u32[]{:S(2)}) %copy-start.1) | copy-done | bytes 2293784
  21.0 1.6 %copy-done.2 = f32[4,70,16,128]{3,2,1,0:T(8,128)S(1)} copy-done((f32[4,70,16,128]{3,2,1,0:T(8,128)S(1)}, f32[4,70,16,128]{3,2,1,0:T(8,128)}, u32[]{:S(2)}) %copy-start.2) | copy-done | bytes 2293784
  23.3 6.4 %shard_map.86 = (bf16[5,280,16,128]{3,2,1,0:T(8,128)(2,1)S(1)}, f32[70,16,128]{2,1,0:T(8,128)S(1)}, f32[70,16,128]{2,1,0:T(8,128)S(1)}) custom-call(bf16[5,2,280,16,128]{4,3,2,1,0:T(8,128)(2,1)S(1)} %bitcast.7, s32[16,128]{1,0:T(8,128)S(1)} %copy-done.5, f32[280,16,128]{2,1,0:T(8,128)S(1)} %bitcast.8, f32[280,16,128]{2,1,0:T(8,128)S(1)} %bitcast.9, ...), custom_call_target="tpu_custom_call" | custom-call | flops 4000000 | bytes 12000000 | tf_op jit(solution)/shard_map/pallas_call | solution.py:28
  29.7 6.0 %shard_map.88 = (f32[5,16,128]{2,1,0:T(8,128)S(1)}, f32[2,48,128]{2,1,0:T(8,128)S(1)}, f32[8,128]{1,0:T(8,128)S(1)}, bf16[70,16,128]{2,1,0:T(8,128)(2,1)S(1)}, bf16[70,16,128]{2,1,0:T(8,128)(2,1)S(1)}) custom-call(s32[3]{0:T(128)S(1)} %pad_add_fusion.ids, f32[6,48,128]{2,1,0:T(8,128)S(1)} %get-tuple-element.21.ext, ...), custom_call_target="tpu_custom_call" | custom-call | flops 2000000 | bytes 6000000 | tf_op jit(solution)/shard_map/pallas_call | solution.py:28
  35.8 1.4 %collective-permute-start.4 = (bf16[70,16,128]{2,1,0:T(8,128)(2,1)S(1)}, bf16[70,16,128]{2,1,0:T(8,128)(2,1)S(1)}, u32[]{:S(2)}, u32[]{:S(2)}) collective-permute-start(bf16[70,16,128]{2,1,0:T(8,128)(2,1)S(1)} %get-tuple-element.26), channel_id=1, source_target_pairs={{0,32},{32,0},{64,96},{96,64},{1,33},{33,1},{65,97},{97,65},{2,34}... | collective-permute-start | bytes 860168 | tf_op jit(solution)/shard_map/ppermute | solution.py:48
  37.1 1.9 %collective-permute-start.5 = (bf16[70,16,128]{2,1,0:T(8,128)(2,1)S(1)}, bf16[70,16,128]{2,1,0:T(8,128)(2,1)S(1)}, u32[]{:S(2)}, u32[]{:S(2)}) collective-permute-start(bf16[70,16,128]{2,1,0:T(8,128)(2,1)S(1)} %get-tuple-element.27), channel_id=1, source_target_pairs={{0,96},{32,64},{64,32},{96,0},{1,97},{33,65},{65,33},{97,1},{2,98}... | collective-permute-start | bytes 860168 | tf_op jit(solution)/shard_map/ppermute | solution.py:48
  39.0 1.2 %shard_map.89 = (f32[70,16,128]{2,1,0:T(8,128)S(1)}, f32[70,16,128]{2,1,0:T(8,128)S(1)}) custom-call(s32[3]{0:T(128)S(1)} %pad_add_fusion.ids, bf16[5,280,16,128]{3,2,1,0:T(8,128)(2,1)S(1)} %get-tuple-element.20.sel, f32[5,16,128]{2,1,0:T(8,128)S(1)} %get-tuple-element.23.w), custom_call_target="tpu_custom_call" | custom-call | flops 500000 | bytes 1500000 | tf_op jit(solution)/shard_map/pallas_call | solution.py:28
  40.3 3.4 %collective-permute-done.4.got1 = bf16[70,16,128]{2,1,0:T(8,128)(2,1)S(1)} collective-permute-done((bf16[70,16,128]{2,1,0:T(8,128)(2,1)S(1)}, bf16[70,16,128]{2,1,0:T(8,128)(2,1)S(1)}, u32[]{:S(2)}, u32[]{:S(2)}) %collective-permute-start.4) | collective-permute-done | bytes 286752 | tf_op jit(solution)/shard_map/ppermute | solution.py:48
  43.7 2.2 %collective-permute-done.5.got2 = bf16[70,16,128]{2,1,0:T(8,128)(2,1)S(1)} collective-permute-done((bf16[70,16,128]{2,1,0:T(8,128)(2,1)S(1)}, bf16[70,16,128]{2,1,0:T(8,128)(2,1)S(1)}, u32[]{:S(2)}, u32[]{:S(2)}) %collective-permute-start.5) | collective-permute-done | bytes 286752 | tf_op jit(solution)/shard_map/ppermute | solution.py:48
  46.6 2.0 %collective-permute-start.6 = (bf16[35,16,128]{2,1,0:T(8,128)(2,1)S(1)}, bf16[35,16,128]{2,1,0:T(8,128)(2,1)S(1)}, u32[]{:S(2)}, u32[]{:S(2)}) collective-permute-start(bf16[35,16,128]{2,1,0:T(8,128)(2,1)S(1)} %get-tuple-element.28), channel_id=1, source_target_pairs={{0,96},{32,64},{64,32},{96,0},{1,97},{33,65},{65,33},{97,1},{2,98}... | collective-permute-start | bytes 430088 | tf_op jit(solution)/shard_map/ppermute | solution.py:48
  48.6 3.3 %collective-permute-done.6.last1 = bf16[35,16,128]{2,1,0:T(8,128)(2,1)S(1)} collective-permute-done((bf16[35,16,128]{2,1,0:T(8,128)(2,1)S(1)}, bf16[35,16,128]{2,1,0:T(8,128)(2,1)S(1)}, u32[]{:S(2)}, u32[]{:S(2)}) %collective-permute-start.6) | collective-permute-done | bytes 143392 | tf_op jit(solution)/shard_map/ppermute | solution.py:48
  53.7 1.0 collective-permute-start.9
  54.7 5.8 %collective-permute-done.9.rest_1_ = bf16[70,16,128]{2,1,0:T(8,128)(2,1)S(1)} collective-permute-done((bf16[70,16,128]{2,1,0:T(8,128)(2,1)S(1)}, bf16[70,16,128]{2,1,0:T(8,128)(2,1)S(1)}, u32[]{:S(2)}, u32[]{:S(2)}) %collective-permute-start.9) | collective-permute-done | bytes 286752 | tf_op jit(solution)/shard_map/ppermute | solution.py:48
  60.6 1.7 %collective-permute-start.11 = (bf16[35,16,128]{2,1,0:T(8,128)(2,1)S(1)}, bf16[35,16,128]{2,1,0:T(8,128)(2,1)S(1)}, u32[]{:S(2)}, u32[]{:S(2)}) collective-permute-start(bf16[35,16,128]{2,1,0:T(8,128)(2,1)S(1)} %slice.9), channel_id=1, source_target_pairs={{0,96},{32,64},{64,32},{96,0},{1,97},{33,65},{65,33},{97,1},{2,98}... | collective-permute-start | bytes 430088 | tf_op jit(solution)/shard_map/ppermute | solution.py:48
  63.2 1.3 %shard_map.93.old = f32[5,16,128]{2,1,0:T(8,128)S(1)} custom-call(s32[3]{0:T(128)S(1)} %pad_add_fusion.ids, bf16[5,280,16,128]{3,2,1,0:T(8,128)(2,1)S(1)} %get-tuple-element.20.sel, f32[5,16,128]{2,1,0:T(8,128)S(1)} %shard_map.92.old, bf16[70,16,128]{2,1,0:T(8,128)(2,1)S(1)} %collective-permute-done.8.rest_0_, ...), custom_call_target="tpu_custom_call" | custom-call | flops 600000 | bytes 1800000 | tf_op jit(solution)/shard_map/pallas_call | solution.py:28
  66.8 1.3 %collective-permute-start.13 = (f32[5,16,128]{2,1,0:T(8,128)S(1)}, f32[5,16,128]{2,1,0:T(8,128)S(1)}, u32[]{:S(2)}, u32[]{:S(2)}) collective-permute-start(f32[5,16,128]{2,1,0:T(8,128)S(1)} %shard_map.94.own), channel_id=1, source_target_pairs={{0,28},{4,8},{8,4},{12,16},{16,12},{20,24},{24,20},{28,0},{1,29},{... | collective-permute-start | bytes 122888 | tf_op jit(solution)/shard_map/ppermute | solution.py:48
  68.1 6.0 %collective-permute-start.16 = (f32[8,128]{1,0:T(8,128)S(1)}, f32[8,128]{1,0:T(8,128)S(1)}, u32[]{:S(2)}, u32[]{:S(2)}) collective-permute-start(f32[8,128]{1,0:T(8,128)S(1)} %get-tuple-element.37), channel_id=1, source_target_pairs={{0,1},{1,0},{2,3},{3,2},{4,5},{5,4},{6,7},{7,6},{8,9},{9,8},{10,11... | collective-permute-start | bytes 12296 | tf_op jit(solution)/shard_map/ppermute | solution.py:53
  74.9 1.7 %collective-permute-start.17 = (f32[8,128]{1,0:T(8,128)S(1)}, f32[8,128]{1,0:T(8,128)S(1)}, u32[]{:S(2)}, u32[]{:S(2)}) collective-permute-start(f32[8,128]{1,0:T(8,128)S(1)} %add.21), channel_id=1, source_target_pairs={{0,4},{4,0},{8,12},{12,8},{16,20},{20,16},{24,28},{28,24},{1,5},{5... | collective-permute-start | bytes 12296 | tf_op jit(solution)/shard_map/ppermute | solution.py:53
  76.6 1.3 %collective-permute-done.17 = f32[8,128]{1,0:T(8,128)S(1)} collective-permute-done((f32[8,128]{1,0:T(8,128)S(1)}, f32[8,128]{1,0:T(8,128)S(1)}, u32[]{:S(2)}, u32[]{:S(2)}) %collective-permute-start.17) | collective-permute-done | bytes 4128 | tf_op jit(solution)/shard_map/ppermute | solution.py:53
  77.9 2.5 %collective-permute-done.18 = f32[8,128]{1,0:T(8,128)S(1)} collective-permute-done((f32[8,128]{1,0:T(8,128)S(1)}, f32[8,128]{1,0:T(8,128)S(1)}, u32[]{:S(2)}, u32[]{:S(2)}) %collective-permute-start.18) | collective-permute-done | bytes 4128 | tf_op jit(solution)/shard_map/ppermute | solution.py:53
  80.9 2.0 %collective-permute-done.19 = f32[8,128]{1,0:T(8,128)S(1)} collective-permute-done((f32[8,128]{1,0:T(8,128)S(1)}, f32[8,128]{1,0:T(8,128)S(1)}, u32[]{:S(2)}, u32[]{:S(2)}) %collective-permute-start.19) | collective-permute-done | bytes 4128 | tf_op jit(solution)/shard_map/ppermute | solution.py:53
  82.9 2.1 %collective-permute-start.20 = (f32[8,128]{1,0:T(8,128)S(1)}, f32[8,128]{1,0:T(8,128)S(1)}, u32[]{:S(2)}, u32[]{:S(2)}) collective-permute-start(f32[8,128]{1,0:T(8,128)S(1)} %add.24), channel_id=1, source_target_pairs={{0,8},{4,12},{8,0},{12,4},{16,24},{20,28},{24,16},{28,20},{1,9},{5... | collective-permute-start | bytes 12296 | tf_op jit(solution)/shard_map/ppermute | solution.py:53
  84.9 1.9 %collective-permute-done.20 = f32[8,128]{1,0:T(8,128)S(1)} collective-permute-done((f32[8,128]{1,0:T(8,128)S(1)}, f32[8,128]{1,0:T(8,128)S(1)}, u32[]{:S(2)}, u32[]{:S(2)}) %collective-permute-start.20) | collective-permute-done | bytes 4128 | tf_op jit(solution)/shard_map/ppermute | solution.py:53
  87.4 3.3 %collective-permute-done.21 = f32[8,128]{1,0:T(8,128)S(1)} collective-permute-done((f32[8,128]{1,0:T(8,128)S(1)}, f32[8,128]{1,0:T(8,128)S(1)}, u32[]{:S(2)}, u32[]{:S(2)}) %collective-permute-start.21) | collective-permute-done | bytes 4128 | tf_op jit(solution)/shard_map/ppermute | solution.py:53
  90.8 2.2 %collective-permute-start.22 = (f32[8,128]{1,0:T(8,128)S(1)}, f32[8,128]{1,0:T(8,128)S(1)}, u32[]{:S(2)}, u32[]{:S(2)}) collective-permute-start(f32[8,128]{1,0:T(8,128)S(1)} %add.26), channel_id=1, source_target_pairs={{0,64},{32,96},{64,0},{96,32},{1,65},{33,97},{65,1},{97,33},{2,66}... | collective-permute-start | bytes 12296 | tf_op jit(solution)/shard_map/ppermute | solution.py:53
  93.7 6.4 %collective-permute-start.15 = (f32[48,128]{1,0:T(8,128)S(1)}, f32[48,128]{1,0:T(8,128)S(1)}, u32[]{:S(2)}, u32[]{:S(2)}) collective-permute-start(f32[48,128]{1,0:T(8,128)S(1)} %get-tuple-element.35), channel_id=1, source_target_pairs={{0,3},{1,2},{2,1},{3,0},{4,7},{5,6},{6,5},{7,4},{8,11},{9,10},{10,... | collective-permute-start | bytes 73736 | tf_op jit(solution)/shard_map/ppermute | solution.py:48
  101.6 5.9 %shard_map.96 = f32[5,16,128]{2,1,0:T(8,128)} custom-call(s32[3]{0:T(128)S(1)} %pad_add_fusion.ids, f32[5,48,128]{2,1,0:T(8,128)S(1)} %get-tuple-element.34.ext, f32[48,128]{1,0:T(8,128)S(1)} %collective-permute-done.14.even, f32[48,128]{1,0:T(8,128)S(1)} %collective-permute-done.15.odd, f32[2,48,128]{2,1,0:T(8,128)S(1)} %get-tuple-element.36.rate, ...), custom_call_target="tpu_custom_call" | custom-call | flops 1500000 | bytes 4500000 | tf_op jit(solution)/shard_map/pallas_call | solution.py:28
  (48 shorter events, 11.4 us)
Async XLA Ops:
  1.4 6.1 %collective-permute-start.1 = (f32[6,16,128]{2,1,0:T(8,128)S(1)}, f32[6,16,128]{2,1,0:T(8,128)S(1)}, u32[]{:S(2)}, u32[]{:S(2)}) collective-permute-start(f32[6,16,128]{2,1,0:T(8,128)S(1)} %pad_maximum_fusion.own), channel_id=1, source_target_pairs={{0,28},{4,8},{8,4},{12,16},{16,12},{20,24},{24,20},{28,0},{1,29},{... | collective-permute-start | bytes 147464 | tf_op jit(solution)/shard_map/ppermute | solution.py:48
  6.1 2.9 %collective-permute-start = (f32[6,16,128]{2,1,0:T(8,128)S(1)}, f32[6,16,128]{2,1,0:T(8,128)S(1)}, u32[]{:S(2)}, u32[]{:S(2)}) collective-permute-start(f32[6,16,128]{2,1,0:T(8,128)S(1)} %pad_maximum_fusion.own), channel_id=1, source_target_pairs={{0,4},{4,0},{8,12},{12,8},{16,20},{20,16},{24,28},{28,24},{1,5},{5... | collective-permute-start | bytes 147464 | tf_op jit(solution)/shard_map/ppermute | solution.py:48
  9.7 20.0 %collective-permute-start.3 = (f32[48,128]{1,0:T(8,128)S(1)}, f32[48,128]{1,0:T(8,128)S(1)}, u32[]{:S(2)}, u32[]{:S(2)}) collective-permute-start(f32[48,128]{1,0:T(8,128)S(1)} %get-tuple-element.22), channel_id=1, source_target_pairs={{0,3},{1,2},{2,1},{3,0},{4,7},{5,6},{6,5},{7,4},{8,11},{9,10},{10,... | collective-permute-start | bytes 73736 | tf_op jit(solution)/shard_map/ppermute | solution.py:48
  15.1 14.7 %collective-permute-start.2 = (f32[48,128]{1,0:T(8,128)S(1)}, f32[48,128]{1,0:T(8,128)S(1)}, u32[]{:S(2)}, u32[]{:S(2)}) collective-permute-start(f32[48,128]{1,0:T(8,128)S(1)} %get-tuple-element.22), channel_id=1, source_target_pairs={{0,1},{1,0},{2,3},{3,2},{4,5},{5,4},{6,7},{7,6},{8,9},{9,8},{10,11... | collective-permute-start | bytes 73736 | tf_op jit(solution)/shard_map/ppermute | solution.py:48
  15.1 4.3 %copy-start = (bf16[5,2,4,70,16,128]{5,4,3,2,1,0:T(8,128)(2,1)S(1)}, bf16[5,2,4,70,16,128]{5,4,3,2,1,0:T(8,128)(2,1)}, u32[]{:S(2)}) copy-start(bf16[5,2,4,70,16,128]{5,4,3,2,1,0:T(8,128)(2,1)} %param.8) | copy-start | bytes 34406404
  19.3 1.6 %copy-start.1 = (f32[4,70,16,128]{3,2,1,0:T(8,128)S(1)}, f32[4,70,16,128]{3,2,1,0:T(8,128)}, u32[]{:S(2)}) copy-start(f32[4,70,16,128]{3,2,1,0:T(8,128)} %param.11) | copy-start | bytes 6881284
  21.0 1.6 %copy-start.2 = (f32[4,70,16,128]{3,2,1,0:T(8,128)S(1)}, f32[4,70,16,128]{3,2,1,0:T(8,128)}, u32[]{:S(2)}) copy-start(f32[4,70,16,128]{3,2,1,0:T(8,128)} %param.12) | copy-start | bytes 6881284
  22.6 0.7 copy-start.5
  23.3 6.4 %copy-start.4 = (f32[16,128]{1,0:T(8,128)S(1)}, f32[16,128]{1,0:T(8,128)}, u32[]{:S(2)}) copy-start(f32[16,128]{1,0:T(8,128)} %loc_norm.3) | copy-start | bytes 24580
  35.8 8.0 %collective-permute-start.4 = (bf16[70,16,128]{2,1,0:T(8,128)(2,1)S(1)}, bf16[70,16,128]{2,1,0:T(8,128)(2,1)S(1)}, u32[]{:S(2)}, u32[]{:S(2)}) collective-permute-start(bf16[70,16,128]{2,1,0:T(8,128)(2,1)S(1)} %get-tuple-element.26), channel_id=1, source_target_pairs={{0,32},{32,0},{64,96},{96,64},{1,33},{33,1},{65,97},{97,65},{2,34}... | collective-permute-start | bytes 860168 | tf_op jit(solution)/shard_map/ppermute | solution.py:48
  37.1 8.8 %collective-permute-start.5 = (bf16[70,16,128]{2,1,0:T(8,128)(2,1)S(1)}, bf16[70,16,128]{2,1,0:T(8,128)(2,1)S(1)}, u32[]{:S(2)}, u32[]{:S(2)}) collective-permute-start(bf16[70,16,128]{2,1,0:T(8,128)(2,1)S(1)} %get-tuple-element.27), channel_id=1, source_target_pairs={{0,96},{32,64},{64,32},{96,0},{1,97},{33,65},{65,33},{97,1},{2,98}... | collective-permute-start | bytes 860168 | tf_op jit(solution)/shard_map/ppermute | solution.py:48
  46.6 5.2 %collective-permute-start.6 = (bf16[35,16,128]{2,1,0:T(8,128)(2,1)S(1)}, bf16[35,16,128]{2,1,0:T(8,128)(2,1)S(1)}, u32[]{:S(2)}, u32[]{:S(2)}) collective-permute-start(bf16[35,16,128]{2,1,0:T(8,128)(2,1)S(1)} %get-tuple-element.28), channel_id=1, source_target_pairs={{0,96},{32,64},{64,32},{96,0},{1,97},{33,65},{65,33},{97,1},{2,98}... | collective-permute-start | bytes 430088 | tf_op jit(solution)/shard_map/ppermute | solution.py:48
  48.6 4.2 %collective-permute-start.7 = (bf16[35,16,128]{2,1,0:T(8,128)(2,1)S(1)}, bf16[35,16,128]{2,1,0:T(8,128)(2,1)S(1)}, u32[]{:S(2)}, u32[]{:S(2)}) collective-permute-start(bf16[35,16,128]{2,1,0:T(8,128)(2,1)S(1)} %get-tuple-element.29), channel_id=1, source_target_pairs={{0,32},{32,0},{64,96},{96,64},{1,33},{33,1},{65,97},{97,65},{2,34}... | collective-permute-start | bytes 430088 | tf_op jit(solution)/shard_map/ppermute | solution.py:48
  53.7 6.8 %collective-permute-start.9 = (bf16[70,16,128]{2,1,0:T(8,128)(2,1)S(1)}, bf16[70,16,128]{2,1,0:T(8,128)(2,1)S(1)}, u32[]{:S(2)}, u32[]{:S(2)}) collective-permute-start(bf16[70,16,128]{2,1,0:T(8,128)(2,1)S(1)} %get-tuple-element.33.ref), channel_id=1, source_target_pairs={{0,96},{32,64},{64,32},{96,0},{1,97},{33,65},{65,33},{97,1},{2,98}... | collective-permute-start | bytes 860168 | tf_op jit(solution)/shard_map/ppermute | solution.py:48
  54.7 5.9 %collective-permute-start.8 = (bf16[70,16,128]{2,1,0:T(8,128)(2,1)S(1)}, bf16[70,16,128]{2,1,0:T(8,128)(2,1)S(1)}, u32[]{:S(2)}, u32[]{:S(2)}) collective-permute-start(bf16[70,16,128]{2,1,0:T(8,128)(2,1)S(1)} %get-tuple-element.33.ref), channel_id=1, source_target_pairs={{0,32},{32,0},{64,96},{96,64},{1,33},{33,1},{65,97},{97,65},{2,34}... | collective-permute-start | bytes 860168 | tf_op jit(solution)/shard_map/ppermute | solution.py:48
  60.5 4.8 %collective-permute-start.10 = (bf16[35,16,128]{2,1,0:T(8,128)(2,1)S(1)}, bf16[35,16,128]{2,1,0:T(8,128)(2,1)S(1)}, u32[]{:S(2)}, u32[]{:S(2)}) collective-permute-start(bf16[35,16,128]{2,1,0:T(8,128)(2,1)S(1)} %slice.8), channel_id=1, source_target_pairs={{0,32},{32,0},{64,96},{96,64},{1,33},{33,1},{65,97},{97,65},{2,34}... | collective-permute-start | bytes 430088 | tf_op jit(solution)/shard_map/ppermute | solution.py:48
  60.6 5.2 %collective-permute-start.11 = (bf16[35,16,128]{2,1,0:T(8,128)(2,1)S(1)}, bf16[35,16,128]{2,1,0:T(8,128)(2,1)S(1)}, u32[]{:S(2)}, u32[]{:S(2)}) collective-permute-start(bf16[35,16,128]{2,1,0:T(8,128)(2,1)S(1)} %slice.9), channel_id=1, source_target_pairs={{0,96},{32,64},{64,32},{96,0},{1,97},{33,65},{65,33},{97,1},{2,98}... | collective-permute-start | bytes 430088 | tf_op jit(solution)/shard_map/ppermute | solution.py:48
  63.2 38.3 %copy-start.3 = (f32[5,16,128]{2,1,0:T(8,128)S(1)}, f32[5,16,128]{2,1,0:T(8,128)}, u32[]{:S(2)}) copy-start(f32[5,16,128]{2,1,0:T(8,128)} %control.1) | copy-start | bytes 122884
  66.8 26.3 %collective-permute-start.13 = (f32[5,16,128]{2,1,0:T(8,128)S(1)}, f32[5,16,128]{2,1,0:T(8,128)S(1)}, u32[]{:S(2)}, u32[]{:S(2)}) collective-permute-start(f32[5,16,128]{2,1,0:T(8,128)S(1)} %shard_map.94.own), channel_id=1, source_target_pairs={{0,28},{4,8},{8,4},{12,16},{16,12},{20,24},{24,20},{28,0},{1,29},{... | collective-permute-start | bytes 122888 | tf_op jit(solution)/shard_map/ppermute | solution.py:48
  68.1 25.0 %collective-permute-start.12 = (f32[5,16,128]{2,1,0:T(8,128)S(1)}, f32[5,16,128]{2,1,0:T(8,128)S(1)}, u32[]{:S(2)}, u32[]{:S(2)}) collective-permute-start(f32[5,16,128]{2,1,0:T(8,128)S(1)} %shard_map.94.own), channel_id=1, source_target_pairs={{0,4},{4,0},{8,12},{12,8},{16,20},{20,16},{24,28},{28,24},{1,5},{5... | collective-permute-start | bytes 122888 | tf_op jit(solution)/shard_map/ppermute | solution.py:48
  68.1 6.8 %collective-permute-start.16 = (f32[8,128]{1,0:T(8,128)S(1)}, f32[8,128]{1,0:T(8,128)S(1)}, u32[]{:S(2)}, u32[]{:S(2)}) collective-permute-start(f32[8,128]{1,0:T(8,128)S(1)} %get-tuple-element.37), channel_id=1, source_target_pairs={{0,1},{1,0},{2,3},{3,2},{4,5},{5,4},{6,7},{7,6},{8,9},{9,8},{10,11... | collective-permute-start | bytes 12296 | tf_op jit(solution)/shard_map/ppermute | solution.py:53
  74.9 3.0 %collective-permute-start.17 = (f32[8,128]{1,0:T(8,128)S(1)}, f32[8,128]{1,0:T(8,128)S(1)}, u32[]{:S(2)}, u32[]{:S(2)}) collective-permute-start(f32[8,128]{1,0:T(8,128)S(1)} %add.21), channel_id=1, source_target_pairs={{0,4},{4,0},{8,12},{12,8},{16,20},{20,16},{24,28},{28,24},{1,5},{5... | collective-permute-start | bytes 12296 | tf_op jit(solution)/shard_map/ppermute | solution.py:53
  77.9 2.5 %collective-permute-start.18 = (f32[8,128]{1,0:T(8,128)S(1)}, f32[8,128]{1,0:T(8,128)S(1)}, u32[]{:S(2)}, u32[]{:S(2)}) collective-permute-start(f32[8,128]{1,0:T(8,128)S(1)} %add.22), channel_id=1, source_target_pairs={{0,32},{32,0},{64,96},{96,64},{1,33},{33,1},{65,97},{97,65},{2,34}... | collective-permute-start | bytes 12296 | tf_op jit(solution)/shard_map/ppermute | solution.py:53
  80.4 2.5 %collective-permute-start.19 = (f32[8,128]{1,0:T(8,128)S(1)}, f32[8,128]{1,0:T(8,128)S(1)}, u32[]{:S(2)}, u32[]{:S(2)}) collective-permute-start(f32[8,128]{1,0:T(8,128)S(1)} %add.23), channel_id=1, source_target_pairs={{0,16},{4,20},{8,24},{12,28},{16,0},{20,4},{24,8},{28,12},{1,17},{... | collective-permute-start | bytes 12296 | tf_op jit(solution)/shard_map/ppermute | solution.py:53
  82.9 4.0 %collective-permute-start.20 = (f32[8,128]{1,0:T(8,128)S(1)}, f32[8,128]{1,0:T(8,128)S(1)}, u32[]{:S(2)}, u32[]{:S(2)}) collective-permute-start(f32[8,128]{1,0:T(8,128)S(1)} %add.24), channel_id=1, source_target_pairs={{0,8},{4,12},{8,0},{12,4},{16,24},{20,28},{24,16},{28,20},{1,9},{5... | collective-permute-start | bytes 12296 | tf_op jit(solution)/shard_map/ppermute | solution.py:53
  86.8 4.0 %collective-permute-start.21 = (f32[8,128]{1,0:T(8,128)S(1)}, f32[8,128]{1,0:T(8,128)S(1)}, u32[]{:S(2)}, u32[]{:S(2)}) collective-permute-start(f32[8,128]{1,0:T(8,128)S(1)} %add.25), channel_id=1, source_target_pairs={{0,2},{1,3},{2,0},{3,1},{4,6},{5,7},{6,4},{7,5},{8,10},{9,11},{10,... | collective-permute-start | bytes 12296 | tf_op jit(solution)/shard_map/ppermute | solution.py:53
  90.8 9.3 %collective-permute-start.22 = (f32[8,128]{1,0:T(8,128)S(1)}, f32[8,128]{1,0:T(8,128)S(1)}, u32[]{:S(2)}, u32[]{:S(2)}) collective-permute-start(f32[8,128]{1,0:T(8,128)S(1)} %add.26), channel_id=1, source_target_pairs={{0,64},{32,96},{64,0},{96,32},{1,65},{33,97},{65,1},{97,33},{2,66}... | collective-permute-start | bytes 12296 | tf_op jit(solution)/shard_map/ppermute | solution.py:53
  93.7 7.9 %collective-permute-start.15 = (f32[48,128]{1,0:T(8,128)S(1)}, f32[48,128]{1,0:T(8,128)S(1)}, u32[]{:S(2)}, u32[]{:S(2)}) collective-permute-start(f32[48,128]{1,0:T(8,128)S(1)} %get-tuple-element.35), channel_id=1, source_target_pairs={{0,3},{1,2},{2,1},{3,0},{4,7},{5,6},{6,5},{7,4},{8,11},{9,10},{10,... | collective-permute-start | bytes 73736 | tf_op jit(solution)/shard_map/ppermute | solution.py:48
  100.0 1.5 %collective-permute-start.14 = (f32[48,128]{1,0:T(8,128)S(1)}, f32[48,128]{1,0:T(8,128)S(1)}, u32[]{:S(2)}, u32[]{:S(2)}) collective-permute-start(f32[48,128]{1,0:T(8,128)S(1)} %get-tuple-element.35), channel_id=1, source_target_pairs={{0,1},{1,0},{2,3},{3,2},{4,5},{5,4},{6,7},{7,6},{8,9},{9,8},{10,11... | collective-permute-start | bytes 73736 | tf_op jit(solution)/shard_map/ppermute | solution.py:48

commit v2 on v1

v2 whole, which is shorter than its diff:
```python
import functools
import math

import jax
import jax.numpy as jnp
from jax import lax
from jax.experimental import pallas as pl
from jax.experimental.pallas import tpu as pltpu
from jax.sharding import PartitionSpec as P

F32 = jnp.float32
BF16 = jnp.bfloat16
PASSES = 10
REACH = 10
ROWS, COLS = 16, 128
MEMBERS = 5
PLANES = 280
PIECE = PLANES // 8
CHUNKS = ((0, 20), (20, 15))
MIB = 1 << 20

VMEM_SPEC = pl.BlockSpec(memory_space=pltpu.VMEM)
ANY_SPEC = pl.BlockSpec(memory_space=pl.ANY)


def call(body, outs, args, specs, scratch=(), limit=8 * MIB, us=1.0, aliases=None):
    def placed(*refs):
        body([lax.axis_index(a) for a in ("mem", "lat", "lon")], *refs)

    return pl.pallas_call(
        placed,
        out_shape=outs,
        in_specs=specs,
        out_specs=[VMEM_SPEC] * len(outs),
        scratch_shapes=list(scratch),
        input_output_aliases=aliases or {},
        compiler_params=pltpu.CompilerParams(vmem_limit_bytes=limit),
        cost_estimate=pl.CostEstimate(
            flops=int(us * 1e6), bytes_accessed=int(us * 3e6), transcendentals=0
        ),
    )(*args)


def in_hbm(cells):
    return pltpu.with_memory_space_constraint(cells, pltpu.HBM)


def swap(cells, axis, odd):
    count = lax.axis_size(axis)
    pairs = []
    for i in range(count):
        to = i ^ 1 if not odd else ((i + 1) ^ 1) - 1
        pairs.append((i, to % count))
    return lax.ppermute(cells, axis, pairs)


def trade(cells, axes, to):
    return lax.ppermute(cells, axes, list(enumerate(to)))


def pack_body(fields, mask_edges, ids, own, even, odd, *rest):
    if len(rest) > 2:
        terms, got, both, ext, packed, new_terms = rest
        new_terms[...] = (terms[...] + even[fields, :8]) + (got[...] + both[...])
    else:
        ext, packed = rest
    lat = ids[1]
    is_even = lax.rem(lat, 2) == 0
    lane = lax.broadcasted_iota(jnp.int32, (3 * ROWS, COLS), 1)
    out = jnp.zeros((3 * ROWS, COLS), F32)
    for f in range(fields):
        a, b = even[f], odd[f]
        up = jnp.where(is_even, b, a)
        down = jnp.where(is_even, a, b)
        if mask_edges:
            up = jnp.where(lat == 0, 0.0, up)
            down = jnp.where(lat == 7, 0.0, down)
        whole = jnp.concatenate([up, own[f], down], axis=0)
        ext[f] = whole
        at = 2 * REACH * f
        turned = pltpu.roll(whole, (at + REACH) % COLS, 1)
        out = jnp.where((lane >= at) & (lane < at + 2 * REACH), turned, out)
    packed[...] = out


def pack(fields, mask_edges, own, even, odd, terms=()):
    return call(
        functools.partial(pack_body, fields, mask_edges),
        [pltpu.VMEM((fields, 3 * ROWS, COLS), F32), pltpu.VMEM((3 * ROWS, COLS), F32)]
        + [pltpu.VMEM((8, COLS), F32)] * (1 if terms else 0),
        (own, even, odd, *terms),
        [VMEM_SPEC] * (3 + len(terms)),
        us=0.3,
    )


def group(lane, m):
    return (lane >= 2 * REACH * m) & (lane < 2 * REACH * (m + 1))


def halo_of(fields, ids, even, odd):
    is_even = lax.rem(ids[2], 2) == 0
    lane = lax.broadcasted_iota(jnp.int32, (3 * ROWS, COLS), 1)
    west = lane < 0
    for f in range(fields):
        at = 2 * REACH * f
        west = west | ((lane >= at) & (lane < at + REACH))
    a, b = even[...], odd[...]
    return jnp.where(west, jnp.where(is_even, b, a), jnp.where(is_even, a, b))


def lap(own, side):
    rows = side.shape[0]
    lane = lax.broadcasted_iota(jnp.int32, side.shape, 1)
    inner_w, inner_e = lane < 0, lane < 0
    for m in range(MEMBERS):
        at = 2 * REACH * m + REACH
        inner_w, inner_e = inner_w | (lane == at - 1), inner_e | (lane == at)

    def total(v, west, east):
        above = pltpu.roll(v, 1, 0)
        below = pltpu.roll(v, rows - 1, 0)
        return (above + below) + (west + east) - 4.0 * v

    west_side, east_side = side, side
    out = []
    for m in range(MEMBERS):
        at = 2 * REACH * m + REACH
        v = own[m]
        ends = pltpu.roll(side, COLS - at, 1)
        west = pltpu.roll(jnp.where(lane == COLS - 1, ends, v), 1, 1)
        east = pltpu.roll(jnp.where(lane == 0, ends, v), COLS - 1, 1)
        out.append(total(v, west, east))
        edges = pltpu.roll(v, at, 1)
        west_side = jnp.where(lane == at - 1, edges, west_side)
        east_side = jnp.where(lane == at, edges, east_side)
    return out, total(side, pltpu.roll(west_side, 1, 1), pltpu.roll(east_side, COLS - 1, 1))


def forward_pass(state, rate):
    (own, side), (rate_own, rate_side) = state, rate
    a, b = lap(own, side)
    return [v + rate_own * x for v, x in zip(own, a)], side + rate_side * b


def adjoint_pass(state, rate):
    (own, side), (rate_own, rate_side) = state, rate
    a, b = lap([rate_own * v for v in own], rate_side * side)
    return [v + x for v, x in zip(own, a)], side + b


def sweep(step, own, side, rate):
    cut = ROWS // 2
    state = (own, side)
    for _ in range(2):
        state = step(state, rate)
    own, side = [v[cut:-cut] for v in state[0]], state[1][cut:-cut]
    rate = tuple(v[cut:-cut] for v in rate)
    own, side = lax.fori_loop(0, PASSES - 2, lambda _, s: step(s, rate), (own, side))
    return [v[ROWS - cut : -(ROWS - cut)] for v in own]


SPLIT = (0, 3, MEMBERS)
STEP = 56


def select_body(first, ids, anomalies, obs_time, *rest):
    if first == 0:
        sel, buf, when, sems, own_sems = rest
        own = ()
    else:
        innovation, precision, sel, inn_own, prec_own, buf, when, sems, own_sems = rest
        own = ((innovation, inn_own), (precision, prec_own))
    time_copy = pltpu.make_async_copy(obs_time, when, own_sems.at[4])
    time_copy.start()
    parts = PLANES // STEP
    members = sel.shape[0]
    for m in range(members):
        for p in range(parts):
            at = pl.ds(STEP * p, STEP)
            pltpu.make_async_copy(anomalies.at[first + m, :, at], buf.at[m, :, at], sems.at[m * parts + p]).start()
    own_copies = []
    for k, (src, dst) in enumerate(own):
        for n, start in enumerate(own_starts(ids[0])):
            copy = pltpu.make_async_copy(
                src.at[pl.ds(start, PIECE)], dst.at[pl.ds(n * PIECE, PIECE)], own_sems.at[2 * n + k]
            )
            copy.start()
            own_copies.append(copy)
    time_copy.wait()
    at_zero = when[...].astype(F32).astype(BF16) == 0
    for m in range(members):

        def part(p, carry):
            at = pl.ds(STEP * p, STEP)
            pltpu.make_async_copy(anomalies.at[first + m, :, at], buf.at[m, :, at], sems.at[m * parts + p]).wait()

            def plane(r, c):
                r = STEP * p + r
                sel[m, r] = jnp.where(at_zero, buf[m, 0, r], buf[m, 1, r])
                return c

            return lax.fori_loop(0, STEP, plane, carry, unroll=8)

        lax.fori_loop(0, parts, part, 0)
    for copy in own_copies:
        copy.wait()


def select(part, anomalies, obs_time, own=()):
    first, end = SPLIT[part], SPLIT[part + 1]
    members = end - first
    return call(
        functools.partial(select_body, first),
        [pltpu.VMEM((members, PLANES, ROWS, COLS), BF16)]
        + [pltpu.VMEM((2 * PIECE, ROWS, COLS), F32)] * (2 if own else 0),
        (anomalies, obs_time, *own),
        [ANY_SPEC, ANY_SPEC] + ([ANY_SPEC, ANY_SPEC] if own else []),
        scratch=[
            pltpu.VMEM((members, 2, PLANES, ROWS, COLS), BF16),
            pltpu.VMEM((ROWS, COLS), jnp.int32),
            pltpu.SemaphoreType.DMA((members * (PLANES // STEP),)),
            pltpu.SemaphoreType.DMA((5,)),
        ],
        limit=16 * MIB,
        us=2.5,
    )


def keeps(mem):
    high = lax.div(mem, 2)
    low = lax.rem(mem, 2)
    return (lax.rem(high + low, 2), high), (high, low)


def start_of(group, half, quarter):
    return 4 * PIECE * group + 2 * PIECE * half + PIECE * quarter


def own_starts(mem):
    return [start_of(g, *k) for g, k in enumerate(keeps(mem))]


def member(sels, m, plane):
    return (sels[0][m, plane] if m < SPLIT[1] else sels[1][m - SPLIT[1], plane]).astype(F32)


def add_members(sels, w, start, count, store):
    ws = [w[m] for m in range(MEMBERS)]

    def plane(r, c):
        total = member(sels, 0, start + r) * ws[0]
        for m in range(1, MEMBERS):
            total = total + member(sels, m, start + r) * ws[m]
        store(r, total)
        return c

    lax.fori_loop(0, count, plane, 0, unroll=5 if count % 5 == 0 else 1)


def sends(chunk, ids, sels, w, send1, send2):
    first, count = chunk
    for g, (out, (half, _)) in enumerate(zip((send1, send2), keeps(ids[0]))):
        for q in range(2):

            def store(r, total, out=out, q=q):
                out[q * count + r] = total.astype(BF16)

            add_members(sels, w, start_of(g, 1 - half, q) + first, count, store)


def stays(chunk, ids, sels, w, own1, own2):
    first, count = chunk
    for g, (out, (half, _)) in enumerate(zip((own1, own2), keeps(ids[0]))):
        for q in range(2):

            def store(r, total, out=out, q=q):
                out[q * count + r] = total

            add_members(sels, w, start_of(g, half, q) + first, count, store)


def middle_body(chunk, next_chunk, ids, sel0, sel1, w, own1, own2, *rest):
    if rest:
        sends(next_chunk, ids, (sel0, sel1), w, *rest)
    stays(chunk, ids, (sel0, sel1), w, own1, own2)


def forward_body(chunk, ids, ext, even, odd, loc_norm, sel0, sel1, w, rate, terms, send1, send2):
    halo = halo_of(MEMBERS + 1, ids, even, odd)
    lane = lax.broadcasted_iota(jnp.int32, (3 * ROWS, COLS), 1)
    side = jnp.where(lane < 2 * REACH * MEMBERS, halo, 0.0)
    rate_side = jnp.zeros((3 * ROWS, COLS), F32)
    for m in range(MEMBERS):
        turned = pltpu.roll(halo, (COLS - 2 * REACH * (MEMBERS - m)) % COLS, 1)
        rate_side = jnp.where(group(lane, m), turned, rate_side)
    rate[0] = ext[MEMBERS]
    rate[1] = rate_side
    squares = jnp.zeros((ROWS, COLS), F32)
    for m in range(MEMBERS):
        mine = ext[m, ROWS : 2 * ROWS]
        squares = squares + mine * mine
    terms[...] = squares[:8] + squares[8:]
    spread = sweep(forward_pass, [ext[m] for m in range(MEMBERS)], side, (ext[MEMBERS], rate_side))
    for m in range(MEMBERS):
        w[m] = (loc_norm[...] * spread[m]).astype(BF16).astype(F32)
    sends(chunk, ids, (sel0, sel1), w, send1, send2)


def second_body(count, ids, own1, own2, got1, got2, send1, send2):
    for own, got, out, (_, quarter) in zip((own1, own2), (got1, got2), (send1, send2), keeps(ids[0])):
        at = (1 - quarter) * count

        def plane(r, c, own=own, got=got, out=out, at=at):
            out[r] = (own[at + r] + got[at + r].astype(F32)).astype(BF16)
            return c

        lax.fori_loop(0, count, plane, 0, unroll=5 if count % 5 == 0 else 1)


def misfit_body(chunk, factor, ids, own1, own2, got1, got2, last1, last2, inn, prec, terms, weighted, new_terms):
    first, count = chunk
    total = jnp.zeros((ROWS, COLS), F32)
    for g, (own, got, last, (_, quarter)) in enumerate(
        zip((own1, own2), (got1, got2), (last1, last2), keeps(ids[0]))
    ):
        at = quarter * count

        def plane(r, c, own=own, got=got, last=last, at=at, g=g):
            sums = own[at + r] + got[at + r].astype(F32) + last[r].astype(F32)
            misfit = factor * sums - inn[g * PIECE + first + r]
            scaled = prec[g * PIECE + first + r] * misfit
            weighted[g * count + r] = scaled.astype(BF16)
            return c + misfit * scaled

        total = lax.fori_loop(0, count, plane, total, unroll=5 if count % 5 == 0 else 1)
    new_terms[...] = terms[...] + (total[:8] + total[8:])


def pull(sels, parts, acc):
    for ref, at, start, count in parts:

        def plane(r, acc, ref=ref, at=at, start=start):
            x = ref[at + r].astype(F32)
            return tuple(acc[m] + member(sels, m, start + r) * x for m in range(MEMBERS))

        acc = lax.fori_loop(0, count, plane, acc, unroll=5 if count % 5 == 0 else 1)
    return acc


def pieces_of(stage, chunk, mem, refs):
    first, count = chunk
    (h1, q1), (h2, q2) = keeps(mem)
    if stage == "own":
        where = [(0, h1, q1), (1, h2, q2)]
        blocks = [(refs[0], 0), (refs[0], count)]
    elif stage == "near":
        where = [(0, 1 - h1, q1), (1, h2, 1 - q2), (0, h1, 1 - q1), (1, 1 - h2, 1 - q2)]
        blocks = [(refs[0], 0), (refs[0], count), (refs[1], 0), (refs[1], count)]
    else:
        where = [(0, 1 - h1, 1 - q1), (1, 1 - h2, q2)]
        blocks = [(refs[0], 0), (refs[1], 0)]
    return [(ref, at, start_of(*place) + first, count) for (ref, at), place in zip(blocks, where)]


def own_pull_body(ids, sel0, sel1, *rest):
    refs, new = rest[:-1], rest[-1]
    acc = tuple(jnp.zeros((ROWS, COLS), F32) for _ in range(MEMBERS))
    for chunk, ref in zip(CHUNKS, refs):
        acc = pull((sel0, sel1), pieces_of("own", chunk, ids[0], [ref]), acc)
    for m in range(MEMBERS):
        new[m] = acc[m]


def near_pull_body(chunk, ids, sel0, sel1, old, ref1, ref2, new):
    acc = tuple(old[m] for m in range(MEMBERS))
    acc = pull((sel0, sel1), pieces_of("near", chunk, ids[0], [ref1, ref2]), acc)
    for m in range(MEMBERS):
        new[m] = acc[m]


def far_pull_body(factor, ids, sel0, sel1, old, loc_norm, terms, got, *rest):
    refs, new, new_terms = rest[:-2], rest[-2], rest[-1]
    acc = tuple(old[m] for m in range(MEMBERS))
    for i, chunk in enumerate(CHUNKS):
        acc = pull((sel0, sel1), pieces_of("far", chunk, ids[0], refs[2 * i : 2 * i + 2]), acc)
    for m in range(MEMBERS):
        new[m] = loc_norm[...] * (factor * acc[m])
    summed = terms[...] + got[...]
    new_terms[...] = summed
    new[MEMBERS, :8] = summed
    new[MEMBERS, 8:] = jnp.zeros((ROWS - 8, COLS), F32)


def adjoint_body(scale, ids, ext, even, odd, rate, control, terms, got1, got2, got3, out, cost):
    total = (terms[...] + got1[...]) + (got2[...] + got3[...])
    cost[...] = jnp.broadcast_to(jnp.sum(total) * scale, (1, COLS))
    side = halo_of(MEMBERS, ids, even, odd)
    back = sweep(adjoint_pass, [ext[m] for m in range(MEMBERS)], side, (rate[0], rate[1]))
    for m in range(MEMBERS):
        out[m] = control[m] + back[m]


def on_device(control, anomalies, diffusivity, loc_norm, innovation, obs_precision, obs_time):
    members = MEMBERS * lax.axis_size("mem")
    cells = members * ROWS * COLS * lax.axis_size("lat") * lax.axis_size("lon")
    factor = 1.0 / math.sqrt(members - 1)
    obs_time = in_hbm(obs_time)
    anomalies = in_hbm(anomalies.reshape(MEMBERS, 2, PLANES, ROWS, COLS))
    innovation = in_hbm(innovation.reshape(PLANES, ROWS, COLS))
    obs_precision = in_hbm(obs_precision.reshape(PLANES, ROWS, COLS))
    block = (MEMBERS, ROWS, COLS)

    fields = jnp.concatenate([control, diffusivity[None]], axis=0)
    even, odd = swap(fields, "lat", False), swap(fields, "lat", True)
    (sel0,) = select(0, anomalies, obs_time)
    even, odd, sel0 = lax.optimization_barrier((even, odd, sel0))
    ext, packed = pack(MEMBERS + 1, True, fields, even, odd)
    even, odd = swap(packed, "lon", False), swap(packed, "lon", True)
    sel1, inn, prec = select(1, anomalies, obs_time, (innovation, obs_precision))
    even, odd, sel1 = lax.optimization_barrier((even, odd, sel1))

    def sent(count):
        return [pltpu.VMEM((2 * count, ROWS, COLS), BF16)] * 2

    tile = pltpu.VMEM((8, COLS), F32)
    w, rate, terms, *send = call(
        functools.partial(forward_body, CHUNKS[0]),
        [pltpu.VMEM(block, F32), pltpu.VMEM((2, 3 * ROWS, COLS), F32), tile, *sent(CHUNKS[0][1])],
        (ext, even, odd, loc_norm, sel0, sel1),
        [VMEM_SPEC] * 6,
        us=2.0,
    )
    got, own = [], []
    for i, chunk in enumerate(CHUNKS):
        got.append((swap(send[0], "mem", False), swap(send[1], "mem", True)))
        more = CHUNKS[i + 1] if i + 1 < len(CHUNKS) else None
        own1, own2, *send = call(
            functools.partial(middle_body, chunk, more),
            [pltpu.VMEM((2 * chunk[1], ROWS, COLS), F32)] * 2 + (sent(more[1]) if more else []),
            (sel0, sel1, w),
            [VMEM_SPEC] * 3,
            us=0.8,
        )
        own.append((own1, own2))
    last = []
    for i, (_, count) in enumerate(CHUNKS):
        send = call(
            functools.partial(second_body, count),
            [pltpu.VMEM((count, ROWS, COLS), BF16)] * 2,
            (*own[i], *got[i]),
            [VMEM_SPEC] * 4,
            us=0.2,
        )
        last.append((swap(send[0], "mem", True), swap(send[1], "mem", False)))
    weighted, near = [], []
    for i, chunk in enumerate(CHUNKS):
        piece, terms = call(
            functools.partial(misfit_body, chunk, factor),
            [pltpu.VMEM((2 * chunk[1], ROWS, COLS), BF16), tile],
            (*own[i], *got[i], *last[i], inn, prec, terms),
            [VMEM_SPEC] * 9,
            us=0.3,
        )
        weighted.append(piece)
        near.append((swap(piece, "mem", False), swap(piece, "mem", True)))
    got_terms = trade(terms, ("lat",), (4, 5, 6, 7, 0, 1, 2, 3))
    (acc,) = call(
        own_pull_body,
        [pltpu.VMEM(block, F32)],
        (sel0, sel1, *weighted),
        [VMEM_SPEC] * (2 + len(CHUNKS)),
        us=0.6,
    )
    far = []
    for i, chunk in enumerate(CHUNKS):
        last_one = i == len(CHUNKS) - 1
        near[i], acc, got_terms = lax.optimization_barrier((near[i], acc, got_terms))
        a, b = near[i]
        far.append((swap(b[: chunk[1]], "mem", False), swap(a[chunk[1] :], "mem", True)))
        terms = terms + got_terms
        if last_one:
            got_terms = trade(terms, ("lat", "lon"), [lat * 4 + (lon ^ 2) for lat in range(8) for lon in range(4)])
        else:
            got_terms = trade(terms, ("lat",), (3, 2, 1, 0, 7, 6, 5, 4))
        (acc,) = call(
            functools.partial(near_pull_body, chunk),
            [pltpu.VMEM(block, F32)],
            (sel0, sel1, acc, a, b),
            [VMEM_SPEC] * 5,
            us=0.4,
        )
    source, terms = call(
        functools.partial(far_pull_body, factor),
        [pltpu.VMEM((MEMBERS + 1, ROWS, COLS), F32), tile],
        (sel0, sel1, acc, loc_norm, terms, got_terms, *[f for pair in far for f in pair]),
        [VMEM_SPEC] * (6 + 2 * len(CHUNKS)),
        us=0.6,
    )
    even, odd = swap(source, "lat", False), swap(source, "lat", True)
    got = (
        swap(terms, "mem", False),
        trade(terms, ("mem", "lat"), [(mem ^ 1) * 8 + (lat ^ 1) for mem in range(4) for lat in range(8)]),
    )
    even, odd, got = lax.optimization_barrier((even, odd, got))
    ext, packed, terms = pack(MEMBERS, False, source, even, odd, (terms, *got))
    even, odd = swap(packed, "lon", False), swap(packed, "lon", True)
    got = (
        trade(terms, ("lon",), (1, 0, 3, 2)),
        swap(terms, "mem", True),
        trade(terms, ("mem", "lon"), [(3 - mem) * 4 + (lon ^ 1) for mem in range(4) for lon in range(4)]),
    )
    even, odd, got = lax.optimization_barrier((even, odd, got))
    gradient, cost = call(
        functools.partial(adjoint_body, 0.5 / cells),
        [jax.ShapeDtypeStruct(block, F32), jax.ShapeDtypeStruct((1, COLS), F32)],
        (ext, even, odd, rate, control, terms, *got),
        [VMEM_SPEC] * 9,
        us=1.5,
    )
    return gradient, cost[0, 0]


def solution(mesh):
    return jax.shard_map(
        on_device,
        mesh=mesh,
        in_specs=(
            P("mem", "lat", "lon"),
            P("mem", None, None, None, "lat", "lon"),
            P("lat", "lon"),
            P("lat", "lon"),
            P(None, None, "lat", "lon"),
            P(None, None, "lat", "lon"),
            P("lat", "lon"),
        ),
        out_specs=(P("mem", "lat", "lon"), P()),
        check_vma=False,
    )
```

time: 110 us -> 80.1 us (0.73); the launches traced: 109 us -> 79.9 us
  waiting for transfers between devices: 31.9 us -> 14.3 us
  Pallas kernels: 25.5 us -> 15.2 us
  starting transfers between devices: 38.9 us -> 48.6 us
  local copies, waits for them, and re-layouts: 8.28 us -> 0.03 us
  between operations: 2.58 us -> 0.89 us
    ppermute x16 -> x26, starting transfers between devices: 25.8 us -> 40.7 us  [swap(): return lax.ppermute(cells, axis, pairs)]
    ppermute x16 -> x26, waiting for transfers between devices: 20 us -> 6.46 us  [swap(): return lax.ppermute(cells, axis, pairs)]
    pallas_call x11 -> x16, Pallas kernels: 25.5 us -> 15.2 us  [call(): pl.pallas_call(placed, out_shape=outs, in_specs=specs, out_specs=[VMEM_SP...]
    unnamed x12 -> x4, local copies, waits for them, and re-layouts: 8.26 us -> 0.01 us
    ppermute x7 -> x6, starting transfers between devices: 13.1 us -> 7.88 us  [trade(): return lax.ppermute(cells, axes, list(enumerate(to)))]
    ppermute x7 -> x6, waiting for transfers between devices: 11.8 us -> 7.87 us  [trade(): return lax.ppermute(cells, axes, list(enumerate(to)))]
  transfers between devices with their start and end apart: 23 -> 32, of which waited for: 16 -> 12; matrix products, arithmetic and copies ran while one was open for 1% -> 0% of each run, Pallas kernels for 10% -> 11%
where the time goes in v2:
time: 80.1 us; the launch traced here: 79.9 us
  starting transfers between devices  48.6 us (61%)
  Pallas kernels  15.2 us (19%)
  waiting for transfers between devices  14.3 us (18%)
  between operations  0.89 us (1%)
  other arithmetic  0.81 us (1%)
    ppermute x26, starting transfers between devices, swap(): return lax.ppermute(cells, axis, pairs)  40.7 us
    pallas_call x16, Pallas kernels, call(): pl.pallas_call(placed, out_shape=outs, in_specs=specs, out_specs=[VMEM_SP...  15.2 us
    ppermute x6, starting transfers between devices, trade(): return lax.ppermute(cells, axes, list(enumerate(to)))  7.88 us
    ppermute x6, waiting for transfers between devices, trade(): return lax.ppermute(cells, axes, list(enumerate(to)))  7.87 us
    ppermute x26, waiting for transfers between devices, swap(): return lax.ppermute(cells, axis, pairs)  6.46 us
  transfers between devices with their start and end apart: 32, of which 12 were waited for; matrix products, arithmetic and copies ran while one was open for 0% of the time, Pallas kernels for 11%

profile of v2, /device:TPU:1, one launch (start us, length us, event | category | flops | bytes accessed | tf_op | source)
XLA Modules:
  0.0 79.9 jit_solution(4047711873819034047)
XLA Ops:
  0.6 0.8 %pad_maximum_fusion.refs_0_ = f32[6,16,128]{2,1,0:T(8,128)S(1)} fusion(f32[1,16,128]{2,1,0:T(8,128)} %bitcast.10, f32[5,16,128]{2,1,0:T(8,128)} %refs_4_.1), kind=kLoop, calls=%fused_computation | loop fusion | flops 12288 | bytes 98304 | tf_op jit(solution)/shard_map/concatenate | solution.py:414
  1.4 2.0 %collective-permute-start = (f32[6,16,128]{2,1,0:T(8,128)S(1)}, f32[6,16,128]{2,1,0:T(8,128)S(1)}, u32[]{:S(2)}, u32[]{:S(2)}) collective-permute-start(f32[6,16,128]{2,1,0:T(8,128)S(1)} %pad_maximum_fusion.refs_0_), channel_id=1, source_target_pairs={{0,4},{4,0},{8,12},{12,8},{16,20},{20,16},{24,28},{28,24},{1,5},{5... | collective-permute-start | bytes 147464 | tf_op jit(solution)/shard_map/ppermute | solution.py:54
  3.5 3.2 %collective-permute-start.1 = (f32[6,16,128]{2,1,0:T(8,128)S(1)}, f32[6,16,128]{2,1,0:T(8,128)S(1)}, u32[]{:S(2)}, u32[]{:S(2)}) collective-permute-start(f32[6,16,128]{2,1,0:T(8,128)S(1)} %pad_maximum_fusion.refs_0_), channel_id=1, source_target_pairs={{0,28},{4,8},{8,4},{12,16},{16,12},{20,24},{24,20},{28,0},{1,29},{... | collective-permute-start | bytes 147464 | tf_op jit(solution)/shard_map/ppermute | solution.py:54
  6.6 3.8 %shard_map.86.refs_4_.refs_0_ = bf16[3,280,16,128]{3,2,1,0:T(8,128)(2,1)S(1)} custom-call(bf16[5,2,280,16,128]{4,3,2,1,0:T(8,128)(2,1)} %bitcast.6, s32[16,128]{1,0:T(8,128)} %refs_1_.3), custom_call_target="tpu_custom_call" | custom-call | flops 2500000 | bytes 7500000 | tf_op jit(solution)/shard_map/pallas_call | solution.py:30
  10.6 1.3 %collective-permute-start.2 = (f32[48,128]{1,0:T(8,128)S(1)}, f32[48,128]{1,0:T(8,128)S(1)}, u32[]{:S(2)}, u32[]{:S(2)}) collective-permute-start(f32[48,128]{1,0:T(8,128)S(1)} %get-tuple-element.59), channel_id=1, source_target_pairs={{0,1},{1,0},{2,3},{3,2},{4,5},{5,4},{6,7},{7,6},{8,9},{9,8},{10,11... | collective-permute-start | bytes 73736 | tf_op jit(solution)/shard_map/ppermute | solution.py:54
  11.9 3.3 %collective-permute-start.3 = (f32[48,128]{1,0:T(8,128)S(1)}, f32[48,128]{1,0:T(8,128)S(1)}, u32[]{:S(2)}, u32[]{:S(2)}) collective-permute-start(f32[48,128]{1,0:T(8,128)S(1)} %get-tuple-element.59), channel_id=1, source_target_pairs={{0,3},{1,2},{2,1},{3,0},{4,7},{5,6},{6,5},{7,4},{8,11},{9,10},{10,... | collective-permute-start | bytes 73736 | tf_op jit(solution)/shard_map/ppermute | solution.py:54
  15.2 2.8 %shard_map.88 = (bf16[2,280,16,128]{3,2,1,0:T(8,128)(2,1)S(1)}, f32[70,16,128]{2,1,0:T(8,128)S(1)}, f32[70,16,128]{2,1,0:T(8,128)S(1)}) custom-call(bf16[5,2,280,16,128]{4,3,2,1,0:T(8,128)(2,1)} %bitcast.7, s32[16,128]{1,0:T(8,128)} %refs_1_.3, f32[280,16,128]{2,1,0:T(8,128)} %bitcast.8, f32[280,16,128]{2,1,0:T(8,128)} %bitcast.9), custom_call_target="tpu_custom_call" | custom-call | flops 2500000 | bytes 7500000 | tf_op jit(solution)/shard_map/pallas_call | solution.py:30
  18.0 2.7 %shard_map.89 = (f32[5,16,128]{2,1,0:T(8,128)S(1)}, f32[2,48,128]{2,1,0:T(8,128)S(1)}, f32[8,128]{1,0:T(8,128)S(1)}, bf16[40,16,128]{2,1,0:T(8,128)(2,1)S(1)}, bf16[40,16,128]{2,1,0:T(8,128)(2,1)S(1)}) custom-call(f32[6,48,128]{2,1,0:T(8,128)S(1)} %get-tuple-element.62.refs_0_, f32[48,128]{1,0:T(8,128)S(1)} %collective-permute-done.2.refs_1_, ...), custom_call_target="tpu_custom_call" | custom-call | flops 2000000 | bytes 6000000 | tf_op jit(solution)/shard_map/pallas_call | solution.py:30
  20.7 1.4 %collective-permute-start.8 = (bf16[40,16,128]{2,1,0:T(8,128)(2,1)S(1)}, bf16[40,16,128]{2,1,0:T(8,128)(2,1)S(1)}, u32[]{:S(2)}, u32[]{:S(2)}) collective-permute-start(bf16[40,16,128]{2,1,0:T(8,128)(2,1)S(1)} %get-tuple-element.76), channel_id=1, source_target_pairs={{0,32},{32,0},{64,96},{96,64},{1,33},{33,1},{65,97},{97,65},{2,34}... | collective-permute-start | bytes 491528 | tf_op jit(solution)/shard_map/ppermute | solution.py:54
  22.1 1.9 %collective-permute-start.9 = (bf16[40,16,128]{2,1,0:T(8,128)(2,1)S(1)}, bf16[40,16,128]{2,1,0:T(8,128)(2,1)S(1)}, u32[]{:S(2)}, u32[]{:S(2)}) collective-permute-start(bf16[40,16,128]{2,1,0:T(8,128)(2,1)S(1)} %get-tuple-element.77), channel_id=1, source_target_pairs={{0,96},{32,64},{64,32},{96,0},{1,97},{33,65},{65,33},{97,1},{2,98}... | collective-permute-start | bytes 491528 | tf_op jit(solution)/shard_map/ppermute | solution.py:54
  26.2 2.2 %collective-permute-done.9.refs_3_ = bf16[40,16,128]{2,1,0:T(8,128)(2,1)S(1)} collective-permute-done((bf16[40,16,128]{2,1,0:T(8,128)(2,1)S(1)}, bf16[40,16,128]{2,1,0:T(8,128)(2,1)S(1)}, u32[]{:S(2)}, u32[]{:S(2)}) %collective-permute-start.9) | collective-permute-done | bytes 163872 | tf_op jit(solution)/shard_map/ppermute | solution.py:54
  28.4 2.0 %collective-permute-start.10 = (bf16[20,16,128]{2,1,0:T(8,128)(2,1)S(1)}, bf16[20,16,128]{2,1,0:T(8,128)(2,1)S(1)}, u32[]{:S(2)}, u32[]{:S(2)}) collective-permute-start(bf16[20,16,128]{2,1,0:T(8,128)(2,1)S(1)} %get-tuple-element.78), channel_id=1, source_target_pairs={{0,96},{32,64},{64,32},{96,0},{1,97},{33,65},{65,33},{97,1},{2,98}... | collective-permute-start | bytes 245768 | tf_op jit(solution)/shard_map/ppermute | solution.py:54
  30.8 2.2 %collective-permute-start.6 = (bf16[15,16,128]{2,1,0:T(8,128)(2,1)S(1)}, bf16[15,16,128]{2,1,0:T(8,128)(2,1)S(1)}, u32[]{:S(2)}, u32[]{:S(2)}) collective-permute-start(bf16[15,16,128]{2,1,0:T(8,128)(2,1)S(1)} %get-tuple-element.70), channel_id=1, source_target_pairs={{0,96},{32,64},{64,32},{96,0},{1,97},{33,65},{65,33},{97,1},{2,98}... | collective-permute-start | bytes 184328 | tf_op jit(solution)/shard_map/ppermute | solution.py:54
  33.9 0.9 %collective-permute-start.14 = (bf16[40,16,128]{2,1,0:T(8,128)(2,1)S(1)}, bf16[40,16,128]{2,1,0:T(8,128)(2,1)S(1)}, u32[]{:S(2)}, u32[]{:S(2)}) collective-permute-start(bf16[40,16,128]{2,1,0:T(8,128)(2,1)S(1)} %get-tuple-element.83.refs_2_), channel_id=1, source_target_pairs={{0,32},{32,0},{64,96},{96,64},{1,33},{33,1},{65,97},{97,65},{2,34}... | collective-permute-start | bytes 491528 | tf_op jit(solution)/shard_map/ppermute | solution.py:54
  35.3 0.8 %collective-permute-done.6.refs_4_ = bf16[15,16,128]{2,1,0:T(8,128)(2,1)S(1)} collective-permute-done((bf16[15,16,128]{2,1,0:T(8,128)(2,1)S(1)}, bf16[15,16,128]{2,1,0:T(8,128)(2,1)S(1)}, u32[]{:S(2)}, u32[]{:S(2)}) %collective-permute-start.6) | collective-permute-done | bytes 61472 | tf_op jit(solution)/shard_map/ppermute | solution.py:54
  36.7 1.3 %collective-permute-start.13 = (bf16[30,16,128]{2,1,0:T(8,128)(2,1)S(1)}, bf16[30,16,128]{2,1,0:T(8,128)(2,1)S(1)}, u32[]{:S(2)}, u32[]{:S(2)}) collective-permute-start(bf16[30,16,128]{2,1,0:T(8,128)(2,1)S(1)} %get-tuple-element.82.refs_3_), channel_id=1, source_target_pairs={{0,96},{32,64},{64,32},{96,0},{1,97},{33,65},{65,33},{97,1},{2,98}... | collective-permute-start | bytes 368648 | tf_op jit(solution)/shard_map/ppermute | solution.py:54
  38.4 2.1 %collective-permute-done.16 = f32[8,128]{1,0:T(8,128)S(1)} collective-permute-done((f32[8,128]{1,0:T(8,128)S(1)}, f32[8,128]{1,0:T(8,128)S(1)}, u32[]{:S(2)}, u32[]{:S(2)}) %collective-permute-start.16) | collective-permute-done | bytes 4128 | tf_op jit(solution)/shard_map/ppermute | solution.py:58
  40.5 0.8 %collective-permute-start.19 = (bf16[20,16,128]{2,1,0:T(8,128)(2,1)S(1)}, bf16[20,16,128]{2,1,0:T(8,128)(2,1)S(1)}, u32[]{:S(2)}, u32[]{:S(2)}) collective-permute-start(bf16[20,16,128]{2,1,0:T(8,128)(2,1)S(1)} %slice.15), channel_id=1, source_target_pairs={{0,32},{32,0},{64,96},{96,64},{1,33},{33,1},{65,97},{97,65},{2,34}... | collective-permute-start | bytes 245768 | tf_op jit(solution)/shard_map/ppermute | solution.py:54
  41.3 1.6 %collective-permute-start.20 = (bf16[20,16,128]{2,1,0:T(8,128)(2,1)S(1)}, bf16[20,16,128]{2,1,0:T(8,128)(2,1)S(1)}, u32[]{:S(2)}, u32[]{:S(2)}) collective-permute-start(bf16[20,16,128]{2,1,0:T(8,128)(2,1)S(1)} %slice.16), channel_id=1, source_target_pairs={{0,96},{32,64},{64,32},{96,0},{1,97},{33,65},{65,33},{97,1},{2,98}... | collective-permute-start | bytes 245768 | tf_op jit(solution)/shard_map/ppermute | solution.py:54
  43.0 1.0 %collective-permute-start.17 = (f32[8,128]{1,0:T(8,128)S(1)}, f32[8,128]{1,0:T(8,128)S(1)}, u32[]{:S(2)}, u32[]{:S(2)}) collective-permute-start(f32[8,128]{1,0:T(8,128)S(1)} %add.6), channel_id=1, source_target_pairs={{0,12},{4,8},{8,4},{12,0},{16,28},{20,24},{24,20},{28,16},{1,13},{... | collective-permute-start | bytes 12296 | tf_op jit(solution)/shard_map/ppermute | solution.py:58
  44.4 2.5 %collective-permute-done.17 = f32[8,128]{1,0:T(8,128)S(1)} collective-permute-done((f32[8,128]{1,0:T(8,128)S(1)}, f32[8,128]{1,0:T(8,128)S(1)}, u32[]{:S(2)}, u32[]{:S(2)}) %collective-permute-start.17) | collective-permute-done | bytes 4128 | tf_op jit(solution)/shard_map/ppermute | solution.py:58
  47.0 0.8 %collective-permute-start.22 = (bf16[15,16,128]{2,1,0:T(8,128)(2,1)S(1)}, bf16[15,16,128]{2,1,0:T(8,128)(2,1)S(1)}, u32[]{:S(2)}, u32[]{:S(2)}) collective-permute-start(bf16[15,16,128]{2,1,0:T(8,128)(2,1)S(1)} %slice.18), channel_id=1, source_target_pairs={{0,96},{32,64},{64,32},{96,0},{1,97},{33,65},{65,33},{97,1},{2,98}... | collective-permute-start | bytes 184328 | tf_op jit(solution)/shard_map/ppermute | solution.py:54
  47.8 3.6 %collective-permute-start.18 = (f32[8,128]{1,0:T(8,128)S(1)}, f32[8,128]{1,0:T(8,128)S(1)}, u32[]{:S(2)}, u32[]{:S(2)}) collective-permute-start(f32[8,128]{1,0:T(8,128)S(1)} %add.7.refs_4_), channel_id=1, source_target_pairs={{0,2},{1,3},{2,0},{3,1},{4,6},{5,7},{6,4},{7,5},{8,10},{9,11},{10,... | collective-permute-start | bytes 12296 | tf_op jit(solution)/shard_map/ppermute | solution.py:58
  52.9 1.8 %collective-permute-start.24 = (f32[6,16,128]{2,1,0:T(8,128)S(1)}, f32[6,16,128]{2,1,0:T(8,128)S(1)}, u32[]{:S(2)}, u32[]{:S(2)}) collective-permute-start(f32[6,16,128]{2,1,0:T(8,128)S(1)} %get-tuple-element.93.refs_0_), channel_id=1, source_target_pairs={{0,28},{4,8},{8,4},{12,16},{16,12},{20,24},{24,20},{28,0},{1,29},{... | collective-permute-start | bytes 147464 | tf_op jit(solution)/shard_map/ppermute | solution.py:54
  55.9 1.4 %collective-permute-done.25.refs_4_ = f32[8,128]{1,0:T(8,128)S(1)} collective-permute-done((f32[8,128]{1,0:T(8,128)S(1)}, f32[8,128]{1,0:T(8,128)S(1)}, u32[]{:S(2)}, u32[]{:S(2)}) %collective-permute-start.25) | collective-permute-done | bytes 4128 | tf_op jit(solution)/shard_map/ppermute | solution.py:54
  57.3 1.2 %collective-permute-done.26.refs_5_ = f32[8,128]{1,0:T(8,128)S(1)} collective-permute-done((f32[8,128]{1,0:T(8,128)S(1)}, f32[8,128]{1,0:T(8,128)S(1)}, u32[]{:S(2)}, u32[]{:S(2)}) %collective-permute-start.26) | collective-permute-done | bytes 4128 | tf_op jit(solution)/shard_map/ppermute | solution.py:58
  58.7 10.7 %collective-permute-start.27 = (f32[48,128]{1,0:T(8,128)S(1)}, f32[48,128]{1,0:T(8,128)S(1)}, u32[]{:S(2)}, u32[]{:S(2)}) collective-permute-start(f32[48,128]{1,0:T(8,128)S(1)} %get-tuple-element.100), channel_id=1, source_target_pairs={{0,1},{1,0},{2,3},{3,2},{4,5},{5,4},{6,7},{7,6},{8,9},{9,8},{10,11... | collective-permute-start | bytes 73736 | tf_op jit(solution)/shard_map/ppermute | solution.py:54
  69.4 2.2 %collective-permute-start.28 = (f32[48,128]{1,0:T(8,128)S(1)}, f32[48,128]{1,0:T(8,128)S(1)}, u32[]{:S(2)}, u32[]{:S(2)}) collective-permute-start(f32[48,128]{1,0:T(8,128)S(1)} %get-tuple-element.100), channel_id=1, source_target_pairs={{0,3},{1,2},{2,1},{3,0},{4,7},{5,6},{6,5},{7,4},{8,11},{9,10},{10,... | collective-permute-start | bytes 73736 | tf_op jit(solution)/shard_map/ppermute | solution.py:54
  72.0 0.8 %collective-permute-start.30 = (f32[8,128]{1,0:T(8,128)S(1)}, f32[8,128]{1,0:T(8,128)S(1)}, u32[]{:S(2)}, u32[]{:S(2)}) collective-permute-start(f32[8,128]{1,0:T(8,128)S(1)} %get-tuple-element.101.refs_5_), channel_id=1, source_target_pairs={{0,96},{32,64},{64,32},{96,0},{1,97},{33,65},{65,33},{97,1},{2,98}... | collective-permute-start | bytes 12296 | tf_op jit(solution)/shard_map/ppermute | solution.py:54
  72.8 2.1 %collective-permute-start.31 = (f32[8,128]{1,0:T(8,128)S(1)}, f32[8,128]{1,0:T(8,128)S(1)}, u32[]{:S(2)}, u32[]{:S(2)}) collective-permute-start(f32[8,128]{1,0:T(8,128)S(1)} %get-tuple-element.101.refs_5_), channel_id=1, source_target_pairs={{0,97},{1,96},{2,99},{3,98},{32,65},{33,64},{34,67},{35,66},{64,33... | collective-permute-start | bytes 12296 | tf_op jit(solution)/shard_map/ppermute | solution.py:58
  75.7 1.4 %collective-permute-done.31.refs_8_ = f32[8,128]{1,0:T(8,128)S(1)} collective-permute-done((f32[8,128]{1,0:T(8,128)S(1)}, f32[8,128]{1,0:T(8,128)S(1)}, u32[]{:S(2)}, u32[]{:S(2)}) %collective-permute-start.31) | collective-permute-done | bytes 4128 | tf_op jit(solution)/shard_map/ppermute | solution.py:58
  77.1 2.8 %shard_map.101 = (f32[5,16,128]{2,1,0:T(8,128)}, f32[1,128]{1,0:T(1,128)}) custom-call(f32[5,48,128]{2,1,0:T(8,128)S(1)} %get-tuple-element.99.refs_0_, f32[48,128]{1,0:T(8,128)S(1)} %collective-permute-done.27.refs_1_, f32[48,128]{1,0:T(8,128)S(1)} %collective-permute-done.28.refs_2_, f32[2,48,128]{2,1,0:T(8,128)S(1)} %get-tuple-element.104.refs_3_, ...), custom_call_target="tpu_custom_call" | custom-call | flops 1500000 | bytes 4500000 | tf_op jit(solution)/shard_map/pallas_call | solution.py:30
  (59 shorter events, 9.5 us)
Async XLA Ops:
  1.4 9.0 %collective-permute-start = (f32[6,16,128]{2,1,0:T(8,128)S(1)}, f32[6,16,128]{2,1,0:T(8,128)S(1)}, u32[]{:S(2)}, u32[]{:S(2)}) collective-permute-start(f32[6,16,128]{2,1,0:T(8,128)S(1)} %pad_maximum_fusion.refs_0_), channel_id=1, source_target_pairs={{0,4},{4,0},{8,12},{12,8},{16,20},{20,16},{24,28},{28,24},{1,5},{5... | collective-permute-start | bytes 147464 | tf_op jit(solution)/shard_map/ppermute | solution.py:54
  3.5 7.0 %collective-permute-start.1 = (f32[6,16,128]{2,1,0:T(8,128)S(1)}, f32[6,16,128]{2,1,0:T(8,128)S(1)}, u32[]{:S(2)}, u32[]{:S(2)}) collective-permute-start(f32[6,16,128]{2,1,0:T(8,128)S(1)} %pad_maximum_fusion.refs_0_), channel_id=1, source_target_pairs={{0,28},{4,8},{8,4},{12,16},{16,12},{20,24},{24,20},{28,0},{1,29},{... | collective-permute-start | bytes 147464 | tf_op jit(solution)/shard_map/ppermute | solution.py:54
  10.6 7.4 %collective-permute-start.2 = (f32[48,128]{1,0:T(8,128)S(1)}, f32[48,128]{1,0:T(8,128)S(1)}, u32[]{:S(2)}, u32[]{:S(2)}) collective-permute-start(f32[48,128]{1,0:T(8,128)S(1)} %get-tuple-element.59), channel_id=1, source_target_pairs={{0,1},{1,0},{2,3},{3,2},{4,5},{5,4},{6,7},{7,6},{8,9},{9,8},{10,11... | collective-permute-start | bytes 73736 | tf_op jit(solution)/shard_map/ppermute | solution.py:54
  11.9 6.1 %collective-permute-start.3 = (f32[48,128]{1,0:T(8,128)S(1)}, f32[48,128]{1,0:T(8,128)S(1)}, u32[]{:S(2)}, u32[]{:S(2)}) collective-permute-start(f32[48,128]{1,0:T(8,128)S(1)} %get-tuple-element.59), channel_id=1, source_target_pairs={{0,3},{1,2},{2,1},{3,0},{4,7},{5,6},{6,5},{7,4},{8,11},{9,10},{10,... | collective-permute-start | bytes 73736 | tf_op jit(solution)/shard_map/ppermute | solution.py:54
  20.7 5.4 %collective-permute-start.8 = (bf16[40,16,128]{2,1,0:T(8,128)(2,1)S(1)}, bf16[40,16,128]{2,1,0:T(8,128)(2,1)S(1)}, u32[]{:S(2)}, u32[]{:S(2)}) collective-permute-start(bf16[40,16,128]{2,1,0:T(8,128)(2,1)S(1)} %get-tuple-element.76), channel_id=1, source_target_pairs={{0,32},{32,0},{64,96},{96,64},{1,33},{33,1},{65,97},{97,65},{2,34}... | collective-permute-start | bytes 491528 | tf_op jit(solution)/shard_map/ppermute | solution.py:54
  22.1 6.2 %collective-permute-start.9 = (bf16[40,16,128]{2,1,0:T(8,128)(2,1)S(1)}, bf16[40,16,128]{2,1,0:T(8,128)(2,1)S(1)}, u32[]{:S(2)}, u32[]{:S(2)}) collective-permute-start(bf16[40,16,128]{2,1,0:T(8,128)(2,1)S(1)} %get-tuple-element.77), channel_id=1, source_target_pairs={{0,96},{32,64},{64,32},{96,0},{1,97},{33,65},{65,33},{97,1},{2,98}... | collective-permute-start | bytes 491528 | tf_op jit(solution)/shard_map/ppermute | solution.py:54
  24.7 6.0 %collective-permute-start.4 = (bf16[30,16,128]{2,1,0:T(8,128)(2,1)S(1)}, bf16[30,16,128]{2,1,0:T(8,128)(2,1)S(1)}, u32[]{:S(2)}, u32[]{:S(2)}) collective-permute-start(bf16[30,16,128]{2,1,0:T(8,128)(2,1)S(1)} %get-tuple-element.68), channel_id=1, source_target_pairs={{0,32},{32,0},{64,96},{96,64},{1,33},{33,1},{65,97},{97,65},{2,34}... | collective-permute-start | bytes 368648 | tf_op jit(solution)/shard_map/ppermute | solution.py:54
  25.2 5.5 %collective-permute-start.5 = (bf16[30,16,128]{2,1,0:T(8,128)(2,1)S(1)}, bf16[30,16,128]{2,1,0:T(8,128)(2,1)S(1)}, u32[]{:S(2)}, u32[]{:S(2)}) collective-permute-start(bf16[30,16,128]{2,1,0:T(8,128)(2,1)S(1)} %get-tuple-element.69), channel_id=1, source_target_pairs={{0,96},{32,64},{64,32},{96,0},{1,97},{33,65},{65,33},{97,1},{2,98}... | collective-permute-start | bytes 368648 | tf_op jit(solution)/shard_map/ppermute | solution.py:54
  28.4 4.6 %collective-permute-start.10 = (bf16[20,16,128]{2,1,0:T(8,128)(2,1)S(1)}, bf16[20,16,128]{2,1,0:T(8,128)(2,1)S(1)}, u32[]{:S(2)}, u32[]{:S(2)}) collective-permute-start(bf16[20,16,128]{2,1,0:T(8,128)(2,1)S(1)} %get-tuple-element.78), channel_id=1, source_target_pairs={{0,96},{32,64},{64,32},{96,0},{1,97},{33,65},{65,33},{97,1},{2,98}... | collective-permute-start | bytes 245768 | tf_op jit(solution)/shard_map/ppermute | solution.py:54
  30.4 3.3 %collective-permute-start.11 = (bf16[20,16,128]{2,1,0:T(8,128)(2,1)S(1)}, bf16[20,16,128]{2,1,0:T(8,128)(2,1)S(1)}, u32[]{:S(2)}, u32[]{:S(2)}) collective-permute-start(bf16[20,16,128]{2,1,0:T(8,128)(2,1)S(1)} %get-tuple-element.79), channel_id=1, source_target_pairs={{0,32},{32,0},{64,96},{96,64},{1,33},{33,1},{65,97},{97,65},{2,34}... | collective-permute-start | bytes 245768 | tf_op jit(solution)/shard_map/ppermute | solution.py:54
  30.8 5.3 %collective-permute-start.6 = (bf16[15,16,128]{2,1,0:T(8,128)(2,1)S(1)}, bf16[15,16,128]{2,1,0:T(8,128)(2,1)S(1)}, u32[]{:S(2)}, u32[]{:S(2)}) collective-permute-start(bf16[15,16,128]{2,1,0:T(8,128)(2,1)S(1)} %get-tuple-element.70), channel_id=1, source_target_pairs={{0,96},{32,64},{64,32},{96,0},{1,97},{33,65},{65,33},{97,1},{2,98}... | collective-permute-start | bytes 184328 | tf_op jit(solution)/shard_map/ppermute | solution.py:54
  33.0 3.3 %collective-permute-start.7 = (bf16[15,16,128]{2,1,0:T(8,128)(2,1)S(1)}, bf16[15,16,128]{2,1,0:T(8,128)(2,1)S(1)}, u32[]{:S(2)}, u32[]{:S(2)}) collective-permute-start(bf16[15,16,128]{2,1,0:T(8,128)(2,1)S(1)} %get-tuple-element.71), channel_id=1, source_target_pairs={{0,32},{32,0},{64,96},{96,64},{1,33},{33,1},{65,97},{97,65},{2,34}... | collective-permute-start | bytes 184328 | tf_op jit(solution)/shard_map/ppermute | solution.py:54
  33.9 6.6 %collective-permute-start.14 = (bf16[40,16,128]{2,1,0:T(8,128)(2,1)S(1)}, bf16[40,16,128]{2,1,0:T(8,128)(2,1)S(1)}, u32[]{:S(2)}, u32[]{:S(2)}) collective-permute-start(bf16[40,16,128]{2,1,0:T(8,128)(2,1)S(1)} %get-tuple-element.83.refs_2_), channel_id=1, source_target_pairs={{0,32},{32,0},{64,96},{96,64},{1,33},{33,1},{65,97},{97,65},{2,34}... | collective-permute-start | bytes 491528 | tf_op jit(solution)/shard_map/ppermute | solution.py:54
  34.8 5.7 %collective-permute-start.15 = (bf16[40,16,128]{2,1,0:T(8,128)(2,1)S(1)}, bf16[40,16,128]{2,1,0:T(8,128)(2,1)S(1)}, u32[]{:S(2)}, u32[]{:S(2)}) collective-permute-start(bf16[40,16,128]{2,1,0:T(8,128)(2,1)S(1)} %get-tuple-element.83.refs_2_), channel_id=1, source_target_pairs={{0,96},{32,64},{64,32},{96,0},{1,97},{33,65},{65,33},{97,1},{2,98}... | collective-permute-start | bytes 491528 | tf_op jit(solution)/shard_map/ppermute | solution.py:54
  36.5 7.9 %collective-permute-start.12 = (bf16[30,16,128]{2,1,0:T(8,128)(2,1)S(1)}, bf16[30,16,128]{2,1,0:T(8,128)(2,1)S(1)}, u32[]{:S(2)}, u32[]{:S(2)}) collective-permute-start(bf16[30,16,128]{2,1,0:T(8,128)(2,1)S(1)} %get-tuple-element.82.refs_3_), channel_id=1, source_target_pairs={{0,32},{32,0},{64,96},{96,64},{1,33},{33,1},{65,97},{97,65},{2,34}... | collective-permute-start | bytes 368648 | tf_op jit(solution)/shard_map/ppermute | solution.py:54
  36.7 7.7 %collective-permute-start.13 = (bf16[30,16,128]{2,1,0:T(8,128)(2,1)S(1)}, bf16[30,16,128]{2,1,0:T(8,128)(2,1)S(1)}, u32[]{:S(2)}, u32[]{:S(2)}) collective-permute-start(bf16[30,16,128]{2,1,0:T(8,128)(2,1)S(1)} %get-tuple-element.82.refs_3_), channel_id=1, source_target_pairs={{0,96},{32,64},{64,32},{96,0},{1,97},{33,65},{65,33},{97,1},{2,98}... | collective-permute-start | bytes 368648 | tf_op jit(solution)/shard_map/ppermute | solution.py:54
  38.0 2.5 %collective-permute-start.16 = (f32[8,128]{1,0:T(8,128)S(1)}, f32[8,128]{1,0:T(8,128)S(1)}, u32[]{:S(2)}, u32[]{:S(2)}) collective-permute-start(f32[8,128]{1,0:T(8,128)S(1)} %get-tuple-element.84), channel_id=1, source_target_pairs={{0,16},{4,20},{8,24},{12,28},{16,0},{20,4},{24,8},{28,12},{1,17},{... | collective-permute-start | bytes 12296 | tf_op jit(solution)/shard_map/ppermute | solution.py:58
  40.5 11.9 %collective-permute-start.19 = (bf16[20,16,128]{2,1,0:T(8,128)(2,1)S(1)}, bf16[20,16,128]{2,1,0:T(8,128)(2,1)S(1)}, u32[]{:S(2)}, u32[]{:S(2)}) collective-permute-start(bf16[20,16,128]{2,1,0:T(8,128)(2,1)S(1)} %slice.15), channel_id=1, source_target_pairs={{0,32},{32,0},{64,96},{96,64},{1,33},{33,1},{65,97},{97,65},{2,34}... | collective-permute-start | bytes 245768 | tf_op jit(solution)/shard_map/ppermute | solution.py:54
  41.3 11.1 %collective-permute-start.20 = (bf16[20,16,128]{2,1,0:T(8,128)(2,1)S(1)}, bf16[20,16,128]{2,1,0:T(8,128)(2,1)S(1)}, u32[]{:S(2)}, u32[]{:S(2)}) collective-permute-start(bf16[20,16,128]{2,1,0:T(8,128)(2,1)S(1)} %slice.16), channel_id=1, source_target_pairs={{0,96},{32,64},{64,32},{96,0},{1,97},{33,65},{65,33},{97,1},{2,98}... | collective-permute-start | bytes 245768 | tf_op jit(solution)/shard_map/ppermute | solution.py:54
  43.0 4.0 %collective-permute-start.17 = (f32[8,128]{1,0:T(8,128)S(1)}, f32[8,128]{1,0:T(8,128)S(1)}, u32[]{:S(2)}, u32[]{:S(2)}) collective-permute-start(f32[8,128]{1,0:T(8,128)S(1)} %add.6), channel_id=1, source_target_pairs={{0,12},{4,8},{8,4},{12,0},{16,28},{20,24},{24,20},{28,16},{1,13},{... | collective-permute-start | bytes 12296 | tf_op jit(solution)/shard_map/ppermute | solution.py:58
  46.9 5.5 %collective-permute-start.21 = (bf16[15,16,128]{2,1,0:T(8,128)(2,1)S(1)}, bf16[15,16,128]{2,1,0:T(8,128)(2,1)S(1)}, u32[]{:S(2)}, u32[]{:S(2)}) collective-permute-start(bf16[15,16,128]{2,1,0:T(8,128)(2,1)S(1)} %slice.17), channel_id=1, source_target_pairs={{0,32},{32,0},{64,96},{96,64},{1,33},{33,1},{65,97},{97,65},{2,34}... | collective-permute-start | bytes 184328 | tf_op jit(solution)/shard_map/ppermute | solution.py:54
  47.0 5.4 %collective-permute-start.22 = (bf16[15,16,128]{2,1,0:T(8,128)(2,1)S(1)}, bf16[15,16,128]{2,1,0:T(8,128)(2,1)S(1)}, u32[]{:S(2)}, u32[]{:S(2)}) collective-permute-start(bf16[15,16,128]{2,1,0:T(8,128)(2,1)S(1)} %slice.18), channel_id=1, source_target_pairs={{0,96},{32,64},{64,32},{96,0},{1,97},{33,65},{65,33},{97,1},{2,98}... | collective-permute-start | bytes 184328 | tf_op jit(solution)/shard_map/ppermute | solution.py:54
  47.8 4.6 %collective-permute-start.18 = (f32[8,128]{1,0:T(8,128)S(1)}, f32[8,128]{1,0:T(8,128)S(1)}, u32[]{:S(2)}, u32[]{:S(2)}) collective-permute-start(f32[8,128]{1,0:T(8,128)S(1)} %add.7.refs_4_), channel_id=1, source_target_pairs={{0,2},{1,3},{2,0},{3,1},{4,6},{5,7},{6,4},{7,5},{8,10},{9,11},{10,... | collective-permute-start | bytes 12296 | tf_op jit(solution)/shard_map/ppermute | solution.py:58
  52.8 5.8 %collective-permute-start.23 = (f32[6,16,128]{2,1,0:T(8,128)S(1)}, f32[6,16,128]{2,1,0:T(8,128)S(1)}, u32[]{:S(2)}, u32[]{:S(2)}) collective-permute-start(f32[6,16,128]{2,1,0:T(8,128)S(1)} %get-tuple-element.93.refs_0_), channel_id=1, source_target_pairs={{0,4},{4,0},{8,12},{12,8},{16,20},{20,16},{24,28},{28,24},{1,5},{5... | collective-permute-start | bytes 147464 | tf_op jit(solution)/shard_map/ppermute | solution.py:54
  52.9 5.7 %collective-permute-start.24 = (f32[6,16,128]{2,1,0:T(8,128)S(1)}, f32[6,16,128]{2,1,0:T(8,128)S(1)}, u32[]{:S(2)}, u32[]{:S(2)}) collective-permute-start(f32[6,16,128]{2,1,0:T(8,128)S(1)} %get-tuple-element.93.refs_0_), channel_id=1, source_target_pairs={{0,28},{4,8},{8,4},{12,16},{16,12},{20,24},{24,20},{28,0},{1,29},{... | collective-permute-start | bytes 147464 | tf_op jit(solution)/shard_map/ppermute | solution.py:54
  54.7 2.6 %collective-permute-start.25 = (f32[8,128]{1,0:T(8,128)S(1)}, f32[8,128]{1,0:T(8,128)S(1)}, u32[]{:S(2)}, u32[]{:S(2)}) collective-permute-start(f32[8,128]{1,0:T(8,128)S(1)} %get-tuple-element.94.refs_3_), channel_id=1, source_target_pairs={{0,32},{32,0},{64,96},{96,64},{1,33},{33,1},{65,97},{97,65},{2,34}... | collective-permute-start | bytes 12296 | tf_op jit(solution)/shard_map/ppermute | solution.py:54
  55.2 3.4 %collective-permute-start.26 = (f32[8,128]{1,0:T(8,128)S(1)}, f32[8,128]{1,0:T(8,128)S(1)}, u32[]{:S(2)}, u32[]{:S(2)}) collective-permute-start(f32[8,128]{1,0:T(8,128)S(1)} %get-tuple-element.94.refs_3_), channel_id=1, source_target_pairs={{0,36},{4,32},{8,44},{12,40},{16,52},{20,48},{24,60},{28,56},{32,4... | collective-permute-start | bytes 12296 | tf_op jit(solution)/shard_map/ppermute | solution.py:58
  58.7 18.4 %collective-permute-start.27 = (f32[48,128]{1,0:T(8,128)S(1)}, f32[48,128]{1,0:T(8,128)S(1)}, u32[]{:S(2)}, u32[]{:S(2)}) collective-permute-start(f32[48,128]{1,0:T(8,128)S(1)} %get-tuple-element.100), channel_id=1, source_target_pairs={{0,1},{1,0},{2,3},{3,2},{4,5},{5,4},{6,7},{7,6},{8,9},{9,8},{10,11... | collective-permute-start | bytes 73736 | tf_op jit(solution)/shard_map/ppermute | solution.py:54
  69.4 7.7 %collective-permute-start.28 = (f32[48,128]{1,0:T(8,128)S(1)}, f32[48,128]{1,0:T(8,128)S(1)}, u32[]{:S(2)}, u32[]{:S(2)}) collective-permute-start(f32[48,128]{1,0:T(8,128)S(1)} %get-tuple-element.100), channel_id=1, source_target_pairs={{0,3},{1,2},{2,1},{3,0},{4,7},{5,6},{6,5},{7,4},{8,11},{9,10},{10,... | collective-permute-start | bytes 73736 | tf_op jit(solution)/shard_map/ppermute | solution.py:54
  71.6 3.4 %collective-permute-start.29 = (f32[8,128]{1,0:T(8,128)S(1)}, f32[8,128]{1,0:T(8,128)S(1)}, u32[]{:S(2)}, u32[]{:S(2)}) collective-permute-start(f32[8,128]{1,0:T(8,128)S(1)} %get-tuple-element.101.refs_5_), channel_id=1, source_target_pairs={{0,1},{1,0},{2,3},{3,2},{4,5},{5,4},{6,7},{7,6},{8,9},{9,8},{10,11... | collective-permute-start | bytes 12296 | tf_op jit(solution)/shard_map/ppermute | solution.py:58
  72.0 3.7 %collective-permute-start.30 = (f32[8,128]{1,0:T(8,128)S(1)}, f32[8,128]{1,0:T(8,128)S(1)}, u32[]{:S(2)}, u32[]{:S(2)}) collective-permute-start(f32[8,128]{1,0:T(8,128)S(1)} %get-tuple-element.101.refs_5_), channel_id=1, source_target_pairs={{0,96},{32,64},{64,32},{96,0},{1,97},{33,65},{65,33},{97,1},{2,98}... | collective-permute-start | bytes 12296 | tf_op jit(solution)/shard_map/ppermute | solution.py:54
  72.8 4.2 %collective-permute-start.31 = (f32[8,128]{1,0:T(8,128)S(1)}, f32[8,128]{1,0:T(8,128)S(1)}, u32[]{:S(2)}, u32[]{:S(2)}) collective-permute-start(f32[8,128]{1,0:T(8,128)S(1)} %get-tuple-element.101.refs_5_), channel_id=1, source_target_pairs={{0,97},{1,96},{2,99},{3,98},{32,65},{33,64},{34,67},{35,66},{64,33... | collective-permute-start | bytes 12296 | tf_op jit(solution)/shard_map/ppermute | solution.py:58
  (2 other events, 28.1 us)

commit v3 on v2

v3 whole, which is shorter than its diff:
```python
import functools
import math

import jax
import jax.numpy as jnp
from jax import lax
from jax.experimental import pallas as pl
from jax.experimental.pallas import tpu as pltpu
from jax.sharding import PartitionSpec as P

F32 = jnp.float32
BF16 = jnp.bfloat16
PASSES = 10
REACH = 10
ROWS, COLS = 16, 128
MEMBERS = 5
PLANES = 280
SHARE = PLANES // 4
CHUNKS = ((0, 35), (35, 35))
PARTNERS = (2, 1, 3)
MIB = 1 << 20

VMEM_SPEC = pl.BlockSpec(memory_space=pltpu.VMEM)
ANY_SPEC = pl.BlockSpec(memory_space=pl.ANY)


def call(body, outs, args, specs, scratch=(), limit=8 * MIB, us=1.0, aliases=None):
    def placed(*refs):
        body([lax.axis_index(a) for a in ("mem", "lat", "lon")], *refs)

    return pl.pallas_call(
        placed,
        out_shape=outs,
        in_specs=specs,
        out_specs=[VMEM_SPEC] * len(outs),
        scratch_shapes=list(scratch),
        input_output_aliases=aliases or {},
        compiler_params=pltpu.CompilerParams(vmem_limit_bytes=limit),
        cost_estimate=pl.CostEstimate(
            flops=int(us * 1e6), bytes_accessed=int(us * 3e6), transcendentals=0
        ),
    )(*args)


def in_hbm(cells):
    return pltpu.with_memory_space_constraint(cells, pltpu.HBM)


def swap(cells, axis, odd):
    count = lax.axis_size(axis)
    pairs = []
    for i in range(count):
        to = i ^ 1 if not odd else ((i + 1) ^ 1) - 1
        pairs.append((i, to % count))
    return lax.ppermute(cells, axis, pairs)


def trade(cells, axes, to):
    return lax.ppermute(cells, axes, list(enumerate(to)))


def share(cells, partner):
    return trade(cells, ("mem",), [i ^ partner for i in range(4)])


def pack_body(fields, mask_edges, ids, own, even, odd, *rest):
    if len(rest) > 2:
        terms, got, ext, packed, new_terms = rest
        summed = (terms[...] + even[fields, :8]) + (got[...] + odd[fields, :8])
        new_terms[...] = summed
        packed[3 * ROWS :] = summed
    else:
        ext, packed = rest
    lat = ids[1]
    is_even = lax.rem(lat, 2) == 0
    lane = lax.broadcasted_iota(jnp.int32, (3 * ROWS, COLS), 1)
    out = jnp.zeros((3 * ROWS, COLS), F32)
    for f in range(fields):
        a, b = even[f], odd[f]
        up = jnp.where(is_even, b, a)
        down = jnp.where(is_even, a, b)
        if mask_edges:
            up = jnp.where(lat == 0, 0.0, up)
            down = jnp.where(lat == 7, 0.0, down)
        whole = jnp.concatenate([up, own[f], down], axis=0)
        ext[f] = whole
        at = 2 * REACH * f
        turned = pltpu.roll(whole, (at + REACH) % COLS, 1)
        out = jnp.where((lane >= at) & (lane < at + 2 * REACH), turned, out)
    packed[: 3 * ROWS] = out


def pack(fields, mask_edges, own, even, odd, terms=()):
    return call(
        functools.partial(pack_body, fields, mask_edges),
        [pltpu.VMEM((fields, 3 * ROWS, COLS), F32), pltpu.VMEM((3 * ROWS + (8 if terms else 0), COLS), F32)]
        + [pltpu.VMEM((8, COLS), F32)] * (1 if terms else 0),
        (own, even, odd, *terms),
        [VMEM_SPEC] * (3 + len(terms)),
        us=0.3,
    )


def group(lane, m):
    return (lane >= 2 * REACH * m) & (lane < 2 * REACH * (m + 1))


def halo_of(fields, ids, even, odd):
    is_even = lax.rem(ids[2], 2) == 0
    lane = lax.broadcasted_iota(jnp.int32, (3 * ROWS, COLS), 1)
    west = lane < 0
    for f in range(fields):
        at = 2 * REACH * f
        west = west | ((lane >= at) & (lane < at + REACH))
    a, b = even[: 3 * ROWS], odd[: 3 * ROWS]
    return jnp.where(west, jnp.where(is_even, b, a), jnp.where(is_even, a, b))


def lap(own, side):
    rows = side.shape[0]
    lane = lax.broadcasted_iota(jnp.int32, side.shape, 1)

    def total(v, west, east):
        above = pltpu.roll(v, 1, 0)
        below = pltpu.roll(v, rows - 1, 0)
        return (above + below) + (west + east) - 4.0 * v

    west_side, east_side = pltpu.roll(side, 1, 1), pltpu.roll(side, COLS - 1, 1)
    out = []
    for m in range(MEMBERS):
        at = 2 * REACH * m + REACH
        v = own[m]
        west = jnp.where(lane == 0, pltpu.roll(side, COLS - at + 1, 1), pltpu.roll(v, 1, 1))
        east = jnp.where(lane == COLS - 1, pltpu.roll(side, COLS - at - 1, 1), pltpu.roll(v, COLS - 1, 1))
        out.append(total(v, west, east))
        west_side = jnp.where(lane == at, pltpu.roll(v, at + 1, 1), west_side)
        east_side = jnp.where(lane == at - 1, pltpu.roll(v, at - 1, 1), east_side)
    return out, total(side, west_side, east_side)


def forward_pass(state, rate):
    (own, side), (rate_own, rate_side) = state, rate
    a, b = lap(own, side)
    return [v + rate_own * x for v, x in zip(own, a)], side + rate_side * b


def adjoint_pass(state, rate):
    (own, side), (rate_own, rate_side) = state, rate
    a, b = lap([rate_own * v for v in own], rate_side * side)
    return [v + x for v, x in zip(own, a)], side + b


def sweep(step, own, side, rate):
    cut = ROWS // 2
    state = (own, side)
    for _ in range(2):
        state = step(state, rate)
    own, side = [v[cut:-cut] for v in state[0]], state[1][cut:-cut]
    rate = tuple(v[cut:-cut] for v in rate)
    own, side = lax.fori_loop(0, PASSES - 2, lambda _, s: step(s, rate), (own, side))
    return [v[ROWS - cut : -(ROWS - cut)] for v in own]


def partner_of(mem, partner):
    return mem + partner - 2 * (lax.rem(mem, 2) * (partner % 2)) - 4 * (lax.div(mem, 2) * (partner // 2))


def select_body(partners, own, ids, anomalies, obs_time, *rest):
    if own:
        innovation, precision, sel, inn_own, prec_own, buf, when, sems, own_sems = rest
        own = ((innovation, inn_own), (precision, prec_own))
    else:
        sel, buf, when, sems, own_sems = rest
        own = ()
    time_copy = pltpu.make_async_copy(obs_time, when, own_sems.at[2])
    time_copy.start()
    copies = []
    for g, partner in enumerate(partners):
        at = pl.ds(SHARE * partner_of(ids[0], partner), SHARE)
        for m in range(MEMBERS):
            copy = pltpu.make_async_copy(anomalies.at[m, :, at], buf.at[g, m], sems.at[g * MEMBERS + m])
            copy.start()
            copies.append(copy)
    own_copies = []
    for k, (src, dst) in enumerate(own):
        copy = pltpu.make_async_copy(src.at[pl.ds(SHARE * ids[0], SHARE)], dst, own_sems.at[k])
        copy.start()
        own_copies.append(copy)
    time_copy.wait()
    at_zero = when[...].astype(F32).astype(BF16) == 0
    for n, copy in enumerate(copies):
        g, m = divmod(n, MEMBERS)
        copy.wait()

        def plane(r, c, g=g, m=m):
            sel[g, m, r] = jnp.where(at_zero, buf[g, m, 0, r], buf[g, m, 1, r])
            return c

        lax.fori_loop(0, SHARE, plane, 0, unroll=7)
    for copy in own_copies:
        copy.wait()


def select(partners, anomalies, obs_time, own=()):
    count = len(partners)
    return call(
        functools.partial(select_body, partners, bool(own)),
        [pltpu.VMEM((count, MEMBERS, SHARE, ROWS, COLS), BF16)]
        + [pltpu.VMEM((SHARE, ROWS, COLS), F32)] * (2 if own else 0),
        (anomalies, obs_time, *own),
        [ANY_SPEC, ANY_SPEC] + ([ANY_SPEC, ANY_SPEC] if own else []),
        scratch=[
            pltpu.VMEM((count, MEMBERS, 2, SHARE, ROWS, COLS), BF16),
            pltpu.VMEM((ROWS, COLS), jnp.int32),
            pltpu.SemaphoreType.DMA((count * MEMBERS,)),
            pltpu.SemaphoreType.DMA((3,)),
        ],
        limit=16 * MIB,
        us=2.5,
    )


def share_sums(chunk, sel, w, dtype, out):
    first, count = chunk
    ws = [w[m] for m in range(MEMBERS)]

    def plane(r, c):
        total = sel[0, first + r].astype(F32) * ws[0]
        for m in range(1, MEMBERS):
            total = total + sel[m, first + r].astype(F32) * ws[m]
        out[r] = total.astype(dtype)
        return c

    lax.fori_loop(0, count, plane, 0, unroll=5 if count % 5 == 0 else 1)


def sends_body(chunk, ids, sent1, sent2, w, *outs):
    for sel, out in zip((sent1.at[0], sent1.at[1], sent2.at[0]), outs):
        share_sums(chunk, sel, w, BF16, out)


def stays_body(ids, kept, w, own):
    share_sums((0, SHARE), kept.at[0], w, F32, own)


def forward_body(chunk, ids, ext, even, odd, loc_norm, sent1, sent2, w, rate, terms, *sends):
    halo = halo_of(MEMBERS + 1, ids, even, odd)
    lane = lax.broadcasted_iota(jnp.int32, (3 * ROWS, COLS), 1)
    side = jnp.where(lane < 2 * REACH * MEMBERS, halo, 0.0)
    rate_side = jnp.zeros((3 * ROWS, COLS), F32)
    for m in range(MEMBERS):
        turned = pltpu.roll(halo, (COLS - 2 * REACH * (MEMBERS - m)) % COLS, 1)
        rate_side = jnp.where(group(lane, m), turned, rate_side)
    rate[0] = ext[MEMBERS]
    rate[1] = rate_side
    squares = jnp.zeros((ROWS, COLS), F32)
    for m in range(MEMBERS):
        mine = ext[m, ROWS : 2 * ROWS]
        squares = squares + mine * mine
    terms[...] = squares[:8] + squares[8:]
    spread = sweep(forward_pass, [ext[m] for m in range(MEMBERS)], side, (ext[MEMBERS], rate_side))
    for m in range(MEMBERS):
        w[m] = (loc_norm[...] * spread[m]).astype(BF16).astype(F32)
    sends_body(chunk, ids, sent1, sent2, w, *sends)


def rides(chunk):
    return 1 if chunk == CHUNKS[-1] else 0


def ridden(plane):
    plane = plane.astype(F32)
    return plane[:8] + plane[8:]


def misfit_body(chunk, factor, ids, own, got1, got2, got3, inn, prec, terms, weighted, new_terms):
    first, count = chunk

    def plane(r, c):
        sums = (own[first + r] + got1[r].astype(F32)) + (got2[r].astype(F32) + got3[r].astype(F32))
        misfit = factor * sums - inn[first + r]
        scaled = prec[first + r] * misfit
        weighted[r] = scaled.astype(BF16)
        return c + misfit * scaled

    total = lax.fori_loop(0, count, plane, jnp.zeros((ROWS, COLS), F32), unroll=5 if count % 5 == 0 else 1)
    summed = terms[...] + (total[:8] + total[8:])
    new_terms[...] = summed
    if rides(chunk):
        high = summed.astype(BF16).astype(F32)
        weighted[count] = jnp.concatenate([high, summed - high], axis=0).astype(BF16)


def pull(sel, chunk, ref, acc):
    first, count = chunk

    def plane(r, acc):
        x = ref[r].astype(F32)
        return tuple(acc[m] + sel[m, first + r].astype(F32) * x for m in range(MEMBERS))

    return lax.fori_loop(0, count, plane, acc, unroll=5 if count % 5 == 0 else 1)


def own_pull_body(ids, kept, *rest):
    refs, new = rest[:-1], rest[-1]
    acc = tuple(jnp.zeros((ROWS, COLS), F32) for _ in range(MEMBERS))
    for chunk, ref in zip(CHUNKS, refs):
        acc = pull(kept.at[0], chunk, ref, acc)
    for m in range(MEMBERS):
        new[m] = acc[m]


def pull_all(chunk, sent1, sent2, old, refs):
    acc = tuple(old[m] for m in range(MEMBERS))
    for sel, ref in zip((sent1.at[0], sent1.at[1], sent2.at[0]), refs):
        acc = pull(sel, chunk, ref, acc)
    return acc


RELAYED = 20


def pull_body(chunk, ids, sent1, sent2, old, ref1, ref2, ref3, ref4, new):
    first, count = chunk
    acc = tuple(old[m] for m in range(MEMBERS))
    acc = pull(sent1.at[0], (first, RELAYED), ref1, acc)
    acc = pull(sent1.at[0], (first + RELAYED, count - RELAYED), ref2, acc)
    acc = pull(sent1.at[1], chunk, ref3, acc)
    acc = pull(sent2.at[0], chunk, ref4, acc)
    for m in range(MEMBERS):
        new[m] = acc[m]


def last_pull_body(factor, ids, sent1, sent2, old, ref1, ref2, ref3, loc_norm, mine, new, terms):
    acc = pull_all(CHUNKS[-1], sent1, sent2, old, (ref1, ref2, ref3))
    for m in range(MEMBERS):
        new[m] = loc_norm[...] * (factor * acc[m])
    at = CHUNKS[-1][1]
    summed = (ridden(mine[at]) + ridden(ref2[at])) + (ridden(ref3[at]) + ridden(ref1[at]))
    row = lax.broadcasted_iota(jnp.int32, (8, COLS), 0)
    summed = jnp.where(row == ids[1], jnp.sum(summed, axis=0, keepdims=True), 0.0)
    terms[...] = summed
    new[MEMBERS, :8] = summed
    new[MEMBERS, 8:] = jnp.zeros((ROWS - 8, COLS), F32)


def pass_body(ids, odd, passed):
    passed[...] = odd[3 * ROWS :]


def cost_body(ids, terms, even, passed, got, summed):
    summed[...] = (terms[...] + even[3 * ROWS :]) + (passed[...] + got[...])


def last_cost_body(scale, ids, summed, got, cost):
    cost[...] = jnp.broadcast_to(jnp.sum(summed[...] + got[...]) * scale, (1, COLS))


def adjoint_body(ids, ext, even, odd, rate, control, out):
    side = halo_of(MEMBERS, ids, even, odd)
    back = sweep(adjoint_pass, [ext[m] for m in range(MEMBERS)], side, (rate[0], rate[1]))
    for m in range(MEMBERS):
        out[m] = control[m] + back[m]


def on_device(control, anomalies, diffusivity, loc_norm, innovation, obs_precision, obs_time):
    members = MEMBERS * lax.axis_size("mem")
    cells = members * ROWS * COLS * lax.axis_size("lat") * lax.axis_size("lon")
    factor = 1.0 / math.sqrt(members - 1)
    obs_time = in_hbm(obs_time)
    anomalies = in_hbm(anomalies.reshape(MEMBERS, 2, PLANES, ROWS, COLS))
    innovation = in_hbm(innovation.reshape(PLANES, ROWS, COLS))
    obs_precision = in_hbm(obs_precision.reshape(PLANES, ROWS, COLS))
    block = (MEMBERS, ROWS, COLS)

    fields = jnp.concatenate([control, diffusivity[None]], axis=0)
    even, odd = swap(fields, "lat", False), swap(fields, "lat", True)
    (sent1,) = select(PARTNERS[:2], anomalies, obs_time)
    even, odd, sent1 = lax.optimization_barrier((even, odd, sent1))
    ext, packed = pack(MEMBERS + 1, True, fields, even, odd)
    even, odd = swap(packed, "lon", False), swap(packed, "lon", True)
    (sent2,) = select(PARTNERS[2:], anomalies, obs_time)
    even, odd, sent2 = lax.optimization_barrier((even, odd, sent2))

    def blocks(count):
        return [pltpu.VMEM((count, ROWS, COLS), BF16)] * 3

    tile = pltpu.VMEM((8, COLS), F32)
    w, rate, terms, *send = call(
        functools.partial(forward_body, CHUNKS[0]),
        [pltpu.VMEM(block, F32), pltpu.VMEM((2, 3 * ROWS, COLS), F32), tile, *blocks(CHUNKS[0][1])],
        (ext, even, odd, loc_norm, sent1, sent2),
        [VMEM_SPEC] * 6,
        us=2.0,
    )
    got = []
    for i, chunk in enumerate(CHUNKS):
        if i > 0:
            send = call(
                functools.partial(sends_body, chunk), blocks(chunk[1]), (sent1, sent2, w), [VMEM_SPEC] * 3, us=0.3
            )
        got.append([share(cells, p) for cells, p in zip(send, PARTNERS)])
    kept, inn, prec = select((0,), anomalies, obs_time, (innovation, obs_precision))
    (own,) = call(stays_body, [pltpu.VMEM((SHARE, ROWS, COLS), F32)], (kept, w), [VMEM_SPEC] * 2, us=0.3)
    weighted, near = [], []
    for i, chunk in enumerate(CHUNKS):
        piece, terms = call(
            functools.partial(misfit_body, chunk, factor),
            [pltpu.VMEM((chunk[1] + rides(chunk), ROWS, COLS), BF16), tile],
            (own, *got[i], inn, prec, terms),
            [VMEM_SPEC] * 7,
            us=0.3,
        )
        weighted.append(piece)
        if i == len(CHUNKS) - 1:
            near.append([share(piece, p) for p in PARTNERS])
        else:
            a, b = share(piece, 1), share(piece, 3)
            near.append([share(b[:RELAYED], 1), share(a[RELAYED:], 3), a, b])
    (acc,) = call(
        own_pull_body,
        [pltpu.VMEM(block, F32)],
        (kept, *weighted),
        [VMEM_SPEC] * (1 + len(CHUNKS)),
        us=0.4,
    )
    for i, chunk in enumerate(CHUNKS[:-1]):
        (acc,) = call(
            functools.partial(pull_body, chunk),
            [pltpu.VMEM(block, F32)],
            (sent1, sent2, acc, *near[i]),
            [VMEM_SPEC] * 7,
            us=0.5,
        )
    source, terms = call(
        functools.partial(last_pull_body, factor),
        [pltpu.VMEM((MEMBERS + 1, ROWS, COLS), F32), tile],
        (sent1, sent2, acc, *near[-1], loc_norm, weighted[-1]),
        [VMEM_SPEC] * 8,
        us=0.5,
    )
    even, odd = swap(source, "lat", False), swap(source, "lat", True)
    got = trade(terms, ("lat",), (2, 3, 0, 1, 6, 7, 4, 5))
    even, odd, got = lax.optimization_barrier((even, odd, got))
    ext, packed, terms = pack(MEMBERS, False, source, even, odd, (terms, got))
    even, odd = swap(packed, "lon", False), swap(packed, "lon", True)
    (passed,) = call(pass_body, [tile], (odd,), [VMEM_SPEC], us=0.1)
    got = swap(passed, "lon", False)
    (terms,) = call(cost_body, [tile], (terms, even, passed, got), [VMEM_SPEC] * 4, us=0.1)
    got = trade(terms, ("lat",), (4, 5, 6, 7, 0, 1, 2, 3))
    even, odd, terms = lax.optimization_barrier((even, odd, terms))
    (gradient,) = call(
        adjoint_body,
        [jax.ShapeDtypeStruct(block, F32)],
        (ext, even, odd, rate, control),
        [VMEM_SPEC] * 5,
        us=3.0,
    )
    (cost,) = call(
        functools.partial(last_cost_body, 0.5 / cells),
        [jax.ShapeDtypeStruct((1, COLS), F32)],
        (terms, got),
        [VMEM_SPEC] * 2,
        us=0.1,
    )
    return gradient, cost[0, 0]


def solution(mesh):
    return jax.shard_map(
        on_device,
        mesh=mesh,
        in_specs=(
            P("mem", "lat", "lon"),
            P("mem", None, None, None, "lat", "lon"),
            P("lat", "lon"),
            P("lat", "lon"),
            P(None, None, "lat", "lon"),
            P(None, None, "lat", "lon"),
            P("lat", "lon"),
        ),
        out_specs=(P("mem", "lat", "lon"), P()),
        check_vma=False,
    )
```

time: 80.1 us -> 68.5 us (0.86)
  starting transfers between devices: 48.6 us -> 36.6 us
  Pallas kernels: 15.2 us -> 16.8 us
  waiting for transfers between devices: 14.3 us -> 13.2 us
    ppermute x26 -> x9, starting transfers between devices: 40.7 us -> 18.4 us  [swap(): return lax.ppermute(cells, axis, pairs)]
    ppermute x6 -> x15, starting transfers between devices: 7.88 us -> 18.2 us  [trade(): return lax.ppermute(cells, axes, list(enumerate(to)))]
    ppermute x26 -> x9, waiting for transfers between devices: 6.46 us -> 2.73 us  [swap(): return lax.ppermute(cells, axis, pairs)]
    ppermute x6 -> x15, waiting for transfers between devices: 7.87 us -> 10.5 us  [trade(): return lax.ppermute(cells, axes, list(enumerate(to)))]
    pallas_call x16 -> x17, Pallas kernels: 15.2 us -> 16.8 us  [call(): pl.pallas_call(placed, out_shape=outs, in_specs=specs, out_specs=[VMEM_SP...]
  transfers between devices with their start and end apart: 32 -> 24, of which waited for: 12 -> 6; matrix products, arithmetic and copies ran while one was open for 0% -> 0% of each run, Pallas kernels for 11% -> 19%
where the time goes in v3:
time: 68.5 us; the launch traced here: 68.3 us
  starting transfers between devices  36.6 us (53%)
  Pallas kernels  16.8 us (25%)
  waiting for transfers between devices  13.2 us (19%)
  between operations  0.85 us (1%)
  other arithmetic  0.8 us (1%)
    ppermute x9, starting transfers between devices, swap(): return lax.ppermute(cells, axis, pairs)  18.4 us
    ppermute x15, starting transfers between devices, trade(): return lax.ppermute(cells, axes, list(enumerate(to)))  18.2 us
    pallas_call x17, Pallas kernels, call(): pl.pallas_call(placed, out_shape=outs, in_specs=specs, out_specs=[VMEM_SP...  16.8 us
    ppermute x15, waiting for transfers between devices, trade(): return lax.ppermute(cells, axes, list(enumerate(to)))  10.5 us
    ppermute x9, waiting for transfers between devices, swap(): return lax.ppermute(cells, axis, pairs)  2.73 us
  transfers between devices with their start and end apart: 24, of which 6 were waited for; matrix products, arithmetic and copies ran while one was open for 0% of the time, Pallas kernels for 19%

profile of v3, /device:TPU:1, one launch (start us, length us, event | category | flops | bytes accessed | tf_op | source)
XLA Modules:
  0.0 68.3 jit_solution(1250008846635951812)
XLA Ops:
  0.6 0.8 %pad_maximum_fusion.refs_0_ = f32[6,16,128]{2,1,0:T(8,128)S(1)} fusion(f32[1,16,128]{2,1,0:T(8,128)} %bitcast.11, f32[5,16,128]{2,1,0:T(8,128)} %refs_4_.1), kind=kLoop, calls=%fused_computation | loop fusion | flops 12288 | bytes 98304 | tf_op jit(solution)/shard_map/concatenate | solution.py:376
  1.4 2.0 %collective-permute-start = (f32[6,16,128]{2,1,0:T(8,128)S(1)}, f32[6,16,128]{2,1,0:T(8,128)S(1)}, u32[]{:S(2)}, u32[]{:S(2)}) collective-permute-start(f32[6,16,128]{2,1,0:T(8,128)S(1)} %pad_maximum_fusion.refs_0_), channel_id=1, source_target_pairs={{0,4},{4,0},{8,12},{12,8},{16,20},{20,16},{24,28},{28,24},{1,5},{5... | collective-permute-start | bytes 147464 | tf_op jit(solution)/shard_map/ppermute | solution.py:55
  3.5 3.2 %collective-permute-start.1 = (f32[6,16,128]{2,1,0:T(8,128)S(1)}, f32[6,16,128]{2,1,0:T(8,128)S(1)}, u32[]{:S(2)}, u32[]{:S(2)}) collective-permute-start(f32[6,16,128]{2,1,0:T(8,128)S(1)} %pad_maximum_fusion.refs_0_), channel_id=1, source_target_pairs={{0,28},{4,8},{8,4},{12,16},{16,12},{20,24},{24,20},{28,0},{1,29},{... | collective-permute-start | bytes 147464 | tf_op jit(solution)/shard_map/ppermute | solution.py:55
  6.6 3.1 %shard_map.86.refs_4_.refs_0_ = bf16[2,5,70,16,128]{4,3,2,1,0:T(8,128)(2,1)S(1)} custom-call(bf16[5,2,280,16,128]{4,3,2,1,0:T(8,128)(2,1)} %bitcast.6, s32[16,128]{1,0:T(8,128)} %refs_1_.5), custom_call_target="tpu_custom_call" | custom-call | flops 2500000 | bytes 7500000 | tf_op jit(solution)/shard_map/pallas_call | solution.py:31
  9.9 1.3 %collective-permute-start.2 = (f32[48,128]{1,0:T(8,128)S(1)}, f32[48,128]{1,0:T(8,128)S(1)}, u32[]{:S(2)}, u32[]{:S(2)}) collective-permute-start(f32[48,128]{1,0:T(8,128)S(1)} %get-tuple-element.39), channel_id=1, source_target_pairs={{0,1},{1,0},{2,3},{3,2},{4,5},{5,4},{6,7},{7,6},{8,9},{9,8},{10,11... | collective-permute-start | bytes 73736 | tf_op jit(solution)/shard_map/ppermute | solution.py:55
  11.2 3.3 %collective-permute-start.3 = (f32[48,128]{1,0:T(8,128)S(1)}, f32[48,128]{1,0:T(8,128)S(1)}, u32[]{:S(2)}, u32[]{:S(2)}) collective-permute-start(f32[48,128]{1,0:T(8,128)S(1)} %get-tuple-element.39), channel_id=1, source_target_pairs={{0,3},{1,2},{2,1},{3,0},{4,7},{5,6},{6,5},{7,4},{8,11},{9,10},{10,... | collective-permute-start | bytes 73736 | tf_op jit(solution)/shard_map/ppermute | solution.py:55
  14.5 1.9 %shard_map.88.refs_5_.refs_1_ = bf16[1,5,70,16,128]{4,3,2,1,0:T(8,128)(2,1)S(1)} custom-call(bf16[5,2,280,16,128]{4,3,2,1,0:T(8,128)(2,1)} %bitcast.7, s32[16,128]{1,0:T(8,128)} %refs_1_.5), custom_call_target="tpu_custom_call" | custom-call | flops 2500000 | bytes 7500000 | tf_op jit(solution)/shard_map/pallas_call | solution.py:31
  16.5 2.7 %shard_map.90 = (f32[5,16,128]{2,1,0:T(8,128)S(1)}, f32[2,48,128]{2,1,0:T(8,128)S(1)}, f32[8,128]{1,0:T(8,128)S(1)}, bf16[35,16,128]{2,1,0:T(8,128)(2,1)S(1)}, b...) custom-call(f32[6,48,128]{2,1,0:T(8,128)S(1)} %get-tuple-element.42.refs_0_, ...), custom_call_target="tpu_custom_call" | custom-call | flops 2000000 | bytes 6000000 | tf_op jit(solution)/shard_map/pallas_call | solution.py:31
  19.2 3.0 %collective-permute-start.4 = (bf16[35,16,128]{2,1,0:T(8,128)(2,1)S(1)}, bf16[35,16,128]{2,1,0:T(8,128)(2,1)S(1)}, u32[]{:S(2)}, u32[]{:S(2)}) collective-permute-start(bf16[35,16,128]{2,1,0:T(8,128)(2,1)S(1)} %get-tuple-element.46), channel_id=1, source_target_pairs={{0,64},{32,96},{64,0},{96,32},{1,65},{33,97},{65,1},{97,33},{2,66}... | collective-permute-start | bytes 430088 | tf_op jit(solution)/shard_map/ppermute | solution.py:59
  22.5 0.4 collective-permute-start.6
  22.9 0.5 shard_map.93
  23.4 2.5 %collective-permute-start.7 = (bf16[35,16,128]{2,1,0:T(8,128)(2,1)S(1)}, bf16[35,16,128]{2,1,0:T(8,128)(2,1)S(1)}, u32[]{:S(2)}, u32[]{:S(2)}) collective-permute-start(bf16[35,16,128]{2,1,0:T(8,128)(2,1)S(1)} %get-tuple-element.53), channel_id=1, source_target_pairs={{0,64},{32,96},{64,0},{96,32},{1,65},{33,97},{65,1},{97,33},{2,66}... | collective-permute-start | bytes 430088 | tf_op jit(solution)/shard_map/ppermute | solution.py:59
  26.4 2.0 %collective-permute-start.9 = (bf16[35,16,128]{2,1,0:T(8,128)(2,1)S(1)}, bf16[35,16,128]{2,1,0:T(8,128)(2,1)S(1)}, u32[]{:S(2)}, u32[]{:S(2)}) collective-permute-start(bf16[35,16,128]{2,1,0:T(8,128)(2,1)S(1)} %get-tuple-element.55), channel_id=1, source_target_pairs={{0,96},{32,64},{64,32},{96,0},{1,97},{33,65},{65,33},{97,1},{2,98}... | collective-permute-start | bytes 430088 | tf_op jit(solution)/shard_map/ppermute | solution.py:59
  28.4 2.2 %shard_map.89 = (bf16[1,5,70,16,128]{4,3,2,1,0:T(8,128)(2,1)S(1)}, f32[70,16,128]{2,1,0:T(8,128)S(1)}, f32[70,16,128]{2,1,0:T(8,128)S(1)}) custom-call(bf16[5,2,280,16,128]{4,3,2,1,0:T(8,128)(2,1)} %bitcast.8, s32[16,128]{1,0:T(8,128)} %refs_1_.5, f32[280,16,128]{2,1,0:T(8,128)} %bitcast.9, f32[280,16,128]{2,1,0:T(8,128)} %bitcast.10), custom_call_target="tpu_custom_call" | custom-call | flops 2500000 | bytes 7500000 | tf_op jit(solution)/shard_map/pallas_call | solution.py:31
  31.1 2.1 %collective-permute-start.10 = (bf16[35,16,128]{2,1,0:T(8,128)(2,1)S(1)}, bf16[35,16,128]{2,1,0:T(8,128)(2,1)S(1)}, u32[]{:S(2)}, u32[]{:S(2)}) collective-permute-start(bf16[35,16,128]{2,1,0:T(8,128)(2,1)S(1)} %get-tuple-element.52.refs_1_), channel_id=1, source_target_pairs={{0,96},{32,64},{64,32},{96,0},{1,97},{33,65},{65,33},{97,1},{2,98}... | collective-permute-start | bytes 430088 | tf_op jit(solution)/shard_map/ppermute | solution.py:59
  33.2 2.0 %collective-permute-done.8.refs_2_ = bf16[35,16,128]{2,1,0:T(8,128)(2,1)S(1)} collective-permute-done((bf16[35,16,128]{2,1,0:T(8,128)(2,1)S(1)}, bf16[35,16,128]{2,1,0:T(8,128)(2,1)S(1)}, u32[]{:S(2)}, u32[]{:S(2)}) %collective-permute-start.8) | collective-permute-done | bytes 143392 | tf_op jit(solution)/shard_map/ppermute | solution.py:59
  35.2 0.5 collective-permute-done.9.refs_3_
  35.7 0.8 %shard_map.94 = (bf16[36,16,128]{2,1,0:T(8,128)(2,1)S(1)}, f32[8,128]{1,0:T(8,128)}) custom-call(f32[70,16,128]{2,1,0:T(8,128)S(1)} %shard_map.91.refs_0_, bf16[35,16,128]{2,1,0:T(8,128)(2,1)S(1)} %collective-permute-done.7.refs_1_, bf16[35,16,128]{2,1,0:T(8,128)(2,1)S(1)} %collective-permute-done.8.refs_2_, ...), custom_call_target="tpu_custom_call" | custom-call | flops 300000 | bytes 900000 | tf_op jit(solution)/shard_map/pallas_call | solution.py:31
  36.5 2.7 %collective-permute-start.14 = (bf16[36,16,128]{2,1,0:T(8,128)(2,1)S(1)}, bf16[36,16,128]{2,1,0:T(8,128)(2,1)S(1)}, u32[]{:S(2)}, u32[]{:S(2)}) collective-permute-start(bf16[36,16,128]{2,1,0:T(8,128)(2,1)S(1)} %get-tuple-element.57.refs_2_.refs_7_), channel_id=1, source_target_pairs={{0,64},{32,96},{64,0},{96,32},{1,65},{33,97},{65,1},{97,33},{2,66}... | collective-permute-start | bytes 442376 | tf_op jit(solution)/shard_map/ppermute | solution.py:59
  39.8 1.0 %collective-permute-start.11 = (bf16[20,16,128]{2,1,0:T(8,128)(2,1)S(1)}, bf16[20,16,128]{2,1,0:T(8,128)(2,1)S(1)}, u32[]{:S(2)}, u32[]{:S(2)}) collective-permute-start(bf16[20,16,128]{2,1,0:T(8,128)(2,1)S(1)} %slice.12), channel_id=1, source_target_pairs={{0,32},{32,0},{64,96},{96,64},{1,33},{33,1},{65,97},{97,65},{2,34}... | collective-permute-start | bytes 245768 | tf_op jit(solution)/shard_map/ppermute | solution.py:59
  40.8 2.1 %collective-permute-start.13 = (bf16[15,16,128]{2,1,0:T(8,128)(2,1)S(1)}, bf16[15,16,128]{2,1,0:T(8,128)(2,1)S(1)}, u32[]{:S(2)}, u32[]{:S(2)}) collective-permute-start(bf16[15,16,128]{2,1,0:T(8,128)(2,1)S(1)} %slice.13), channel_id=1, source_target_pairs={{0,96},{32,64},{64,32},{96,0},{1,97},{33,65},{65,33},{97,1},{2,98}... | collective-permute-start | bytes 184328 | tf_op jit(solution)/shard_map/ppermute | solution.py:59
  43.3 4.7 %collective-permute-done.13.refs_4_ = bf16[15,16,128]{2,1,0:T(8,128)(2,1)S(1)} collective-permute-done((bf16[15,16,128]{2,1,0:T(8,128)(2,1)S(1)}, bf16[15,16,128]{2,1,0:T(8,128)(2,1)S(1)}, u32[]{:S(2)}, u32[]{:S(2)}) %collective-permute-start.13) | collective-permute-done | bytes 61472 | tf_op jit(solution)/shard_map/ppermute | solution.py:59
  48.0 0.5 shard_map.96.refs_2_
  48.6 0.6 shard_map.97
  49.3 2.4 %collective-permute-start.18 = (f32[6,16,128]{2,1,0:T(8,128)S(1)}, f32[6,16,128]{2,1,0:T(8,128)S(1)}, u32[]{:S(2)}, u32[]{:S(2)}) collective-permute-start(f32[6,16,128]{2,1,0:T(8,128)S(1)} %get-tuple-element.58.refs_0_), channel_id=1, source_target_pairs={{0,28},{4,8},{8,4},{12,16},{16,12},{20,24},{24,20},{28,0},{1,29},{... | collective-permute-start | bytes 147464 | tf_op jit(solution)/shard_map/ppermute | solution.py:55
  51.7 0.8 %collective-permute-start.19 = (f32[8,128]{1,0:T(8,128)S(1)}, f32[8,128]{1,0:T(8,128)S(1)}, u32[]{:S(2)}, u32[]{:S(2)}) collective-permute-start(f32[8,128]{1,0:T(8,128)S(1)} %get-tuple-element.59.refs_3_), channel_id=1, source_target_pairs={{0,8},{4,12},{8,0},{12,4},{16,24},{20,28},{24,16},{28,20},{1,9},{5... | collective-permute-start | bytes 12296 | tf_op jit(solution)/shard_map/ppermute | solution.py:59
  52.5 3.2 %collective-permute-done.19.refs_4_ = f32[8,128]{1,0:T(8,128)S(1)} collective-permute-done((f32[8,128]{1,0:T(8,128)S(1)}, f32[8,128]{1,0:T(8,128)S(1)}, u32[]{:S(2)}, u32[]{:S(2)}) %collective-permute-start.19) | collective-permute-done | bytes 4128 | tf_op jit(solution)/shard_map/ppermute | solution.py:59
  55.9 6.1 %collective-permute-start.21 = (f32[56,128]{1,0:T(8,128)S(1)}, f32[56,128]{1,0:T(8,128)S(1)}, u32[]{:S(2)}, u32[]{:S(2)}) collective-permute-start(f32[56,128]{1,0:T(8,128)S(1)} %get-tuple-element.64), channel_id=1, source_target_pairs={{0,3},{1,2},{2,1},{3,0},{4,7},{5,6},{6,5},{7,4},{8,11},{9,10},{10,... | collective-permute-start | bytes 86024 | tf_op jit(solution)/shard_map/ppermute | solution.py:55
  61.9 1.6 %collective-permute-done.21.refs_0_.refs_2_ = f32[56,128]{1,0:T(8,128)S(1)} collective-permute-done((f32[56,128]{1,0:T(8,128)S(1)}, f32[56,128]{1,0:T(8,128)S(1)}, u32[]{:S(2)}, u32[]{:S(2)}) %collective-permute-start.21) | collective-permute-done | bytes 28704 | tf_op jit(solution)/shard_map/ppermute | solution.py:55
  63.5 1.2 %collective-permute-done.22.refs_3_ = f32[8,128]{1,0:T(8,128)S(1)} collective-permute-done((f32[8,128]{1,0:T(8,128)S(1)}, f32[8,128]{1,0:T(8,128)S(1)}, u32[]{:S(2)}, u32[]{:S(2)}) %collective-permute-start.22) | collective-permute-done | bytes 4128 | tf_op jit(solution)/shard_map/ppermute | solution.py:55
  64.9 2.8 %shard_map.101 = f32[5,16,128]{2,1,0:T(8,128)} custom-call(f32[5,48,128]{2,1,0:T(8,128)S(1)} %get-tuple-element.63.refs_0_, f32[56,128]{1,0:T(8,128)S(1)} %collective-permute-done.20.refs_1_, f32[56,128]{1,0:T(8,128)S(1)} %collective-permute-done.21.refs_0_.refs_2_, f32[2,48,128]{2,1,0:T(8,128)S(1)} %get-tuple-element.68.refs_3_, f32[5,16,128]{2,1,0:T(8,128)S(1)} %copy-done), custom_call_target="tpu_custom_call" | custom-call | flops 3000000 | bytes 9000000 | tf_op jit(solution)/shard_map/pallas_call | solution.py:31
  67.6 0.6 shard_map.102
  (40 shorter events, 2.8 us)
Async XLA Ops:
  1.4 8.4 %collective-permute-start = (f32[6,16,128]{2,1,0:T(8,128)S(1)}, f32[6,16,128]{2,1,0:T(8,128)S(1)}, u32[]{:S(2)}, u32[]{:S(2)}) collective-permute-start(f32[6,16,128]{2,1,0:T(8,128)S(1)} %pad_maximum_fusion.refs_0_), channel_id=1, source_target_pairs={{0,4},{4,0},{8,12},{12,8},{16,20},{20,16},{24,28},{28,24},{1,5},{5... | collective-permute-start | bytes 147464 | tf_op jit(solution)/shard_map/ppermute | solution.py:55
  3.5 6.3 %collective-permute-start.1 = (f32[6,16,128]{2,1,0:T(8,128)S(1)}, f32[6,16,128]{2,1,0:T(8,128)S(1)}, u32[]{:S(2)}, u32[]{:S(2)}) collective-permute-start(f32[6,16,128]{2,1,0:T(8,128)S(1)} %pad_maximum_fusion.refs_0_), channel_id=1, source_target_pairs={{0,28},{4,8},{8,4},{12,16},{16,12},{20,24},{24,20},{28,0},{1,29},{... | collective-permute-start | bytes 147464 | tf_op jit(solution)/shard_map/ppermute | solution.py:55
  9.9 6.5 %copy-start.1 = (f32[16,128]{1,0:T(8,128)S(1)}, f32[16,128]{1,0:T(8,128)}, u32[]{:S(2)}) copy-start(f32[16,128]{1,0:T(8,128)} %refs_6_.1) | copy-start | bytes 24580
  9.9 6.5 %collective-permute-start.2 = (f32[48,128]{1,0:T(8,128)S(1)}, f32[48,128]{1,0:T(8,128)S(1)}, u32[]{:S(2)}, u32[]{:S(2)}) collective-permute-start(f32[48,128]{1,0:T(8,128)S(1)} %get-tuple-element.39), channel_id=1, source_target_pairs={{0,1},{1,0},{2,3},{3,2},{4,5},{5,4},{6,7},{7,6},{8,9},{9,8},{10,11... | collective-permute-start | bytes 73736 | tf_op jit(solution)/shard_map/ppermute | solution.py:55
  11.2 5.2 %collective-permute-start.3 = (f32[48,128]{1,0:T(8,128)S(1)}, f32[48,128]{1,0:T(8,128)S(1)}, u32[]{:S(2)}, u32[]{:S(2)}) collective-permute-start(f32[48,128]{1,0:T(8,128)S(1)} %get-tuple-element.39), channel_id=1, source_target_pairs={{0,3},{1,2},{2,1},{3,0},{4,7},{5,6},{6,5},{7,4},{8,11},{9,10},{10,... | collective-permute-start | bytes 73736 | tf_op jit(solution)/shard_map/ppermute | solution.py:55
  19.2 7.2 %collective-permute-start.4 = (bf16[35,16,128]{2,1,0:T(8,128)(2,1)S(1)}, bf16[35,16,128]{2,1,0:T(8,128)(2,1)S(1)}, u32[]{:S(2)}, u32[]{:S(2)}) collective-permute-start(bf16[35,16,128]{2,1,0:T(8,128)(2,1)S(1)} %get-tuple-element.46), channel_id=1, source_target_pairs={{0,64},{32,96},{64,0},{96,32},{1,65},{33,97},{65,1},{97,33},{2,66}... | collective-permute-start | bytes 430088 | tf_op jit(solution)/shard_map/ppermute | solution.py:59
  22.1 8.8 %collective-permute-start.5 = (bf16[35,16,128]{2,1,0:T(8,128)(2,1)S(1)}, bf16[35,16,128]{2,1,0:T(8,128)(2,1)S(1)}, u32[]{:S(2)}, u32[]{:S(2)}) collective-permute-start(bf16[35,16,128]{2,1,0:T(8,128)(2,1)S(1)} %get-tuple-element.47), channel_id=1, source_target_pairs={{0,32},{32,0},{64,96},{96,64},{1,33},{33,1},{65,97},{97,65},{2,34}... | collective-permute-start | bytes 430088 | tf_op jit(solution)/shard_map/ppermute | solution.py:59
  22.5 8.4 %collective-permute-start.6 = (bf16[35,16,128]{2,1,0:T(8,128)(2,1)S(1)}, bf16[35,16,128]{2,1,0:T(8,128)(2,1)S(1)}, u32[]{:S(2)}, u32[]{:S(2)}) collective-permute-start(bf16[35,16,128]{2,1,0:T(8,128)(2,1)S(1)} %get-tuple-element.48), channel_id=1, source_target_pairs={{0,96},{32,64},{64,32},{96,0},{1,97},{33,65},{65,33},{97,1},{2,98}... | collective-permute-start | bytes 430088 | tf_op jit(solution)/shard_map/ppermute | solution.py:59
  23.4 9.8 %collective-permute-start.7 = (bf16[35,16,128]{2,1,0:T(8,128)(2,1)S(1)}, bf16[35,16,128]{2,1,0:T(8,128)(2,1)S(1)}, u32[]{:S(2)}, u32[]{:S(2)}) collective-permute-start(bf16[35,16,128]{2,1,0:T(8,128)(2,1)S(1)} %get-tuple-element.53), channel_id=1, source_target_pairs={{0,64},{32,96},{64,0},{96,32},{1,65},{33,97},{65,1},{97,33},{2,66}... | collective-permute-start | bytes 430088 | tf_op jit(solution)/shard_map/ppermute | solution.py:59
  26.0 9.2 %collective-permute-start.8 = (bf16[35,16,128]{2,1,0:T(8,128)(2,1)S(1)}, bf16[35,16,128]{2,1,0:T(8,128)(2,1)S(1)}, u32[]{:S(2)}, u32[]{:S(2)}) collective-permute-start(bf16[35,16,128]{2,1,0:T(8,128)(2,1)S(1)} %get-tuple-element.54), channel_id=1, source_target_pairs={{0,32},{32,0},{64,96},{96,64},{1,33},{33,1},{65,97},{97,65},{2,34}... | collective-permute-start | bytes 430088 | tf_op jit(solution)/shard_map/ppermute | solution.py:59
  26.4 9.3 %collective-permute-start.9 = (bf16[35,16,128]{2,1,0:T(8,128)(2,1)S(1)}, bf16[35,16,128]{2,1,0:T(8,128)(2,1)S(1)}, u32[]{:S(2)}, u32[]{:S(2)}) collective-permute-start(bf16[35,16,128]{2,1,0:T(8,128)(2,1)S(1)} %get-tuple-element.55), channel_id=1, source_target_pairs={{0,96},{32,64},{64,32},{96,0},{1,97},{33,65},{65,33},{97,1},{2,98}... | collective-permute-start | bytes 430088 | tf_op jit(solution)/shard_map/ppermute | solution.py:59
  31.1 8.6 %collective-permute-start.10 = (bf16[35,16,128]{2,1,0:T(8,128)(2,1)S(1)}, bf16[35,16,128]{2,1,0:T(8,128)(2,1)S(1)}, u32[]{:S(2)}, u32[]{:S(2)}) collective-permute-start(bf16[35,16,128]{2,1,0:T(8,128)(2,1)S(1)} %get-tuple-element.52.refs_1_), channel_id=1, source_target_pairs={{0,96},{32,64},{64,32},{96,0},{1,97},{33,65},{65,33},{97,1},{2,98}... | collective-permute-start | bytes 430088 | tf_op jit(solution)/shard_map/ppermute | solution.py:59
  33.2 7.5 %collective-permute-start.12 = (bf16[35,16,128]{2,1,0:T(8,128)(2,1)S(1)}, bf16[35,16,128]{2,1,0:T(8,128)(2,1)S(1)}, u32[]{:S(2)}, u32[]{:S(2)}) collective-permute-start(bf16[35,16,128]{2,1,0:T(8,128)(2,1)S(1)} %get-tuple-element.52.refs_1_), channel_id=1, source_target_pairs={{0,32},{32,0},{64,96},{96,64},{1,33},{33,1},{65,97},{97,65},{2,34}... | collective-permute-start | bytes 430088 | tf_op jit(solution)/shard_map/ppermute | solution.py:59
  36.5 12.1 %collective-permute-start.14 = (bf16[36,16,128]{2,1,0:T(8,128)(2,1)S(1)}, bf16[36,16,128]{2,1,0:T(8,128)(2,1)S(1)}, u32[]{:S(2)}, u32[]{:S(2)}) collective-permute-start(bf16[36,16,128]{2,1,0:T(8,128)(2,1)S(1)} %get-tuple-element.57.refs_2_.refs_7_), channel_id=1, source_target_pairs={{0,64},{32,96},{64,0},{96,32},{1,65},{33,97},{65,1},{97,33},{2,66}... | collective-permute-start | bytes 442376 | tf_op jit(solution)/shard_map/ppermute | solution.py:59
  39.2 9.4 %collective-permute-start.15 = (bf16[36,16,128]{2,1,0:T(8,128)(2,1)S(1)}, bf16[36,16,128]{2,1,0:T(8,128)(2,1)S(1)}, u32[]{:S(2)}, u32[]{:S(2)}) collective-permute-start(bf16[36,16,128]{2,1,0:T(8,128)(2,1)S(1)} %get-tuple-element.57.refs_2_.refs_7_), channel_id=1, source_target_pairs={{0,32},{32,0},{64,96},{96,64},{1,33},{33,1},{65,97},{97,65},{2,34}... | collective-permute-start | bytes 442376 | tf_op jit(solution)/shard_map/ppermute | solution.py:59
  39.5 9.1 %collective-permute-start.16 = (bf16[36,16,128]{2,1,0:T(8,128)(2,1)S(1)}, bf16[36,16,128]{2,1,0:T(8,128)(2,1)S(1)}, u32[]{:S(2)}, u32[]{:S(2)}) collective-permute-start(bf16[36,16,128]{2,1,0:T(8,128)(2,1)S(1)} %get-tuple-element.57.refs_2_.refs_7_), channel_id=1, source_target_pairs={{0,96},{32,64},{64,32},{96,0},{1,97},{33,65},{65,33},{97,1},{2,98}... | collective-permute-start | bytes 442376 | tf_op jit(solution)/shard_map/ppermute | solution.py:59
  39.8 8.3 %collective-permute-start.11 = (bf16[20,16,128]{2,1,0:T(8,128)(2,1)S(1)}, bf16[20,16,128]{2,1,0:T(8,128)(2,1)S(1)}, u32[]{:S(2)}, u32[]{:S(2)}) collective-permute-start(bf16[20,16,128]{2,1,0:T(8,128)(2,1)S(1)} %slice.12), channel_id=1, source_target_pairs={{0,32},{32,0},{64,96},{96,64},{1,33},{33,1},{65,97},{97,65},{2,34}... | collective-permute-start | bytes 245768 | tf_op jit(solution)/shard_map/ppermute | solution.py:59
  40.8 7.2 %collective-permute-start.13 = (bf16[15,16,128]{2,1,0:T(8,128)(2,1)S(1)}, bf16[15,16,128]{2,1,0:T(8,128)(2,1)S(1)}, u32[]{:S(2)}, u32[]{:S(2)}) collective-permute-start(bf16[15,16,128]{2,1,0:T(8,128)(2,1)S(1)} %slice.13), channel_id=1, source_target_pairs={{0,96},{32,64},{64,32},{96,0},{1,97},{33,65},{65,33},{97,1},{2,98}... | collective-permute-start | bytes 184328 | tf_op jit(solution)/shard_map/ppermute | solution.py:59
  48.6 16.3 %copy-start = (f32[5,16,128]{2,1,0:T(8,128)S(1)}, f32[5,16,128]{2,1,0:T(8,128)}, u32[]{:S(2)}) copy-start(f32[5,16,128]{2,1,0:T(8,128)} %refs_4_.1) | copy-start | bytes 122884
  49.2 6.6 %collective-permute-start.17 = (f32[6,16,128]{2,1,0:T(8,128)S(1)}, f32[6,16,128]{2,1,0:T(8,128)S(1)}, u32[]{:S(2)}, u32[]{:S(2)}) collective-permute-start(f32[6,16,128]{2,1,0:T(8,128)S(1)} %get-tuple-element.58.refs_0_), channel_id=1, source_target_pairs={{0,4},{4,0},{8,12},{12,8},{16,20},{20,16},{24,28},{28,24},{1,5},{5... | collective-permute-start | bytes 147464 | tf_op jit(solution)/shard_map/ppermute | solution.py:55
  49.3 6.5 %collective-permute-start.18 = (f32[6,16,128]{2,1,0:T(8,128)S(1)}, f32[6,16,128]{2,1,0:T(8,128)S(1)}, u32[]{:S(2)}, u32[]{:S(2)}) collective-permute-start(f32[6,16,128]{2,1,0:T(8,128)S(1)} %get-tuple-element.58.refs_0_), channel_id=1, source_target_pairs={{0,28},{4,8},{8,4},{12,16},{16,12},{20,24},{24,20},{28,0},{1,29},{... | collective-permute-start | bytes 147464 | tf_op jit(solution)/shard_map/ppermute | solution.py:55
  51.7 4.1 %collective-permute-start.19 = (f32[8,128]{1,0:T(8,128)S(1)}, f32[8,128]{1,0:T(8,128)S(1)}, u32[]{:S(2)}, u32[]{:S(2)}) collective-permute-start(f32[8,128]{1,0:T(8,128)S(1)} %get-tuple-element.59.refs_3_), channel_id=1, source_target_pairs={{0,8},{4,12},{8,0},{12,4},{16,24},{20,28},{24,16},{28,20},{1,9},{5... | collective-permute-start | bytes 12296 | tf_op jit(solution)/shard_map/ppermute | solution.py:59
  55.9 7.6 %collective-permute-start.21 = (f32[56,128]{1,0:T(8,128)S(1)}, f32[56,128]{1,0:T(8,128)S(1)}, u32[]{:S(2)}, u32[]{:S(2)}) collective-permute-start(f32[56,128]{1,0:T(8,128)S(1)} %get-tuple-element.64), channel_id=1, source_target_pairs={{0,3},{1,2},{2,1},{3,0},{4,7},{5,6},{6,5},{7,4},{8,11},{9,10},{10,... | collective-permute-start | bytes 86024 | tf_op jit(solution)/shard_map/ppermute | solution.py:55
  61.9 1.6 %collective-permute-start.20 = (f32[56,128]{1,0:T(8,128)S(1)}, f32[56,128]{1,0:T(8,128)S(1)}, u32[]{:S(2)}, u32[]{:S(2)}) collective-permute-start(f32[56,128]{1,0:T(8,128)S(1)} %get-tuple-element.64), channel_id=1, source_target_pairs={{0,1},{1,0},{2,3},{3,2},{4,5},{5,4},{6,7},{7,6},{8,9},{9,8},{10,11... | collective-permute-start | bytes 86024 | tf_op jit(solution)/shard_map/ppermute | solution.py:55
  63.5 1.2 %collective-permute-start.22 = (f32[8,128]{1,0:T(8,128)S(1)}, f32[8,128]{1,0:T(8,128)S(1)}, u32[]{:S(2)}, u32[]{:S(2)}) collective-permute-start(f32[8,128]{1,0:T(8,128)S(1)} %shard_map.99.refs_2_), channel_id=1, source_target_pairs={{0,1},{1,0},{2,3},{3,2},{4,5},{5,4},{6,7},{7,6},{8,9},{9,8},{10,11... | collective-permute-start | bytes 12296 | tf_op jit(solution)/shard_map/ppermute | solution.py:55
  64.7 3.0 %collective-permute-start.23 = (f32[8,128]{1,0:T(8,128)S(1)}, f32[8,128]{1,0:T(8,128)S(1)}, u32[]{:S(2)}, u32[]{:S(2)}) collective-permute-start(f32[8,128]{1,0:T(8,128)S(1)} %shard_map.100.refs_0_), channel_id=1, source_target_pairs={{0,16},{4,20},{8,24},{12,28},{16,0},{20,4},{24,8},{28,12},{1,17},{... | collective-permute-start | bytes 12296 | tf_op jit(solution)/shard_map/ppermute | solution.py:59

commit v4 on v3

--- a/solution.py
+++ b/solution.py
@@ -63,102 +63,117 @@
     return trade(cells, ("mem",), [i ^ partner for i in range(4)])
 
 
-def pack_body(fields, mask_edges, ids, own, even, odd, *rest):
-    if len(rest) > 2:
-        terms, got, ext, packed, new_terms = rest
-        summed = (terms[...] + even[fields, :8]) + (got[...] + odd[fields, :8])
-        new_terms[...] = summed
-        packed[3 * ROWS :] = summed
+SUB = 8
+TALL = 3 * ROWS
+TILES = (TALL * SUB, COLS)
+
+
+def put(ref, f, rows):
+    ref[pl.ds(f, TALL, stride=SUB)] = rows
+
+
+def pack_body(fields, first, ids, own, even, odd, *rest):
+    if first:
+        ext, rate, packed = rest
     else:
-        ext, packed = rest
+        terms, ext, packed, new_terms = rest
+        new_terms[...] = (terms[...] + even[fields, :8]) + odd[fields, :8]
     lat = ids[1]
     is_even = lax.rem(lat, 2) == 0
-    lane = lax.broadcasted_iota(jnp.int32, (3 * ROWS, COLS), 1)
-    out = jnp.zeros((3 * ROWS, COLS), F32)
+    lane = lax.broadcasted_iota(jnp.int32, (TALL, COLS), 1)
+    out = jnp.zeros((TALL, COLS), F32)
     for f in range(fields):
         a, b = even[f], odd[f]
         up = jnp.where(is_even, b, a)
         down = jnp.where(is_even, a, b)
-        if mask_edges:
+        if first:
             up = jnp.where(lat == 0, 0.0, up)
             down = jnp.where(lat == 7, 0.0, down)
         whole = jnp.concatenate([up, own[f], down], axis=0)
-        ext[f] = whole
+        if f < MEMBERS:
+            put(ext, f, whole)
+        else:
+            for sub in range(SUB):
+                put(rate, sub, whole)
         at = 2 * REACH * f
         turned = pltpu.roll(whole, (at + REACH) % COLS, 1)
         out = jnp.where((lane >= at) & (lane < at + 2 * REACH), turned, out)
-    packed[: 3 * ROWS] = out
-
-
-def pack(fields, mask_edges, own, even, odd, terms=()):
+    packed[:TALL] = out
+
+
+def pack(fields, own, even, odd, terms=()):
     return call(
-        functools.partial(pack_body, fields, mask_edges),
-        [pltpu.VMEM((fields, 3 * ROWS, COLS), F32), pltpu.VMEM((3 * ROWS + (8 if terms else 0), COLS), F32)]
-        + [pltpu.VMEM((8, COLS), F32)] * (1 if terms else 0),
+        functools.partial(pack_body, fields, not terms),
+        [pltpu.VMEM(TILES, F32)] * (1 if terms else 2)
+        + [pltpu.VMEM((TALL + (8 if terms else 0), COLS), F32)]
+        + [pltpu.VMEM((8, COLS), F32)] * len(terms),
         (own, even, odd, *terms),
         [VMEM_SPEC] * (3 + len(terms)),
         us=0.3,
     )
 
 
-def group(lane, m):
-    return (lane >= 2 * REACH * m) & (lane < 2 * REACH * (m + 1))
+def ride_body(ids, held, terms, got, packed, new_terms):
+    summed = terms[...] + got[...]
+    new_terms[...] = summed
+    packed[TALL:] = summed
 
 
 def halo_of(fields, ids, even, odd):
     is_even = lax.rem(ids[2], 2) == 0
-    lane = lax.broadcasted_iota(jnp.int32, (3 * ROWS, COLS), 1)
+    lane = lax.broadcasted_iota(jnp.int32, (TALL, COLS), 1)
     west = lane < 0
     for f in range(fields):
         at = 2 * REACH * f
         west = west | ((lane >= at) & (lane < at + REACH))
-    a, b = even[: 3 * ROWS], odd[: 3 * ROWS]
+    a, b = even[:TALL], odd[:TALL]
     return jnp.where(west, jnp.where(is_even, b, a), jnp.where(is_even, a, b))
 
 
-def lap(own, side):
-    rows = side.shape[0]
-    lane = lax.broadcasted_iota(jnp.int32, side.shape, 1)
-
-    def total(v, west, east):
-        above = pltpu.roll(v, 1, 0)
-        below = pltpu.roll(v, rows - 1, 0)
-        return (above + below) + (west + east) - 4.0 * v
-
-    west_side, east_side = pltpu.roll(side, 1, 1), pltpu.roll(side, COLS - 1, 1)
-    out = []
-    for m in range(MEMBERS):
-        at = 2 * REACH * m + REACH
-        v = own[m]
-        west = jnp.where(lane == 0, pltpu.roll(side, COLS - at + 1, 1), pltpu.roll(v, 1, 1))
-        east = jnp.where(lane == COLS - 1, pltpu.roll(side, COLS - at - 1, 1), pltpu.roll(v, COLS - 1, 1))
-        out.append(total(v, west, east))
-        west_side = jnp.where(lane == at, pltpu.roll(v, at + 1, 1), west_side)
-        east_side = jnp.where(lane == at - 1, pltpu.roll(v, at - 1, 1), east_side)
-    return out, total(side, west_side, east_side)
-
-
-def forward_pass(state, rate):
-    (own, side), (rate_own, rate_side) = state, rate
-    a, b = lap(own, side)
-    return [v + rate_own * x for v, x in zip(own, a)], side + rate_side * b
-
-
-def adjoint_pass(state, rate):
-    (own, side), (rate_own, rate_side) = state, rate
-    a, b = lap([rate_own * v for v in own], rate_side * side)
-    return [v + x for v, x in zip(own, a)], side + b
-
-
-def sweep(step, own, side, rate):
-    cut = ROWS // 2
-    state = (own, side)
-    for _ in range(2):
-        state = step(state, rate)
-    own, side = [v[cut:-cut] for v in state[0]], state[1][cut:-cut]
-    rate = tuple(v[cut:-cut] for v in rate)
-    own, side = lax.fori_loop(0, PASSES - 2, lambda _, s: step(s, rate), (own, side))
-    return [v[ROWS - cut : -(ROWS - cut)] for v in own]
+def spread_halo(halo, f):
+    return pltpu.roll(halo, (2 * COLS - REACH - 2 * REACH * f) % COLS, 1)
+
+
+def sweep(adjoint, ext, side, rate):
+    lane = lax.broadcasted_iota(jnp.int32, (SUB, COLS), 1)
+    first, last = lane == 0, lane == COLS - 1
+    low = ROWS - REACH
+
+    def tile(row):
+        return pl.ds(SUB * row, SUB)
+
+    own = [ext[tile(low + r)] for r in range(ROWS + 2 * REACH)]
+    halo = [side[tile(low + r)] for r in range(ROWS + 2 * REACH)]
+    for _ in range(PASSES):
+        count = len(own)
+        rate_own = [rate[0, tile(low + r)] for r in range(count)]
+        rate_halo = [rate[1, tile(low + r)] for r in range(count)]
+        if adjoint:
+            a = [v * d for v, d in zip(own, rate_own)]
+            b = [v * d for v, d in zip(halo, rate_halo)]
+        else:
+            a, b = own, halo
+        new_own, new_halo = [], []
+        for r in range(1, count - 1):
+            a_west, b_west = pltpu.roll(a[r], 1, 1), pltpu.roll(b[r], 1, 1)
+            a_east, b_east = pltpu.roll(a[r], COLS - 1, 1), pltpu.roll(b[r], COLS - 1, 1)
+            beside_a = jnp.where(first, b_west, a_west) + jnp.where(last, b_east, a_east)
+            beside_b = jnp.where(first, a_west, b_west) + jnp.where(last, a_east, b_east)
+            lap_a = (a[r - 1] + a[r + 1]) + beside_a - 4.0 * a[r]
+            lap_b = (b[r - 1] + b[r + 1]) + beside_b - 4.0 * b[r]
+            if not adjoint:
+                lap_a, lap_b = rate_own[r] * lap_a, rate_halo[r] * lap_b
+            new_own.append(own[r] + lap_a)
+            new_halo.append(halo[r] + lap_b)
+        own, halo = new_own, new_halo
+        low += 1
+    return own
+
+
+def members_of(tiles, room):
+    for r, tile in enumerate(tiles):
+        room[pl.ds(SUB * r, SUB)] = tile
+    return [room[pl.ds(m, ROWS, stride=SUB)] for m in range(MEMBERS)]
 
 
 def partner_of(mem, partner):
@@ -243,24 +258,23 @@
     share_sums((0, SHARE), kept.at[0], w, F32, own)
 
 
-def forward_body(chunk, ids, ext, even, odd, loc_norm, sent1, sent2, w, rate, terms, *sends):
+def forward_body(chunk, ids, ext, rate_own, own, even, odd, loc_norm, sent1, sent2, w, rate, terms, *rest):
+    sends, side, room = rest[:-2], rest[-2], rest[-1]
     halo = halo_of(MEMBERS + 1, ids, even, odd)
-    lane = lax.broadcasted_iota(jnp.int32, (3 * ROWS, COLS), 1)
-    side = jnp.where(lane < 2 * REACH * MEMBERS, halo, 0.0)
-    rate_side = jnp.zeros((3 * ROWS, COLS), F32)
+    lane = lax.broadcasted_iota(jnp.int32, (TALL, COLS), 1)
+    near = (lane < REACH) | (lane >= COLS - REACH)
+    rate_side = jnp.where(near, spread_halo(halo, MEMBERS), 0.0)
+    rate[0] = rate_own[...]
+    for sub in range(SUB):
+        put(rate.at[1], sub, rate_side)
     for m in range(MEMBERS):
-        turned = pltpu.roll(halo, (COLS - 2 * REACH * (MEMBERS - m)) % COLS, 1)
-        rate_side = jnp.where(group(lane, m), turned, rate_side)
-    rate[0] = ext[MEMBERS]
-    rate[1] = rate_side
+        put(side, m, spread_halo(halo, m))
     squares = jnp.zeros((ROWS, COLS), F32)
     for m in range(MEMBERS):
-        mine = ext[m, ROWS : 2 * ROWS]
-        squares = squares + mine * mine
+        squares = squares + own[m] * own[m]
     terms[...] = squares[:8] + squares[8:]
-    spread = sweep(forward_pass, [ext[m] for m in range(MEMBERS)], side, (ext[MEMBERS], rate_side))
-    for m in range(MEMBERS):
-        w[m] = (loc_norm[...] * spread[m]).astype(BF16).astype(F32)
+    for m, spread in enumerate(members_of(sweep(False, ext, side, rate), room)):
+        w[m] = (loc_norm[...] * spread).astype(BF16).astype(F32)
     sends_body(chunk, ids, sent1, sent2, w, *sends)
 
 
@@ -273,7 +287,7 @@
     return plane[:8] + plane[8:]
 
 
-def misfit_body(chunk, factor, ids, own, got1, got2, got3, inn, prec, terms, weighted, new_terms):
+def misfit_body(chunk, factor, ids, own, got1, got2, got3, inn, prec, terms, weighted, *new_terms):
     first, count = chunk
 
     def plane(r, c):
@@ -285,8 +299,9 @@
 
     total = lax.fori_loop(0, count, plane, jnp.zeros((ROWS, COLS), F32), unroll=5 if count % 5 == 0 else 1)
     summed = terms[...] + (total[:8] + total[8:])
-    new_terms[...] = summed
-    if rides(chunk):
+    if not rides(chunk):
+        new_terms[0][...] = summed
+    else:
         high = summed.astype(BF16).astype(F32)
         weighted[count] = jnp.concatenate([high, summed - high], axis=0).astype(BF16)
 
@@ -344,23 +359,24 @@
     new[MEMBERS, 8:] = jnp.zeros((ROWS - 8, COLS), F32)
 
 
-def pass_body(ids, odd, passed):
-    passed[...] = odd[3 * ROWS :]
-
-
-def cost_body(ids, terms, even, passed, got, summed):
-    summed[...] = (terms[...] + even[3 * ROWS :]) + (passed[...] + got[...])
-
-
-def last_cost_body(scale, ids, summed, got, cost):
-    cost[...] = jnp.broadcast_to(jnp.sum(summed[...] + got[...]) * scale, (1, COLS))
-
-
-def adjoint_body(ids, ext, even, odd, rate, control, out):
-    side = halo_of(MEMBERS, ids, even, odd)
-    back = sweep(adjoint_pass, [ext[m] for m in range(MEMBERS)], side, (rate[0], rate[1]))
+def pass_body(ids, terms, even, odd, pair, passed):
+    pair[:8] = terms[...] + even[TALL:]
+    pair[8:] = odd[TALL:]
+    passed[...] = odd[TALL:]
+
+
+def cost_body(scale, ids, pair, got, far_pair, far_got, cost):
+    mine = pair[:8] + (pair[8:] + got[...])
+    far = far_pair[:8] + (far_pair[8:] + far_got[...])
+    cost[...] = jnp.broadcast_to(jnp.sum(mine + far) * scale, (1, COLS))
+
+
+def adjoint_body(ids, ext, even, odd, rate, control, out, side, room):
+    halo = halo_of(MEMBERS, ids, even, odd)
     for m in range(MEMBERS):
-        out[m] = control[m] + back[m]
+        put(side, m, spread_halo(halo, m))
+    for m, back in enumerate(members_of(sweep(True, ext, side, rate), room)):
+        out[m] = control[m] + back
 
 
 def on_device(control, anomalies, diffusivity, loc_norm, innovation, obs_precision, obs_time):
@@ -377,7 +393,7 @@
     even, odd = swap(fields, "lat", False), swap(fields, "lat", True)
     (sent1,) = select(PARTNERS[:2], anomalies, obs_time)
     even, odd, sent1 = lax.optimization_barrier((even, odd, sent1))
-    ext, packed = pack(MEMBERS + 1, True, fields, even, odd)
+    ext, rate, packed = pack(MEMBERS + 1, fields, even, odd)
     even, odd = swap(packed, "lon", False), swap(packed, "lon", True)
     (sent2,) = select(PARTNERS[2:], anomalies, obs_time)
     even, odd, sent2 = lax.optimization_barrier((even, odd, sent2))
@@ -388,9 +404,10 @@
     tile = pltpu.VMEM((8, COLS), F32)
     w, rate, terms, *send = call(
         functools.partial(forward_body, CHUNKS[0]),
-        [pltpu.VMEM(block, F32), pltpu.VMEM((2, 3 * ROWS, COLS), F32), tile, *blocks(CHUNKS[0][1])],
-        (ext, even, odd, loc_norm, sent1, sent2),
-        [VMEM_SPEC] * 6,
+        [pltpu.VMEM(block, F32), pltpu.VMEM((2, *TILES), F32), tile, *blocks(CHUNKS[0][1])],
+        (ext, rate, fields, even, odd, loc_norm, sent1, sent2),
+        [VMEM_SPEC] * 8,
+        scratch=[pltpu.VMEM(TILES, F32), pltpu.VMEM((ROWS * SUB, COLS), F32)],
         us=2.0,
     )
     got = []
@@ -404,13 +421,14 @@
     (own,) = call(stays_body, [pltpu.VMEM((SHARE, ROWS, COLS), F32)], (kept, w), [VMEM_SPEC] * 2, us=0.3)
     weighted, near = [], []
     for i, chunk in enumerate(CHUNKS):
-        piece, terms = call(
+        piece, *rest = call(
             functools.partial(misfit_body, chunk, factor),
-            [pltpu.VMEM((chunk[1] + rides(chunk), ROWS, COLS), BF16), tile],
+            [pltpu.VMEM((chunk[1] + rides(chunk), ROWS, COLS), BF16)] + [tile] * (1 - rides(chunk)),
             (own, *got[i], inn, prec, terms),
             [VMEM_SPEC] * 7,
             us=0.3,
         )
+        terms = rest[0] if rest else None
         weighted.append(piece)
         if i == len(CHUNKS) - 1:
             near.append([share(piece, p) for p in PARTNERS])
@@ -441,26 +459,36 @@
     )
     even, odd = swap(source, "lat", False), swap(source, "lat", True)
     got = trade(terms, ("lat",), (2, 3, 0, 1, 6, 7, 4, 5))
-    even, odd, got = lax.optimization_barrier((even, odd, got))
-    ext, packed, terms = pack(MEMBERS, False, source, even, odd, (terms, got))
+    ext, packed, terms = pack(MEMBERS, source, even, odd, (terms,))
+    packed, terms = call(
+        ride_body,
+        [pltpu.VMEM((TALL + 8, COLS), F32), tile],
+        (packed, terms, got),
+        [VMEM_SPEC] * 3,
+        us=0.1,
+        aliases={0: 0},
+    )
     even, odd = swap(packed, "lon", False), swap(packed, "lon", True)
-    (passed,) = call(pass_body, [tile], (odd,), [VMEM_SPEC], us=0.1)
+    pair, passed = call(
+        pass_body, [pltpu.VMEM((16, COLS), F32), tile], (terms, even, odd), [VMEM_SPEC] * 3, us=0.1
+    )
     got = swap(passed, "lon", False)
-    (terms,) = call(cost_body, [tile], (terms, even, passed, got), [VMEM_SPEC] * 4, us=0.1)
-    got = trade(terms, ("lat",), (4, 5, 6, 7, 0, 1, 2, 3))
-    even, odd, terms = lax.optimization_barrier((even, odd, terms))
+    far_pair = trade(pair, ("lat",), (4, 5, 6, 7, 0, 1, 2, 3))
+    far_got = trade(passed, ("lat", "lon"), [(lat ^ 4) * 4 + (lon ^ 1) for lat in range(8) for lon in range(4)])
+    even, odd, pair = lax.optimization_barrier((even, odd, pair))
     (gradient,) = call(
         adjoint_body,
         [jax.ShapeDtypeStruct(block, F32)],
         (ext, even, odd, rate, control),
         [VMEM_SPEC] * 5,
+        scratch=[pltpu.VMEM(TILES, F32), pltpu.VMEM((ROWS * SUB, COLS), F32)],
         us=3.0,
     )
     (cost,) = call(
-        functools.partial(last_cost_body, 0.5 / cells),
+        functools.partial(cost_body, 0.5 / cells),
         [jax.ShapeDtypeStruct((1, COLS), F32)],
-        (terms, got),
-        [VMEM_SPEC] * 2,
+        (pair, got, far_pair, far_got),
+        [VMEM_SPEC] * 4,
         us=0.1,
     )
     return gradient, cost[0, 0]

time: 68.5 us -> 67.1 us (0.980)
  Pallas kernels: 16.8 us -> 14.4 us
  starting transfers between devices: 36.6 us -> 38.1 us
    pallas_call x17, Pallas kernels: 16.8 us -> 14.4 us  [call(): pl.pallas_call(placed, out_shape=outs, in_specs=specs, out_specs=[VMEM_SP...]
    ppermute x15 -> x16, starting transfers between devices: 18.2 us -> 20.1 us  [trade(): return lax.ppermute(cells, axes, list(enumerate(to)))]
    ppermute x15 -> x16, waiting for transfers between devices: 10.5 us -> 9.15 us  [trade(): return lax.ppermute(cells, axes, list(enumerate(to)))]
    ppermute x9, waiting for transfers between devices: 2.73 us -> 3.58 us  [swap(): return lax.ppermute(cells, axis, pairs)]
  transfers between devices with their start and end apart: 24 -> 25, of which waited for: 6 -> 7; matrix products, arithmetic and copies ran while one was open for 0% -> 0% of each run, Pallas kernels for 19% -> 17%
where the time goes in v4:
time: 67.1 us; the launch traced here: 66.9 us
  starting transfers between devices  38.1 us (57%)
  Pallas kernels  14.4 us (21%)
  waiting for transfers between devices  12.7 us (19%)
  between operations  0.84 us (1%)
  other arithmetic  0.8 us (1%)
    ppermute x16, starting transfers between devices, trade(): return lax.ppermute(cells, axes, list(enumerate(to)))  20.1 us
    ppermute x9, starting transfers between devices, swap(): return lax.ppermute(cells, axis, pairs)  18 us
    pallas_call x17, Pallas kernels, call(): pl.pallas_call(placed, out_shape=outs, in_specs=specs, out_specs=[VMEM_SP...  14.4 us
    ppermute x16, waiting for transfers between devices, trade(): return lax.ppermute(cells, axes, list(enumerate(to)))  9.15 us
    ppermute x9, waiting for transfers between devices, swap(): return lax.ppermute(cells, axis, pairs)  3.58 us
  transfers between devices with their start and end apart: 25, of which 7 were waited for; matrix products, arithmetic and copies ran while one was open for 0% of the time, Pallas kernels for 17%

profile of v4, /device:TPU:1, one launch (start us, length us, event | category | flops | bytes accessed | tf_op | source)
XLA Modules:
  0.0 66.9 jit_solution(2365833905780000244)
XLA Ops:
  0.6 0.8 %pad_maximum_fusion.refs_0_.refs_2_ = f32[6,16,128]{2,1,0:T(8,128)S(1)} fusion(f32[1,16,128]{2,1,0:T(8,128)} %bitcast.11, f32[5,16,128]{2,1,0:T(8,128)} %refs_4_.1), kind=kLoop, calls=%fused_computation | loop fusion | flops 12288 | bytes 98304 | tf_op jit(solution)/shard_map/concatenate | solution.py:392
  1.4 2.0 %collective-permute-start = (f32[6,16,128]{2,1,0:T(8,128)S(1)}, f32[6,16,128]{2,1,0:T(8,128)S(1)}, u32[]{:S(2)}, u32[]{:S(2)}) collective-permute-start(f32[6,16,128]{2,1,0:T(8,128)S(1)} %pad_maximum_fusion.refs_0_.refs_2_), channel_id=1, source_target_pairs={{0,4},{4,0},{8,12},{12,8},{16,20},{20,16},{24,28},{28,24},{1,5},{5... | collective-permute-start | bytes 147464 | tf_op jit(solution)/shard_map/ppermute | solution.py:55
  3.5 3.2 %collective-permute-start.1 = (f32[6,16,128]{2,1,0:T(8,128)S(1)}, f32[6,16,128]{2,1,0:T(8,128)S(1)}, u32[]{:S(2)}, u32[]{:S(2)}) collective-permute-start(f32[6,16,128]{2,1,0:T(8,128)S(1)} %pad_maximum_fusion.refs_0_.refs_2_), channel_id=1, source_target_pairs={{0,28},{4,8},{8,4},{12,16},{16,12},{20,24},{24,20},{28,0},{1,29},{... | collective-permute-start | bytes 147464 | tf_op jit(solution)/shard_map/ppermute | solution.py:55
  6.6 3.1 %shard_map.86.refs_6_.refs_0_ = bf16[2,5,70,16,128]{4,3,2,1,0:T(8,128)(2,1)S(1)} custom-call(bf16[5,2,280,16,128]{4,3,2,1,0:T(8,128)(2,1)} %bitcast.6, s32[16,128]{1,0:T(8,128)} %refs_1_.5), custom_call_target="tpu_custom_call" | custom-call | flops 2500000 | bytes 7500000 | tf_op jit(solution)/shard_map/pallas_call | solution.py:31
  9.9 1.3 %collective-permute-start.2 = (f32[48,128]{1,0:T(8,128)S(1)}, f32[48,128]{1,0:T(8,128)S(1)}, u32[]{:S(2)}, u32[]{:S(2)}) collective-permute-start(f32[48,128]{1,0:T(8,128)S(1)} %get-tuple-element.40), channel_id=1, source_target_pairs={{0,1},{1,0},{2,3},{3,2},{4,5},{5,4},{6,7},{7,6},{8,9},{9,8},{10,11... | collective-permute-start | bytes 73736 | tf_op jit(solution)/shard_map/ppermute | solution.py:55
  11.3 3.3 %collective-permute-start.3 = (f32[48,128]{1,0:T(8,128)S(1)}, f32[48,128]{1,0:T(8,128)S(1)}, u32[]{:S(2)}, u32[]{:S(2)}) collective-permute-start(f32[48,128]{1,0:T(8,128)S(1)} %get-tuple-element.40), channel_id=1, source_target_pairs={{0,3},{1,2},{2,1},{3,0},{4,7},{5,6},{6,5},{7,4},{8,11},{9,10},{10,... | collective-permute-start | bytes 73736 | tf_op jit(solution)/shard_map/ppermute | solution.py:55
  14.5 1.9 %shard_map.88.refs_7_.refs_1_ = bf16[1,5,70,16,128]{4,3,2,1,0:T(8,128)(2,1)S(1)} custom-call(bf16[5,2,280,16,128]{4,3,2,1,0:T(8,128)(2,1)} %bitcast.7, s32[16,128]{1,0:T(8,128)} %refs_1_.5), custom_call_target="tpu_custom_call" | custom-call | flops 2500000 | bytes 7500000 | tf_op jit(solution)/shard_map/pallas_call | solution.py:31
  16.5 1.8 %shard_map.90 = (f32[5,16,128]{2,1,0:T(8,128)S(1)}, f32[2,384,128]{2,1,0:T(8,128)S(1)}, f32[8,128]{1,0:T(8,128)S(1)}, bf16[35,16,128]{2,1,0:T(8,128)(2,1)S(1)}, ...) custom-call(f32[384,128]{1,0:T(8,128)S(1)} %get-tuple-element.43.refs_0_, ...), custom_call_target="tpu_custom_call" | custom-call | flops 2000000 | bytes 6000000 | tf_op jit(solution)/shard_map/pallas_call | solution.py:31
  18.3 3.0 %collective-permute-start.4 = (bf16[35,16,128]{2,1,0:T(8,128)(2,1)S(1)}, bf16[35,16,128]{2,1,0:T(8,128)(2,1)S(1)}, u32[]{:S(2)}, u32[]{:S(2)}) collective-permute-start(bf16[35,16,128]{2,1,0:T(8,128)(2,1)S(1)} %get-tuple-element.48), channel_id=1, source_target_pairs={{0,64},{32,96},{64,0},{96,32},{1,65},{33,97},{65,1},{97,33},{2,66}... | collective-permute-start | bytes 430088 | tf_op jit(solution)/shard_map/ppermute | solution.py:59
  22.0 0.5 shard_map.93
  22.6 2.5 %collective-permute-start.7 = (bf16[35,16,128]{2,1,0:T(8,128)(2,1)S(1)}, bf16[35,16,128]{2,1,0:T(8,128)(2,1)S(1)}, u32[]{:S(2)}, u32[]{:S(2)}) collective-permute-start(bf16[35,16,128]{2,1,0:T(8,128)(2,1)S(1)} %get-tuple-element.55), channel_id=1, source_target_pairs={{0,64},{32,96},{64,0},{96,32},{1,65},{33,97},{65,1},{97,33},{2,66}... | collective-permute-start | bytes 430088 | tf_op jit(solution)/shard_map/ppermute | solution.py:59
  25.5 2.0 %collective-permute-start.9 = (bf16[35,16,128]{2,1,0:T(8,128)(2,1)S(1)}, bf16[35,16,128]{2,1,0:T(8,128)(2,1)S(1)}, u32[]{:S(2)}, u32[]{:S(2)}) collective-permute-start(bf16[35,16,128]{2,1,0:T(8,128)(2,1)S(1)} %get-tuple-element.57), channel_id=1, source_target_pairs={{0,96},{32,64},{64,32},{96,0},{1,97},{33,65},{65,33},{97,1},{2,98}... | collective-permute-start | bytes 430088 | tf_op jit(solution)/shard_map/ppermute | solution.py:59
  27.5 2.2 %shard_map.89 = (bf16[1,5,70,16,128]{4,3,2,1,0:T(8,128)(2,1)S(1)}, f32[70,16,128]{2,1,0:T(8,128)S(1)}, f32[70,16,128]{2,1,0:T(8,128)S(1)}) custom-call(bf16[5,2,280,16,128]{4,3,2,1,0:T(8,128)(2,1)} %bitcast.8, s32[16,128]{1,0:T(8,128)} %refs_1_.5, f32[280,16,128]{2,1,0:T(8,128)} %bitcast.9, f32[280,16,128]{2,1,0:T(8,128)} %bitcast.10), custom_call_target="tpu_custom_call" | custom-call | flops 2500000 | bytes 7500000 | tf_op jit(solution)/shard_map/pallas_call | solution.py:31
  30.2 2.1 %collective-permute-start.10 = (bf16[35,16,128]{2,1,0:T(8,128)(2,1)S(1)}, bf16[35,16,128]{2,1,0:T(8,128)(2,1)S(1)}, u32[]{:S(2)}, u32[]{:S(2)}) collective-permute-start(bf16[35,16,128]{2,1,0:T(8,128)(2,1)S(1)} %get-tuple-element.54.refs_1_), channel_id=1, source_target_pairs={{0,96},{32,64},{64,32},{96,0},{1,97},{33,65},{65,33},{97,1},{2,98}... | collective-permute-start | bytes 430088 | tf_op jit(solution)/shard_map/ppermute | solution.py:59
  32.3 2.0 %collective-permute-done.8.refs_2_ = bf16[35,16,128]{2,1,0:T(8,128)(2,1)S(1)} collective-permute-done((bf16[35,16,128]{2,1,0:T(8,128)(2,1)S(1)}, bf16[35,16,128]{2,1,0:T(8,128)(2,1)S(1)}, u32[]{:S(2)}, u32[]{:S(2)}) %collective-permute-start.8) | collective-permute-done | bytes 143392 | tf_op jit(solution)/shard_map/ppermute | solution.py:59
  35.0 2.8 %collective-permute-start.14 = (bf16[36,16,128]{2,1,0:T(8,128)(2,1)S(1)}, bf16[36,16,128]{2,1,0:T(8,128)(2,1)S(1)}, u32[]{:S(2)}, u32[]{:S(2)}) collective-permute-start(bf16[36,16,128]{2,1,0:T(8,128)(2,1)S(1)} %shard_map.94.refs_2_.refs_7_), channel_id=1, source_target_pairs={{0,64},{32,96},{64,0},{96,32},{1,65},{33,97},{65,1},{97,33},{2,66}... | collective-permute-start | bytes 442376 | tf_op jit(solution)/shard_map/ppermute | solution.py:59
  38.4 1.0 %collective-permute-start.11 = (bf16[20,16,128]{2,1,0:T(8,128)(2,1)S(1)}, bf16[20,16,128]{2,1,0:T(8,128)(2,1)S(1)}, u32[]{:S(2)}, u32[]{:S(2)}) collective-permute-start(bf16[20,16,128]{2,1,0:T(8,128)(2,1)S(1)} %slice.12), channel_id=1, source_target_pairs={{0,32},{32,0},{64,96},{96,64},{1,33},{33,1},{65,97},{97,65},{2,34}... | collective-permute-start | bytes 245768 | tf_op jit(solution)/shard_map/ppermute | solution.py:59
  39.4 2.1 %collective-permute-start.13 = (bf16[15,16,128]{2,1,0:T(8,128)(2,1)S(1)}, bf16[15,16,128]{2,1,0:T(8,128)(2,1)S(1)}, u32[]{:S(2)}, u32[]{:S(2)}) collective-permute-start(bf16[15,16,128]{2,1,0:T(8,128)(2,1)S(1)} %slice.13), channel_id=1, source_target_pairs={{0,96},{32,64},{64,32},{96,0},{1,97},{33,65},{65,33},{97,1},{2,98}... | collective-permute-start | bytes 184328 | tf_op jit(solution)/shard_map/ppermute | solution.py:59
  41.9 5.4 %collective-permute-done.13.refs_4_ = bf16[15,16,128]{2,1,0:T(8,128)(2,1)S(1)} collective-permute-done((bf16[15,16,128]{2,1,0:T(8,128)(2,1)S(1)}, bf16[15,16,128]{2,1,0:T(8,128)(2,1)S(1)}, u32[]{:S(2)}, u32[]{:S(2)}) %collective-permute-start.13) | collective-permute-done | bytes 61472 | tf_op jit(solution)/shard_map/ppermute | solution.py:59
  47.3 0.5 shard_map.96.refs_2_
  47.9 0.6 shard_map.97
  48.5 2.1 %collective-permute-start.18 = (f32[6,16,128]{2,1,0:T(8,128)S(1)}, f32[6,16,128]{2,1,0:T(8,128)S(1)}, u32[]{:S(2)}, u32[]{:S(2)}) collective-permute-start(f32[6,16,128]{2,1,0:T(8,128)S(1)} %get-tuple-element.59.refs_0_), channel_id=1, source_target_pairs={{0,28},{4,8},{8,4},{12,16},{16,12},{20,24},{24,20},{28,0},{1,29},{... | collective-permute-start | bytes 147464 | tf_op jit(solution)/shard_map/ppermute | solution.py:55
  50.7 1.1 %collective-permute-start.19 = (f32[8,128]{1,0:T(8,128)S(1)}, f32[8,128]{1,0:T(8,128)S(1)}, u32[]{:S(2)}, u32[]{:S(2)}) collective-permute-start(f32[8,128]{1,0:T(8,128)S(1)} %get-tuple-element.60.refs_3_), channel_id=1, source_target_pairs={{0,8},{4,12},{8,0},{12,4},{16,24},{20,28},{24,16},{28,20},{1,9},{5... | collective-permute-start | bytes 12296 | tf_op jit(solution)/shard_map/ppermute | solution.py:59
  51.8 1.9 %collective-permute-done.18.refs_2_ = f32[6,16,128]{2,1,0:T(8,128)S(1)} collective-permute-done((f32[6,16,128]{2,1,0:T(8,128)S(1)}, f32[6,16,128]{2,1,0:T(8,128)S(1)}, u32[]{:S(2)}, u32[]{:S(2)}) %collective-permute-start.18) | collective-permute-done | bytes 49184 | tf_op jit(solution)/shard_map/ppermute | solution.py:55
  53.8 0.9 %collective-permute-done.19.refs_2_ = f32[8,128]{1,0:T(8,128)S(1)} collective-permute-done((f32[8,128]{1,0:T(8,128)S(1)}, f32[8,128]{1,0:T(8,128)S(1)}, u32[]{:S(2)}, u32[]{:S(2)}) %collective-permute-start.19) | collective-permute-done | bytes 4128 | tf_op jit(solution)/shard_map/ppermute | solution.py:59
  54.7 2.6 %collective-permute-start.20 = (f32[56,128]{1,0:T(8,128)S(1)}, f32[56,128]{1,0:T(8,128)S(1)}, u32[]{:S(2)}, u32[]{:S(2)}) collective-permute-start(f32[56,128]{1,0:T(8,128)S(1)} %get-tuple-element.64), channel_id=1, source_target_pairs={{0,1},{1,0},{2,3},{3,2},{4,5},{5,4},{6,7},{7,6},{8,9},{9,8},{10,11... | collective-permute-start | bytes 86024 | tf_op jit(solution)/shard_map/ppermute | solution.py:55
  57.2 3.1 %collective-permute-start.21 = (f32[56,128]{1,0:T(8,128)S(1)}, f32[56,128]{1,0:T(8,128)S(1)}, u32[]{:S(2)}, u32[]{:S(2)}) collective-permute-start(f32[56,128]{1,0:T(8,128)S(1)} %get-tuple-element.64), channel_id=1, source_target_pairs={{0,3},{1,2},{2,1},{3,0},{4,7},{5,6},{6,5},{7,4},{8,11},{9,10},{10,... | collective-permute-start | bytes 86024 | tf_op jit(solution)/shard_map/ppermute | solution.py:55
  60.4 1.7 %collective-permute-done.21.refs_2_ = f32[56,128]{1,0:T(8,128)S(1)} collective-permute-done((f32[56,128]{1,0:T(8,128)S(1)}, f32[56,128]{1,0:T(8,128)S(1)}, u32[]{:S(2)}, u32[]{:S(2)}) %collective-permute-start.21) | collective-permute-done | bytes 28704 | tf_op jit(solution)/shard_map/ppermute | solution.py:55
  62.0 0.9 %collective-permute-start.23 = (f32[16,128]{1,0:T(8,128)S(1)}, f32[16,128]{1,0:T(8,128)S(1)}, u32[]{:S(2)}, u32[]{:S(2)}) collective-permute-start(f32[16,128]{1,0:T(8,128)S(1)} %get-tuple-element.70.refs_0_), channel_id=1, source_target_pairs={{0,16},{4,20},{8,24},{12,28},{16,0},{20,4},{24,8},{28,12},{1,17},{... | collective-permute-start | bytes 24584 | tf_op jit(solution)/shard_map/ppermute | solution.py:59
  63.3 0.8 %collective-permute-start.24 = (f32[8,128]{1,0:T(8,128)S(1)}, f32[8,128]{1,0:T(8,128)S(1)}, u32[]{:S(2)}, u32[]{:S(2)}) collective-permute-start(f32[8,128]{1,0:T(8,128)S(1)} %get-tuple-element.71), channel_id=1, source_target_pairs={{0,17},{1,16},{2,19},{3,18},{4,21},{5,20},{6,23},{7,22},{8,25},{9,... | collective-permute-start | bytes 12296 | tf_op jit(solution)/shard_map/ppermute | solution.py:59
  64.1 1.9 %shard_map.101 = f32[5,16,128]{2,1,0:T(8,128)} custom-call(f32[384,128]{1,0:T(8,128)S(1)} %get-tuple-element.61.refs_0_, f32[56,128]{1,0:T(8,128)S(1)} %collective-permute-done.20.refs_1_, f32[56,128]{1,0:T(8,128)S(1)} %collective-permute-done.21.refs_2_, f32[2,384,128]{2,1,0:T(8,128)S(1)} %get-tuple-element.69.refs_3_, f32[5,16,128]{2,1,0:T(8,128)S(1)} %copy-done), custom_call_target="tpu_custom_call" | custom-call | flops 3000000 | bytes 9000000 | tf_op jit(solution)/shard_map/pallas_call | solution.py:31
  66.3 0.6 shard_map.102
  (42 shorter events, 4.3 us)
Async XLA Ops:
  1.4 8.4 %collective-permute-start = (f32[6,16,128]{2,1,0:T(8,128)S(1)}, f32[6,16,128]{2,1,0:T(8,128)S(1)}, u32[]{:S(2)}, u32[]{:S(2)}) collective-permute-start(f32[6,16,128]{2,1,0:T(8,128)S(1)} %pad_maximum_fusion.refs_0_.refs_2_), channel_id=1, source_target_pairs={{0,4},{4,0},{8,12},{12,8},{16,20},{20,16},{24,28},{28,24},{1,5},{5... | collective-permute-start | bytes 147464 | tf_op jit(solution)/shard_map/ppermute | solution.py:55
  3.5 6.3 %collective-permute-start.1 = (f32[6,16,128]{2,1,0:T(8,128)S(1)}, f32[6,16,128]{2,1,0:T(8,128)S(1)}, u32[]{:S(2)}, u32[]{:S(2)}) collective-permute-start(f32[6,16,128]{2,1,0:T(8,128)S(1)} %pad_maximum_fusion.refs_0_.refs_2_), channel_id=1, source_target_pairs={{0,28},{4,8},{8,4},{12,16},{16,12},{20,24},{24,20},{28,0},{1,29},{... | collective-permute-start | bytes 147464 | tf_op jit(solution)/shard_map/ppermute | solution.py:55
  9.9 6.5 %copy-start.1 = (f32[16,128]{1,0:T(8,128)S(1)}, f32[16,128]{1,0:T(8,128)}, u32[]{:S(2)}) copy-start(f32[16,128]{1,0:T(8,128)} %refs_6_.1) | copy-start | bytes 24580
  9.9 6.5 %collective-permute-start.2 = (f32[48,128]{1,0:T(8,128)S(1)}, f32[48,128]{1,0:T(8,128)S(1)}, u32[]{:S(2)}, u32[]{:S(2)}) collective-permute-start(f32[48,128]{1,0:T(8,128)S(1)} %get-tuple-element.40), channel_id=1, source_target_pairs={{0,1},{1,0},{2,3},{3,2},{4,5},{5,4},{6,7},{7,6},{8,9},{9,8},{10,11... | collective-permute-start | bytes 73736 | tf_op jit(solution)/shard_map/ppermute | solution.py:55
  11.3 5.2 %collective-permute-start.3 = (f32[48,128]{1,0:T(8,128)S(1)}, f32[48,128]{1,0:T(8,128)S(1)}, u32[]{:S(2)}, u32[]{:S(2)}) collective-permute-start(f32[48,128]{1,0:T(8,128)S(1)} %get-tuple-element.40), channel_id=1, source_target_pairs={{0,3},{1,2},{2,1},{3,0},{4,7},{5,6},{6,5},{7,4},{8,11},{9,10},{10,... | collective-permute-start | bytes 73736 | tf_op jit(solution)/shard_map/ppermute | solution.py:55
  18.3 7.2 %collective-permute-start.4 = (bf16[35,16,128]{2,1,0:T(8,128)(2,1)S(1)}, bf16[35,16,128]{2,1,0:T(8,128)(2,1)S(1)}, u32[]{:S(2)}, u32[]{:S(2)}) collective-permute-start(bf16[35,16,128]{2,1,0:T(8,128)(2,1)S(1)} %get-tuple-element.48), channel_id=1, source_target_pairs={{0,64},{32,96},{64,0},{96,32},{1,65},{33,97},{65,1},{97,33},{2,66}... | collective-permute-start | bytes 430088 | tf_op jit(solution)/shard_map/ppermute | solution.py:59
  21.2 8.8 %collective-permute-start.5 = (bf16[35,16,128]{2,1,0:T(8,128)(2,1)S(1)}, bf16[35,16,128]{2,1,0:T(8,128)(2,1)S(1)}, u32[]{:S(2)}, u32[]{:S(2)}) collective-permute-start(bf16[35,16,128]{2,1,0:T(8,128)(2,1)S(1)} %get-tuple-element.49), channel_id=1, source_target_pairs={{0,32},{32,0},{64,96},{96,64},{1,33},{33,1},{65,97},{97,65},{2,34}... | collective-permute-start | bytes 430088 | tf_op jit(solution)/shard_map/ppermute | solution.py:59
  21.6 8.4 %collective-permute-start.6 = (bf16[35,16,128]{2,1,0:T(8,128)(2,1)S(1)}, bf16[35,16,128]{2,1,0:T(8,128)(2,1)S(1)}, u32[]{:S(2)}, u32[]{:S(2)}) collective-permute-start(bf16[35,16,128]{2,1,0:T(8,128)(2,1)S(1)} %get-tuple-element.50), channel_id=1, source_target_pairs={{0,96},{32,64},{64,32},{96,0},{1,97},{33,65},{65,33},{97,1},{2,98}... | collective-permute-start | bytes 430088 | tf_op jit(solution)/shard_map/ppermute | solution.py:59
  22.6 9.8 %collective-permute-start.7 = (bf16[35,16,128]{2,1,0:T(8,128)(2,1)S(1)}, bf16[35,16,128]{2,1,0:T(8,128)(2,1)S(1)}, u32[]{:S(2)}, u32[]{:S(2)}) collective-permute-start(bf16[35,16,128]{2,1,0:T(8,128)(2,1)S(1)} %get-tuple-element.55), channel_id=1, source_target_pairs={{0,64},{32,96},{64,0},{96,32},{1,65},{33,97},{65,1},{97,33},{2,66}... | collective-permute-start | bytes 430088 | tf_op jit(solution)/shard_map/ppermute | solution.py:59
  25.1 9.2 %collective-permute-start.8 = (bf16[35,16,128]{2,1,0:T(8,128)(2,1)S(1)}, bf16[35,16,128]{2,1,0:T(8,128)(2,1)S(1)}, u32[]{:S(2)}, u32[]{:S(2)}) collective-permute-start(bf16[35,16,128]{2,1,0:T(8,128)(2,1)S(1)} %get-tuple-element.56), channel_id=1, source_target_pairs={{0,32},{32,0},{64,96},{96,64},{1,33},{33,1},{65,97},{97,65},{2,34}... | collective-permute-start | bytes 430088 | tf_op jit(solution)/shard_map/ppermute | solution.py:59
  25.5 9.3 %collective-permute-start.9 = (bf16[35,16,128]{2,1,0:T(8,128)(2,1)S(1)}, bf16[35,16,128]{2,1,0:T(8,128)(2,1)S(1)}, u32[]{:S(2)}, u32[]{:S(2)}) collective-permute-start(bf16[35,16,128]{2,1,0:T(8,128)(2,1)S(1)} %get-tuple-element.57), channel_id=1, source_target_pairs={{0,96},{32,64},{64,32},{96,0},{1,97},{33,65},{65,33},{97,1},{2,98}... | collective-permute-start | bytes 430088 | tf_op jit(solution)/shard_map/ppermute | solution.py:59
  30.2 8.1 %collective-permute-start.10 = (bf16[35,16,128]{2,1,0:T(8,128)(2,1)S(1)}, bf16[35,16,128]{2,1,0:T(8,128)(2,1)S(1)}, u32[]{:S(2)}, u32[]{:S(2)}) collective-permute-start(bf16[35,16,128]{2,1,0:T(8,128)(2,1)S(1)} %get-tuple-element.54.refs_1_), channel_id=1, source_target_pairs={{0,96},{32,64},{64,32},{96,0},{1,97},{33,65},{65,33},{97,1},{2,98}... | collective-permute-start | bytes 430088 | tf_op jit(solution)/shard_map/ppermute | solution.py:59
  32.3 7.0 %collective-permute-start.12 = (bf16[35,16,128]{2,1,0:T(8,128)(2,1)S(1)}, bf16[35,16,128]{2,1,0:T(8,128)(2,1)S(1)}, u32[]{:S(2)}, u32[]{:S(2)}) collective-permute-start(bf16[35,16,128]{2,1,0:T(8,128)(2,1)S(1)} %get-tuple-element.54.refs_1_), channel_id=1, source_target_pairs={{0,32},{32,0},{64,96},{96,64},{1,33},{33,1},{65,97},{97,65},{2,34}... | collective-permute-start | bytes 430088 | tf_op jit(solution)/shard_map/ppermute | solution.py:59
  35.0 12.9 %collective-permute-start.14 = (bf16[36,16,128]{2,1,0:T(8,128)(2,1)S(1)}, bf16[36,16,128]{2,1,0:T(8,128)(2,1)S(1)}, u32[]{:S(2)}, u32[]{:S(2)}) collective-permute-start(bf16[36,16,128]{2,1,0:T(8,128)(2,1)S(1)} %shard_map.94.refs_2_.refs_7_), channel_id=1, source_target_pairs={{0,64},{32,96},{64,0},{96,32},{1,65},{33,97},{65,1},{97,33},{2,66}... | collective-permute-start | bytes 442376 | tf_op jit(solution)/shard_map/ppermute | solution.py:59
  37.8 10.1 %collective-permute-start.15 = (bf16[36,16,128]{2,1,0:T(8,128)(2,1)S(1)}, bf16[36,16,128]{2,1,0:T(8,128)(2,1)S(1)}, u32[]{:S(2)}, u32[]{:S(2)}) collective-permute-start(bf16[36,16,128]{2,1,0:T(8,128)(2,1)S(1)} %shard_map.94.refs_2_.refs_7_), channel_id=1, source_target_pairs={{0,32},{32,0},{64,96},{96,64},{1,33},{33,1},{65,97},{97,65},{2,34}... | collective-permute-start | bytes 442376 | tf_op jit(solution)/shard_map/ppermute | solution.py:59
  38.1 9.8 %collective-permute-start.16 = (bf16[36,16,128]{2,1,0:T(8,128)(2,1)S(1)}, bf16[36,16,128]{2,1,0:T(8,128)(2,1)S(1)}, u32[]{:S(2)}, u32[]{:S(2)}) collective-permute-start(bf16[36,16,128]{2,1,0:T(8,128)(2,1)S(1)} %shard_map.94.refs_2_.refs_7_), channel_id=1, source_target_pairs={{0,96},{32,64},{64,32},{96,0},{1,97},{33,65},{65,33},{97,1},{2,98}... | collective-permute-start | bytes 442376 | tf_op jit(solution)/shard_map/ppermute | solution.py:59
  38.4 9.0 %collective-permute-start.11 = (bf16[20,16,128]{2,1,0:T(8,128)(2,1)S(1)}, bf16[20,16,128]{2,1,0:T(8,128)(2,1)S(1)}, u32[]{:S(2)}, u32[]{:S(2)}) collective-permute-start(bf16[20,16,128]{2,1,0:T(8,128)(2,1)S(1)} %slice.12), channel_id=1, source_target_pairs={{0,32},{32,0},{64,96},{96,64},{1,33},{33,1},{65,97},{97,65},{2,34}... | collective-permute-start | bytes 245768 | tf_op jit(solution)/shard_map/ppermute | solution.py:59
  39.4 7.9 %collective-permute-start.13 = (bf16[15,16,128]{2,1,0:T(8,128)(2,1)S(1)}, bf16[15,16,128]{2,1,0:T(8,128)(2,1)S(1)}, u32[]{:S(2)}, u32[]{:S(2)}) collective-permute-start(bf16[15,16,128]{2,1,0:T(8,128)(2,1)S(1)} %slice.13), channel_id=1, source_target_pairs={{0,96},{32,64},{64,32},{96,0},{1,97},{33,65},{65,33},{97,1},{2,98}... | collective-permute-start | bytes 184328 | tf_op jit(solution)/shard_map/ppermute | solution.py:59
  47.8 16.2 %copy-start = (f32[5,16,128]{2,1,0:T(8,128)S(1)}, f32[5,16,128]{2,1,0:T(8,128)}, u32[]{:S(2)}) copy-start(f32[5,16,128]{2,1,0:T(8,128)} %refs_4_.1) | copy-start | bytes 122884
  48.4 3.3 %collective-permute-start.17 = (f32[6,16,128]{2,1,0:T(8,128)S(1)}, f32[6,16,128]{2,1,0:T(8,128)S(1)}, u32[]{:S(2)}, u32[]{:S(2)}) collective-permute-start(f32[6,16,128]{2,1,0:T(8,128)S(1)} %get-tuple-element.59.refs_0_), channel_id=1, source_target_pairs={{0,4},{4,0},{8,12},{12,8},{16,20},{20,16},{24,28},{28,24},{1,5},{5... | collective-permute-start | bytes 147464 | tf_op jit(solution)/shard_map/ppermute | solution.py:55
  48.5 5.1 %collective-permute-start.18 = (f32[6,16,128]{2,1,0:T(8,128)S(1)}, f32[6,16,128]{2,1,0:T(8,128)S(1)}, u32[]{:S(2)}, u32[]{:S(2)}) collective-permute-start(f32[6,16,128]{2,1,0:T(8,128)S(1)} %get-tuple-element.59.refs_0_), channel_id=1, source_target_pairs={{0,28},{4,8},{8,4},{12,16},{16,12},{20,24},{24,20},{28,0},{1,29},{... | collective-permute-start | bytes 147464 | tf_op jit(solution)/shard_map/ppermute | solution.py:55
  50.7 4.0 %collective-permute-start.19 = (f32[8,128]{1,0:T(8,128)S(1)}, f32[8,128]{1,0:T(8,128)S(1)}, u32[]{:S(2)}, u32[]{:S(2)}) collective-permute-start(f32[8,128]{1,0:T(8,128)S(1)} %get-tuple-element.60.refs_3_), channel_id=1, source_target_pairs={{0,8},{4,12},{8,0},{12,4},{16,24},{20,28},{24,16},{28,20},{1,9},{5... | collective-permute-start | bytes 12296 | tf_op jit(solution)/shard_map/ppermute | solution.py:59
  54.7 5.7 %collective-permute-start.20 = (f32[56,128]{1,0:T(8,128)S(1)}, f32[56,128]{1,0:T(8,128)S(1)}, u32[]{:S(2)}, u32[]{:S(2)}) collective-permute-start(f32[56,128]{1,0:T(8,128)S(1)} %get-tuple-element.64), channel_id=1, source_target_pairs={{0,1},{1,0},{2,3},{3,2},{4,5},{5,4},{6,7},{7,6},{8,9},{9,8},{10,11... | collective-permute-start | bytes 86024 | tf_op jit(solution)/shard_map/ppermute | solution.py:55
  57.2 4.8 %collective-permute-start.21 = (f32[56,128]{1,0:T(8,128)S(1)}, f32[56,128]{1,0:T(8,128)S(1)}, u32[]{:S(2)}, u32[]{:S(2)}) collective-permute-start(f32[56,128]{1,0:T(8,128)S(1)} %get-tuple-element.64), channel_id=1, source_target_pairs={{0,3},{1,2},{2,1},{3,0},{4,7},{5,6},{6,5},{7,4},{8,11},{9,10},{10,... | collective-permute-start | bytes 86024 | tf_op jit(solution)/shard_map/ppermute | solution.py:55
  62.0 4.3 %collective-permute-start.23 = (f32[16,128]{1,0:T(8,128)S(1)}, f32[16,128]{1,0:T(8,128)S(1)}, u32[]{:S(2)}, u32[]{:S(2)}) collective-permute-start(f32[16,128]{1,0:T(8,128)S(1)} %get-tuple-element.70.refs_0_), channel_id=1, source_target_pairs={{0,16},{4,20},{8,24},{12,28},{16,0},{20,4},{24,8},{28,12},{1,17},{... | collective-permute-start | bytes 24584 | tf_op jit(solution)/shard_map/ppermute | solution.py:59
  63.0 3.0 %collective-permute-start.22 = (f32[8,128]{1,0:T(8,128)S(1)}, f32[8,128]{1,0:T(8,128)S(1)}, u32[]{:S(2)}, u32[]{:S(2)}) collective-permute-start(f32[8,128]{1,0:T(8,128)S(1)} %get-tuple-element.71), channel_id=1, source_target_pairs={{0,1},{1,0},{2,3},{3,2},{4,5},{5,4},{6,7},{7,6},{8,9},{9,8},{10,11... | collective-permute-start | bytes 12296 | tf_op jit(solution)/shard_map/ppermute | solution.py:55
  63.3 3.0 %collective-permute-start.24 = (f32[8,128]{1,0:T(8,128)S(1)}, f32[8,128]{1,0:T(8,128)S(1)}, u32[]{:S(2)}, u32[]{:S(2)}) collective-permute-start(f32[8,128]{1,0:T(8,128)S(1)} %get-tuple-element.71), channel_id=1, source_target_pairs={{0,17},{1,16},{2,19},{3,18},{4,21},{5,20},{6,23},{7,22},{8,25},{9,... | collective-permute-start | bytes 12296 | tf_op jit(solution)/shard_map/ppermute | solution.py:59

commit v5 on v4

--- a/solution.py
+++ b/solution.py
@@ -16,7 +16,7 @@
 MEMBERS = 5
 PLANES = 280
 SHARE = PLANES // 4
-CHUNKS = ((0, 35), (35, 35))
+CHUNKS = ((0, 40), (40, 30))
 PARTNERS = (2, 1, 3)
 MIB = 1 << 20
 
@@ -254,8 +254,40 @@
         share_sums(chunk, sel, w, BF16, out)
 
 
-def stays_body(ids, kept, w, own):
-    share_sums((0, SHARE), kept.at[0], w, F32, own)
+def next_sends_body(chunk, ids, sent1, sent2, w, own, *outs):
+    sends_body(chunk, ids, sent1, sent2, w, *outs)
+
+
+def stays_body(ids, anomalies, obs_time, w, kept, own, buf, when, sems, time_sem):
+    time_copy = pltpu.make_async_copy(obs_time, when, time_sem.at[0])
+    time_copy.start()
+    copies = []
+    for n, (first, count) in enumerate(CHUNKS):
+        at = pl.ds(SHARE * ids[0] + first, count)
+        for m in range(MEMBERS):
+            copy = pltpu.make_async_copy(
+                anomalies.at[m, :, at], buf.at[m, :, pl.ds(first, count)], sems.at[n * MEMBERS + m]
+            )
+            copy.start()
+            copies.append(copy)
+    time_copy.wait()
+    at_zero = when[...].astype(F32).astype(BF16) == 0
+    ws = [w[m] for m in range(MEMBERS)]
+    for n, (first, count) in enumerate(CHUNKS):
+        for copy in copies[n * MEMBERS : (n + 1) * MEMBERS]:
+            copy.wait()
+
+        def plane(r, c, first=first):
+            total = None
+            for m in range(MEMBERS):
+                picked = jnp.where(at_zero, buf[m, 0, first + r], buf[m, 1, first + r])
+                kept[m, first + r] = picked
+                term = picked.astype(F32) * ws[m]
+                total = term if total is None else total + term
+            own[first + r] = total
+            return c
+
+        lax.fori_loop(0, count, plane, 0, unroll=5)
 
 
 def forward_body(chunk, ids, ext, rate_own, own, even, odd, loc_norm, sent1, sent2, w, rate, terms, *rest):
@@ -320,7 +352,7 @@
     refs, new = rest[:-1], rest[-1]
     acc = tuple(jnp.zeros((ROWS, COLS), F32) for _ in range(MEMBERS))
     for chunk, ref in zip(CHUNKS, refs):
-        acc = pull(kept.at[0], chunk, ref, acc)
+        acc = pull(kept, chunk, ref, acc)
     for m in range(MEMBERS):
         new[m] = acc[m]
 
@@ -365,10 +397,12 @@
     passed[...] = odd[TALL:]
 
 
-def cost_body(scale, ids, pair, got, far_pair, far_got, cost):
+def finish_body(scale, ids, held, pair, got, far_pair, far_got, out, cost):
     mine = pair[:8] + (pair[8:] + got[...])
     far = far_pair[:8] + (far_pair[8:] + far_got[...])
     cost[...] = jnp.broadcast_to(jnp.sum(mine + far) * scale, (1, COLS))
+    for m in range(MEMBERS):
+        out[m] = held[m]
 
 
 def adjoint_body(ids, ext, even, odd, rate, control, out, side, room):
@@ -391,7 +425,7 @@
 
     fields = jnp.concatenate([control, diffusivity[None]], axis=0)
     even, odd = swap(fields, "lat", False), swap(fields, "lat", True)
-    (sent1,) = select(PARTNERS[:2], anomalies, obs_time)
+    sent1, inn, prec = select(PARTNERS[:2], anomalies, obs_time, (innovation, obs_precision))
     even, odd, sent1 = lax.optimization_barrier((even, odd, sent1))
     ext, rate, packed = pack(MEMBERS + 1, fields, even, odd)
     even, odd = swap(packed, "lon", False), swap(packed, "lon", True)
@@ -410,15 +444,31 @@
         scratch=[pltpu.VMEM(TILES, F32), pltpu.VMEM((ROWS * SUB, COLS), F32)],
         us=2.0,
     )
+    kept, own = call(
+        stays_body,
+        [pltpu.VMEM((MEMBERS, SHARE, ROWS, COLS), BF16), pltpu.VMEM((SHARE, ROWS, COLS), F32)],
+        (anomalies, obs_time, w),
+        [ANY_SPEC, ANY_SPEC, VMEM_SPEC],
+        scratch=[
+            pltpu.VMEM((MEMBERS, 2, SHARE, ROWS, COLS), BF16),
+            pltpu.VMEM((ROWS, COLS), jnp.int32),
+            pltpu.SemaphoreType.DMA((len(CHUNKS) * MEMBERS,)),
+            pltpu.SemaphoreType.DMA((1,)),
+        ],
+        limit=16 * MIB,
+        us=2.0,
+    )
     got = []
     for i, chunk in enumerate(CHUNKS):
         if i > 0:
             send = call(
-                functools.partial(sends_body, chunk), blocks(chunk[1]), (sent1, sent2, w), [VMEM_SPEC] * 3, us=0.3
+                functools.partial(next_sends_body, chunk),
+                blocks(chunk[1]),
+                (sent1, sent2, w, own),
+                [VMEM_SPEC] * 3 + [ANY_SPEC],
+                us=0.3,
             )
         got.append([share(cells, p) for cells, p in zip(send, PARTNERS)])
-    kept, inn, prec = select((0,), anomalies, obs_time, (innovation, obs_precision))
-    (own,) = call(stays_body, [pltpu.VMEM((SHARE, ROWS, COLS), F32)], (kept, w), [VMEM_SPEC] * 2, us=0.3)
     weighted, near = [], []
     for i, chunk in enumerate(CHUNKS):
         piece, *rest = call(
@@ -476,19 +526,19 @@
     far_pair = trade(pair, ("lat",), (4, 5, 6, 7, 0, 1, 2, 3))
     far_got = trade(passed, ("lat", "lon"), [(lat ^ 4) * 4 + (lon ^ 1) for lat in range(8) for lon in range(4)])
     even, odd, pair = lax.optimization_barrier((even, odd, pair))
-    (gradient,) = call(
+    (held,) = call(
         adjoint_body,
-        [jax.ShapeDtypeStruct(block, F32)],
+        [pltpu.VMEM(block, F32)],
         (ext, even, odd, rate, control),
         [VMEM_SPEC] * 5,
         scratch=[pltpu.VMEM(TILES, F32), pltpu.VMEM((ROWS * SUB, COLS), F32)],
         us=3.0,
     )
-    (cost,) = call(
-        functools.partial(cost_body, 0.5 / cells),
-        [jax.ShapeDtypeStruct((1, COLS), F32)],
-        (pair, got, far_pair, far_got),
-        [VMEM_SPEC] * 4,
+    gradient, cost = call(
+        functools.partial(finish_body, 0.5 / cells),
+        [jax.ShapeDtypeStruct(block, F32), jax.ShapeDtypeStruct((1, COLS), F32)],
+        (held, pair, got, far_pair, far_got),
+        [VMEM_SPEC] * 5,
         us=0.1,
     )
     return gradient, cost[0, 0]

time: 67.1 us -> 66.5 us (level)
  starting transfers between devices: 38.1 us -> 39.2 us
  Pallas kernels: 14.4 us -> 13.3 us
    pallas_call x17 -> x16, Pallas kernels: 14.4 us -> 13.3 us  [call(): pl.pallas_call(placed, out_shape=outs, in_specs=specs, out_specs=[VMEM_SP...]
  transfers between devices with their start and end apart: 25 -> 25, of which waited for: 7 -> 8; matrix products, arithmetic and copies ran while one was open for 0% -> 0% of each run, Pallas kernels for 17% -> 15%
where the time goes in v5:
time: 66.5 us; the launch traced here: 66.3 us
  starting transfers between devices  39.2 us (59%)
  Pallas kernels  13.3 us (20%)
  waiting for transfers between devices  12.1 us (18%)
  between operations  0.83 us (1%)
  other arithmetic  0.8 us (1%)
    ppermute x16, starting transfers between devices, trade(): return lax.ppermute(cells, axes, list(enumerate(to)))  20.6 us
    ppermute x9, starting transfers between devices, swap(): return lax.ppermute(cells, axis, pairs)  18.6 us
    pallas_call x16, Pallas kernels, call(): pl.pallas_call(placed, out_shape=outs, in_specs=specs, out_specs=[VMEM_SP...  13.3 us
    ppermute x16, waiting for transfers between devices, trade(): return lax.ppermute(cells, axes, list(enumerate(to)))  8.55 us
    ppermute x9, waiting for transfers between devices, swap(): return lax.ppermute(cells, axis, pairs)  3.59 us
  transfers between devices with their start and end apart: 25, of which 8 were waited for; matrix products, arithmetic and copies ran while one was open for 0% of the time, Pallas kernels for 15%

profile of v5, /device:TPU:1, one launch (start us, length us, event | category | flops | bytes accessed | tf_op | source)
XLA Modules:
  0.0 66.3 jit_solution(3154459347902252200)
XLA Ops:
  0.6 0.8 %pad_maximum_fusion.refs_0_.refs_2_ = f32[6,16,128]{2,1,0:T(8,128)S(1)} fusion(f32[1,16,128]{2,1,0:T(8,128)} %bitcast.11, f32[5,16,128]{2,1,0:T(8,128)} %refs_4_.1), kind=kLoop, calls=%fused_computation | loop fusion | flops 12288 | bytes 98304 | tf_op jit(solution)/shard_map/concatenate | solution.py:426
  1.4 2.0 %collective-permute-start = (f32[6,16,128]{2,1,0:T(8,128)S(1)}, f32[6,16,128]{2,1,0:T(8,128)S(1)}, u32[]{:S(2)}, u32[]{:S(2)}) collective-permute-start(f32[6,16,128]{2,1,0:T(8,128)S(1)} %pad_maximum_fusion.refs_0_.refs_2_), channel_id=1, source_target_pairs={{0,4},{4,0},{8,12},{12,8},{16,20},{20,16},{24,28},{28,24},{1,5},{5... | collective-permute-start | bytes 147464 | tf_op jit(solution)/shard_map/ppermute | solution.py:55
  3.5 3.2 %collective-permute-start.1 = (f32[6,16,128]{2,1,0:T(8,128)S(1)}, f32[6,16,128]{2,1,0:T(8,128)S(1)}, u32[]{:S(2)}, u32[]{:S(2)}) collective-permute-start(f32[6,16,128]{2,1,0:T(8,128)S(1)} %pad_maximum_fusion.refs_0_.refs_2_), channel_id=1, source_target_pairs={{0,28},{4,8},{8,4},{12,16},{16,12},{20,24},{24,20},{28,0},{1,29},{... | collective-permute-start | bytes 147464 | tf_op jit(solution)/shard_map/ppermute | solution.py:55
  6.6 3.1 %shard_map.86 = (bf16[2,5,70,16,128]{4,3,2,1,0:T(8,128)(2,1)S(1)}, f32[70,16,128]{2,1,0:T(8,128)S(1)}, f32[70,16,128]{2,1,0:T(8,128)S(1)}) custom-call(bf16[5,2,280,16,128]{4,3,2,1,0:T(8,128)(2,1)} %bitcast.6, s32[16,128]{1,0:T(8,128)} %refs_1_.5, f32[280,16,128]{2,1,0:T(8,128)} %bitcast.9, f32[280,16,128]{2,1,0:T(8,128)} %bitcast.10), custom_call_target="tpu_custom_call" | custom-call | flops 2500000 | bytes 7500000 | tf_op jit(solution)/shard_map/pallas_call | solution.py:31
  9.9 1.3 %collective-permute-start.2 = (f32[48,128]{1,0:T(8,128)S(1)}, f32[48,128]{1,0:T(8,128)S(1)}, u32[]{:S(2)}, u32[]{:S(2)}) collective-permute-start(f32[48,128]{1,0:T(8,128)S(1)} %get-tuple-element.45), channel_id=1, source_target_pairs={{0,1},{1,0},{2,3},{3,2},{4,5},{5,4},{6,7},{7,6},{8,9},{9,8},{10,11... | collective-permute-start | bytes 73736 | tf_op jit(solution)/shard_map/ppermute | solution.py:55
  11.2 3.3 %collective-permute-start.3 = (f32[48,128]{1,0:T(8,128)S(1)}, f32[48,128]{1,0:T(8,128)S(1)}, u32[]{:S(2)}, u32[]{:S(2)}) collective-permute-start(f32[48,128]{1,0:T(8,128)S(1)} %get-tuple-element.45), channel_id=1, source_target_pairs={{0,3},{1,2},{2,1},{3,0},{4,7},{5,6},{6,5},{7,4},{8,11},{9,10},{10,... | collective-permute-start | bytes 73736 | tf_op jit(solution)/shard_map/ppermute | solution.py:55
  14.5 1.9 %shard_map.88.refs_7_.refs_1_ = bf16[1,5,70,16,128]{4,3,2,1,0:T(8,128)(2,1)S(1)} custom-call(bf16[5,2,280,16,128]{4,3,2,1,0:T(8,128)(2,1)} %bitcast.7, s32[16,128]{1,0:T(8,128)} %refs_1_.5), custom_call_target="tpu_custom_call" | custom-call | flops 2500000 | bytes 7500000 | tf_op jit(solution)/shard_map/pallas_call | solution.py:31
  16.4 1.9 %shard_map.89 = (f32[5,16,128]{2,1,0:T(8,128)S(1)}, f32[2,384,128]{2,1,0:T(8,128)S(1)}, f32[8,128]{1,0:T(8,128)S(1)}, bf16[40,16,128]{2,1,0:T(8,128)(2,1)S(1)}, ...) custom-call(f32[384,128]{1,0:T(8,128)S(1)} %get-tuple-element.47.refs_0_, ...), custom_call_target="tpu_custom_call" | custom-call | flops 2000000 | bytes 6000000 | tf_op jit(solution)/shard_map/pallas_call | solution.py:31
  18.3 3.1 %collective-permute-start.4 = (bf16[40,16,128]{2,1,0:T(8,128)(2,1)S(1)}, bf16[40,16,128]{2,1,0:T(8,128)(2,1)S(1)}, u32[]{:S(2)}, u32[]{:S(2)}) collective-permute-start(bf16[40,16,128]{2,1,0:T(8,128)(2,1)S(1)} %get-tuple-element.54), channel_id=1, source_target_pairs={{0,64},{32,96},{64,0},{96,32},{1,65},{33,97},{65,1},{97,33},{2,66}... | collective-permute-start | bytes 491528 | tf_op jit(solution)/shard_map/ppermute | solution.py:59
  22.1 2.1 %shard_map.90 = (bf16[5,70,16,128]{3,2,1,0:T(8,128)(2,1)S(1)}, f32[70,16,128]{2,1,0:T(8,128)S(1)}) custom-call(bf16[5,2,280,16,128]{4,3,2,1,0:T(8,128)(2,1)} %bitcast.8, s32[16,128]{1,0:T(8,128)} %refs_1_.5, f32[5,16,128]{2,1,0:T(8,128)S(1)} %get-tuple-element.51.refs_2_), custom_call_target="tpu_custom_call" | custom-call | flops 2000000 | bytes 6000000 | tf_op jit(solution)/shard_map/pallas_call | solution.py:31
  24.6 2.7 %collective-permute-start.7 = (bf16[30,16,128]{2,1,0:T(8,128)(2,1)S(1)}, bf16[30,16,128]{2,1,0:T(8,128)(2,1)S(1)}, u32[]{:S(2)}, u32[]{:S(2)}) collective-permute-start(bf16[30,16,128]{2,1,0:T(8,128)(2,1)S(1)} %get-tuple-element.61), channel_id=1, source_target_pairs={{0,64},{32,96},{64,0},{96,32},{1,65},{33,97},{65,1},{97,33},{2,66}... | collective-permute-start | bytes 368648 | tf_op jit(solution)/shard_map/ppermute | solution.py:59
  28.0 1.1 %collective-permute-done.5.refs_2_ = bf16[40,16,128]{2,1,0:T(8,128)(2,1)S(1)} collective-permute-done((bf16[40,16,128]{2,1,0:T(8,128)(2,1)S(1)}, bf16[40,16,128]{2,1,0:T(8,128)(2,1)S(1)}, u32[]{:S(2)}, u32[]{:S(2)}) %collective-permute-start.5) | collective-permute-done | bytes 163872 | tf_op jit(solution)/shard_map/ppermute | solution.py:59
  29.3 3.9 %collective-permute-start.10 = (bf16[40,16,128]{2,1,0:T(8,128)(2,1)S(1)}, bf16[40,16,128]{2,1,0:T(8,128)(2,1)S(1)}, u32[]{:S(2)}, u32[]{:S(2)}) collective-permute-start(bf16[40,16,128]{2,1,0:T(8,128)(2,1)S(1)} %get-tuple-element.60.refs_1_), channel_id=1, source_target_pairs={{0,96},{32,64},{64,32},{96,0},{1,97},{33,65},{65,33},{97,1},{2,98}... | collective-permute-start | bytes 491528 | tf_op jit(solution)/shard_map/ppermute | solution.py:59
  33.3 1.1 %collective-permute-done.8.refs_2_ = bf16[30,16,128]{2,1,0:T(8,128)(2,1)S(1)} collective-permute-done((bf16[30,16,128]{2,1,0:T(8,128)(2,1)S(1)}, bf16[30,16,128]{2,1,0:T(8,128)(2,1)S(1)}, u32[]{:S(2)}, u32[]{:S(2)}) %collective-permute-start.8) | collective-permute-done | bytes 122912 | tf_op jit(solution)/shard_map/ppermute | solution.py:59
  34.5 3.4 %collective-permute-start.14 = (bf16[31,16,128]{2,1,0:T(8,128)(2,1)S(1)}, bf16[31,16,128]{2,1,0:T(8,128)(2,1)S(1)}, u32[]{:S(2)}, u32[]{:S(2)}) collective-permute-start(bf16[31,16,128]{2,1,0:T(8,128)(2,1)S(1)} %shard_map.93.refs_2_.refs_7_), channel_id=1, source_target_pairs={{0,64},{32,96},{64,0},{96,32},{1,65},{33,97},{65,1},{97,33},{2,66}... | collective-permute-start | bytes 380936 | tf_op jit(solution)/shard_map/ppermute | solution.py:59
  38.3 1.2 %collective-permute-start.11 = (bf16[20,16,128]{2,1,0:T(8,128)(2,1)S(1)}, bf16[20,16,128]{2,1,0:T(8,128)(2,1)S(1)}, u32[]{:S(2)}, u32[]{:S(2)}) collective-permute-start(bf16[20,16,128]{2,1,0:T(8,128)(2,1)S(1)} %slice.12), channel_id=1, source_target_pairs={{0,32},{32,0},{64,96},{96,64},{1,33},{33,1},{65,97},{97,65},{2,34}... | collective-permute-start | bytes 245768 | tf_op jit(solution)/shard_map/ppermute | solution.py:59
  39.5 2.2 %collective-permute-start.13 = (bf16[20,16,128]{2,1,0:T(8,128)(2,1)S(1)}, bf16[20,16,128]{2,1,0:T(8,128)(2,1)S(1)}, u32[]{:S(2)}, u32[]{:S(2)}) collective-permute-start(bf16[20,16,128]{2,1,0:T(8,128)(2,1)S(1)} %slice.13), channel_id=1, source_target_pairs={{0,96},{32,64},{64,32},{96,0},{1,97},{33,65},{65,33},{97,1},{2,98}... | collective-permute-start | bytes 245768 | tf_op jit(solution)/shard_map/ppermute | solution.py:59
  42.0 3.3 %collective-permute-done.11.refs_3_ = bf16[20,16,128]{2,1,0:T(8,128)(2,1)S(1)} collective-permute-done((bf16[20,16,128]{2,1,0:T(8,128)(2,1)S(1)}, bf16[20,16,128]{2,1,0:T(8,128)(2,1)S(1)}, u32[]{:S(2)}, u32[]{:S(2)}) %collective-permute-start.11) | collective-permute-done | bytes 81952 | tf_op jit(solution)/shard_map/ppermute | solution.py:59
  45.2 1.1 %collective-permute-done.13.refs_4_ = bf16[20,16,128]{2,1,0:T(8,128)(2,1)S(1)} collective-permute-done((bf16[20,16,128]{2,1,0:T(8,128)(2,1)S(1)}, bf16[20,16,128]{2,1,0:T(8,128)(2,1)S(1)}, u32[]{:S(2)}, u32[]{:S(2)}) %collective-permute-start.13) | collective-permute-done | bytes 81952 | tf_op jit(solution)/shard_map/ppermute | solution.py:59
  46.3 0.6 shard_map.95.refs_2_
  47.6 2.5 %collective-permute-start.18 = (f32[6,16,128]{2,1,0:T(8,128)S(1)}, f32[6,16,128]{2,1,0:T(8,128)S(1)}, u32[]{:S(2)}, u32[]{:S(2)}) collective-permute-start(f32[6,16,128]{2,1,0:T(8,128)S(1)} %get-tuple-element.65.refs_0_), channel_id=1, source_target_pairs={{0,28},{4,8},{8,4},{12,16},{16,12},{20,24},{24,20},{28,0},{1,29},{... | collective-permute-start | bytes 147464 | tf_op jit(solution)/shard_map/ppermute | solution.py:55
  50.1 0.7 %collective-permute-start.19 = (f32[8,128]{1,0:T(8,128)S(1)}, f32[8,128]{1,0:T(8,128)S(1)}, u32[]{:S(2)}, u32[]{:S(2)}) collective-permute-start(f32[8,128]{1,0:T(8,128)S(1)} %get-tuple-element.66.refs_3_), channel_id=1, source_target_pairs={{0,8},{4,12},{8,0},{12,4},{16,24},{20,28},{24,16},{28,20},{1,9},{5... | collective-permute-start | bytes 12296 | tf_op jit(solution)/shard_map/ppermute | solution.py:59
  50.8 1.9 %collective-permute-done.18.refs_2_ = f32[6,16,128]{2,1,0:T(8,128)S(1)} collective-permute-done((f32[6,16,128]{2,1,0:T(8,128)S(1)}, f32[6,16,128]{2,1,0:T(8,128)S(1)}, u32[]{:S(2)}, u32[]{:S(2)}) %collective-permute-start.18) | collective-permute-done | bytes 49184 | tf_op jit(solution)/shard_map/ppermute | solution.py:55
  52.8 1.3 %collective-permute-done.19.refs_2_ = f32[8,128]{1,0:T(8,128)S(1)} collective-permute-done((f32[8,128]{1,0:T(8,128)S(1)}, f32[8,128]{1,0:T(8,128)S(1)}, u32[]{:S(2)}, u32[]{:S(2)}) %collective-permute-start.19) | collective-permute-done | bytes 4128 | tf_op jit(solution)/shard_map/ppermute | solution.py:59
  54.2 2.8 %collective-permute-start.20 = (f32[56,128]{1,0:T(8,128)S(1)}, f32[56,128]{1,0:T(8,128)S(1)}, u32[]{:S(2)}, u32[]{:S(2)}) collective-permute-start(f32[56,128]{1,0:T(8,128)S(1)} %get-tuple-element.70), channel_id=1, source_target_pairs={{0,1},{1,0},{2,3},{3,2},{4,5},{5,4},{6,7},{7,6},{8,9},{9,8},{10,11... | collective-permute-start | bytes 86024 | tf_op jit(solution)/shard_map/ppermute | solution.py:55
  56.9 3.1 %collective-permute-start.21 = (f32[56,128]{1,0:T(8,128)S(1)}, f32[56,128]{1,0:T(8,128)S(1)}, u32[]{:S(2)}, u32[]{:S(2)}) collective-permute-start(f32[56,128]{1,0:T(8,128)S(1)} %get-tuple-element.70), channel_id=1, source_target_pairs={{0,3},{1,2},{2,1},{3,0},{4,7},{5,6},{6,5},{7,4},{8,11},{9,10},{10,... | collective-permute-start | bytes 86024 | tf_op jit(solution)/shard_map/ppermute | solution.py:55
  60.0 1.7 %collective-permute-done.21.refs_2_ = f32[56,128]{1,0:T(8,128)S(1)} collective-permute-done((f32[56,128]{1,0:T(8,128)S(1)}, f32[56,128]{1,0:T(8,128)S(1)}, u32[]{:S(2)}, u32[]{:S(2)}) %collective-permute-start.21) | collective-permute-done | bytes 28704 | tf_op jit(solution)/shard_map/ppermute | solution.py:55
  61.7 0.6 collective-permute-start.23
  62.6 1.1 %collective-permute-start.24 = (f32[8,128]{1,0:T(8,128)S(1)}, f32[8,128]{1,0:T(8,128)S(1)}, u32[]{:S(2)}, u32[]{:S(2)}) collective-permute-start(f32[8,128]{1,0:T(8,128)S(1)} %get-tuple-element.77), channel_id=1, source_target_pairs={{0,17},{1,16},{2,19},{3,18},{4,21},{5,20},{6,23},{7,22},{8,25},{9,... | collective-permute-start | bytes 12296 | tf_op jit(solution)/shard_map/ppermute | solution.py:59
  63.7 1.3 %shard_map.100.refs_0_ = f32[5,16,128]{2,1,0:T(8,128)S(1)} custom-call(f32[384,128]{1,0:T(8,128)S(1)} %get-tuple-element.67.refs_0_, f32[56,128]{1,0:T(8,128)S(1)} %collective-permute-done.20.refs_1_, f32[56,128]{1,0:T(8,128)S(1)} %collective-permute-done.21.refs_2_, f32[2,384,128]{2,1,0:T(8,128)S(1)} %get-tuple-element.75.refs_3_, f32[5,16,128]{2,1,0:T(8,128)S(1)} %copy-done), custom_call_target="tpu_custom_call" | custom-call | flops 3000000 | bytes 9000000 | tf_op jit(solution)/shard_map/pallas_call | solution.py:31
  65.0 0.6 collective-permute-done.24.refs_4_
  65.6 0.6 shard_map.101
  (41 shorter events, 4.1 us)
Async XLA Ops:
  1.4 8.3 %collective-permute-start = (f32[6,16,128]{2,1,0:T(8,128)S(1)}, f32[6,16,128]{2,1,0:T(8,128)S(1)}, u32[]{:S(2)}, u32[]{:S(2)}) collective-permute-start(f32[6,16,128]{2,1,0:T(8,128)S(1)} %pad_maximum_fusion.refs_0_.refs_2_), channel_id=1, source_target_pairs={{0,4},{4,0},{8,12},{12,8},{16,20},{20,16},{24,28},{28,24},{1,5},{5... | collective-permute-start | bytes 147464 | tf_op jit(solution)/shard_map/ppermute | solution.py:55
  3.5 6.3 %collective-permute-start.1 = (f32[6,16,128]{2,1,0:T(8,128)S(1)}, f32[6,16,128]{2,1,0:T(8,128)S(1)}, u32[]{:S(2)}, u32[]{:S(2)}) collective-permute-start(f32[6,16,128]{2,1,0:T(8,128)S(1)} %pad_maximum_fusion.refs_0_.refs_2_), channel_id=1, source_target_pairs={{0,28},{4,8},{8,4},{12,16},{16,12},{20,24},{24,20},{28,0},{1,29},{... | collective-permute-start | bytes 147464 | tf_op jit(solution)/shard_map/ppermute | solution.py:55
  9.9 6.5 %copy-start.1 = (f32[16,128]{1,0:T(8,128)S(1)}, f32[16,128]{1,0:T(8,128)}, u32[]{:S(2)}) copy-start(f32[16,128]{1,0:T(8,128)} %refs_6_.1) | copy-start | bytes 24580
  9.9 6.5 %collective-permute-start.2 = (f32[48,128]{1,0:T(8,128)S(1)}, f32[48,128]{1,0:T(8,128)S(1)}, u32[]{:S(2)}, u32[]{:S(2)}) collective-permute-start(f32[48,128]{1,0:T(8,128)S(1)} %get-tuple-element.45), channel_id=1, source_target_pairs={{0,1},{1,0},{2,3},{3,2},{4,5},{5,4},{6,7},{7,6},{8,9},{9,8},{10,11... | collective-permute-start | bytes 73736 | tf_op jit(solution)/shard_map/ppermute | solution.py:55
  11.2 5.2 %collective-permute-start.3 = (f32[48,128]{1,0:T(8,128)S(1)}, f32[48,128]{1,0:T(8,128)S(1)}, u32[]{:S(2)}, u32[]{:S(2)}) collective-permute-start(f32[48,128]{1,0:T(8,128)S(1)} %get-tuple-element.45), channel_id=1, source_target_pairs={{0,3},{1,2},{2,1},{3,0},{4,7},{5,6},{6,5},{7,4},{8,11},{9,10},{10,... | collective-permute-start | bytes 73736 | tf_op jit(solution)/shard_map/ppermute | solution.py:55
  18.3 9.3 %collective-permute-start.4 = (bf16[40,16,128]{2,1,0:T(8,128)(2,1)S(1)}, bf16[40,16,128]{2,1,0:T(8,128)(2,1)S(1)}, u32[]{:S(2)}, u32[]{:S(2)}) collective-permute-start(bf16[40,16,128]{2,1,0:T(8,128)(2,1)S(1)} %get-tuple-element.54), channel_id=1, source_target_pairs={{0,64},{32,96},{64,0},{96,32},{1,65},{33,97},{65,1},{97,33},{2,66}... | collective-permute-start | bytes 491528 | tf_op jit(solution)/shard_map/ppermute | solution.py:59
  21.4 7.8 %collective-permute-start.5 = (bf16[40,16,128]{2,1,0:T(8,128)(2,1)S(1)}, bf16[40,16,128]{2,1,0:T(8,128)(2,1)S(1)}, u32[]{:S(2)}, u32[]{:S(2)}) collective-permute-start(bf16[40,16,128]{2,1,0:T(8,128)(2,1)S(1)} %get-tuple-element.55), channel_id=1, source_target_pairs={{0,32},{32,0},{64,96},{96,64},{1,33},{33,1},{65,97},{97,65},{2,34}... | collective-permute-start | bytes 491528 | tf_op jit(solution)/shard_map/ppermute | solution.py:59
  21.7 7.4 %collective-permute-start.6 = (bf16[40,16,128]{2,1,0:T(8,128)(2,1)S(1)}, bf16[40,16,128]{2,1,0:T(8,128)(2,1)S(1)}, u32[]{:S(2)}, u32[]{:S(2)}) collective-permute-start(bf16[40,16,128]{2,1,0:T(8,128)(2,1)S(1)} %get-tuple-element.56), channel_id=1, source_target_pairs={{0,96},{32,64},{64,32},{96,0},{1,97},{33,65},{65,33},{97,1},{2,98}... | collective-permute-start | bytes 491528 | tf_op jit(solution)/shard_map/ppermute | solution.py:59
  24.6 8.6 %collective-permute-start.7 = (bf16[30,16,128]{2,1,0:T(8,128)(2,1)S(1)}, bf16[30,16,128]{2,1,0:T(8,128)(2,1)S(1)}, u32[]{:S(2)}, u32[]{:S(2)}) collective-permute-start(bf16[30,16,128]{2,1,0:T(8,128)(2,1)S(1)} %get-tuple-element.61), channel_id=1, source_target_pairs={{0,64},{32,96},{64,0},{96,32},{1,65},{33,97},{65,1},{97,33},{2,66}... | collective-permute-start | bytes 368648 | tf_op jit(solution)/shard_map/ppermute | solution.py:59
  27.3 7.1 %collective-permute-start.8 = (bf16[30,16,128]{2,1,0:T(8,128)(2,1)S(1)}, bf16[30,16,128]{2,1,0:T(8,128)(2,1)S(1)}, u32[]{:S(2)}, u32[]{:S(2)}) collective-permute-start(bf16[30,16,128]{2,1,0:T(8,128)(2,1)S(1)} %get-tuple-element.62), channel_id=1, source_target_pairs={{0,32},{32,0},{64,96},{96,64},{1,33},{33,1},{65,97},{97,65},{2,34}... | collective-permute-start | bytes 368648 | tf_op jit(solution)/shard_map/ppermute | solution.py:59
  27.6 6.8 %collective-permute-start.9 = (bf16[30,16,128]{2,1,0:T(8,128)(2,1)S(1)}, bf16[30,16,128]{2,1,0:T(8,128)(2,1)S(1)}, u32[]{:S(2)}, u32[]{:S(2)}) collective-permute-start(bf16[30,16,128]{2,1,0:T(8,128)(2,1)S(1)} %get-tuple-element.63), channel_id=1, source_target_pairs={{0,96},{32,64},{64,32},{96,0},{1,97},{33,65},{65,33},{97,1},{2,98}... | collective-permute-start | bytes 368648 | tf_op jit(solution)/shard_map/ppermute | solution.py:59
  29.3 9.0 %collective-permute-start.10 = (bf16[40,16,128]{2,1,0:T(8,128)(2,1)S(1)}, bf16[40,16,128]{2,1,0:T(8,128)(2,1)S(1)}, u32[]{:S(2)}, u32[]{:S(2)}) collective-permute-start(bf16[40,16,128]{2,1,0:T(8,128)(2,1)S(1)} %get-tuple-element.60.refs_1_), channel_id=1, source_target_pairs={{0,96},{32,64},{64,32},{96,0},{1,97},{33,65},{65,33},{97,1},{2,98}... | collective-permute-start | bytes 491528 | tf_op jit(solution)/shard_map/ppermute | solution.py:59
  33.2 6.2 %collective-permute-start.12 = (bf16[40,16,128]{2,1,0:T(8,128)(2,1)S(1)}, bf16[40,16,128]{2,1,0:T(8,128)(2,1)S(1)}, u32[]{:S(2)}, u32[]{:S(2)}) collective-permute-start(bf16[40,16,128]{2,1,0:T(8,128)(2,1)S(1)} %get-tuple-element.60.refs_1_), channel_id=1, source_target_pairs={{0,32},{32,0},{64,96},{96,64},{1,33},{33,1},{65,97},{97,65},{2,34}... | collective-permute-start | bytes 491528 | tf_op jit(solution)/shard_map/ppermute | solution.py:59
  34.5 12.4 %collective-permute-start.14 = (bf16[31,16,128]{2,1,0:T(8,128)(2,1)S(1)}, bf16[31,16,128]{2,1,0:T(8,128)(2,1)S(1)}, u32[]{:S(2)}, u32[]{:S(2)}) collective-permute-start(bf16[31,16,128]{2,1,0:T(8,128)(2,1)S(1)} %shard_map.93.refs_2_.refs_7_), channel_id=1, source_target_pairs={{0,64},{32,96},{64,0},{96,32},{1,65},{33,97},{65,1},{97,33},{2,66}... | collective-permute-start | bytes 380936 | tf_op jit(solution)/shard_map/ppermute | solution.py:59
  37.9 9.1 %collective-permute-start.15 = (bf16[31,16,128]{2,1,0:T(8,128)(2,1)S(1)}, bf16[31,16,128]{2,1,0:T(8,128)(2,1)S(1)}, u32[]{:S(2)}, u32[]{:S(2)}) collective-permute-start(bf16[31,16,128]{2,1,0:T(8,128)(2,1)S(1)} %shard_map.93.refs_2_.refs_7_), channel_id=1, source_target_pairs={{0,32},{32,0},{64,96},{96,64},{1,33},{33,1},{65,97},{97,65},{2,34}... | collective-permute-start | bytes 380936 | tf_op jit(solution)/shard_map/ppermute | solution.py:59
  38.1 8.8 %collective-permute-start.16 = (bf16[31,16,128]{2,1,0:T(8,128)(2,1)S(1)}, bf16[31,16,128]{2,1,0:T(8,128)(2,1)S(1)}, u32[]{:S(2)}, u32[]{:S(2)}) collective-permute-start(bf16[31,16,128]{2,1,0:T(8,128)(2,1)S(1)} %shard_map.93.refs_2_.refs_7_), channel_id=1, source_target_pairs={{0,96},{32,64},{64,32},{96,0},{1,97},{33,65},{65,33},{97,1},{2,98}... | collective-permute-start | bytes 380936 | tf_op jit(solution)/shard_map/ppermute | solution.py:59
  38.3 7.0 %collective-permute-start.11 = (bf16[20,16,128]{2,1,0:T(8,128)(2,1)S(1)}, bf16[20,16,128]{2,1,0:T(8,128)(2,1)S(1)}, u32[]{:S(2)}, u32[]{:S(2)}) collective-permute-start(bf16[20,16,128]{2,1,0:T(8,128)(2,1)S(1)} %slice.12), channel_id=1, source_target_pairs={{0,32},{32,0},{64,96},{96,64},{1,33},{33,1},{65,97},{97,65},{2,34}... | collective-permute-start | bytes 245768 | tf_op jit(solution)/shard_map/ppermute | solution.py:59
  39.5 6.9 %collective-permute-start.13 = (bf16[20,16,128]{2,1,0:T(8,128)(2,1)S(1)}, bf16[20,16,128]{2,1,0:T(8,128)(2,1)S(1)}, u32[]{:S(2)}, u32[]{:S(2)}) collective-permute-start(bf16[20,16,128]{2,1,0:T(8,128)(2,1)S(1)} %slice.13), channel_id=1, source_target_pairs={{0,96},{32,64},{64,32},{96,0},{1,97},{33,65},{65,33},{97,1},{2,98}... | collective-permute-start | bytes 245768 | tf_op jit(solution)/shard_map/ppermute | solution.py:59
  46.9 16.8 %copy-start = (f32[5,16,128]{2,1,0:T(8,128)S(1)}, f32[5,16,128]{2,1,0:T(8,128)}, u32[]{:S(2)}) copy-start(f32[5,16,128]{2,1,0:T(8,128)} %refs_4_.1) | copy-start | bytes 122884
  47.5 3.3 %collective-permute-start.17 = (f32[6,16,128]{2,1,0:T(8,128)S(1)}, f32[6,16,128]{2,1,0:T(8,128)S(1)}, u32[]{:S(2)}, u32[]{:S(2)}) collective-permute-start(f32[6,16,128]{2,1,0:T(8,128)S(1)} %get-tuple-element.65.refs_0_), channel_id=1, source_target_pairs={{0,4},{4,0},{8,12},{12,8},{16,20},{20,16},{24,28},{28,24},{1,5},{5... | collective-permute-start | bytes 147464 | tf_op jit(solution)/shard_map/ppermute | solution.py:55
  47.6 5.1 %collective-permute-start.18 = (f32[6,16,128]{2,1,0:T(8,128)S(1)}, f32[6,16,128]{2,1,0:T(8,128)S(1)}, u32[]{:S(2)}, u32[]{:S(2)}) collective-permute-start(f32[6,16,128]{2,1,0:T(8,128)S(1)} %get-tuple-element.65.refs_0_), channel_id=1, source_target_pairs={{0,28},{4,8},{8,4},{12,16},{16,12},{20,24},{24,20},{28,0},{1,29},{... | collective-permute-start | bytes 147464 | tf_op jit(solution)/shard_map/ppermute | solution.py:55
  50.1 4.1 %collective-permute-start.19 = (f32[8,128]{1,0:T(8,128)S(1)}, f32[8,128]{1,0:T(8,128)S(1)}, u32[]{:S(2)}, u32[]{:S(2)}) collective-permute-start(f32[8,128]{1,0:T(8,128)S(1)} %get-tuple-element.66.refs_3_), channel_id=1, source_target_pairs={{0,8},{4,12},{8,0},{12,4},{16,24},{20,28},{24,16},{28,20},{1,9},{5... | collective-permute-start | bytes 12296 | tf_op jit(solution)/shard_map/ppermute | solution.py:59
  54.2 5.9 %collective-permute-start.20 = (f32[56,128]{1,0:T(8,128)S(1)}, f32[56,128]{1,0:T(8,128)S(1)}, u32[]{:S(2)}, u32[]{:S(2)}) collective-permute-start(f32[56,128]{1,0:T(8,128)S(1)} %get-tuple-element.70), channel_id=1, source_target_pairs={{0,1},{1,0},{2,3},{3,2},{4,5},{5,4},{6,7},{7,6},{8,9},{9,8},{10,11... | collective-permute-start | bytes 86024 | tf_op jit(solution)/shard_map/ppermute | solution.py:55
  56.9 4.8 %collective-permute-start.21 = (f32[56,128]{1,0:T(8,128)S(1)}, f32[56,128]{1,0:T(8,128)S(1)}, u32[]{:S(2)}, u32[]{:S(2)}) collective-permute-start(f32[56,128]{1,0:T(8,128)S(1)} %get-tuple-element.70), channel_id=1, source_target_pairs={{0,3},{1,2},{2,1},{3,0},{4,7},{5,6},{6,5},{7,4},{8,11},{9,10},{10,... | collective-permute-start | bytes 86024 | tf_op jit(solution)/shard_map/ppermute | solution.py:55
  61.7 3.9 %collective-permute-start.23 = (f32[16,128]{1,0:T(8,128)S(1)}, f32[16,128]{1,0:T(8,128)S(1)}, u32[]{:S(2)}, u32[]{:S(2)}) collective-permute-start(f32[16,128]{1,0:T(8,128)S(1)} %get-tuple-element.76.refs_1_), channel_id=1, source_target_pairs={{0,16},{4,20},{8,24},{12,28},{16,0},{20,4},{24,8},{28,12},{1,17},{... | collective-permute-start | bytes 24584 | tf_op jit(solution)/shard_map/ppermute | solution.py:59
  62.3 2.7 %collective-permute-start.22 = (f32[8,128]{1,0:T(8,128)S(1)}, f32[8,128]{1,0:T(8,128)S(1)}, u32[]{:S(2)}, u32[]{:S(2)}) collective-permute-start(f32[8,128]{1,0:T(8,128)S(1)} %get-tuple-element.77), channel_id=1, source_target_pairs={{0,1},{1,0},{2,3},{3,2},{4,5},{5,4},{6,7},{7,6},{8,9},{9,8},{10,11... | collective-permute-start | bytes 12296 | tf_op jit(solution)/shard_map/ppermute | solution.py:55
  62.6 3.0 %collective-permute-start.24 = (f32[8,128]{1,0:T(8,128)S(1)}, f32[8,128]{1,0:T(8,128)S(1)}, u32[]{:S(2)}, u32[]{:S(2)}) collective-permute-start(f32[8,128]{1,0:T(8,128)S(1)} %get-tuple-element.77), channel_id=1, source_target_pairs={{0,17},{1,16},{2,19},{3,18},{4,21},{5,20},{6,23},{7,22},{8,25},{9,... | collective-permute-start | bytes 12296 | tf_op jit(solution)/shard_map/ppermute | solution.py:59

commit v6 on v5

--- a/solution.py
+++ b/solution.py
@@ -72,21 +72,45 @@
     ref[pl.ds(f, TALL, stride=SUB)] = rows
 
 
-def pack_body(fields, first, ids, own, even, odd, *rest):
-    if first:
-        ext, rate, packed = rest
+def split(terms):
+    high = terms.astype(BF16).astype(F32)
+    return jnp.concatenate([high, terms - high], axis=0).astype(BF16)
+
+
+def ridden(plane):
+    plane = plane.astype(F32)
+    return plane[:8] + plane[8:]
+
+
+def join_body(ids, control, diffusivity, out, room, sems):
+    copies = (
+        pltpu.make_async_copy(control, room.at[pl.ds(0, MEMBERS)], sems.at[0]),
+        pltpu.make_async_copy(diffusivity, room.at[MEMBERS], sems.at[1]),
+    )
+    for copy in copies:
+        copy.start()
+    for copy in copies:
+        copy.wait()
+    out[...] = room[...].astype(BF16)
+
+
+def pack_body(fields, ids, *refs):
+    if fields > MEMBERS:
+        control, diffusivity, even, odd, ext, rate, packed = refs
+        own = [control[m] for m in range(MEMBERS)] + [diffusivity[...]]
     else:
-        terms, ext, packed, new_terms = rest
-        new_terms[...] = (terms[...] + even[fields, :8]) + odd[fields, :8]
+        source, terms, even, odd, ext, packed, new_terms = refs
+        own = [source[m] for m in range(MEMBERS)]
+        new_terms[...] = (terms[...] + ridden(even[fields])) + ridden(odd[fields])
     lat = ids[1]
     is_even = lax.rem(lat, 2) == 0
     lane = lax.broadcasted_iota(jnp.int32, (TALL, COLS), 1)
     out = jnp.zeros((TALL, COLS), F32)
     for f in range(fields):
-        a, b = even[f], odd[f]
+        a, b = even[f].astype(F32), odd[f].astype(F32)
         up = jnp.where(is_even, b, a)
         down = jnp.where(is_even, a, b)
-        if first:
+        if fields > MEMBERS:
             up = jnp.where(lat == 0, 0.0, up)
             down = jnp.where(lat == 7, 0.0, down)
         whole = jnp.concatenate([up, own[f], down], axis=0)
@@ -98,25 +122,26 @@
         at = 2 * REACH * f
         turned = pltpu.roll(whole, (at + REACH) % COLS, 1)
         out = jnp.where((lane >= at) & (lane < at + 2 * REACH), turned, out)
-    packed[:TALL] = out
-
-
-def pack(fields, own, even, odd, terms=()):
+    packed[:TALL] = out.astype(BF16)
+
+
+def pack(fields, own, even, odd):
+    first = fields > MEMBERS
     return call(
-        functools.partial(pack_body, fields, not terms),
-        [pltpu.VMEM(TILES, F32)] * (1 if terms else 2)
-        + [pltpu.VMEM((TALL + (8 if terms else 0), COLS), F32)]
-        + [pltpu.VMEM((8, COLS), F32)] * len(terms),
-        (own, even, odd, *terms),
-        [VMEM_SPEC] * (3 + len(terms)),
+        functools.partial(pack_body, fields),
+        [pltpu.VMEM(TILES, F32)] * (2 if first else 1)
+        + [pltpu.VMEM((TALL + (0 if first else 16), COLS), BF16)]
+        + [pltpu.VMEM((8, COLS), F32)] * (0 if first else 1),
+        (*own, even, odd),
+        [VMEM_SPEC] * 4,
         us=0.3,
     )
 
 
 def ride_body(ids, held, terms, got, packed, new_terms):
-    summed = terms[...] + got[...]
-    new_terms[...] = summed
-    packed[TALL:] = summed
+    plane = split(terms[...] + got[...])
+    new_terms[...] = ridden(plane)
+    packed[TALL:] = plane
 
 
 def halo_of(fields, ids, even, odd):
@@ -126,7 +151,7 @@
     for f in range(fields):
         at = 2 * REACH * f
         west = west | ((lane >= at) & (lane < at + REACH))
-    a, b = even[:TALL], odd[:TALL]
+    a, b = even[:TALL].astype(F32), odd[:TALL].astype(F32)
     return jnp.where(west, jnp.where(is_even, b, a), jnp.where(is_even, a, b))
 
 
@@ -290,7 +315,7 @@
         lax.fori_loop(0, count, plane, 0, unroll=5)
 
 
-def forward_body(chunk, ids, ext, rate_own, own, even, odd, loc_norm, sent1, sent2, w, rate, terms, *rest):
+def forward_body(chunk, ids, ext, rate_own, control, even, odd, loc_norm, sent1, sent2, w, rate, terms, *rest):
     sends, side, room = rest[:-2], rest[-2], rest[-1]
     halo = halo_of(MEMBERS + 1, ids, even, odd)
     lane = lax.broadcasted_iota(jnp.int32, (TALL, COLS), 1)
@@ -303,7 +328,7 @@
         put(side, m, spread_halo(halo, m))
     squares = jnp.zeros((ROWS, COLS), F32)
     for m in range(MEMBERS):
-        squares = squares + own[m] * own[m]
+        squares = squares + control[m] * control[m]
     terms[...] = squares[:8] + squares[8:]
     for m, spread in enumerate(members_of(sweep(False, ext, side, rate), room)):
         w[m] = (loc_norm[...] * spread).astype(BF16).astype(F32)
@@ -312,11 +337,6 @@
 
 def rides(chunk):
     return 1 if chunk == CHUNKS[-1] else 0
-
-
-def ridden(plane):
-    plane = plane.astype(F32)
-    return plane[:8] + plane[8:]
 
 
 def misfit_body(chunk, factor, ids, own, got1, got2, got3, inn, prec, terms, weighted, *new_terms):
@@ -334,8 +354,7 @@
     if not rides(chunk):
         new_terms[0][...] = summed
     else:
-        high = summed.astype(BF16).astype(F32)
-        weighted[count] = jnp.concatenate([high, summed - high], axis=0).astype(BF16)
+        weighted[count] = split(summed)
 
 
 def pull(sel, chunk, ref, acc):
@@ -378,23 +397,25 @@
         new[m] = acc[m]
 
 
-def last_pull_body(factor, ids, sent1, sent2, old, ref1, ref2, ref3, loc_norm, mine, new, terms):
+def last_pull_body(factor, ids, sent1, sent2, old, ref1, ref2, ref3, loc_norm, mine, new, halo, terms):
     acc = pull_all(CHUNKS[-1], sent1, sent2, old, (ref1, ref2, ref3))
     for m in range(MEMBERS):
-        new[m] = loc_norm[...] * (factor * acc[m])
+        source = loc_norm[...] * (factor * acc[m])
+        new[m] = source
+        halo[m] = source.astype(BF16)
     at = CHUNKS[-1][1]
     summed = (ridden(mine[at]) + ridden(ref2[at])) + (ridden(ref3[at]) + ridden(ref1[at]))
     row = lax.broadcasted_iota(jnp.int32, (8, COLS), 0)
-    summed = jnp.where(row == ids[1], jnp.sum(summed, axis=0, keepdims=True), 0.0)
-    terms[...] = summed
-    new[MEMBERS, :8] = summed
-    new[MEMBERS, 8:] = jnp.zeros((ROWS - 8, COLS), F32)
+    plane = split(jnp.where(row == ids[1], jnp.sum(summed, axis=0, keepdims=True), 0.0))
+    halo[MEMBERS] = plane
+    terms[...] = ridden(plane)
 
 
 def pass_body(ids, terms, even, odd, pair, passed):
-    pair[:8] = terms[...] + even[TALL:]
-    pair[8:] = odd[TALL:]
-    passed[...] = odd[TALL:]
+    other = ridden(odd[TALL:])
+    pair[:8] = terms[...] + ridden(even[TALL:])
+    pair[8:] = other
+    passed[...] = other
 
 
 def finish_body(scale, ids, held, pair, got, far_pair, far_got, out, cost):
@@ -423,11 +444,18 @@
     obs_precision = in_hbm(obs_precision.reshape(PLANES, ROWS, COLS))
     block = (MEMBERS, ROWS, COLS)
 
-    fields = jnp.concatenate([control, diffusivity[None]], axis=0)
+    (fields,) = call(
+        join_body,
+        [pltpu.VMEM((MEMBERS + 1, ROWS, COLS), BF16)],
+        (in_hbm(control), in_hbm(diffusivity)),
+        [ANY_SPEC] * 2,
+        scratch=[pltpu.VMEM((MEMBERS + 1, ROWS, COLS), F32), pltpu.SemaphoreType.DMA((2,))],
+        us=0.5,
+    )
     even, odd = swap(fields, "lat", False), swap(fields, "lat", True)
     sent1, inn, prec = select(PARTNERS[:2], anomalies, obs_time, (innovation, obs_precision))
     even, odd, sent1 = lax.optimization_barrier((even, odd, sent1))
-    ext, rate, packed = pack(MEMBERS + 1, fields, even, odd)
+    ext, rate, packed = pack(MEMBERS + 1, (control, diffusivity), even, odd)
     even, odd = swap(packed, "lon", False), swap(packed, "lon", True)
     (sent2,) = select(PARTNERS[2:], anomalies, obs_time)
     even, odd, sent2 = lax.optimization_barrier((even, odd, sent2))
@@ -439,7 +467,7 @@
     w, rate, terms, *send = call(
         functools.partial(forward_body, CHUNKS[0]),
         [pltpu.VMEM(block, F32), pltpu.VMEM((2, *TILES), F32), tile, *blocks(CHUNKS[0][1])],
-        (ext, rate, fields, even, odd, loc_norm, sent1, sent2),
+        (ext, rate, control, even, odd, loc_norm, sent1, sent2),
         [VMEM_SPEC] * 8,
         scratch=[pltpu.VMEM(TILES, F32), pltpu.VMEM((ROWS * SUB, COLS), F32)],
         us=2.0,
@@ -500,19 +528,23 @@
             [VMEM_SPEC] * 7,
             us=0.5,
         )
-    source, terms = call(
+    source, halo, terms = call(
         functools.partial(last_pull_body, factor),
-        [pltpu.VMEM((MEMBERS + 1, ROWS, COLS), F32), tile],
+        [
+            pltpu.VMEM(block, F32),
+            pltpu.VMEM((MEMBERS + 1, ROWS, COLS), BF16),
+            tile,
+        ],
         (sent1, sent2, acc, *near[-1], loc_norm, weighted[-1]),
         [VMEM_SPEC] * 8,
         us=0.5,
     )
-    even, odd = swap(source, "lat", False), swap(source, "lat", True)
     got = trade(terms, ("lat",), (2, 3, 0, 1, 6, 7, 4, 5))
-    ext, packed, terms = pack(MEMBERS, source, even, odd, (terms,))
+    even, odd = swap(halo, "lat", False), swap(halo, "lat", True)
+    ext, packed, terms = pack(MEMBERS, (source, terms), even, odd)
     packed, terms = call(
         ride_body,
-        [pltpu.VMEM((TALL + 8, COLS), F32), tile],
+        [pltpu.VMEM((TALL + 16, COLS), BF16), tile],
         (packed, terms, got),
         [VMEM_SPEC] * 3,
         us=0.1,

time: 66.5 us -> 66.3 us (level)
  other arithmetic: 0.8 us -> 0 us
  Pallas kernels: 13.3 us -> 14 us
    concatenate x1 -> x0, other arithmetic: 0.8 us -> none  [on_device(): fields = jnp.concatenate([control, diffusivity[None]], axis=0)]
    pallas_call x16 -> x17, Pallas kernels: 13.3 us -> 14 us  [call(): pl.pallas_call(placed, out_shape=outs, in_specs=specs, out_specs=[VMEM_SP...]
where the time goes in v6:
time: 66.3 us; the launch traced here: 66 us
  starting transfers between devices  39.4 us (59%)
  Pallas kernels  14 us (21%)
  waiting for transfers between devices  11.7 us (18%)
  between operations  0.84 us (1%)
    ppermute x16, starting transfers between devices, trade(): return lax.ppermute(cells, axes, list(enumerate(to)))  21 us
    ppermute x9, starting transfers between devices, swap(): return lax.ppermute(cells, axis, pairs)  18.4 us
    pallas_call x17, Pallas kernels, call(): pl.pallas_call(placed, out_shape=outs, in_specs=specs, out_specs=[VMEM_SP...  14 us
    ppermute x16, waiting for transfers between devices, trade(): return lax.ppermute(cells, axes, list(enumerate(to)))  8.59 us
    ppermute x9, waiting for transfers between devices, swap(): return lax.ppermute(cells, axis, pairs)  3.15 us
  transfers between devices with their start and end apart: 25, of which 8 were waited for; matrix products, arithmetic and copies ran while one was open for 0% of the time, Pallas kernels for 15%

profile of v6, /device:TPU:1, one launch (start us, length us, event | category | flops | bytes accessed | tf_op | source)
XLA Modules:
  0.0 66.0 jit_solution(14105697059773330459)
XLA Ops:
  0.6 0.8 %shard_map.86 = bf16[6,16,128]{2,1,0:T(8,128)(2,1)S(1)} custom-call(f32[5,16,128]{2,1,0:T(8,128)} %refs_4_.1, f32[16,128]{1,0:T(8,128)} %refs_1_.7), custom_call_target="tpu_custom_call" | custom-call | flops 500000 | bytes 1500000 | tf_op jit(solution)/shard_map/pallas_call | solution.py:31
  1.4 2.1 %collective-permute-start = (bf16[6,16,128]{2,1,0:T(8,128)(2,1)S(1)}, bf16[6,16,128]{2,1,0:T(8,128)(2,1)S(1)}, u32[]{:S(2)}, u32[]{:S(2)}) collective-permute-start(bf16[6,16,128]{2,1,0:T(8,128)(2,1)S(1)} %shard_map.86), channel_id=1, source_target_pairs={{0,4},{4,0},{8,12},{12,8},{16,20},{20,16},{24,28},{28,24},{1,5},{5... | collective-permute-start | bytes 73736 | tf_op jit(solution)/shard_map/ppermute | solution.py:55
  3.6 3.2 %collective-permute-start.1 = (bf16[6,16,128]{2,1,0:T(8,128)(2,1)S(1)}, bf16[6,16,128]{2,1,0:T(8,128)(2,1)S(1)}, u32[]{:S(2)}, u32[]{:S(2)}) collective-permute-start(bf16[6,16,128]{2,1,0:T(8,128)(2,1)S(1)} %shard_map.86), channel_id=1, source_target_pairs={{0,28},{4,8},{8,4},{12,16},{16,12},{20,24},{24,20},{28,0},{1,29},{... | collective-permute-start | bytes 73736 | tf_op jit(solution)/shard_map/ppermute | solution.py:55
  6.7 3.1 %shard_map.87 = (bf16[2,5,70,16,128]{4,3,2,1,0:T(8,128)(2,1)S(1)}, f32[70,16,128]{2,1,0:T(8,128)S(1)}, f32[70,16,128]{2,1,0:T(8,128)S(1)}) custom-call(bf16[5,2,280,16,128]{4,3,2,1,0:T(8,128)(2,1)} %bitcast.5, s32[16,128]{1,0:T(8,128)} %refs_1_.9, f32[280,16,128]{2,1,0:T(8,128)} %bitcast.8, f32[280,16,128]{2,1,0:T(8,128)} %bitcast.9), custom_call_target="tpu_custom_call" | custom-call | flops 2500000 | bytes 7500000 | tf_op jit(solution)/shard_map/pallas_call | solution.py:31
  10.0 1.3 %collective-permute-start.2 = (bf16[48,128]{1,0:T(8,128)(2,1)S(1)}, bf16[48,128]{1,0:T(8,128)(2,1)S(1)}, u32[]{:S(2)}, u32[]{:S(2)}) collective-permute-start(bf16[48,128]{1,0:T(8,128)(2,1)S(1)} %get-tuple-element.46), channel_id=1, source_target_pairs={{0,1},{1,0},{2,3},{3,2},{4,5},{5,4},{6,7},{7,6},{8,9},{9,8},{10,11... | collective-permute-start | bytes 36872 | tf_op jit(solution)/shard_map/ppermute | solution.py:55
  11.3 3.3 %collective-permute-start.3 = (bf16[48,128]{1,0:T(8,128)(2,1)S(1)}, bf16[48,128]{1,0:T(8,128)(2,1)S(1)}, u32[]{:S(2)}, u32[]{:S(2)}) collective-permute-start(bf16[48,128]{1,0:T(8,128)(2,1)S(1)} %get-tuple-element.46), channel_id=1, source_target_pairs={{0,3},{1,2},{2,1},{3,0},{4,7},{5,6},{6,5},{7,4},{8,11},{9,10},{10,... | collective-permute-start | bytes 36872 | tf_op jit(solution)/shard_map/ppermute | solution.py:55
  14.6 1.9 %shard_map.89.refs_7_.refs_1_ = bf16[1,5,70,16,128]{4,3,2,1,0:T(8,128)(2,1)S(1)} custom-call(bf16[5,2,280,16,128]{4,3,2,1,0:T(8,128)(2,1)} %bitcast.6, s32[16,128]{1,0:T(8,128)} %refs_1_.9), custom_call_target="tpu_custom_call" | custom-call | flops 2500000 | bytes 7500000 | tf_op jit(solution)/shard_map/pallas_call | solution.py:31
  16.5 1.9 %shard_map.90 = (f32[5,16,128]{2,1,0:T(8,128)S(1)}, f32[2,384,128]{2,1,0:T(8,128)S(1)}, f32[8,128]{1,0:T(8,128)S(1)}, bf16[40,16,128]{2,1,0:T(8,128)(2,1)S(1)}, ...) custom-call(f32[384,128]{1,0:T(8,128)S(1)} %get-tuple-element.48.refs_0_, ...), custom_call_target="tpu_custom_call" | custom-call | flops 2000000 | bytes 6000000 | tf_op jit(solution)/shard_map/pallas_call | solution.py:31
  18.4 3.1 %collective-permute-start.4 = (bf16[40,16,128]{2,1,0:T(8,128)(2,1)S(1)}, bf16[40,16,128]{2,1,0:T(8,128)(2,1)S(1)}, u32[]{:S(2)}, u32[]{:S(2)}) collective-permute-start(bf16[40,16,128]{2,1,0:T(8,128)(2,1)S(1)} %get-tuple-element.55), channel_id=1, source_target_pairs={{0,64},{32,96},{64,0},{96,32},{1,65},{33,97},{65,1},{97,33},{2,66}... | collective-permute-start | bytes 491528 | tf_op jit(solution)/shard_map/ppermute | solution.py:59
  22.2 2.1 %shard_map.91 = (bf16[5,70,16,128]{3,2,1,0:T(8,128)(2,1)S(1)}, f32[70,16,128]{2,1,0:T(8,128)S(1)}) custom-call(bf16[5,2,280,16,128]{4,3,2,1,0:T(8,128)(2,1)} %bitcast.7, s32[16,128]{1,0:T(8,128)} %refs_1_.9, f32[5,16,128]{2,1,0:T(8,128)S(1)} %get-tuple-element.52.refs_2_), custom_call_target="tpu_custom_call" | custom-call | flops 2000000 | bytes 6000000 | tf_op jit(solution)/shard_map/pallas_call | solution.py:31
  24.8 2.7 %collective-permute-start.7 = (bf16[30,16,128]{2,1,0:T(8,128)(2,1)S(1)}, bf16[30,16,128]{2,1,0:T(8,128)(2,1)S(1)}, u32[]{:S(2)}, u32[]{:S(2)}) collective-permute-start(bf16[30,16,128]{2,1,0:T(8,128)(2,1)S(1)} %get-tuple-element.62), channel_id=1, source_target_pairs={{0,64},{32,96},{64,0},{96,32},{1,65},{33,97},{65,1},{97,33},{2,66}... | collective-permute-start | bytes 368648 | tf_op jit(solution)/shard_map/ppermute | solution.py:59
  28.1 1.1 %collective-permute-done.5.refs_2_ = bf16[40,16,128]{2,1,0:T(8,128)(2,1)S(1)} collective-permute-done((bf16[40,16,128]{2,1,0:T(8,128)(2,1)S(1)}, bf16[40,16,128]{2,1,0:T(8,128)(2,1)S(1)}, u32[]{:S(2)}, u32[]{:S(2)}) %collective-permute-start.5) | collective-permute-done | bytes 163872 | tf_op jit(solution)/shard_map/ppermute | solution.py:59
  29.4 3.9 %collective-permute-start.10 = (bf16[40,16,128]{2,1,0:T(8,128)(2,1)S(1)}, bf16[40,16,128]{2,1,0:T(8,128)(2,1)S(1)}, u32[]{:S(2)}, u32[]{:S(2)}) collective-permute-start(bf16[40,16,128]{2,1,0:T(8,128)(2,1)S(1)} %get-tuple-element.61.refs_1_), channel_id=1, source_target_pairs={{0,96},{32,64},{64,32},{96,0},{1,97},{33,65},{65,33},{97,1},{2,98}... | collective-permute-start | bytes 491528 | tf_op jit(solution)/shard_map/ppermute | solution.py:59
  33.4 1.1 %collective-permute-done.8.refs_2_ = bf16[30,16,128]{2,1,0:T(8,128)(2,1)S(1)} collective-permute-done((bf16[30,16,128]{2,1,0:T(8,128)(2,1)S(1)}, bf16[30,16,128]{2,1,0:T(8,128)(2,1)S(1)}, u32[]{:S(2)}, u32[]{:S(2)}) %collective-permute-start.8) | collective-permute-done | bytes 122912 | tf_op jit(solution)/shard_map/ppermute | solution.py:59
  34.6 3.4 %collective-permute-start.14 = (bf16[31,16,128]{2,1,0:T(8,128)(2,1)S(1)}, bf16[31,16,128]{2,1,0:T(8,128)(2,1)S(1)}, u32[]{:S(2)}, u32[]{:S(2)}) collective-permute-start(bf16[31,16,128]{2,1,0:T(8,128)(2,1)S(1)} %shard_map.94.refs_2_.refs_7_), channel_id=1, source_target_pairs={{0,64},{32,96},{64,0},{96,32},{1,65},{33,97},{65,1},{97,33},{2,66}... | collective-permute-start | bytes 380936 | tf_op jit(solution)/shard_map/ppermute | solution.py:59
  38.4 1.2 %collective-permute-start.11 = (bf16[20,16,128]{2,1,0:T(8,128)(2,1)S(1)}, bf16[20,16,128]{2,1,0:T(8,128)(2,1)S(1)}, u32[]{:S(2)}, u32[]{:S(2)}) collective-permute-start(bf16[20,16,128]{2,1,0:T(8,128)(2,1)S(1)} %slice.12), channel_id=1, source_target_pairs={{0,32},{32,0},{64,96},{96,64},{1,33},{33,1},{65,97},{97,65},{2,34}... | collective-permute-start | bytes 245768 | tf_op jit(solution)/shard_map/ppermute | solution.py:59
  39.6 2.2 %collective-permute-start.13 = (bf16[20,16,128]{2,1,0:T(8,128)(2,1)S(1)}, bf16[20,16,128]{2,1,0:T(8,128)(2,1)S(1)}, u32[]{:S(2)}, u32[]{:S(2)}) collective-permute-start(bf16[20,16,128]{2,1,0:T(8,128)(2,1)S(1)} %slice.13), channel_id=1, source_target_pairs={{0,96},{32,64},{64,32},{96,0},{1,97},{33,65},{65,33},{97,1},{2,98}... | collective-permute-start | bytes 245768 | tf_op jit(solution)/shard_map/ppermute | solution.py:59
  42.1 3.3 %collective-permute-done.11.refs_3_ = bf16[20,16,128]{2,1,0:T(8,128)(2,1)S(1)} collective-permute-done((bf16[20,16,128]{2,1,0:T(8,128)(2,1)S(1)}, bf16[20,16,128]{2,1,0:T(8,128)(2,1)S(1)}, u32[]{:S(2)}, u32[]{:S(2)}) %collective-permute-start.11) | collective-permute-done | bytes 81952 | tf_op jit(solution)/shard_map/ppermute | solution.py:59
  45.4 1.1 %collective-permute-done.13.refs_4_ = bf16[20,16,128]{2,1,0:T(8,128)(2,1)S(1)} collective-permute-done((bf16[20,16,128]{2,1,0:T(8,128)(2,1)S(1)}, bf16[20,16,128]{2,1,0:T(8,128)(2,1)S(1)}, u32[]{:S(2)}, u32[]{:S(2)}) %collective-permute-start.13) | collective-permute-done | bytes 81952 | tf_op jit(solution)/shard_map/ppermute | solution.py:59
  46.4 0.6 shard_map.96.refs_2_
  47.6 2.1 %collective-permute-start.18 = (bf16[6,16,128]{2,1,0:T(8,128)(2,1)S(1)}, bf16[6,16,128]{2,1,0:T(8,128)(2,1)S(1)}, u32[]{:S(2)}, u32[]{:S(2)}) collective-permute-start(bf16[6,16,128]{2,1,0:T(8,128)(2,1)S(1)} %get-tuple-element.68), channel_id=1, source_target_pairs={{0,28},{4,8},{8,4},{12,16},{16,12},{20,24},{24,20},{28,0},{1,29},{... | collective-permute-start | bytes 73736 | tf_op jit(solution)/shard_map/ppermute | solution.py:55
  49.7 1.1 %collective-permute-start.19 = (f32[8,128]{1,0:T(8,128)S(1)}, f32[8,128]{1,0:T(8,128)S(1)}, u32[]{:S(2)}, u32[]{:S(2)}) collective-permute-start(f32[8,128]{1,0:T(8,128)S(1)} %get-tuple-element.67.refs_1_), channel_id=1, source_target_pairs={{0,8},{4,12},{8,0},{12,4},{16,24},{20,28},{24,16},{28,20},{1,9},{5... | collective-permute-start | bytes 12296 | tf_op jit(solution)/shard_map/ppermute | solution.py:59
  50.9 1.6 %collective-permute-done.18.refs_3_ = bf16[6,16,128]{2,1,0:T(8,128)(2,1)S(1)} collective-permute-done((bf16[6,16,128]{2,1,0:T(8,128)(2,1)S(1)}, bf16[6,16,128]{2,1,0:T(8,128)(2,1)S(1)}, u32[]{:S(2)}, u32[]{:S(2)}) %collective-permute-start.18) | collective-permute-done | bytes 24608 | tf_op jit(solution)/shard_map/ppermute | solution.py:55
  52.6 1.2 %collective-permute-done.19.refs_2_ = f32[8,128]{1,0:T(8,128)S(1)} collective-permute-done((f32[8,128]{1,0:T(8,128)S(1)}, f32[8,128]{1,0:T(8,128)S(1)}, u32[]{:S(2)}, u32[]{:S(2)}) %collective-permute-start.19) | collective-permute-done | bytes 4128 | tf_op jit(solution)/shard_map/ppermute | solution.py:59
  53.8 2.8 %collective-permute-start.20 = (bf16[64,128]{1,0:T(8,128)(2,1)S(1)}, bf16[64,128]{1,0:T(8,128)(2,1)S(1)}, u32[]{:S(2)}, u32[]{:S(2)}) collective-permute-start(bf16[64,128]{1,0:T(8,128)(2,1)S(1)} %get-tuple-element.72), channel_id=1, source_target_pairs={{0,1},{1,0},{2,3},{3,2},{4,5},{5,4},{6,7},{7,6},{8,9},{9,8},{10,11... | collective-permute-start | bytes 49160 | tf_op jit(solution)/shard_map/ppermute | solution.py:55
  56.6 3.2 %collective-permute-start.21 = (bf16[64,128]{1,0:T(8,128)(2,1)S(1)}, bf16[64,128]{1,0:T(8,128)(2,1)S(1)}, u32[]{:S(2)}, u32[]{:S(2)}) collective-permute-start(bf16[64,128]{1,0:T(8,128)(2,1)S(1)} %get-tuple-element.72), channel_id=1, source_target_pairs={{0,3},{1,2},{2,1},{3,0},{4,7},{5,6},{6,5},{7,4},{8,11},{9,10},{10,... | collective-permute-start | bytes 49160 | tf_op jit(solution)/shard_map/ppermute | solution.py:55
  59.8 1.5 %collective-permute-done.21.refs_2_ = bf16[64,128]{1,0:T(8,128)(2,1)S(1)} collective-permute-done((bf16[64,128]{1,0:T(8,128)(2,1)S(1)}, bf16[64,128]{1,0:T(8,128)(2,1)S(1)}, u32[]{:S(2)}, u32[]{:S(2)}) %collective-permute-start.21) | collective-permute-done | bytes 16416 | tf_op jit(solution)/shard_map/ppermute | solution.py:55
  61.3 0.7 %collective-permute-start.23 = (f32[16,128]{1,0:T(8,128)S(1)}, f32[16,128]{1,0:T(8,128)S(1)}, u32[]{:S(2)}, u32[]{:S(2)}) collective-permute-start(f32[16,128]{1,0:T(8,128)S(1)} %get-tuple-element.78.refs_1_), channel_id=1, source_target_pairs={{0,16},{4,20},{8,24},{12,28},{16,0},{20,4},{24,8},{28,12},{1,17},{... | collective-permute-start | bytes 24584 | tf_op jit(solution)/shard_map/ppermute | solution.py:59
  62.4 0.9 %collective-permute-start.24 = (f32[8,128]{1,0:T(8,128)S(1)}, f32[8,128]{1,0:T(8,128)S(1)}, u32[]{:S(2)}, u32[]{:S(2)}) collective-permute-start(f32[8,128]{1,0:T(8,128)S(1)} %get-tuple-element.79), channel_id=1, source_target_pairs={{0,17},{1,16},{2,19},{3,18},{4,21},{5,20},{6,23},{7,22},{8,25},{9,... | collective-permute-start | bytes 12296 | tf_op jit(solution)/shard_map/ppermute | solution.py:59
  63.3 1.2 %shard_map.101.refs_0_ = f32[5,16,128]{2,1,0:T(8,128)S(1)} custom-call(f32[384,128]{1,0:T(8,128)S(1)} %get-tuple-element.69.refs_0_, bf16[64,128]{1,0:T(8,128)(2,1)S(1)} %collective-permute-done.20.refs_1_, bf16[64,128]{1,0:T(8,128)(2,1)S(1)} %collective-permute-done.21.refs_2_, f32[2,384,128]{2,1,0:T(8,128)S(1)} %get-tuple-element.77.refs_3_, ...), custom_call_target="tpu_custom_call" | custom-call | flops 3000000 | bytes 9000000 | tf_op jit(solution)/shard_map/pallas_call | solution.py:31
  64.6 0.8 %collective-permute-done.24.refs_4_ = f32[8,128]{1,0:T(8,128)S(1)} collective-permute-done((f32[8,128]{1,0:T(8,128)S(1)}, f32[8,128]{1,0:T(8,128)S(1)}, u32[]{:S(2)}, u32[]{:S(2)}) %collective-permute-start.24) | collective-permute-done | bytes 4128 | tf_op jit(solution)/shard_map/ppermute | solution.py:59
  65.4 0.6 shard_map.102
  (43 shorter events, 4.2 us)
Async XLA Ops:
  1.4 8.4 %collective-permute-start = (bf16[6,16,128]{2,1,0:T(8,128)(2,1)S(1)}, bf16[6,16,128]{2,1,0:T(8,128)(2,1)S(1)}, u32[]{:S(2)}, u32[]{:S(2)}) collective-permute-start(bf16[6,16,128]{2,1,0:T(8,128)(2,1)S(1)} %shard_map.86), channel_id=1, source_target_pairs={{0,4},{4,0},{8,12},{12,8},{16,20},{20,16},{24,28},{28,24},{1,5},{5... | collective-permute-start | bytes 73736 | tf_op jit(solution)/shard_map/ppermute | solution.py:55
  3.6 6.3 %collective-permute-start.1 = (bf16[6,16,128]{2,1,0:T(8,128)(2,1)S(1)}, bf16[6,16,128]{2,1,0:T(8,128)(2,1)S(1)}, u32[]{:S(2)}, u32[]{:S(2)}) collective-permute-start(bf16[6,16,128]{2,1,0:T(8,128)(2,1)S(1)} %shard_map.86), channel_id=1, source_target_pairs={{0,28},{4,8},{8,4},{12,16},{16,12},{20,24},{24,20},{28,0},{1,29},{... | collective-permute-start | bytes 73736 | tf_op jit(solution)/shard_map/ppermute | solution.py:55
  6.7 3.1 %copy-start = (f32[5,16,128]{2,1,0:T(8,128)S(1)}, f32[5,16,128]{2,1,0:T(8,128)}, u32[]{:S(2)}) copy-start(f32[5,16,128]{2,1,0:T(8,128)} %refs_4_.1) | copy-start | bytes 122884
  6.7 3.1 %copy-start.2 = (f32[16,128]{1,0:T(8,128)S(1)}, f32[16,128]{1,0:T(8,128)}, u32[]{:S(2)}) copy-start(f32[16,128]{1,0:T(8,128)} %refs_1_.7) | copy-start | bytes 24580
  10.0 6.5 %copy-start.1 = (f32[16,128]{1,0:T(8,128)S(1)}, f32[16,128]{1,0:T(8,128)}, u32[]{:S(2)}) copy-start(f32[16,128]{1,0:T(8,128)} %refs_6_.1) | copy-start | bytes 24580
  10.0 6.5 %collective-permute-start.2 = (bf16[48,128]{1,0:T(8,128)(2,1)S(1)}, bf16[48,128]{1,0:T(8,128)(2,1)S(1)}, u32[]{:S(2)}, u32[]{:S(2)}) collective-permute-start(bf16[48,128]{1,0:T(8,128)(2,1)S(1)} %get-tuple-element.46), channel_id=1, source_target_pairs={{0,1},{1,0},{2,3},{3,2},{4,5},{5,4},{6,7},{7,6},{8,9},{9,8},{10,11... | collective-permute-start | bytes 36872 | tf_op jit(solution)/shard_map/ppermute | solution.py:55
  11.3 5.2 %collective-permute-start.3 = (bf16[48,128]{1,0:T(8,128)(2,1)S(1)}, bf16[48,128]{1,0:T(8,128)(2,1)S(1)}, u32[]{:S(2)}, u32[]{:S(2)}) collective-permute-start(bf16[48,128]{1,0:T(8,128)(2,1)S(1)} %get-tuple-element.46), channel_id=1, source_target_pairs={{0,3},{1,2},{2,1},{3,0},{4,7},{5,6},{6,5},{7,4},{8,11},{9,10},{10,... | collective-permute-start | bytes 36872 | tf_op jit(solution)/shard_map/ppermute | solution.py:55
  18.4 9.3 %collective-permute-start.4 = (bf16[40,16,128]{2,1,0:T(8,128)(2,1)S(1)}, bf16[40,16,128]{2,1,0:T(8,128)(2,1)S(1)}, u32[]{:S(2)}, u32[]{:S(2)}) collective-permute-start(bf16[40,16,128]{2,1,0:T(8,128)(2,1)S(1)} %get-tuple-element.55), channel_id=1, source_target_pairs={{0,64},{32,96},{64,0},{96,32},{1,65},{33,97},{65,1},{97,33},{2,66}... | collective-permute-start | bytes 491528 | tf_op jit(solution)/shard_map/ppermute | solution.py:59
  21.5 7.7 %collective-permute-start.5 = (bf16[40,16,128]{2,1,0:T(8,128)(2,1)S(1)}, bf16[40,16,128]{2,1,0:T(8,128)(2,1)S(1)}, u32[]{:S(2)}, u32[]{:S(2)}) collective-permute-start(bf16[40,16,128]{2,1,0:T(8,128)(2,1)S(1)} %get-tuple-element.56), channel_id=1, source_target_pairs={{0,32},{32,0},{64,96},{96,64},{1,33},{33,1},{65,97},{97,65},{2,34}... | collective-permute-start | bytes 491528 | tf_op jit(solution)/shard_map/ppermute | solution.py:59
  21.8 7.4 %collective-permute-start.6 = (bf16[40,16,128]{2,1,0:T(8,128)(2,1)S(1)}, bf16[40,16,128]{2,1,0:T(8,128)(2,1)S(1)}, u32[]{:S(2)}, u32[]{:S(2)}) collective-permute-start(bf16[40,16,128]{2,1,0:T(8,128)(2,1)S(1)} %get-tuple-element.57), channel_id=1, source_target_pairs={{0,96},{32,64},{64,32},{96,0},{1,97},{33,65},{65,33},{97,1},{2,98}... | collective-permute-start | bytes 491528 | tf_op jit(solution)/shard_map/ppermute | solution.py:59
  24.8 8.6 %collective-permute-start.7 = (bf16[30,16,128]{2,1,0:T(8,128)(2,1)S(1)}, bf16[30,16,128]{2,1,0:T(8,128)(2,1)S(1)}, u32[]{:S(2)}, u32[]{:S(2)}) collective-permute-start(bf16[30,16,128]{2,1,0:T(8,128)(2,1)S(1)} %get-tuple-element.62), channel_id=1, source_target_pairs={{0,64},{32,96},{64,0},{96,32},{1,65},{33,97},{65,1},{97,33},{2,66}... | collective-permute-start | bytes 368648 | tf_op jit(solution)/shard_map/ppermute | solution.py:59
  27.4 7.1 %collective-permute-start.8 = (bf16[30,16,128]{2,1,0:T(8,128)(2,1)S(1)}, bf16[30,16,128]{2,1,0:T(8,128)(2,1)S(1)}, u32[]{:S(2)}, u32[]{:S(2)}) collective-permute-start(bf16[30,16,128]{2,1,0:T(8,128)(2,1)S(1)} %get-tuple-element.63), channel_id=1, source_target_pairs={{0,32},{32,0},{64,96},{96,64},{1,33},{33,1},{65,97},{97,65},{2,34}... | collective-permute-start | bytes 368648 | tf_op jit(solution)/shard_map/ppermute | solution.py:59
  27.7 6.8 %collective-permute-start.9 = (bf16[30,16,128]{2,1,0:T(8,128)(2,1)S(1)}, bf16[30,16,128]{2,1,0:T(8,128)(2,1)S(1)}, u32[]{:S(2)}, u32[]{:S(2)}) collective-permute-start(bf16[30,16,128]{2,1,0:T(8,128)(2,1)S(1)} %get-tuple-element.64), channel_id=1, source_target_pairs={{0,96},{32,64},{64,32},{96,0},{1,97},{33,65},{65,33},{97,1},{2,98}... | collective-permute-start | bytes 368648 | tf_op jit(solution)/shard_map/ppermute | solution.py:59
  29.4 9.0 %collective-permute-start.10 = (bf16[40,16,128]{2,1,0:T(8,128)(2,1)S(1)}, bf16[40,16,128]{2,1,0:T(8,128)(2,1)S(1)}, u32[]{:S(2)}, u32[]{:S(2)}) collective-permute-start(bf16[40,16,128]{2,1,0:T(8,128)(2,1)S(1)} %get-tuple-element.61.refs_1_), channel_id=1, source_target_pairs={{0,96},{32,64},{64,32},{96,0},{1,97},{33,65},{65,33},{97,1},{2,98}... | collective-permute-start | bytes 491528 | tf_op jit(solution)/shard_map/ppermute | solution.py:59
  33.4 6.2 %collective-permute-start.12 = (bf16[40,16,128]{2,1,0:T(8,128)(2,1)S(1)}, bf16[40,16,128]{2,1,0:T(8,128)(2,1)S(1)}, u32[]{:S(2)}, u32[]{:S(2)}) collective-permute-start(bf16[40,16,128]{2,1,0:T(8,128)(2,1)S(1)} %get-tuple-element.61.refs_1_), channel_id=1, source_target_pairs={{0,32},{32,0},{64,96},{96,64},{1,33},{33,1},{65,97},{97,65},{2,34}... | collective-permute-start | bytes 491528 | tf_op jit(solution)/shard_map/ppermute | solution.py:59
  34.6 12.4 %collective-permute-start.14 = (bf16[31,16,128]{2,1,0:T(8,128)(2,1)S(1)}, bf16[31,16,128]{2,1,0:T(8,128)(2,1)S(1)}, u32[]{:S(2)}, u32[]{:S(2)}) collective-permute-start(bf16[31,16,128]{2,1,0:T(8,128)(2,1)S(1)} %shard_map.94.refs_2_.refs_7_), channel_id=1, source_target_pairs={{0,64},{32,96},{64,0},{96,32},{1,65},{33,97},{65,1},{97,33},{2,66}... | collective-permute-start | bytes 380936 | tf_op jit(solution)/shard_map/ppermute | solution.py:59
  38.0 9.0 %collective-permute-start.15 = (bf16[31,16,128]{2,1,0:T(8,128)(2,1)S(1)}, bf16[31,16,128]{2,1,0:T(8,128)(2,1)S(1)}, u32[]{:S(2)}, u32[]{:S(2)}) collective-permute-start(bf16[31,16,128]{2,1,0:T(8,128)(2,1)S(1)} %shard_map.94.refs_2_.refs_7_), channel_id=1, source_target_pairs={{0,32},{32,0},{64,96},{96,64},{1,33},{33,1},{65,97},{97,65},{2,34}... | collective-permute-start | bytes 380936 | tf_op jit(solution)/shard_map/ppermute | solution.py:59
  38.2 8.8 %collective-permute-start.16 = (bf16[31,16,128]{2,1,0:T(8,128)(2,1)S(1)}, bf16[31,16,128]{2,1,0:T(8,128)(2,1)S(1)}, u32[]{:S(2)}, u32[]{:S(2)}) collective-permute-start(bf16[31,16,128]{2,1,0:T(8,128)(2,1)S(1)} %shard_map.94.refs_2_.refs_7_), channel_id=1, source_target_pairs={{0,96},{32,64},{64,32},{96,0},{1,97},{33,65},{65,33},{97,1},{2,98}... | collective-permute-start | bytes 380936 | tf_op jit(solution)/shard_map/ppermute | solution.py:59
  38.4 7.0 %collective-permute-start.11 = (bf16[20,16,128]{2,1,0:T(8,128)(2,1)S(1)}, bf16[20,16,128]{2,1,0:T(8,128)(2,1)S(1)}, u32[]{:S(2)}, u32[]{:S(2)}) collective-permute-start(bf16[20,16,128]{2,1,0:T(8,128)(2,1)S(1)} %slice.12), channel_id=1, source_target_pairs={{0,32},{32,0},{64,96},{96,64},{1,33},{33,1},{65,97},{97,65},{2,34}... | collective-permute-start | bytes 245768 | tf_op jit(solution)/shard_map/ppermute | solution.py:59
  39.6 6.8 %collective-permute-start.13 = (bf16[20,16,128]{2,1,0:T(8,128)(2,1)S(1)}, bf16[20,16,128]{2,1,0:T(8,128)(2,1)S(1)}, u32[]{:S(2)}, u32[]{:S(2)}) collective-permute-start(bf16[20,16,128]{2,1,0:T(8,128)(2,1)S(1)} %slice.13), channel_id=1, source_target_pairs={{0,96},{32,64},{64,32},{96,0},{1,97},{33,65},{65,33},{97,1},{2,98}... | collective-permute-start | bytes 245768 | tf_op jit(solution)/shard_map/ppermute | solution.py:59
  47.5 3.3 %collective-permute-start.17 = (bf16[6,16,128]{2,1,0:T(8,128)(2,1)S(1)}, bf16[6,16,128]{2,1,0:T(8,128)(2,1)S(1)}, u32[]{:S(2)}, u32[]{:S(2)}) collective-permute-start(bf16[6,16,128]{2,1,0:T(8,128)(2,1)S(1)} %get-tuple-element.68), channel_id=1, source_target_pairs={{0,4},{4,0},{8,12},{12,8},{16,20},{20,16},{24,28},{28,24},{1,5},{5... | collective-permute-start | bytes 73736 | tf_op jit(solution)/shard_map/ppermute | solution.py:55
  47.6 4.9 %collective-permute-start.18 = (bf16[6,16,128]{2,1,0:T(8,128)(2,1)S(1)}, bf16[6,16,128]{2,1,0:T(8,128)(2,1)S(1)}, u32[]{:S(2)}, u32[]{:S(2)}) collective-permute-start(bf16[6,16,128]{2,1,0:T(8,128)(2,1)S(1)} %get-tuple-element.68), channel_id=1, source_target_pairs={{0,28},{4,8},{8,4},{12,16},{16,12},{20,24},{24,20},{28,0},{1,29},{... | collective-permute-start | bytes 73736 | tf_op jit(solution)/shard_map/ppermute | solution.py:55
  49.7 4.1 %collective-permute-start.19 = (f32[8,128]{1,0:T(8,128)S(1)}, f32[8,128]{1,0:T(8,128)S(1)}, u32[]{:S(2)}, u32[]{:S(2)}) collective-permute-start(f32[8,128]{1,0:T(8,128)S(1)} %get-tuple-element.67.refs_1_), channel_id=1, source_target_pairs={{0,8},{4,12},{8,0},{12,4},{16,24},{20,28},{24,16},{28,20},{1,9},{5... | collective-permute-start | bytes 12296 | tf_op jit(solution)/shard_map/ppermute | solution.py:59
  53.8 6.0 %collective-permute-start.20 = (bf16[64,128]{1,0:T(8,128)(2,1)S(1)}, bf16[64,128]{1,0:T(8,128)(2,1)S(1)}, u32[]{:S(2)}, u32[]{:S(2)}) collective-permute-start(bf16[64,128]{1,0:T(8,128)(2,1)S(1)} %get-tuple-element.72), channel_id=1, source_target_pairs={{0,1},{1,0},{2,3},{3,2},{4,5},{5,4},{6,7},{7,6},{8,9},{9,8},{10,11... | collective-permute-start | bytes 49160 | tf_op jit(solution)/shard_map/ppermute | solution.py:55
  56.6 4.7 %collective-permute-start.21 = (bf16[64,128]{1,0:T(8,128)(2,1)S(1)}, bf16[64,128]{1,0:T(8,128)(2,1)S(1)}, u32[]{:S(2)}, u32[]{:S(2)}) collective-permute-start(bf16[64,128]{1,0:T(8,128)(2,1)S(1)} %get-tuple-element.72), channel_id=1, source_target_pairs={{0,3},{1,2},{2,1},{3,0},{4,7},{5,6},{6,5},{7,4},{8,11},{9,10},{10,... | collective-permute-start | bytes 49160 | tf_op jit(solution)/shard_map/ppermute | solution.py:55
  61.3 4.1 %collective-permute-start.23 = (f32[16,128]{1,0:T(8,128)S(1)}, f32[16,128]{1,0:T(8,128)S(1)}, u32[]{:S(2)}, u32[]{:S(2)}) collective-permute-start(f32[16,128]{1,0:T(8,128)S(1)} %get-tuple-element.78.refs_1_), channel_id=1, source_target_pairs={{0,16},{4,20},{8,24},{12,28},{16,0},{20,4},{24,8},{28,12},{1,17},{... | collective-permute-start | bytes 24584 | tf_op jit(solution)/shard_map/ppermute | solution.py:59
  62.0 2.6 %collective-permute-start.22 = (f32[8,128]{1,0:T(8,128)S(1)}, f32[8,128]{1,0:T(8,128)S(1)}, u32[]{:S(2)}, u32[]{:S(2)}) collective-permute-start(f32[8,128]{1,0:T(8,128)S(1)} %get-tuple-element.79), channel_id=1, source_target_pairs={{0,1},{1,0},{2,3},{3,2},{4,5},{5,4},{6,7},{7,6},{8,9},{9,8},{10,11... | collective-permute-start | bytes 12296 | tf_op jit(solution)/shard_map/ppermute | solution.py:55
  62.4 3.0 %collective-permute-start.24 = (f32[8,128]{1,0:T(8,128)S(1)}, f32[8,128]{1,0:T(8,128)S(1)}, u32[]{:S(2)}, u32[]{:S(2)}) collective-permute-start(f32[8,128]{1,0:T(8,128)S(1)} %get-tuple-element.79), channel_id=1, source_target_pairs={{0,17},{1,16},{2,19},{3,18},{4,21},{5,20},{6,23},{7,22},{8,25},{9,... | collective-permute-start | bytes 12296 | tf_op jit(solution)/shard_map/ppermute | solution.py:59

commit v7 on v6

--- a/solution.py
+++ b/solution.py
@@ -205,7 +205,7 @@
     return mem + partner - 2 * (lax.rem(mem, 2) * (partner % 2)) - 4 * (lax.div(mem, 2) * (partner // 2))
 
 
-def select_body(partners, own, ids, anomalies, obs_time, *rest):
+def select_body(partners, planes, own, ids, anomalies, obs_time, *rest):
     if own:
         innovation, precision, sel, inn_own, prec_own, buf, when, sems, own_sems = rest
         own = ((innovation, inn_own), (precision, prec_own))
@@ -216,7 +216,7 @@
     time_copy.start()
     copies = []
     for g, partner in enumerate(partners):
-        at = pl.ds(SHARE * partner_of(ids[0], partner), SHARE)
+        at = pl.ds(SHARE * partner_of(ids[0], partner), planes)
         for m in range(MEMBERS):
             copy = pltpu.make_async_copy(anomalies.at[m, :, at], buf.at[g, m], sems.at[g * MEMBERS + m])
             copy.start()
@@ -236,21 +236,21 @@
             sel[g, m, r] = jnp.where(at_zero, buf[g, m, 0, r], buf[g, m, 1, r])
             return c
 
-        lax.fori_loop(0, SHARE, plane, 0, unroll=7)
+        lax.fori_loop(0, planes, plane, 0, unroll=5)
     for copy in own_copies:
         copy.wait()
 
 
-def select(partners, anomalies, obs_time, own=()):
+def select(partners, planes, anomalies, obs_time, own=()):
     count = len(partners)
     return call(
-        functools.partial(select_body, partners, bool(own)),
-        [pltpu.VMEM((count, MEMBERS, SHARE, ROWS, COLS), BF16)]
+        functools.partial(select_body, partners, planes, bool(own)),
+        [pltpu.VMEM((count, MEMBERS, planes, ROWS, COLS), BF16)]
         + [pltpu.VMEM((SHARE, ROWS, COLS), F32)] * (2 if own else 0),
         (anomalies, obs_time, *own),
         [ANY_SPEC, ANY_SPEC] + ([ANY_SPEC, ANY_SPEC] if own else []),
         scratch=[
-            pltpu.VMEM((count, MEMBERS, 2, SHARE, ROWS, COLS), BF16),
+            pltpu.VMEM((count, MEMBERS, 2, planes, ROWS, COLS), BF16),
             pltpu.VMEM((ROWS, COLS), jnp.int32),
             pltpu.SemaphoreType.DMA((count * MEMBERS,)),
             pltpu.SemaphoreType.DMA((3,)),
@@ -279,11 +279,13 @@
         share_sums(chunk, sel, w, BF16, out)
 
 
-def next_sends_body(chunk, ids, sent1, sent2, w, own, *outs):
-    sends_body(chunk, ids, sent1, sent2, w, *outs)
-
-
-def stays_body(ids, anomalies, obs_time, w, kept, own, buf, when, sems, time_sem):
+def next_sends_body(chunk, ids, sent1, later, w, own, out1, out2, out3):
+    share_sums(chunk, sent1.at[0], w, BF16, out1)
+    share_sums(chunk, sent1.at[1], w, BF16, out2)
+    share_sums((0, chunk[1]), later, w, BF16, out3)
+
+
+def stays_body(ids, anomalies, obs_time, w, kept, own, later, buf, rest, when, sems, time_sem):
     time_copy = pltpu.make_async_copy(obs_time, when, time_sem.at[0])
     time_copy.start()
     copies = []
@@ -295,6 +297,13 @@
             )
             copy.start()
             copies.append(copy)
+    first, count = CHUNKS[1]
+    at = pl.ds(SHARE * partner_of(ids[0], PARTNERS[2]) + first, count)
+    rest_copies = []
+    for m in range(MEMBERS):
+        copy = pltpu.make_async_copy(anomalies.at[m, :, at], rest.at[m], sems.at[len(CHUNKS) * MEMBERS + m])
+        copy.start()
+        rest_copies.append(copy)
     time_copy.wait()
     at_zero = when[...].astype(F32).astype(BF16) == 0
     ws = [w[m] for m in range(MEMBERS)]
@@ -313,6 +322,14 @@
             return c
 
         lax.fori_loop(0, count, plane, 0, unroll=5)
+    for m, copy in enumerate(rest_copies):
+        copy.wait()
+
+        def plane_of_rest(r, c, m=m):
+            later[m, r] = jnp.where(at_zero, rest[m, 0, r], rest[m, 1, r])
+            return c
+
+        lax.fori_loop(0, CHUNKS[1][1], plane_of_rest, 0, unroll=5)
 
 
 def forward_body(chunk, ids, ext, rate_own, control, even, odd, loc_norm, sent1, sent2, w, rate, terms, *rest):
@@ -376,10 +393,11 @@
         new[m] = acc[m]
 
 
-def pull_all(chunk, sent1, sent2, old, refs):
+def pull_all(chunk, sent1, later, old, refs):
     acc = tuple(old[m] for m in range(MEMBERS))
-    for sel, ref in zip((sent1.at[0], sent1.at[1], sent2.at[0]), refs):
-        acc = pull(sel, chunk, ref, acc)
+    parts = (sent1.at[0], chunk), (sent1.at[1], chunk), (later, (0, chunk[1]))
+    for (sel, planes), ref in zip(parts, refs):
+        acc = pull(sel, planes, ref, acc)
     return acc
 
 
@@ -453,11 +471,11 @@
         us=0.5,
     )
     even, odd = swap(fields, "lat", False), swap(fields, "lat", True)
-    sent1, inn, prec = select(PARTNERS[:2], anomalies, obs_time, (innovation, obs_precision))
+    sent1, inn, prec = select(PARTNERS[:2], SHARE, anomalies, obs_time, (innovation, obs_precision))
     even, odd, sent1 = lax.optimization_barrier((even, odd, sent1))
     ext, rate, packed = pack(MEMBERS + 1, (control, diffusivity), even, odd)
     even, odd = swap(packed, "lon", False), swap(packed, "lon", True)
-    (sent2,) = select(PARTNERS[2:], anomalies, obs_time)
+    (sent2,) = select(PARTNERS[2:], CHUNKS[0][1], anomalies, obs_time)
     even, odd, sent2 = lax.optimization_barrier((even, odd, sent2))
 
     def blocks(count):
@@ -472,15 +490,20 @@
         scratch=[pltpu.VMEM(TILES, F32), pltpu.VMEM((ROWS * SUB, COLS), F32)],
         us=2.0,
     )
-    kept, own = call(
+    kept, own, later = call(
         stays_body,
-        [pltpu.VMEM((MEMBERS, SHARE, ROWS, COLS), BF16), pltpu.VMEM((SHARE, ROWS, COLS), F32)],
+        [
+            pltpu.VMEM((MEMBERS, SHARE, ROWS, COLS), BF16),
+            pltpu.VMEM((SHARE, ROWS, COLS), F32),
+            pltpu.VMEM((MEMBERS, CHUNKS[1][1], ROWS, COLS), BF16),
+        ],
         (anomalies, obs_time, w),
         [ANY_SPEC, ANY_SPEC, VMEM_SPEC],
         scratch=[
             pltpu.VMEM((MEMBERS, 2, SHARE, ROWS, COLS), BF16),
+            pltpu.VMEM((MEMBERS, 2, CHUNKS[1][1], ROWS, COLS), BF16),
             pltpu.VMEM((ROWS, COLS), jnp.int32),
-            pltpu.SemaphoreType.DMA((len(CHUNKS) * MEMBERS,)),
+            pltpu.SemaphoreType.DMA(((len(CHUNKS) + 1) * MEMBERS,)),
             pltpu.SemaphoreType.DMA((1,)),
         ],
         limit=16 * MIB,
@@ -492,7 +515,7 @@
             send = call(
                 functools.partial(next_sends_body, chunk),
                 blocks(chunk[1]),
-                (sent1, sent2, w, own),
+                (sent1, later, w, own),
                 [VMEM_SPEC] * 3 + [ANY_SPEC],
                 us=0.3,
             )
@@ -535,7 +558,7 @@
             pltpu.VMEM((MEMBERS + 1, ROWS, COLS), BF16),
             tile,
         ],
-        (sent1, sent2, acc, *near[-1], loc_norm, weighted[-1]),
+        (sent1, later, acc, *near[-1], loc_norm, weighted[-1]),
         [VMEM_SPEC] * 8,
         us=0.5,
     )

time: 66.3 us -> 66.2 us (level)
  starting transfers between devices: 39.4 us -> 38.7 us
    ppermute x16, starting transfers between devices: 21 us -> 19.8 us  [trade(): return lax.ppermute(cells, axes, list(enumerate(to)))]
  transfers between devices with their start and end apart: 25 -> 25, of which waited for: 8 -> 8; matrix products, arithmetic and copies ran while one was open for 0% -> 0% of each run, Pallas kernels for 15% -> 16%
where the time goes in v7:
time: 66.2 us; the launch traced here: 66 us
  starting transfers between devices  38.7 us (58%)
  Pallas kernels  14.2 us (21%)
  waiting for transfers between devices  12.2 us (18%)
  between operations  0.84 us (1%)
    ppermute x16, starting transfers between devices, trade(): return lax.ppermute(cells, axes, list(enumerate(to)))  19.8 us
    ppermute x9, starting transfers between devices, swap(): return lax.ppermute(cells, axis, pairs)  19 us
    pallas_call x17, Pallas kernels, call(): pl.pallas_call(placed, out_shape=outs, in_specs=specs, out_specs=[VMEM_SP...  14.2 us
    ppermute x16, waiting for transfers between devices, trade(): return lax.ppermute(cells, axes, list(enumerate(to)))  9.11 us
    ppermute x9, waiting for transfers between devices, swap(): return lax.ppermute(cells, axis, pairs)  3.09 us
  transfers between devices with their start and end apart: 25, of which 8 were waited for; matrix products, arithmetic and copies ran while one was open for 0% of the time, Pallas kernels for 16%

profile of v7, /device:TPU:1, one launch (start us, length us, event | category | flops | bytes accessed | tf_op | source)
XLA Modules:
  0.0 66.0 jit_solution(16424199915668055664)
XLA Ops:
  0.6 0.8 %shard_map.86 = bf16[6,16,128]{2,1,0:T(8,128)(2,1)S(1)} custom-call(f32[5,16,128]{2,1,0:T(8,128)} %refs_4_.1, f32[16,128]{1,0:T(8,128)} %refs_1_.7), custom_call_target="tpu_custom_call" | custom-call | flops 500000 | bytes 1500000 | tf_op jit(solution)/shard_map/pallas_call | solution.py:31
  1.4 2.1 %collective-permute-start = (bf16[6,16,128]{2,1,0:T(8,128)(2,1)S(1)}, bf16[6,16,128]{2,1,0:T(8,128)(2,1)S(1)}, u32[]{:S(2)}, u32[]{:S(2)}) collective-permute-start(bf16[6,16,128]{2,1,0:T(8,128)(2,1)S(1)} %shard_map.86), channel_id=1, source_target_pairs={{0,4},{4,0},{8,12},{12,8},{16,20},{20,16},{24,28},{28,24},{1,5},{5... | collective-permute-start | bytes 73736 | tf_op jit(solution)/shard_map/ppermute | solution.py:55
  3.6 3.2 %collective-permute-start.1 = (bf16[6,16,128]{2,1,0:T(8,128)(2,1)S(1)}, bf16[6,16,128]{2,1,0:T(8,128)(2,1)S(1)}, u32[]{:S(2)}, u32[]{:S(2)}) collective-permute-start(bf16[6,16,128]{2,1,0:T(8,128)(2,1)S(1)} %shard_map.86), channel_id=1, source_target_pairs={{0,28},{4,8},{8,4},{12,16},{16,12},{20,24},{24,20},{28,0},{1,29},{... | collective-permute-start | bytes 73736 | tf_op jit(solution)/shard_map/ppermute | solution.py:55
  6.7 3.1 %shard_map.87 = (bf16[2,5,70,16,128]{4,3,2,1,0:T(8,128)(2,1)S(1)}, f32[70,16,128]{2,1,0:T(8,128)S(1)}, f32[70,16,128]{2,1,0:T(8,128)S(1)}) custom-call(bf16[5,2,280,16,128]{4,3,2,1,0:T(8,128)(2,1)} %bitcast.5, s32[16,128]{1,0:T(8,128)} %refs_1_.9, f32[280,16,128]{2,1,0:T(8,128)} %bitcast.8, f32[280,16,128]{2,1,0:T(8,128)} %bitcast.9), custom_call_target="tpu_custom_call" | custom-call | flops 2500000 | bytes 7500000 | tf_op jit(solution)/shard_map/pallas_call | solution.py:31
  10.0 1.3 %collective-permute-start.2 = (bf16[48,128]{1,0:T(8,128)(2,1)S(1)}, bf16[48,128]{1,0:T(8,128)(2,1)S(1)}, u32[]{:S(2)}, u32[]{:S(2)}) collective-permute-start(bf16[48,128]{1,0:T(8,128)(2,1)S(1)} %get-tuple-element.49), channel_id=1, source_target_pairs={{0,1},{1,0},{2,3},{3,2},{4,5},{5,4},{6,7},{7,6},{8,9},{9,8},{10,11... | collective-permute-start | bytes 36872 | tf_op jit(solution)/shard_map/ppermute | solution.py:55
  11.3 3.3 %collective-permute-start.3 = (bf16[48,128]{1,0:T(8,128)(2,1)S(1)}, bf16[48,128]{1,0:T(8,128)(2,1)S(1)}, u32[]{:S(2)}, u32[]{:S(2)}) collective-permute-start(bf16[48,128]{1,0:T(8,128)(2,1)S(1)} %get-tuple-element.49), channel_id=1, source_target_pairs={{0,3},{1,2},{2,1},{3,0},{4,7},{5,6},{6,5},{7,4},{8,11},{9,10},{10,... | collective-permute-start | bytes 36872 | tf_op jit(solution)/shard_map/ppermute | solution.py:55
  14.6 1.5 %shard_map.89.refs_7_.refs_1_ = bf16[1,5,40,16,128]{4,3,2,1,0:T(8,128)(2,1)S(1)} custom-call(bf16[5,2,280,16,128]{4,3,2,1,0:T(8,128)(2,1)} %bitcast.6, s32[16,128]{1,0:T(8,128)} %refs_1_.9), custom_call_target="tpu_custom_call" | custom-call | flops 2500000 | bytes 7500000 | tf_op jit(solution)/shard_map/pallas_call | solution.py:31
  16.1 1.9 %shard_map.90 = (f32[5,16,128]{2,1,0:T(8,128)S(1)}, f32[2,384,128]{2,1,0:T(8,128)S(1)}, f32[8,128]{1,0:T(8,128)S(1)}, bf16[40,16,128]{2,1,0:T(8,128)(2,1)S(1)}, ...) custom-call(f32[384,128]{1,0:T(8,128)S(1)} %get-tuple-element.47.refs_0_, ...), custom_call_target="tpu_custom_call" | custom-call | flops 2000000 | bytes 6000000 | tf_op jit(solution)/shard_map/pallas_call | solution.py:31
  18.0 3.1 %collective-permute-start.4 = (bf16[40,16,128]{2,1,0:T(8,128)(2,1)S(1)}, bf16[40,16,128]{2,1,0:T(8,128)(2,1)S(1)}, u32[]{:S(2)}, u32[]{:S(2)}) collective-permute-start(bf16[40,16,128]{2,1,0:T(8,128)(2,1)S(1)} %get-tuple-element.57), channel_id=1, source_target_pairs={{0,64},{32,96},{64,0},{96,32},{1,65},{33,97},{65,1},{97,33},{2,66}... | collective-permute-start | bytes 491528 | tf_op jit(solution)/shard_map/ppermute | solution.py:59
  21.4 0.4 collective-permute-start.6
  21.8 2.7 %shard_map.91 = (bf16[5,70,16,128]{3,2,1,0:T(8,128)(2,1)S(1)}, f32[70,16,128]{2,1,0:T(8,128)S(1)}, bf16[5,30,16,128]{3,2,1,0:T(8,128)(2,1)S(1)}) custom-call(bf16[5,2,280,16,128]{4,3,2,1,0:T(8,128)(2,1)} %bitcast.7, s32[16,128]{1,0:T(8,128)} %refs_1_.9, f32[5,16,128]{2,1,0:T(8,128)S(1)} %get-tuple-element.53.refs_2_), custom_call_target="tpu_custom_call" | custom-call | flops 2000000 | bytes 6000000 | tf_op jit(solution)/shard_map/pallas_call | solution.py:31
  24.5 0.4 shard_map.93
  24.9 2.6 %collective-permute-start.7 = (bf16[30,16,128]{2,1,0:T(8,128)(2,1)S(1)}, bf16[30,16,128]{2,1,0:T(8,128)(2,1)S(1)}, u32[]{:S(2)}, u32[]{:S(2)}) collective-permute-start(bf16[30,16,128]{2,1,0:T(8,128)(2,1)S(1)} %get-tuple-element.64), channel_id=1, source_target_pairs={{0,64},{32,96},{64,0},{96,32},{1,65},{33,97},{65,1},{97,33},{2,66}... | collective-permute-start | bytes 368648 | tf_op jit(solution)/shard_map/ppermute | solution.py:59
  28.3 0.6 collective-permute-done.5.refs_2_
  29.0 3.5 %collective-permute-start.10 = (bf16[40,16,128]{2,1,0:T(8,128)(2,1)S(1)}, bf16[40,16,128]{2,1,0:T(8,128)(2,1)S(1)}, u32[]{:S(2)}, u32[]{:S(2)}) collective-permute-start(bf16[40,16,128]{2,1,0:T(8,128)(2,1)S(1)} %get-tuple-element.63.refs_1_), channel_id=1, source_target_pairs={{0,96},{32,64},{64,32},{96,0},{1,97},{33,65},{65,33},{97,1},{2,98}... | collective-permute-start | bytes 491528 | tf_op jit(solution)/shard_map/ppermute | solution.py:59
  32.5 1.2 %collective-permute-done.8.refs_2_ = bf16[30,16,128]{2,1,0:T(8,128)(2,1)S(1)} collective-permute-done((bf16[30,16,128]{2,1,0:T(8,128)(2,1)S(1)}, bf16[30,16,128]{2,1,0:T(8,128)(2,1)S(1)}, u32[]{:S(2)}, u32[]{:S(2)}) %collective-permute-start.8) | collective-permute-done | bytes 122912 | tf_op jit(solution)/shard_map/ppermute | solution.py:59
  33.9 3.5 %collective-permute-start.14 = (bf16[31,16,128]{2,1,0:T(8,128)(2,1)S(1)}, bf16[31,16,128]{2,1,0:T(8,128)(2,1)S(1)}, u32[]{:S(2)}, u32[]{:S(2)}) collective-permute-start(bf16[31,16,128]{2,1,0:T(8,128)(2,1)S(1)} %shard_map.94.refs_2_.refs_7_), channel_id=1, source_target_pairs={{0,64},{32,96},{64,0},{96,32},{1,65},{33,97},{65,1},{97,33},{2,66}... | collective-permute-start | bytes 380936 | tf_op jit(solution)/shard_map/ppermute | solution.py:59
  37.8 1.2 %collective-permute-start.11 = (bf16[20,16,128]{2,1,0:T(8,128)(2,1)S(1)}, bf16[20,16,128]{2,1,0:T(8,128)(2,1)S(1)}, u32[]{:S(2)}, u32[]{:S(2)}) collective-permute-start(bf16[20,16,128]{2,1,0:T(8,128)(2,1)S(1)} %slice.12), channel_id=1, source_target_pairs={{0,32},{32,0},{64,96},{96,64},{1,33},{33,1},{65,97},{97,65},{2,34}... | collective-permute-start | bytes 245768 | tf_op jit(solution)/shard_map/ppermute | solution.py:59
  38.9 2.2 %collective-permute-start.13 = (bf16[20,16,128]{2,1,0:T(8,128)(2,1)S(1)}, bf16[20,16,128]{2,1,0:T(8,128)(2,1)S(1)}, u32[]{:S(2)}, u32[]{:S(2)}) collective-permute-start(bf16[20,16,128]{2,1,0:T(8,128)(2,1)S(1)} %slice.13), channel_id=1, source_target_pairs={{0,96},{32,64},{64,32},{96,0},{1,97},{33,65},{65,33},{97,1},{2,98}... | collective-permute-start | bytes 245768 | tf_op jit(solution)/shard_map/ppermute | solution.py:59
  41.5 2.7 %collective-permute-done.11.refs_3_ = bf16[20,16,128]{2,1,0:T(8,128)(2,1)S(1)} collective-permute-done((bf16[20,16,128]{2,1,0:T(8,128)(2,1)S(1)}, bf16[20,16,128]{2,1,0:T(8,128)(2,1)S(1)}, u32[]{:S(2)}, u32[]{:S(2)}) %collective-permute-start.11) | collective-permute-done | bytes 81952 | tf_op jit(solution)/shard_map/ppermute | solution.py:59
  44.2 2.0 %collective-permute-done.13.refs_4_ = bf16[20,16,128]{2,1,0:T(8,128)(2,1)S(1)} collective-permute-done((bf16[20,16,128]{2,1,0:T(8,128)(2,1)S(1)}, bf16[20,16,128]{2,1,0:T(8,128)(2,1)S(1)}, u32[]{:S(2)}, u32[]{:S(2)}) %collective-permute-start.13) | collective-permute-done | bytes 81952 | tf_op jit(solution)/shard_map/ppermute | solution.py:59
  46.2 0.6 shard_map.96.refs_2_
  46.8 0.5 shard_map.97
  47.4 3.1 %collective-permute-start.18 = (bf16[6,16,128]{2,1,0:T(8,128)(2,1)S(1)}, bf16[6,16,128]{2,1,0:T(8,128)(2,1)S(1)}, u32[]{:S(2)}, u32[]{:S(2)}) collective-permute-start(bf16[6,16,128]{2,1,0:T(8,128)(2,1)S(1)} %get-tuple-element.70), channel_id=1, source_target_pairs={{0,28},{4,8},{8,4},{12,16},{16,12},{20,24},{24,20},{28,0},{1,29},{... | collective-permute-start | bytes 73736 | tf_op jit(solution)/shard_map/ppermute | solution.py:55
  50.6 1.6 %collective-permute-done.18.refs_3_ = bf16[6,16,128]{2,1,0:T(8,128)(2,1)S(1)} collective-permute-done((bf16[6,16,128]{2,1,0:T(8,128)(2,1)S(1)}, bf16[6,16,128]{2,1,0:T(8,128)(2,1)S(1)}, u32[]{:S(2)}, u32[]{:S(2)}) %collective-permute-start.18) | collective-permute-done | bytes 24608 | tf_op jit(solution)/shard_map/ppermute | solution.py:55
  52.3 2.3 %collective-permute-done.19.refs_2_ = f32[8,128]{1,0:T(8,128)S(1)} collective-permute-done((f32[8,128]{1,0:T(8,128)S(1)}, f32[8,128]{1,0:T(8,128)S(1)}, u32[]{:S(2)}, u32[]{:S(2)}) %collective-permute-start.19) | collective-permute-done | bytes 4128 | tf_op jit(solution)/shard_map/ppermute | solution.py:59
  54.6 2.3 %collective-permute-start.20 = (bf16[64,128]{1,0:T(8,128)(2,1)S(1)}, bf16[64,128]{1,0:T(8,128)(2,1)S(1)}, u32[]{:S(2)}, u32[]{:S(2)}) collective-permute-start(bf16[64,128]{1,0:T(8,128)(2,1)S(1)} %get-tuple-element.74), channel_id=1, source_target_pairs={{0,1},{1,0},{2,3},{3,2},{4,5},{5,4},{6,7},{7,6},{8,9},{9,8},{10,11... | collective-permute-start | bytes 49160 | tf_op jit(solution)/shard_map/ppermute | solution.py:55
  57.0 3.3 %collective-permute-start.21 = (bf16[64,128]{1,0:T(8,128)(2,1)S(1)}, bf16[64,128]{1,0:T(8,128)(2,1)S(1)}, u32[]{:S(2)}, u32[]{:S(2)}) collective-permute-start(bf16[64,128]{1,0:T(8,128)(2,1)S(1)} %get-tuple-element.74), channel_id=1, source_target_pairs={{0,3},{1,2},{2,1},{3,0},{4,7},{5,6},{6,5},{7,4},{8,11},{9,10},{10,... | collective-permute-start | bytes 49160 | tf_op jit(solution)/shard_map/ppermute | solution.py:55
  60.2 1.4 %collective-permute-done.21.refs_2_ = bf16[64,128]{1,0:T(8,128)(2,1)S(1)} collective-permute-done((bf16[64,128]{1,0:T(8,128)(2,1)S(1)}, bf16[64,128]{1,0:T(8,128)(2,1)S(1)}, u32[]{:S(2)}, u32[]{:S(2)}) %collective-permute-start.21) | collective-permute-done | bytes 16416 | tf_op jit(solution)/shard_map/ppermute | solution.py:55
  62.2 1.6 %collective-permute-start.24 = (f32[8,128]{1,0:T(8,128)S(1)}, f32[8,128]{1,0:T(8,128)S(1)}, u32[]{:S(2)}, u32[]{:S(2)}) collective-permute-start(f32[8,128]{1,0:T(8,128)S(1)} %get-tuple-element.81), channel_id=1, source_target_pairs={{0,17},{1,16},{2,19},{3,18},{4,21},{5,20},{6,23},{7,22},{8,25},{9,... | collective-permute-start | bytes 12296 | tf_op jit(solution)/shard_map/ppermute | solution.py:59
  63.8 1.2 %shard_map.101.refs_0_ = f32[5,16,128]{2,1,0:T(8,128)S(1)} custom-call(f32[384,128]{1,0:T(8,128)S(1)} %get-tuple-element.71.refs_0_, bf16[64,128]{1,0:T(8,128)(2,1)S(1)} %collective-permute-done.20.refs_1_, bf16[64,128]{1,0:T(8,128)(2,1)S(1)} %collective-permute-done.21.refs_2_, f32[2,384,128]{2,1,0:T(8,128)S(1)} %get-tuple-element.79.refs_3_, ...), custom_call_target="tpu_custom_call" | custom-call | flops 3000000 | bytes 9000000 | tf_op jit(solution)/shard_map/pallas_call | solution.py:31
  65.4 0.6 shard_map.102
  (43 shorter events, 3.5 us)
Async XLA Ops:
  1.4 8.4 %collective-permute-start = (bf16[6,16,128]{2,1,0:T(8,128)(2,1)S(1)}, bf16[6,16,128]{2,1,0:T(8,128)(2,1)S(1)}, u32[]{:S(2)}, u32[]{:S(2)}) collective-permute-start(bf16[6,16,128]{2,1,0:T(8,128)(2,1)S(1)} %shard_map.86), channel_id=1, source_target_pairs={{0,4},{4,0},{8,12},{12,8},{16,20},{20,16},{24,28},{28,24},{1,5},{5... | collective-permute-start | bytes 73736 | tf_op jit(solution)/shard_map/ppermute | solution.py:55
  3.6 6.3 %collective-permute-start.1 = (bf16[6,16,128]{2,1,0:T(8,128)(2,1)S(1)}, bf16[6,16,128]{2,1,0:T(8,128)(2,1)S(1)}, u32[]{:S(2)}, u32[]{:S(2)}) collective-permute-start(bf16[6,16,128]{2,1,0:T(8,128)(2,1)S(1)} %shard_map.86), channel_id=1, source_target_pairs={{0,28},{4,8},{8,4},{12,16},{16,12},{20,24},{24,20},{28,0},{1,29},{... | collective-permute-start | bytes 73736 | tf_op jit(solution)/shard_map/ppermute | solution.py:55
  6.7 3.1 %copy-start = (f32[5,16,128]{2,1,0:T(8,128)S(1)}, f32[5,16,128]{2,1,0:T(8,128)}, u32[]{:S(2)}) copy-start(f32[5,16,128]{2,1,0:T(8,128)} %refs_4_.1) | copy-start | bytes 122884
  6.7 3.1 %copy-start.2 = (f32[16,128]{1,0:T(8,128)S(1)}, f32[16,128]{1,0:T(8,128)}, u32[]{:S(2)}) copy-start(f32[16,128]{1,0:T(8,128)} %refs_1_.7) | copy-start | bytes 24580
  10.0 6.1 %copy-start.1 = (f32[16,128]{1,0:T(8,128)S(1)}, f32[16,128]{1,0:T(8,128)}, u32[]{:S(2)}) copy-start(f32[16,128]{1,0:T(8,128)} %refs_6_.1) | copy-start | bytes 24580
  10.0 6.1 %collective-permute-start.2 = (bf16[48,128]{1,0:T(8,128)(2,1)S(1)}, bf16[48,128]{1,0:T(8,128)(2,1)S(1)}, u32[]{:S(2)}, u32[]{:S(2)}) collective-permute-start(bf16[48,128]{1,0:T(8,128)(2,1)S(1)} %get-tuple-element.49), channel_id=1, source_target_pairs={{0,1},{1,0},{2,3},{3,2},{4,5},{5,4},{6,7},{7,6},{8,9},{9,8},{10,11... | collective-permute-start | bytes 36872 | tf_op jit(solution)/shard_map/ppermute | solution.py:55
  11.3 4.8 %collective-permute-start.3 = (bf16[48,128]{1,0:T(8,128)(2,1)S(1)}, bf16[48,128]{1,0:T(8,128)(2,1)S(1)}, u32[]{:S(2)}, u32[]{:S(2)}) collective-permute-start(bf16[48,128]{1,0:T(8,128)(2,1)S(1)} %get-tuple-element.49), channel_id=1, source_target_pairs={{0,3},{1,2},{2,1},{3,0},{4,7},{5,6},{6,5},{7,4},{8,11},{9,10},{10,... | collective-permute-start | bytes 36872 | tf_op jit(solution)/shard_map/ppermute | solution.py:55
  18.0 9.9 %collective-permute-start.4 = (bf16[40,16,128]{2,1,0:T(8,128)(2,1)S(1)}, bf16[40,16,128]{2,1,0:T(8,128)(2,1)S(1)}, u32[]{:S(2)}, u32[]{:S(2)}) collective-permute-start(bf16[40,16,128]{2,1,0:T(8,128)(2,1)S(1)} %get-tuple-element.57), channel_id=1, source_target_pairs={{0,64},{32,96},{64,0},{96,32},{1,65},{33,97},{65,1},{97,33},{2,66}... | collective-permute-start | bytes 491528 | tf_op jit(solution)/shard_map/ppermute | solution.py:59
  21.1 7.7 %collective-permute-start.5 = (bf16[40,16,128]{2,1,0:T(8,128)(2,1)S(1)}, bf16[40,16,128]{2,1,0:T(8,128)(2,1)S(1)}, u32[]{:S(2)}, u32[]{:S(2)}) collective-permute-start(bf16[40,16,128]{2,1,0:T(8,128)(2,1)S(1)} %get-tuple-element.58), channel_id=1, source_target_pairs={{0,32},{32,0},{64,96},{96,64},{1,33},{33,1},{65,97},{97,65},{2,34}... | collective-permute-start | bytes 491528 | tf_op jit(solution)/shard_map/ppermute | solution.py:59
  21.4 7.4 %collective-permute-start.6 = (bf16[40,16,128]{2,1,0:T(8,128)(2,1)S(1)}, bf16[40,16,128]{2,1,0:T(8,128)(2,1)S(1)}, u32[]{:S(2)}, u32[]{:S(2)}) collective-permute-start(bf16[40,16,128]{2,1,0:T(8,128)(2,1)S(1)} %get-tuple-element.59), channel_id=1, source_target_pairs={{0,96},{32,64},{64,32},{96,0},{1,97},{33,65},{65,33},{97,1},{2,98}... | collective-permute-start | bytes 491528 | tf_op jit(solution)/shard_map/ppermute | solution.py:59
  24.9 7.6 %collective-permute-start.7 = (bf16[30,16,128]{2,1,0:T(8,128)(2,1)S(1)}, bf16[30,16,128]{2,1,0:T(8,128)(2,1)S(1)}, u32[]{:S(2)}, u32[]{:S(2)}) collective-permute-start(bf16[30,16,128]{2,1,0:T(8,128)(2,1)S(1)} %get-tuple-element.64), channel_id=1, source_target_pairs={{0,64},{32,96},{64,0},{96,32},{1,65},{33,97},{65,1},{97,33},{2,66}... | collective-permute-start | bytes 368648 | tf_op jit(solution)/shard_map/ppermute | solution.py:59
  27.6 6.1 %collective-permute-start.8 = (bf16[30,16,128]{2,1,0:T(8,128)(2,1)S(1)}, bf16[30,16,128]{2,1,0:T(8,128)(2,1)S(1)}, u32[]{:S(2)}, u32[]{:S(2)}) collective-permute-start(bf16[30,16,128]{2,1,0:T(8,128)(2,1)S(1)} %get-tuple-element.65), channel_id=1, source_target_pairs={{0,32},{32,0},{64,96},{96,64},{1,33},{33,1},{65,97},{97,65},{2,34}... | collective-permute-start | bytes 368648 | tf_op jit(solution)/shard_map/ppermute | solution.py:59
  27.9 5.8 %collective-permute-start.9 = (bf16[30,16,128]{2,1,0:T(8,128)(2,1)S(1)}, bf16[30,16,128]{2,1,0:T(8,128)(2,1)S(1)}, u32[]{:S(2)}, u32[]{:S(2)}) collective-permute-start(bf16[30,16,128]{2,1,0:T(8,128)(2,1)S(1)} %get-tuple-element.66), channel_id=1, source_target_pairs={{0,96},{32,64},{64,32},{96,0},{1,97},{33,65},{65,33},{97,1},{2,98}... | collective-permute-start | bytes 368648 | tf_op jit(solution)/shard_map/ppermute | solution.py:59
  29.0 8.7 %collective-permute-start.10 = (bf16[40,16,128]{2,1,0:T(8,128)(2,1)S(1)}, bf16[40,16,128]{2,1,0:T(8,128)(2,1)S(1)}, u32[]{:S(2)}, u32[]{:S(2)}) collective-permute-start(bf16[40,16,128]{2,1,0:T(8,128)(2,1)S(1)} %get-tuple-element.63.refs_1_), channel_id=1, source_target_pairs={{0,96},{32,64},{64,32},{96,0},{1,97},{33,65},{65,33},{97,1},{2,98}... | collective-permute-start | bytes 491528 | tf_op jit(solution)/shard_map/ppermute | solution.py:59
  32.5 6.4 %collective-permute-start.12 = (bf16[40,16,128]{2,1,0:T(8,128)(2,1)S(1)}, bf16[40,16,128]{2,1,0:T(8,128)(2,1)S(1)}, u32[]{:S(2)}, u32[]{:S(2)}) collective-permute-start(bf16[40,16,128]{2,1,0:T(8,128)(2,1)S(1)} %get-tuple-element.63.refs_1_), channel_id=1, source_target_pairs={{0,32},{32,0},{64,96},{96,64},{1,33},{33,1},{65,97},{97,65},{2,34}... | collective-permute-start | bytes 491528 | tf_op jit(solution)/shard_map/ppermute | solution.py:59
  33.9 12.9 %collective-permute-start.14 = (bf16[31,16,128]{2,1,0:T(8,128)(2,1)S(1)}, bf16[31,16,128]{2,1,0:T(8,128)(2,1)S(1)}, u32[]{:S(2)}, u32[]{:S(2)}) collective-permute-start(bf16[31,16,128]{2,1,0:T(8,128)(2,1)S(1)} %shard_map.94.refs_2_.refs_7_), channel_id=1, source_target_pairs={{0,64},{32,96},{64,0},{96,32},{1,65},{33,97},{65,1},{97,33},{2,66}... | collective-permute-start | bytes 380936 | tf_op jit(solution)/shard_map/ppermute | solution.py:59
  37.4 9.4 %collective-permute-start.15 = (bf16[31,16,128]{2,1,0:T(8,128)(2,1)S(1)}, bf16[31,16,128]{2,1,0:T(8,128)(2,1)S(1)}, u32[]{:S(2)}, u32[]{:S(2)}) collective-permute-start(bf16[31,16,128]{2,1,0:T(8,128)(2,1)S(1)} %shard_map.94.refs_2_.refs_7_), channel_id=1, source_target_pairs={{0,32},{32,0},{64,96},{96,64},{1,33},{33,1},{65,97},{97,65},{2,34}... | collective-permute-start | bytes 380936 | tf_op jit(solution)/shard_map/ppermute | solution.py:59
  37.6 9.2 %collective-permute-start.16 = (bf16[31,16,128]{2,1,0:T(8,128)(2,1)S(1)}, bf16[31,16,128]{2,1,0:T(8,128)(2,1)S(1)}, u32[]{:S(2)}, u32[]{:S(2)}) collective-permute-start(bf16[31,16,128]{2,1,0:T(8,128)(2,1)S(1)} %shard_map.94.refs_2_.refs_7_), channel_id=1, source_target_pairs={{0,96},{32,64},{64,32},{96,0},{1,97},{33,65},{65,33},{97,1},{2,98}... | collective-permute-start | bytes 380936 | tf_op jit(solution)/shard_map/ppermute | solution.py:59
  37.8 6.4 %collective-permute-start.11 = (bf16[20,16,128]{2,1,0:T(8,128)(2,1)S(1)}, bf16[20,16,128]{2,1,0:T(8,128)(2,1)S(1)}, u32[]{:S(2)}, u32[]{:S(2)}) collective-permute-start(bf16[20,16,128]{2,1,0:T(8,128)(2,1)S(1)} %slice.12), channel_id=1, source_target_pairs={{0,32},{32,0},{64,96},{96,64},{1,33},{33,1},{65,97},{97,65},{2,34}... | collective-permute-start | bytes 245768 | tf_op jit(solution)/shard_map/ppermute | solution.py:59
  38.9 7.2 %collective-permute-start.13 = (bf16[20,16,128]{2,1,0:T(8,128)(2,1)S(1)}, bf16[20,16,128]{2,1,0:T(8,128)(2,1)S(1)}, u32[]{:S(2)}, u32[]{:S(2)}) collective-permute-start(bf16[20,16,128]{2,1,0:T(8,128)(2,1)S(1)} %slice.13), channel_id=1, source_target_pairs={{0,96},{32,64},{64,32},{96,0},{1,97},{33,65},{65,33},{97,1},{2,98}... | collective-permute-start | bytes 245768 | tf_op jit(solution)/shard_map/ppermute | solution.py:59
  47.3 3.3 %collective-permute-start.17 = (bf16[6,16,128]{2,1,0:T(8,128)(2,1)S(1)}, bf16[6,16,128]{2,1,0:T(8,128)(2,1)S(1)}, u32[]{:S(2)}, u32[]{:S(2)}) collective-permute-start(bf16[6,16,128]{2,1,0:T(8,128)(2,1)S(1)} %get-tuple-element.70), channel_id=1, source_target_pairs={{0,4},{4,0},{8,12},{12,8},{16,20},{20,16},{24,28},{28,24},{1,5},{5... | collective-permute-start | bytes 73736 | tf_op jit(solution)/shard_map/ppermute | solution.py:55
  47.4 4.9 %collective-permute-start.18 = (bf16[6,16,128]{2,1,0:T(8,128)(2,1)S(1)}, bf16[6,16,128]{2,1,0:T(8,128)(2,1)S(1)}, u32[]{:S(2)}, u32[]{:S(2)}) collective-permute-start(bf16[6,16,128]{2,1,0:T(8,128)(2,1)S(1)} %get-tuple-element.70), channel_id=1, source_target_pairs={{0,28},{4,8},{8,4},{12,16},{16,12},{20,24},{24,20},{28,0},{1,29},{... | collective-permute-start | bytes 73736 | tf_op jit(solution)/shard_map/ppermute | solution.py:55
  50.4 4.2 %collective-permute-start.19 = (f32[8,128]{1,0:T(8,128)S(1)}, f32[8,128]{1,0:T(8,128)S(1)}, u32[]{:S(2)}, u32[]{:S(2)}) collective-permute-start(f32[8,128]{1,0:T(8,128)S(1)} %get-tuple-element.69.refs_1_), channel_id=1, source_target_pairs={{0,8},{4,12},{8,0},{12,4},{16,24},{20,28},{24,16},{28,20},{1,9},{5... | collective-permute-start | bytes 12296 | tf_op jit(solution)/shard_map/ppermute | solution.py:59
  54.6 5.6 %collective-permute-start.20 = (bf16[64,128]{1,0:T(8,128)(2,1)S(1)}, bf16[64,128]{1,0:T(8,128)(2,1)S(1)}, u32[]{:S(2)}, u32[]{:S(2)}) collective-permute-start(bf16[64,128]{1,0:T(8,128)(2,1)S(1)} %get-tuple-element.74), channel_id=1, source_target_pairs={{0,1},{1,0},{2,3},{3,2},{4,5},{5,4},{6,7},{7,6},{8,9},{9,8},{10,11... | collective-permute-start | bytes 49160 | tf_op jit(solution)/shard_map/ppermute | solution.py:55
  57.0 4.7 %collective-permute-start.21 = (bf16[64,128]{1,0:T(8,128)(2,1)S(1)}, bf16[64,128]{1,0:T(8,128)(2,1)S(1)}, u32[]{:S(2)}, u32[]{:S(2)}) collective-permute-start(bf16[64,128]{1,0:T(8,128)(2,1)S(1)} %get-tuple-element.74), channel_id=1, source_target_pairs={{0,3},{1,2},{2,1},{3,0},{4,7},{5,6},{6,5},{7,4},{8,11},{9,10},{10,... | collective-permute-start | bytes 49160 | tf_op jit(solution)/shard_map/ppermute | solution.py:55
  61.7 3.7 %collective-permute-start.23 = (f32[16,128]{1,0:T(8,128)S(1)}, f32[16,128]{1,0:T(8,128)S(1)}, u32[]{:S(2)}, u32[]{:S(2)}) collective-permute-start(f32[16,128]{1,0:T(8,128)S(1)} %get-tuple-element.80.refs_1_), channel_id=1, source_target_pairs={{0,16},{4,20},{8,24},{12,28},{16,0},{20,4},{24,8},{28,12},{1,17},{... | collective-permute-start | bytes 24584 | tf_op jit(solution)/shard_map/ppermute | solution.py:59
  61.8 3.2 %collective-permute-start.22 = (f32[8,128]{1,0:T(8,128)S(1)}, f32[8,128]{1,0:T(8,128)S(1)}, u32[]{:S(2)}, u32[]{:S(2)}) collective-permute-start(f32[8,128]{1,0:T(8,128)S(1)} %get-tuple-element.81), channel_id=1, source_target_pairs={{0,1},{1,0},{2,3},{3,2},{4,5},{5,4},{6,7},{7,6},{8,9},{9,8},{10,11... | collective-permute-start | bytes 12296 | tf_op jit(solution)/shard_map/ppermute | solution.py:55
  62.2 3.2 %collective-permute-start.24 = (f32[8,128]{1,0:T(8,128)S(1)}, f32[8,128]{1,0:T(8,128)S(1)}, u32[]{:S(2)}, u32[]{:S(2)}) collective-permute-start(f32[8,128]{1,0:T(8,128)S(1)} %get-tuple-element.81), channel_id=1, source_target_pairs={{0,17},{1,16},{2,19},{3,18},{4,21},{5,20},{6,23},{7,22},{8,25},{9,... | collective-permute-start | bytes 12296 | tf_op jit(solution)/shard_map/ppermute | solution.py:59
